TPU v7x, 256 devices: a whole 4x4x8 slice. The times are simulated.
256 devices in a mesh: grp: 8 (over z_lo, y), rep: 32 (over x, z_hi, core).
Axes of the slice: x: 4, y: 4, z: 8 (z_hi: 4, z_lo: 2; z = z_hi * 2 + z_lo), core: 2. Of those that a mesh axis runs over, the one named last changes fastest.
Arguments:
- tokens: bfloat16 [1024, 14848], P('grp', 'rep'), may hold values from -6 to 6
- first_weight: bfloat16 [14848, 7424], P('rep', 'grp'), may hold values from -0.046875 to 0.046875
- second_weight: bfloat16 [7424, 14848], P('grp', 'rep'), may hold values from -0.0625 to 0.0625
- cotangent: bfloat16 [1024, 14848], P('grp', 'rep'), may hold values from -6 to 6
Outputs:
- output: bfloat16 [1024, 14848], P('grp', 'rep')
- input_grad: bfloat16 [1024, 14848], P('grp', 'rep')
- first_grad: bfloat16 [14848, 7424], P('rep', 'grp')
- second_grad: bfloat16 [7424, 14848], P('grp', 'rep')
All inputs are finite; a program needn't handle non-finite values.
Results may differ from a plain program's by a relative error of at most 0.017.
Values may be sent and summed in bfloat16 or wider, within the bound.
No kernel may reach another device: no remote copies, remote signals or barrier semaphores. Data moves between devices by JAX's collectives and lax.ppermute only.
A program may use at most 128 MiB of HBM per device.

v0:
```python
import math

import jax
import jax.numpy as jnp
from jax import lax
from jax.sharding import PartitionSpec as P


def slope(hidden):
    normal_cdf = 0.5 * (1.0 + jax.scipy.special.erf(hidden * (1.0 / math.sqrt(2.0))))
    density = jnp.exp(-0.5 * hidden * hidden) * (1.0 / math.sqrt(2.0 * math.pi))
    return normal_cdf + hidden * density


def rounded(term):
    return lax.optimization_barrier(term.astype(jnp.bfloat16)).astype(jnp.float32)


def inner_rows(left, right):
    return lax.dot_general(
        left, right, (((0,), (0,)), ((), ())), preferred_element_type=jnp.float32
    )


def inner_cols(left, right):
    return lax.dot_general(
        left, right, (((1,), (1,)), ((), ())), preferred_element_type=jnp.float32
    )


def forward_hidden(partial_value):
    summed = lax.psum(partial_value, "rep")
    active = jax.nn.gelu(summed, approximate=False).astype(jnp.bfloat16)
    return (active, summed)


def backward_hidden(partial_value, stored):
    summed = lax.psum(partial_value, "rep")
    deltas = (summed * slope(stored)).astype(jnp.bfloat16)
    return deltas


def body(tokens, first_weight, second_weight, cotangent):
    tok_rows = tokens.shape[0]
    group_count = lax.axis_size("grp")
    factor = float(tok_rows * group_count) ** (-0.5)
    first_full = lax.all_gather(first_weight, "grp", axis=1, tiled=True)
    second_full = lax.all_gather(second_weight, "grp", axis=0, tiled=True)
    partial_value = jnp.dot(tokens, first_full, preferred_element_type=jnp.float32)
    active, stored = forward_hidden(partial_value)
    output = jnp.dot(active, second_full, preferred_element_type=jnp.float32).astype(jnp.bfloat16)
    upward = inner_cols(cotangent, second_full)
    deltas = backward_hidden(upward, stored)
    input_grad = inner_cols(deltas, first_full).astype(jnp.bfloat16)
    columns = deltas
    first_sum = lax.psum_scatter(
        rounded(factor * inner_rows(columns, tokens)).astype(jnp.bfloat16),
        "grp",
        scatter_dimension=0,
        tiled=True,
    ).astype(jnp.float32)
    columns = active
    second_sum = lax.psum_scatter(
        rounded(factor * inner_rows(columns, cotangent)).astype(jnp.bfloat16),
        "grp",
        scatter_dimension=0,
        tiled=True,
    )
    first_grad = first_sum.T.astype(jnp.bfloat16)
    return (output, input_grad, first_grad, second_sum)


def solution(mesh):
    in_specs = (P("grp", "rep"), P("rep", "grp"), P("grp", "rep"), P("grp", "rep"))
    out_specs = (P("grp", "rep"), P("grp", "rep"), P("rep", "grp"), P("grp", "rep"))
    return jax.shard_map(body, mesh=mesh, in_specs=in_specs, out_specs=out_specs, check_vma=False)
```

profile of v0, /device:TPU:1, one launch (start us, length us, event | category | flops | bytes accessed | tf_op | source)
XLA Modules:
  0.0 726.6 jit_solution(15817100667031839993)
XLA Ops:
  7.2 0.0 copy-start
  7.2 0.0 all-gather.3.cloned.1.call-start
  7.2 2.2 copy.9
  9.4 0.0 all-gather.3.cloned.1.call-update
  9.5 0.0 all-gather.5.cloned.1.call-start
  9.5 0.7 all-gather.5.cloned.1.call-update
  10.2 0.0 copy-start.5
  10.2 0.0 all-reduce.3.cloned.1.call-start
  10.3 91.1 %all-gather.3.cloned.1.call-done = bf16[464,7424]{0,1:T(8,128)(2,1)} async-done(((bf16[464,928]{0,1:T(8,128)(2,1)}), bf16[464,7424]{0,1:T(8,128)(2,1)}) %all-gather.3.cloned.1.call-update) | async-done | bytes 6889488 | tf_op jit(solution)/shard_map/all_gather | solution.py:47
  101.4 0.0 copy-done
  101.4 7.6 %fusion.16 = f32[128,7424]{1,0:T(8,128)} fusion(bf16[128,464]{0,1:T(8,128)(2,1)S(1)} %copy-done, bf16[464,7424]{0,1:T(8,128)(2,1)} %all-gather.3.cloned.1.call-done), kind=kOutput, calls=%fused_computation.30 | convolution fusion | flops 881852416 | bytes 10809344 | tf_op jit(solution)/shard_map/dot_general | solution.py:49
  109.0 80.1 %all-gather.5.cloned.1.call-done = bf16[7424,464]{1,0:T(8,128)(2,1)} async-done(((bf16[928,464]{1,0:T(8,128)(2,1)}), bf16[7424,464]{1,0:T(8,128)(2,1)}) %all-gather.5.cloned.1.call-update) | async-done | bytes 6889488 | tf_op jit(solution)/shard_map/all_gather | solution.py:48
  189.1 0.0 copy-done.5
  189.1 7.8 %fusion.17 = f32[128,7424]{1,0:T(8,128)} fusion(bf16[128,464]{0,1:T(8,128)(2,1)S(1)} %copy-done.5, bf16[7424,464]{1,0:T(8,128)(2,1)} %all-gather.5.cloned.1.call-done), kind=kOutput, calls=%fused_computation.31 | convolution fusion | flops 881852416 | bytes 10809344 | tf_op jit(solution)/shard_map/dot_general | solution.py:26
  196.9 0.0 all-reduce.3.cloned.1.call-update
  197.0 0.0 reduce-scatter.7.cloned.1.call-start
  197.0 317.3 %all-reduce.3.cloned.1.call-done = (f32[128,7424]{1,0:T(8,128)}, f32[128,7424]{1,0:T(8,128)}) async-done(((f32[128,7424]{1,0:T(8,128)}, f32[128,7424]{1,0:T(8,128)}), (f32[128,7424]{1,0:T(8,128)}, f32[128,7424]{1,0:T(8,128)})) %all-reduce.3.cloned.1.call-update) | async-done | bytes 7602192 | tf_op jit(solution)/shard_map/psum | solution.py:32
  514.3 10.9 %fusion.8 = (bf16[128,7424]{1,0:T(8,128)(2,1)S(1)}, bf16[128,7424]{1,0:T(8,128)(2,1)S(1)}) fusion(f32[128,7424]{1,0:T(8,128)} %get-tuple-element.13, f32[128,7424]{1,0:T(8,128)} %get-tuple-element.12), kind=kLoop, calls=%fused_computation.12 | loop fusion | flops 71270400 | bytes 11403264 | tf_op jit(solution)/shard_map/convert_element_type | solution.py:39
  525.2 0.0 copy-start.2
  525.2 0.0 copy-start.4
  525.2 1.2 copy-done.2
  526.4 4.7 multiply_convert_fusion.1
  531.2 10.2 %copy.11 = bf16[7424,464]{1,0:T(8,128)(2,1)} copy(bf16[7424,464]{0,1:T(8,128)(2,1)} %multiply_convert_fusion.1) | data formatting | bytes 13778944
  541.4 0.0 reduce-scatter.7.cloned.1.call-update
  541.4 0.2 reduce-scatter.9.cloned.1.call-start
  541.6 0.0 copy-done.4
  541.6 4.7 multiply_convert_fusion
  546.4 10.2 %copy.13 = bf16[7424,464]{1,0:T(8,128)(2,1)} copy(bf16[7424,464]{0,1:T(8,128)(2,1)} %multiply_convert_fusion) | data formatting | bytes 13778944
  556.6 0.0 slice-start
  556.6 0.0 reduce-scatter.9.cloned.1.call-update
  556.6 0.0 slice-start.1
  556.6 0.0 copy-start.3
  556.6 0.0 copy-start.1
  556.6 7.4 %convolution_convert_fusion.1 = bf16[128,464]{0,1:T(8,128)(2,1)} fusion(bf16[128,7424]{1,0:T(8,128)(2,1)} %copy-done.4, bf16[7424,464]{1,0:T(8,128)(2,1)} %all-gather.5.cloned.1.call-done), kind=kOutput, calls=%fused_computation.29 | convolution fusion | flops 881911808 | bytes 8908800 | tf_op jit(solution)/shard_map/dot_general | solution.py:51
  564.1 0.0 slice-done
  564.1 0.0 slice-done.1
  564.1 0.0 copy-done.3
  564.1 3.6 convolution_convert_fusion
  567.7 62.5 %reduce-scatter.7.cloned.1.call-done = bf16[928,464]{1,0:T(8,128)(2,1)} async-done(((bf16[7424,464]{1,0:T(8,128)(2,1)}), bf16[928,464]{1,0:T(8,128)(2,1)}) %reduce-scatter.7.cloned.1.call-update) | async-done | bytes 861200
  630.2 2.2 copy.12
  632.4 87.6 %reduce-scatter.9.cloned.1.call-done = bf16[928,464]{1,0:T(8,128)(2,1)} async-done(((bf16[7424,464]{1,0:T(8,128)(2,1)}), bf16[928,464]{1,0:T(8,128)(2,1)}) %reduce-scatter.9.cloned.1.call-update) | async-done | bytes 861200
  720.0 0.0 copy-done.1
  (1 shorter events, 0.0 us)
Async XLA Ops:
  7.2 94.2 %copy-start = (bf16[128,464]{0,1:T(8,128)(2,1)S(1)}, bf16[128,464]{0,1:T(8,128)(2,1)}, u32[]{:S(2)}) copy-start(bf16[128,464]{0,1:T(8,128)(2,1)} %param.4) | copy-start | bytes 356356
  7.2 94.2 %all-gather.3.cloned.1.call-start = ((), (), s32[]{:S(2)}) async-start(), calls=%async_computation.2 | async-start | bytes 8552448 | tf_op jit(solution)/shard_map/all_gather | solution.py:47
  9.5 179.7 %all-gather.5.cloned.1.call-start = ((), (), s32[]{:S(2)}) async-start(), calls=%async_computation.3 | async-start | bytes 8552448 | tf_op jit(solution)/shard_map/all_gather | solution.py:48
  10.2 178.9 %copy-start.5 = (bf16[128,464]{0,1:T(8,128)(2,1)S(1)}, bf16[128,464]{0,1:T(8,128)(2,1)}, u32[]{:S(2)}) copy-start(bf16[128,464]{0,1:T(8,128)(2,1)} %param.7) | copy-start | bytes 356356
  10.2 504.0 %all-reduce.3.cloned.1.call-start = ((), (), s32[]{:S(2)}) async-start(), calls=%async_computation.6 | async-start | bytes 15204352 | tf_op jit(solution)/shard_map/psum | solution.py:32
  197.0 433.2 %reduce-scatter.7.cloned.1.call-start = ((), (), s32[]{:S(2)}) async-start(), calls=%async_computation.4 | async-start | bytes 8552448
  525.2 1.2 copy-start.2
  525.2 16.4 %copy-start.4 = (bf16[128,7424]{1,0:T(8,128)(2,1)}, bf16[128,7424]{1,0:T(8,128)(2,1)S(1)}, u32[]{:S(2)}) copy-start(bf16[128,7424]{1,0:T(8,128)(2,1)S(1)} %get-tuple-element.15) | copy-start | bytes 5701636
  541.4 178.6 %reduce-scatter.9.cloned.1.call-start = ((), (), s32[]{:S(2)}) async-start(), calls=%async_computation.5 | async-start | bytes 8552448
  556.6 7.5 %slice-start = ((s8[7602176]{0:T(1024)(128)(4,1)}), s8[3407872]{0:T(1024)(128)(4,1)S(1)}, s32[]{:S(2)}) async-start(s8[7602176]{0:T(1024)(128)(4,1)} %bitcast.15), calls=%async_computation.7 | async-start | bytes 6815744
  556.6 7.5 %slice-start.1 = ((s8[7602176]{0:T(1024)(128)(4,1)}), s8[4194304]{0:T(1024)(128)(4,1)S(1)}, s32[]{:S(2)}) async-start(s8[7602176]{0:T(1024)(128)(4,1)} %bitcast.15), calls=%async_computation.8 | async-start | bytes 8388608
  556.6 7.5 %copy-start.3 = (bf16[128,7424]{1,0:T(8,128)(2,1)S(1)}, bf16[128,7424]{1,0:T(8,128)(2,1)}, u32[]{:S(2)}) copy-start(bf16[128,7424]{1,0:T(8,128)(2,1)} %copy-done.2) | copy-start | bytes 5701636
  556.6 163.4 %copy-start.1 = (bf16[128,464]{0,1:T(8,128)(2,1)S(1)}, bf16[128,464]{0,1:T(8,128)(2,1)}, u32[]{:S(2)}) copy-start(bf16[128,464]{0,1:T(8,128)(2,1)} %param.4) | copy-start | bytes 356356
Sparse Core Ops, SparseCore 0:
  10.4 90.9 all-gather.2
  103.2 85.8 all-gather.4
  197.1 317.1 all-reduce.2
  541.5 88.6 reduce-scatter.6
  633.4 86.6 reduce-scatter.8
where the time goes:
time: 727 us
  waiting for transfers between devices  639 us (88%)
  matrix products  36 us (5%)
  local copies, waits for them, and re-layouts  26.1 us (4%)
  between operations  13.9 us (2%)
  other arithmetic  10.9 us (1%)
    psum x1, waiting for transfers between devices, forward_hidden(): summed = lax.psum(partial_value, 'rep')  317 us
    unnamed x7, waiting for transfers between devices  151 us
    all_gather x1, waiting for transfers between devices, body(): first_full = lax.all_gather(first_weight, 'grp', axis=1, tiled=True)  91.1 us
    all_gather x1, waiting for transfers between devices, body(): second_full = lax.all_gather(second_weight, 'grp', axis=0, tiled=True)  80.1 us
    unnamed x20, local copies, waits for them, and re-layouts  26.1 us
  transfers between devices with their start and end apart: 5, of which 5 were waited for; matrix products, arithmetic and copies ran while one was open for 5% of the time, Pallas kernels for 0%

commit v1 on v0

v1 whole, which is shorter than its diff:
```python
import math

import jax
import jax.numpy as jnp
from jax import lax
from jax.sharding import PartitionSpec as P

BF = jnp.bfloat16
F32 = jnp.float32
GRP = 8
X, Z, C = 4, 4, 2


def rep_index(x, z, c):
    return (x * Z + z) * C + c


X_GROUPS = [[rep_index(x, z, c) for x in range(X)] for z in range(Z) for c in range(C)]
Z_GROUPS = [[rep_index(x, z, c) for z in range(Z)] for x in range(X) for c in range(C)]
C_GROUPS = [[rep_index(x, z, c) for c in range(C)] for x in range(X) for z in range(Z)]


def slope(hidden):
    normal_cdf = 0.5 * (1.0 + jax.scipy.special.erf(hidden * (1.0 / math.sqrt(2.0))))
    density = jnp.exp(-0.5 * hidden * hidden) * (1.0 / math.sqrt(2.0 * math.pi))
    return normal_cdf + hidden * density


def dot(left, right, dims):
    return lax.dot_general(left, right, (dims, ((), ())), preferred_element_type=F32)


def exchange(value, groups, axis="rep"):
    return lax.all_to_all(value, axis, 0, 0, axis_index_groups=groups)


def scatter_sum(value, groups, axis="rep"):
    return jnp.sum(exchange(value.astype(BF), groups, axis).astype(F32), axis=0)


def gather(value, groups, count, axis="rep"):
    return exchange(jnp.broadcast_to(value[None], (count,) + value.shape), groups, axis)


def body(tokens, first_weight, second_weight, cotangent):
    rows, width = tokens.shape
    hid = first_weight.shape[1]
    total = rows * GRP
    factor = float(total) ** (-0.5)
    part = total // (C * X * Z)

    both = gather(jnp.stack([tokens, cotangent]), None, GRP, "grp")
    tok = both[:, 0].reshape(total, width)
    cot = both[:, 1].reshape(total, width)

    partial_hidden = dot(tok, first_weight, ((1,), (0,)))
    partial_upward = dot(cot, second_weight, ((1,), (1,)))
    sums = jnp.stack(
        [v.reshape(C, X, Z, part, hid) for v in (partial_hidden, partial_upward)], axis=3
    )
    sums = scatter_sum(sums, C_GROUPS)
    sums = scatter_sum(sums, X_GROUPS)
    sums = scatter_sum(sums, Z_GROUPS)
    hidden, upward = sums[0], sums[1]
    active = jax.nn.gelu(hidden, approximate=False).astype(BF)
    deltas = (upward * slope(hidden)).astype(BF)

    acts = jnp.stack([active, deltas])
    acts = gather(acts, Z_GROUPS, Z)
    acts = gather(acts, X_GROUPS, X)
    acts = gather(acts, C_GROUPS, C)
    active = acts[:, :, :, 0].reshape(total, hid)
    deltas = acts[:, :, :, 1].reshape(total, hid)

    out = dot(active, second_weight, ((1,), (0,)))
    back = dot(deltas, first_weight, ((1,), (1,)))
    outs = jnp.stack([v.reshape(GRP, rows, width) for v in (out, back)], axis=1)
    outs = scatter_sum(outs, None, "grp").astype(BF)
    first_grad = (factor * dot(tok, deltas, ((0,), (0,)))).astype(BF)
    second_grad = (factor * dot(active, cot, ((0,), (0,)))).astype(BF)
    return (outs[0], outs[1], first_grad, second_grad)


def solution(mesh):
    in_specs = (P("grp", "rep"), P("rep", "grp"), P("grp", "rep"), P("grp", "rep"))
    out_specs = (P("grp", "rep"), P("grp", "rep"), P("rep", "grp"), P("grp", "rep"))
    return jax.shard_map(body, mesh=mesh, in_specs=in_specs, out_specs=out_specs, check_vma=False)
```

time: 727 us -> 203 us (0.28)
  waiting for transfers between devices: 639 us -> 17.9 us
  blocking collectives: 0 us -> 146 us
  matrix products: 36 us -> 10.7 us
  local copies, waits for them, and re-layouts: 26.1 us -> 12 us
  between operations: 13.9 us -> 0.87 us
    psum x1 -> x0, waiting for transfers between devices: 317 us -> none  [forward_hidden(): summed = lax.psum(partial_value, 'rep')]
    all_gather x2 -> x0, waiting for transfers between devices: 171 us -> none  [the longest x1 91.1 us: body(): first_full = lax.all_gather(first_weight, 'grp', axis=1, tiled=True)]
    unnamed x7 -> x0, waiting for transfers between devices: 151 us -> none
    all_to_all x0 -> x7, blocking collectives: none -> 146 us  [exchange(): return lax.all_to_all(value, axis, 0, 0, axis_index_groups=groups)]
    dot_general x6, matrix products: 36 us -> 10.7 us  [dot(): lax.dot_general(left, right, (dims, ((), ())), preferred_element_type=F32)]
    unnamed x20 -> x16, local copies, waits for them, and re-layouts: 26.1 us -> 1.81 us
    all_to_all x0 -> x1, waiting for transfers between devices: none -> 17.9 us  [exchange(): return lax.all_to_all(value, axis, 0, 0, axis_index_groups=groups)]
    convert_element_type x1, other arithmetic: 10.9 us -> 0.34 us  [body(): active = jax.nn.gelu(hidden, approximate=False).astype(BF)]
  transfers between devices with their start and end apart: 5 -> 1, of which waited for: 5 -> 1; matrix products, arithmetic and copies ran while one was open for 5% -> 2% of each run, Pallas kernels for 0% -> 0%
where the time goes in v1:
time: 203 us
  blocking collectives  146 us (72%)
  waiting for transfers between devices  17.9 us (9%)
  local copies, waits for them, and re-layouts  12 us (6%)
  other arithmetic  11.2 us (6%)
  matrix products  10.7 us (5%)
  starting transfers between devices  4.5 us (2%)
    all_to_all x7, blocking collectives, exchange(): return lax.all_to_all(value, axis, 0, 0, axis_index_groups=groups)  146 us
    all_to_all x1, waiting for transfers between devices, exchange(): return lax.all_to_all(value, axis, 0, 0, axis_index_groups=groups)  17.9 us
    dot_general x6, matrix products, dot(): lax.dot_general(left, right, (dims, ((), ())), preferred_element_type=F32)  10.7 us
    reduce_sum x4, other arithmetic, scatter_sum(): return jnp.sum(exchange(value.astype(BF), groups, axis).astype(F32), axis=0)  9.19 us
    all_to_all x1, starting transfers between devices, exchange(): return lax.all_to_all(value, axis, 0, 0, axis_index_groups=groups)  4.5 us
  transfers between devices with their start and end apart: 1, of which 1 were waited for; matrix products, arithmetic and copies ran while one was open for 2% of the time, Pallas kernels for 0%

profile of v1, /device:TPU:1, one launch (start us, length us, event | category | flops | bytes accessed | tf_op | source)
XLA Modules:
  0.0 202.8 jit_solution(8421650696057025714)
XLA Ops:
  0.6 0.0 copy-start
  0.6 1.1 pad_maximum_fusion.2
  1.7 0.2 broadcast_in_dim.8
  2.0 30.0 %all_to_all.40 = bf16[8,2,128,464]{2,3,1,0:T(8,128)(2,1)S(1)} all-to-all(bf16[8,2,128,464]{2,3,1,0:T(8,128)(2,1)S(1)} %broadcast_in_dim.8), channel_id=1, replica_groups=mesh['grp'=8,'rep'=32] {'grp'}, dimensions={0} | all-to-all | bytes 3801088 | tf_op jit(solution)/shard_map/all_to_all | solution.py:34
  32.0 0.1 fusion.27
  32.1 1.3 copy.50
  33.4 1.3 copy.51
  34.7 0.0 copy-done
  34.7 2.7 %convert_bitcast_fusion = bf16[2,4,4,1,32,928]{5,4,2,1,0,3:T(8,128)(2,1)S(1)} fusion(bf16[2,4,4,32,464]{4,3,2,1,0:T(8,128)(2,1)} %bitcast.61, bf16[928,464]{1,0:T(8,128)(2,1)S(1)} %copy-done), kind=kOutput, calls=%fused_computation.1 | convolution fusion | flops 882802688 | bytes 3712000 | tf_op jit(solution)/shard_map/dot_general | solution.py:30
  37.4 0.0 copy-done.5
  37.4 0.0 copy-done.6
  37.4 1.3 convert_bitcast_fusion.1
  38.7 0.4 pad_maximum_fusion
  39.1 0.8 copy.52
  39.9 10.1 %all_to_all.41 = bf16[2,4,4,2,32,928]{5,4,2,1,3,0:T(8,128)(2,1)} all-to-all(bf16[2,4,4,2,32,928]{5,4,2,1,3,0:T(8,128)(2,1)S(1)} %copy.52), channel_id=1, replica_groups={{0,1},{2,3},{4,5},{6,7},{8,9},{10,11},{12,13},{14,15},{16,17},{18,19},{..., dimensions={0} | all-to-all | bytes 7602176 | tf_op jit(solution)/shard_map/all_to_all | solution.py:34
  50.0 5.2 %reduce_sum.45 = bf16[4,4,2,32,928]{4,3,1,0,2:T(8,128)(2,1)} reduce(bf16[2,4,4,2,32,928]{5,4,2,1,3,0:T(8,128)(2,1)} %all_to_all.41, bf16[]{:T(256)} %constant.34.clone.1), dimensions={0}, to_apply=%region_0.0 | reduce | flops 950272 | bytes 5701634 | tf_op jit(solution)/shard_map/reduce_sum | solution.py:38
  55.2 1.8 copy.54
  57.0 29.4 %all_to_all.42 = bf16[4,4,2,32,928]{4,3,1,2,0:T(8,128)(2,1)} all-to-all(bf16[4,4,2,32,928]{4,3,1,2,0:T(8,128)(2,1)S(1)} %copy.54), channel_id=1, replica_groups={{0,8,16,24},{1,9,17,25},{2,10,18,26},{3,11,19,27},{4,12,20,28},{5,13,21..., dimensions={0} | all-to-all | bytes 3801088 | tf_op jit(solution)/shard_map/all_to_all | solution.py:34
  86.4 2.0 %reduce_sum.46 = bf16[4,2,32,928]{3,2,0,1:T(8,128)(2,1)S(1)} reduce(bf16[4,4,2,32,928]{4,3,1,2,0:T(8,128)(2,1)} %all_to_all.42, bf16[]{:T(256)} %constant.34.clone.1), dimensions={0}, to_apply=%region_1.0 | reduce | flops 712704 | bytes 2375682 | tf_op jit(solution)/shard_map/reduce_sum | solution.py:38
  88.4 21.7 %all_to_all.43 = bf16[4,2,32,928]{3,2,1,0:T(8,128)(2,1)S(1)} all-to-all(bf16[4,2,32,928]{3,2,1,0:T(8,128)(2,1)S(1)} %copy.56), channel_id=1, replica_groups={{0,2,4,6},{1,3,5,7},{8,10,12,14},{9,11,13,15},{16,18,20,22},{17,19,21,2..., dimensions={0} | all-to-all | bytes 950272 | tf_op jit(solution)/shard_map/all_to_all | solution.py:34
  110.1 0.1 convert_reduce_fusion
  110.2 0.3 fusion.12
  110.6 0.1 broadcast_in_dim.9
  110.6 17.9 %all_to_all.44 = bf16[4,2,32,928]{3,2,1,0:T(8,128)(2,1)S(1)} all-to-all(bf16[4,2,32,928]{3,2,1,0:T(8,128)(2,1)S(1)} %broadcast_in_dim.9), channel_id=1, replica_groups={{0,2,4,6},{1,3,5,7},{8,10,12,14},{9,11,13,15},{16,18,20,22},{17,19,21,2..., dimensions={0} | all-to-all | bytes 950272 | tf_op jit(solution)/shard_map/all_to_all | solution.py:34
  128.5 0.3 broadcast_in_dim.10
  128.8 25.6 %all_to_all.45 = bf16[4,4,2,32,928]{4,3,1,2,0:T(8,128)(2,1)S(1)} all-to-all(bf16[4,4,2,32,928]{4,3,1,2,0:T(8,128)(2,1)S(1)} %broadcast_in_dim.10), channel_id=1, replica_groups={{0,8,16,24},{1,9,17,25},{2,10,18,26},{3,11,19,27},{4,12,20,28},{5,13,21..., dimensions={0} | all-to-all | bytes 3801088 | tf_op jit(solution)/shard_map/all_to_all | solution.py:34
  154.4 0.2 copy.58
  154.7 0.7 broadcast_in_dim.11
  155.3 10.9 %all_to_all.46 = bf16[2,4,4,2,32,928]{5,4,2,1,3,0:T(8,128)(2,1)S(1)} all-to-all(bf16[2,4,4,2,32,928]{5,4,2,1,3,0:T(8,128)(2,1)S(1)} %broadcast_in_dim.11), channel_id=1, replica_groups={{0,1},{2,3},{4,5},{6,7},{8,9},{10,11},{12,13},{14,15},{16,17},{18,19},{..., dimensions={0} | all-to-all | bytes 7602176 | tf_op jit(solution)/shard_map/all_to_all | solution.py:34
  166.2 0.8 fusion.26
  167.0 0.0 copy-start.3
  167.0 0.0 copy-start.1
  167.0 0.0 copy-start.7
  167.1 1.2 fusion
  168.3 0.1 copy-done.3
  168.3 0.7 copy-done.1
  169.0 1.2 fusion.1
  170.2 0.2 pad_maximum_fusion.1
  170.4 1.4 copy.62
  171.8 4.5 %all-to-all-start.7 = ((bf16[8,2,128,464]{2,3,1,0:T(8,128)(2,1)}), bf16[8,2,128,464]{2,3,1,0:T(8,128)(2,1)}, u32[]{:S(2)}, u32[]{:S(2)}) async-start(bf16[8,2,128,464]{2,3,1,0:T(8,128)(2,1)} %copy.62), calls=%async_computation.7 | async-start | bytes 3801088 | tf_op jit(solution)/shard_map/all_to_all | solution.py:34
  176.3 0.2 copy.63
  176.5 0.2 copy.64
  176.8 1.1 copy-done.4
  177.9 2.3 %multiply_convert_fusion = bf16[928,464]{1,0:T(8,128)(2,1)} fusion(bf16[1024,928]{1,0:T(8,128)(2,1)S(1)} %bitcast.59, bf16[58,8,8,128]{3,2,1,0:T(8,128)(2,1)S(1)} %bitcast.63), kind=kOutput, calls=%fused_computation.4 | convolution fusion | flops 882713600 | bytes 3712000 | tf_op jit(solution)/shard_map/dot_general | solution.py:30
  180.2 2.1 %multiply_convert_fusion.1 = bf16[464,928]{1,0:T(8,128)(2,1)} fusion(bf16[1024,928]{1,0:T(8,128)(2,1)S(1)} %bitcast.57, bf16[58,8,8,128]{3,2,1,0:T(8,128)(2,1)S(1)} %bitcast.62), kind=kOutput, calls=%fused_computation.5 | convolution fusion | flops 882713600 | bytes 3712000 | tf_op jit(solution)/shard_map/dot_general | solution.py:30
  182.3 17.9 %all-to-all-done.7 = bf16[8,2,128,464]{2,3,1,0:T(8,128)(2,1)} async-done(((bf16[8,2,128,464]{2,3,1,0:T(8,128)(2,1)}), bf16[8,2,128,464]{2,3,1,0:T(8,128)(2,1)}, u32[]{:S(2)}, u32[]{:S(2)}) %all-to-all-start.7) | async-done | bytes 1900576 | tf_op jit(solution)/shard_map/all_to_all | solution.py:34
  200.2 1.9 reduce_sum.48
  202.1 0.7 slice_bitcast_fusion
  (9 shorter events, 0.1 us)
Async XLA Ops:
  0.6 34.1 %copy-start = (bf16[928,464]{1,0:T(8,128)(2,1)S(1)}, bf16[928,464]{1,0:T(8,128)(2,1)}, u32[]{:S(2)}) copy-start(bf16[928,464]{1,0:T(8,128)(2,1)} %param.6) | copy-start | bytes 2583556
  34.7 2.7 %copy-start.5 = (bf16[8,1,128,464]{3,2,0,1:T(8,128)(2,1)S(1)}, bf16[8,1,128,464]{3,2,0,1:T(8,128)(2,1)}, u32[]{:S(2)}) copy-start(bf16[8,1,128,464]{3,2,0,1:T(8,128)(2,1)} %copy.50) | copy-start | bytes 2850820
  34.7 2.7 %copy-start.6 = (bf16[464,928]{1,0:T(8,128)(2,1)S(1)}, bf16[464,928]{1,0:T(8,128)(2,1)}, u32[]{:S(2)}) copy-start(bf16[464,928]{1,0:T(8,128)(2,1)} %param.5) | copy-start | bytes 2583556
  167.0 1.3 copy-start.3
  167.0 2.0 copy-start.1
  167.0 2.0 copy-start.7
  171.8 28.4 %all-to-all-start.7 = ((bf16[8,2,128,464]{2,3,1,0:T(8,128)(2,1)}), bf16[8,2,128,464]{2,3,1,0:T(8,128)(2,1)}, u32[]{:S(2)}, u32[]{:S(2)}) async-start(bf16[8,2,128,464]{2,3,1,0:T(8,128)(2,1)} %copy.62), calls=%async_computation.7 | async-start | bytes 3801088 | tf_op jit(solution)/shard_map/all_to_all | solution.py:34
  176.3 1.6 copy-start.4
  177.8 2.3 %copy-start.2 = (bf16[2,4,4,1,32,928]{5,4,2,1,3,0:T(8,128)(2,1)S(1)}, bf16[2,4,4,1,32,928]{5,4,2,1,3,0:T(8,128)(2,1)}, u32[]{:S(2)}) copy-start(bf16[2,4,4,1,32,928]{5,4,2,1,3,0:T(8,128)(2,1)} %copy-done.1) | copy-start | bytes 5701636

commit v2 on v1

v2 whole, which is shorter than its diff:
```python
import math

import jax
import jax.numpy as jnp
from jax import lax
from jax.experimental import pallas as pl
from jax.experimental.pallas import tpu as pltpu
from jax.sharding import PartitionSpec as P

BF = jnp.bfloat16
F32 = jnp.float32
GRP = 8
X, Z, C = 4, 4, 2
LANES = 128


def rep_index(x, z, c):
    return (x * Z + z) * C + c


def rep_pairs(dx, dc):
    return [
        (rep_index(x, z, c), rep_index((x + dx) % X, z, (c + dc) % C))
        for x in range(X)
        for z in range(Z)
        for c in range(C)
    ]


Z_GROUPS = [[rep_index(x, z, c) for z in range(Z)] for x in range(X) for c in range(C)]


def after(value, *others):
    return lax.optimization_barrier((value,) + others)[0]


def slope(hidden):
    normal_cdf = 0.5 * (1.0 + jax.scipy.special.erf(hidden * (1.0 / math.sqrt(2.0))))
    density = jnp.exp(-0.5 * hidden * hidden) * (1.0 / math.sqrt(2.0 * math.pi))
    return normal_cdf + hidden * density


def dot(left, right, dims):
    return lax.dot_general(left, right, (dims, ((), ())), preferred_element_type=F32)


PLAIN = ((1,), (0,))
LAST = ((1,), (1,))


def shaped(shape, dtype):
    return jax.ShapeDtypeStruct(shape, dtype)


def kernel_call(kernel, outs, flops, pos, operands, scratch=()):
    moved = sum(math.prod(o.shape) * o.dtype.itemsize for o in [*operands, *outs])
    vmem = pl.BlockSpec(memory_space=pltpu.VMEM)
    return pl.pallas_call(
        kernel,
        out_shape=outs,
        in_specs=[pl.BlockSpec(memory_space=pltpu.SMEM)] + [vmem] * len(operands),
        out_specs=[vmem] * len(outs),
        scratch_shapes=scratch,
        compiler_params=pltpu.CompilerParams(vmem_limit_bytes=24 * 1024 * 1024),
        cost_estimate=pl.CostEstimate(flops=flops, bytes_accessed=moved, transcendentals=0),
    )(pos, *operands)


def half_of(ref, half, x):
    return jnp.concatenate([ref[half * X + ((x + d) & 3)] for d in range(X)], axis=1)


def wide(refs):
    return jnp.concatenate([ref[...] for ref in refs], axis=1)


def block(value, d):
    return value[:, d * LANES : (d + 1) * LANES]


def other_half(pos, rows, weight):
    depth, width = weight.shape

    def kernel(pos_ref, rows_ref, weight_ref, out_ref):
        rows = half_of(rows_ref, 1 - pos_ref[1], pos_ref[0])
        product = dot(weight_ref[...], rows, PLAIN).astype(BF)
        for d in range(X):
            out_ref[d] = block(product, d)

    outs = [shaped((X, depth, LANES), BF)]
    return kernel_call(kernel, outs, 2 * depth * width * X * LANES, pos, [rows, weight])[0]


def own_half(pos, rows, weight, arrived):
    depth, width = weight.shape

    def kernel(pos_ref, rows_ref, weight_ref, arrived_ref, keep_ref, *sent):
        product = dot(weight_ref[...], half_of(rows_ref, pos_ref[1], pos_ref[0]), PLAIN)
        for d in range(X):
            total = block(product, d) + arrived_ref[d].astype(F32)
            if d == 0:
                keep_ref[...] = total
            else:
                sent[d - 1][...] = total.astype(BF)

    outs = [shaped((depth, LANES), F32)] + [shaped((depth, LANES), BF)] * (X - 1)
    flops = 2 * depth * width * X * LANES
    keep, *sent = kernel_call(kernel, outs, flops, pos, [rows, weight, arrived])
    return keep, sent


def both_halves(pos, blocks, weight):
    depth, width = weight.shape

    def kernel(pos_ref, *refs):
        weight_ref, out_ref = refs[-2:]
        x, c = pos_ref[0], pos_ref[1]
        for part, half in ((refs[:X], c), (refs[X : 2 * X], 1 - c)):
            product = dot(weight_ref[...], wide(part), PLAIN).astype(BF)
            for d in range(X):
                out_ref[half * X + ((x + d) & 3)] = block(product, d)

    outs = [shaped((2 * X, depth, LANES), BF)]
    flops = 2 * depth * width * 2 * X * LANES
    return kernel_call(kernel, outs, flops, pos, [*blocks, weight])[0]


def weight_grad(pos, factor, rows, blocks, rows_first):
    width, depth = rows.shape[1], blocks[0].shape[0]

    def kernel(pos_ref, rows_ref, *refs):
        out_ref, total = refs[-1], None
        x, c = pos_ref[0], pos_ref[1]
        for part, half in ((refs[:X], c), (refs[X : 2 * X], 1 - c)):
            pair = half_of(rows_ref, half, x), wide(part)
            term = dot(*(pair if rows_first else pair[::-1]), LAST)
            total = term if total is None else total + term
        out_ref[...] = (factor * total).astype(BF)

    outs = [shaped((width, depth) if rows_first else (depth, width), BF)]
    flops = 2 * depth * width * 2 * X * LANES
    return kernel_call(kernel, outs, flops, pos, [rows, *blocks])[0]


def exchange(value, axis, groups=None):
    return lax.all_to_all(value, axis, 0, 0, axis_index_groups=groups)


def copies(value, count):
    return jnp.broadcast_to(value[None], (count,) + value.shape)


def swap_cores(value):
    return lax.ppermute(value, "rep", rep_pairs(0, 1))


def move_x(value, d):
    return lax.ppermute(value, "rep", rep_pairs(d, 0))


def total_of(value):
    return jnp.sum(value.astype(F32), axis=0)


def sum_x(keep, sent):
    arrived = lax.optimization_barrier(tuple(move_x(sent[d - 1], d) for d in range(1, X)))
    for part in arrived:
        keep = keep + part.astype(F32)
    return keep.astype(BF)


def sum_z(value):
    value = value.reshape(Z, value.shape[0] // Z, LANES)
    return total_of(exchange(value, "rep", Z_GROUPS))


def spread_z(value):
    whole = exchange(copies(value, Z), "rep", Z_GROUPS)
    return whole.reshape(Z * value.shape[0], LANES)


def spread_x(value):
    own = [value] + [move_x(value, -d) for d in range(1, X)]
    return own + [swap_cores(part) for part in own]


def body(tokens, first_weight, second_weight, cotangent):
    factor = float(GRP * tokens.shape[0]) ** (-0.5)
    rep = lax.axis_index("rep")
    pos = jnp.stack([rep >> 3, rep & 1]).astype(jnp.int32)

    tok = exchange(copies(tokens.T, GRP), "grp")
    first_turned, second_turned = first_weight.T, second_weight.T
    sent = other_half(pos, tok, first_turned)
    cot = exchange(copies(after(cotangent.T, sent), GRP), "grp")
    keep, sent = own_half(pos, tok, first_turned, swap_cores(sent))
    value = sum_x(keep, sent)
    hidden = sum_z(value)
    active = jax.nn.gelu(hidden, approximate=False).astype(BF)
    active, hidden = lax.optimization_barrier((active, hidden))

    sent = other_half(pos, after(cot, value), second_weight)
    keep, sent = own_half(pos, cot, second_weight, swap_cores(sent))
    upward = sum_z(sum_x(keep, sent))
    deltas = (upward * slope(hidden)).astype(BF)

    act = spread_x(spread_z(active))
    dlt = spread_x(spread_z(deltas))
    out = exchange(both_halves(pos, act, second_turned), "grp")
    back = exchange(both_halves(pos, dlt, first_weight), "grp")
    second_grad = weight_grad(pos, factor, cot, act, False)
    first_grad = weight_grad(pos, factor, tok, dlt, True)
    return (total_of(out).astype(BF).T, total_of(back).astype(BF).T, first_grad, second_grad)


def solution(mesh):
    in_specs = (P("grp", "rep"), P("rep", "grp"), P("grp", "rep"), P("grp", "rep"))
    out_specs = (P("grp", "rep"), P("grp", "rep"), P("rep", "grp"), P("grp", "rep"))
    return jax.shard_map(body, mesh=mesh, in_specs=in_specs, out_specs=out_specs, check_vma=False)
```

time: 203 us -> 167 us (0.82)
  blocking collectives: 146 us -> 16.2 us
  starting transfers between devices: 4.5 us -> 59.4 us
  waiting for transfers between devices: 17.9 us -> 48.3 us
  Pallas kernels: 0 us -> 16.4 us
  matrix products: 10.7 us -> 0 us
  local copies, waits for them, and re-layouts: 12 us -> 18.3 us
  other arithmetic: 11.2 us -> 6.79 us
    all_to_all x7 -> x1, blocking collectives: 146 us -> 16.2 us  [exchange(): return lax.all_to_all(value, axis, 0, 0, axis_index_groups=groups)]
    ppermute x0 -> x22, starting transfers between devices: none -> 28.1 us  [the longest x12 15.4 us: move_x(): return lax.ppermute(value, 'rep', rep_pairs(d, 0))]
    all_to_all x1 -> x7, starting transfers between devices: 4.5 us -> 31.2 us  [exchange(): return lax.all_to_all(value, axis, 0, 0, axis_index_groups=groups)]
    ppermute x0 -> x22, waiting for transfers between devices: none -> 23.9 us  [the longest x12 19.8 us: move_x(): return lax.ppermute(value, 'rep', rep_pairs(d, 0))]
    pallas_call x0 -> x8, Pallas kernels: none -> 16.4 us  [kernel_call(): pl.pallas_call(kernel, out_shape=outs, in_specs=[pl.BlockSpec(memory_spac...]
    unnamed x16 -> x48, local copies, waits for them, and re-layouts: 1.81 us -> 13.7 us
    dot_general x6 -> x0, matrix products: 10.7 us -> none  [dot(): lax.dot_general(left, right, (dims, ((), ())), preferred_element_type=F32)]
    all_to_all x1 -> x7, waiting for transfers between devices: 17.9 us -> 24.4 us  [exchange(): return lax.all_to_all(value, axis, 0, 0, axis_index_groups=groups)]
  transfers between devices with their start and end apart: 1 -> 29, of which waited for: 1 -> 15; matrix products, arithmetic and copies ran while one was open for 2% -> 5% of each run, Pallas kernels for 0% -> 7%
where the time goes in v2:
time: 167 us; the launch traced here: 166 us
  starting transfers between devices  59.4 us (36%)
  waiting for transfers between devices  48.3 us (29%)
  local copies, waits for them, and re-layouts  18.3 us (11%)
  Pallas kernels  16.4 us (10%)
  blocking collectives  16.2 us (10%)
  other arithmetic  6.79 us (4%)
    all_to_all x7, starting transfers between devices, exchange(): return lax.all_to_all(value, axis, 0, 0, axis_index_groups=groups)  31.2 us
    all_to_all x7, waiting for transfers between devices, exchange(): return lax.all_to_all(value, axis, 0, 0, axis_index_groups=groups)  24.4 us
    ppermute x12, waiting for transfers between devices, move_x(): return lax.ppermute(value, 'rep', rep_pairs(d, 0))  19.8 us
    pallas_call x8, Pallas kernels, kernel_call(): pl.pallas_call(kernel, out_shape=outs, in_specs=[pl.BlockSpec(memory_spac...  16.4 us
    all_to_all x1, blocking collectives, exchange(): return lax.all_to_all(value, axis, 0, 0, axis_index_groups=groups)  16.2 us
    ppermute x12, starting transfers between devices, move_x(): return lax.ppermute(value, 'rep', rep_pairs(d, 0))  15.4 us
    unnamed x48, local copies, waits for them, and re-layouts  13.7 us
    ppermute x10, starting transfers between devices, swap_cores(): return lax.ppermute(value, 'rep', rep_pairs(0, 1))  12.8 us
  transfers between devices with their start and end apart: 29, of which 15 were waited for; matrix products, arithmetic and copies ran while one was open for 5% of the time, Pallas kernels for 7%

profile of v2, /device:TPU:1, one launch (start us, length us, event | category | flops | bytes accessed | tf_op | source)
XLA Modules:
  0.0 166.2 jit_solution(17582967773664981588)
XLA Ops:
  0.6 2.0 %broadcast_in_dim.8 = bf16[8,464,128]{2,1,0:T(8,128)(2,1)} broadcast(bf16[464,128]{1,0:T(8,128)(2,1)} %bitcast.29), dimensions={1,2} | broadcast | bytes 1069056 | tf_op jit(solution)/shard_map/broadcast_in_dim | solution.py:150
  2.6 6.5 %all-to-all-start = ((bf16[8,464,128]{2,1,0:T(8,128)(2,1)}), bf16[8,464,128]{2,1,0:T(8,128)(2,1)S(1)}, u32[]{:S(2)}, u32[]{:S(2)}) async-start(bf16[8,464,128]{2,1,0:T(8,128)(2,1)} %broadcast_in_dim.8), calls=%async_computation | async-start | bytes 1900544 | tf_op jit(solution)/shard_map/all_to_all | solution.py:146
  9.9 12.8 %all-to-all-done.rows_ref = bf16[8,464,128]{2,1,0:T(8,128)(2,1)S(1)} async-done(((bf16[8,464,128]{2,1,0:T(8,128)(2,1)}), bf16[8,464,128]{2,1,0:T(8,128)(2,1)S(1)}, u32[]{:S(2)}, u32[]{:S(2)}) %all-to-all-start) | async-done | bytes 950304 | tf_op jit(solution)/shard_map/all_to_all | solution.py:146
  22.7 1.2 shard_map.75
  23.9 1.2 broadcast_in_dim.10
  25.1 4.0 %all-to-all-start.4 = ((bf16[8,464,128]{2,1,0:T(8,128)(2,1)}), bf16[8,464,128]{2,1,0:T(8,128)(2,1)S(1)}, u32[]{:S(2)}, u32[]{:S(2)}) async-start(bf16[8,464,128]{2,1,0:T(8,128)(2,1)} %broadcast_in_dim.10), calls=%async_computation.4 | async-start | bytes 1900544 | tf_op jit(solution)/shard_map/all_to_all | solution.py:146
  29.9 2.4 %collective-permute-done.arrived_ref = bf16[4,928,128]{2,1,0:T(8,128)(2,1)S(1)} collective-permute-done((bf16[4,928,128]{2,1,0:T(8,128)(2,1)}, bf16[4,928,128]{2,1,0:T(8,128)(2,1)S(1)}, u32[]{:S(2)}, u32[]{:S(2)}) %collective-permute-start) | collective-permute-done | bytes 950304 | tf_op jit(solution)/shard_map/ppermute | solution.py:154
  32.3 1.2 shard_map.76
  33.5 1.3 collective-permute-start.1
  34.8 2.5 %collective-permute-start.2 = (bf16[928,128]{1,0:T(8,128)(2,1)S(1)}, bf16[928,128]{1,0:T(8,128)(2,1)S(1)}, u32[]{:S(2)}, u32[]{:S(2)}) collective-permute-start(bf16[928,128]{1,0:T(8,128)(2,1)S(1)} %get-tuple-element.24), channel_id=1, source_target_pairs={{0,16},{1,17},{2,18},{3,19},{4,20},{5,21},{6,22},{7,23},{8,24},{9,... | collective-permute-start | bytes 712712 | tf_op jit(solution)/shard_map/ppermute | solution.py:158
  37.3 1.2 collective-permute-start.3
  38.4 3.4 %collective-permute-done.1 = bf16[928,128]{1,0:T(8,128)(2,1)S(1)} collective-permute-done((bf16[928,128]{1,0:T(8,128)(2,1)S(1)}, bf16[928,128]{1,0:T(8,128)(2,1)S(1)}, u32[]{:S(2)}, u32[]{:S(2)}) %collective-permute-start.1) | collective-permute-done | bytes 237600 | tf_op jit(solution)/shard_map/ppermute | solution.py:158
  41.8 6.1 %collective-permute-done.2 = bf16[928,128]{1,0:T(8,128)(2,1)S(1)} collective-permute-done((bf16[928,128]{1,0:T(8,128)(2,1)S(1)}, bf16[928,128]{1,0:T(8,128)(2,1)S(1)}, u32[]{:S(2)}, u32[]{:S(2)}) %collective-permute-start.2) | collective-permute-done | bytes 237600 | tf_op jit(solution)/shard_map/ppermute | solution.py:158
  48.0 1.2 shard_map.78
  49.2 1.3 collective-permute-start.11
  50.5 16.2 %all_to_all.40 = bf16[4,232,128]{2,1,0:T(8,128)(2,1)S(1)} all-to-all(bf16[4,232,128]{2,1,0:T(8,128)(2,1)S(1)} %bitcast.28), channel_id=1, replica_groups={{0,2,4,6},{1,3,5,7},{8,10,12,14},{9,11,13,15},{16,18,20,22},{17,19,21,2..., dimensions={0} | all-to-all | bytes 475136 | tf_op jit(solution)/shard_map/all_to_all | solution.py:146
  66.8 2.0 %shard_map.79 = (f32[928,128]{1,0:T(8,128)S(1)}, bf16[928,128]{1,0:T(8,128)(2,1)}, bf16[928,128]{1,0:T(8,128)(2,1)}, bf16[928,128]{1,0:T(8,128)(2,1)S(1)}) custom-call(s32[2]{0:T(128)S(1)} %pad_add_fusion.pos_ref, bf16[8,464,128]{2,1,0:T(8,128)(2,1)S(1)} %all-to-all-done.4.rows_ref, bf16[928,464]{1,0:T(8,128)(2,1)S(1)} %copy-done, ...), custom_call_target="tpu_custom_call" | custom-call | flops 440926208 | bytes 3949568 | tf_op jit(solution)/shard_map/pallas_call | solution.py:58
  69.6 1.1 collective-permute-start.12
  70.6 2.1 %collective-permute-start.13 = (bf16[928,128]{1,0:T(8,128)(2,1)}, bf16[928,128]{1,0:T(8,128)(2,1)}, u32[]{:S(2)}, u32[]{:S(2)}) collective-permute-start(bf16[928,128]{1,0:T(8,128)(2,1)} %get-tuple-element.34), channel_id=1, source_target_pairs={{0,16},{1,17},{2,18},{3,19},{4,20},{5,21},{6,22},{7,23},{8,24},{9,... | collective-permute-start | bytes 712712 | tf_op jit(solution)/shard_map/ppermute | solution.py:158
  72.7 1.3 collective-permute-start.14
  75.0 3.7 %all-to-all-start.2 = ((bf16[4,232,128]{2,1,0:T(8,128)(2,1)}), bf16[4,232,128]{2,1,0:T(8,128)(2,1)S(1)}, u32[]{:S(2)}, u32[]{:S(2)}) async-start(bf16[4,232,128]{2,1,0:T(8,128)(2,1)} %broadcast_in_dim.9), calls=%async_computation.2 | async-start | bytes 475136 | tf_op jit(solution)/shard_map/all_to_all | solution.py:146
  78.7 2.1 %collective-permute-done.13 = bf16[928,128]{1,0:T(8,128)(2,1)} collective-permute-done((bf16[928,128]{1,0:T(8,128)(2,1)}, bf16[928,128]{1,0:T(8,128)(2,1)}, u32[]{:S(2)}, u32[]{:S(2)}) %collective-permute-start.13) | collective-permute-done | bytes 237600 | tf_op jit(solution)/shard_map/ppermute | solution.py:158
  81.4 2.1 %add_convert_fusion = bf16[928,128]{1,0:T(8,128)(2,1)} fusion(bf16[928,128]{1,0:T(8,128)(2,1)} %collective-permute-done.14, bf16[928,128]{1,0:T(8,128)(2,1)} %collective-permute-done.13, f32[928,128]{1,0:T(8,128)} %copy-done.21, bf16[928,128]{1,0:T(8,128)(2,1)} %collective-permute-done.12), kind=kLoop, calls=%fused_computation.1 | loop fusion | flops 831488 | bytes 1425408 | tf_op jit(solution)/shard_map/convert_element_type | solution.py:169
  83.5 3.7 %all-to-all-done.2 = bf16[4,232,128]{2,1,0:T(8,128)(2,1)S(1)} async-done(((bf16[4,232,128]{2,1,0:T(8,128)(2,1)}), bf16[4,232,128]{2,1,0:T(8,128)(2,1)S(1)}, u32[]{:S(2)}, u32[]{:S(2)}) %all-to-all-start.2) | async-done | bytes 237600 | tf_op jit(solution)/shard_map/all_to_all | solution.py:146
  87.2 3.4 %all-to-all-start.5 = ((bf16[4,232,128]{2,1,0:T(8,128)(2,1)}), bf16[4,232,128]{2,1,0:T(8,128)(2,1)S(1)}, u32[]{:S(2)}, u32[]{:S(2)}) async-start(bf16[4,232,128]{2,1,0:T(8,128)(2,1)} %bitcast.27), calls=%async_computation.5 | async-start | bytes 475136 | tf_op jit(solution)/shard_map/all_to_all | solution.py:146
  91.0 2.9 %collective-permute-start.5 = (bf16[928,128]{1,0:T(8,128)(2,1)S(1)}, bf16[928,128]{1,0:T(8,128)(2,1)}, u32[]{:S(2)}, u32[]{:S(2)}) collective-permute-start(bf16[928,128]{1,0:T(8,128)(2,1)S(1)} %bitcast.16), channel_id=1, source_target_pairs={{0,16},{1,17},{2,18},{3,19},{4,20},{5,21},{6,22},{7,23},{8,24},{9,... | collective-permute-start | bytes 712712 | tf_op jit(solution)/shard_map/ppermute | solution.py:158
  93.9 5.2 %all-to-all-done.5 = bf16[4,232,128]{2,1,0:T(8,128)(2,1)S(1)} async-done(((bf16[4,232,128]{2,1,0:T(8,128)(2,1)}), bf16[4,232,128]{2,1,0:T(8,128)(2,1)S(1)}, u32[]{:S(2)}, u32[]{:S(2)}) %all-to-all-start.5) | async-done | bytes 237600 | tf_op jit(solution)/shard_map/all_to_all | solution.py:146
  99.9 3.4 %all-to-all-start.6 = ((bf16[4,232,128]{2,1,0:T(8,128)(2,1)}), bf16[4,232,128]{2,1,0:T(8,128)(2,1)S(1)}, u32[]{:S(2)}, u32[]{:S(2)}) async-start(bf16[4,232,128]{2,1,0:T(8,128)(2,1)} %broadcast_in_dim.11), calls=%async_computation.6 | async-start | bytes 475136 | tf_op jit(solution)/shard_map/all_to_all | solution.py:146
  103.3 5.3 %collective-permute-start.7 = (bf16[928,128]{1,0:T(8,128)(2,1)S(1)}, bf16[928,128]{1,0:T(8,128)(2,1)}, u32[]{:S(2)}, u32[]{:S(2)}) collective-permute-start(bf16[928,128]{1,0:T(8,128)(2,1)S(1)} %bitcast.18), channel_id=1, source_target_pairs={{0,1},{1,0},{2,3},{3,2},{4,5},{5,4},{6,7},{7,6},{8,9},{9,8},{10,11... | collective-permute-start | bytes 712712 | tf_op jit(solution)/shard_map/ppermute | solution.py:154
  109.2 1.4 copy.9
  111.1 1.2 copy-done.5
  112.3 2.7 %shard_map.77 = bf16[8,464,128]{2,1,0:T(8,128)(2,1)S(1)} custom-call(s32[2]{0:T(128)S(1)} %pad_add_fusion.pos_ref, bf16[928,128]{1,0:T(8,128)(2,1)S(1)} %bitcast.19, bf16[928,128]{1,0:T(8,128)(2,1)} %collective-permute-done.4.refs_1_, bf16[928,128]{1,0:T(8,128)(2,1)} %collective-permute-done.5.refs_2_, bf16[928,128]{1,0:T(8,128)(2,1)} %collective-permute-done.6.refs_3_, ...), custom_call_target="tpu_custom_call" | custom-call | flops 881852416 | bytes 3712000 | tf_op jit(solution)/shard_map/pallas_call | solution.py:58
  116.0 5.1 %all-to-all-start.3 = ((bf16[8,464,128]{2,1,0:T(8,128)(2,1)}), bf16[8,464,128]{2,1,0:T(8,128)(2,1)}, u32[]{:S(2)}, u32[]{:S(2)}) async-start(bf16[8,464,128]{2,1,0:T(8,128)(2,1)} %copy-done.3), calls=%async_computation.3 | async-start | bytes 1900544 | tf_op jit(solution)/shard_map/all_to_all | solution.py:146
  122.2 1.7 %collective-permute-start.15 = (bf16[928,128]{1,0:T(8,128)(2,1)S(1)}, bf16[928,128]{1,0:T(8,128)(2,1)S(1)}, u32[]{:S(2)}, u32[]{:S(2)}) collective-permute-start(bf16[928,128]{1,0:T(8,128)(2,1)S(1)} %bitcast.23), channel_id=1, source_target_pairs={{0,24},{1,25},{2,26},{3,27},{4,28},{5,29},{6,30},{7,31},{8,0},{9,1... | collective-permute-start | bytes 712712 | tf_op jit(solution)/shard_map/ppermute | solution.py:158
  123.9 2.3 %collective-permute-start.18 = (bf16[928,128]{1,0:T(8,128)(2,1)S(1)}, bf16[928,128]{1,0:T(8,128)(2,1)S(1)}, u32[]{:S(2)}, u32[]{:S(2)}) collective-permute-start(bf16[928,128]{1,0:T(8,128)(2,1)S(1)} %bitcast.24), channel_id=1, source_target_pairs={{0,1},{1,0},{2,3},{3,2},{4,5},{5,4},{6,7},{7,6},{8,9},{9,8},{10,11... | collective-permute-start | bytes 712712 | tf_op jit(solution)/shard_map/ppermute | solution.py:154
  126.2 7.7 %collective-permute-done.17.refs_3_ = bf16[928,128]{1,0:T(8,128)(2,1)S(1)} collective-permute-done((bf16[928,128]{1,0:T(8,128)(2,1)S(1)}, bf16[928,128]{1,0:T(8,128)(2,1)S(1)}, u32[]{:S(2)}, u32[]{:S(2)}) %collective-permute-start.17) | collective-permute-done | bytes 237600 | tf_op jit(solution)/shard_map/ppermute | solution.py:158
  133.9 1.8 %collective-permute-start.21 = (bf16[928,128]{1,0:T(8,128)(2,1)S(1)}, bf16[928,128]{1,0:T(8,128)(2,1)S(1)}, u32[]{:S(2)}, u32[]{:S(2)}) collective-permute-start(bf16[928,128]{1,0:T(8,128)(2,1)S(1)} %collective-permute-done.17.refs_3_), channel_id=1, source_target_pairs={{0,1},{1,0},{2,3},{3,2},{4,5},{5,4},{6,7},{7,6},{8,9},{9,8},{10,11... | collective-permute-start | bytes 712712 | tf_op jit(solution)/shard_map/ppermute | solution.py:154
  137.5 1.8 %shard_map.80 = bf16[8,464,128]{2,1,0:T(8,128)(2,1)S(1)} custom-call(s32[2]{0:T(128)S(1)} %pad_add_fusion.pos_ref, bf16[928,128]{1,0:T(8,128)(2,1)S(1)} %bitcast.25, bf16[928,128]{1,0:T(8,128)(2,1)S(1)} %collective-permute-done.15.refs_1_, bf16[928,128]{1,0:T(8,128)(2,1)S(1)} %collective-permute-done.16.refs_2_, ...), custom_call_target="tpu_custom_call" | custom-call | flops 881852416 | bytes 3712000 | tf_op jit(solution)/shard_map/pallas_call | solution.py:58
  139.3 1.0 copy-done.4
  145.1 5.1 %all-to-all-start.7 = ((bf16[8,464,128]{2,1,0:T(8,128)(2,1)}), bf16[8,464,128]{2,1,0:T(8,128)(2,1)}, u32[]{:S(2)}, u32[]{:S(2)}) async-start(bf16[8,464,128]{2,1,0:T(8,128)(2,1)} %copy-done.4), calls=%async_computation.7 | async-start | bytes 1900544 | tf_op jit(solution)/shard_map/all_to_all | solution.py:146
  150.2 3.6 %shard_map.82 = bf16[928,464]{1,0:T(8,128)(2,1)} custom-call(s32[2]{0:T(128)S(1)} %pad_add_fusion.pos_ref, bf16[8,464,128]{2,1,0:T(8,128)(2,1)S(1)} %all-to-all-done.4.rows_ref, bf16[928,128]{1,0:T(8,128)(2,1)S(1)} %bitcast.20, bf16[928,128]{1,0:T(8,128)(2,1)} %collective-permute-done.4.refs_1_, bf16[928,128]{1,0:T(8,128)(2,1)} %collective-permute-done.5.refs_2_, ...), custom_call_target="tpu_custom_call" | custom-call | flops 881852416 | bytes 3712000 | tf_op jit(solution)/shard_map/pallas_call | solution.py:58
  153.9 2.1 %reduce_sum.43 = bf16[464,128]{1,0:T(8,128)(2,1)} reduce(bf16[8,464,128]{2,1,0:T(8,128)(2,1)} %all-to-all-done.3, bf16[]{:T(256)} %constant.35.clone.1), dimensions={0}, to_apply=%region_1.0 | reduce | flops 415744 | bytes 1069058 | tf_op jit(solution)/shard_map/reduce_sum | solution.py:162
  156.0 0.9 copy-done.16
  156.9 0.9 copy-done.18
  157.9 0.9 copy-done.20
  158.8 2.7 %shard_map.81 = bf16[464,928]{1,0:T(8,128)(2,1)} custom-call(s32[2]{0:T(128)S(1)} %pad_add_fusion.pos_ref, bf16[8,464,128]{2,1,0:T(8,128)(2,1)S(1)} %all-to-all-done.rows_ref, bf16[928,128]{1,0:T(8,128)(2,1)S(1)} %bitcast.26, bf16[928,128]{1,0:T(8,128)(2,1)S(1)} %copy-done.12, bf16[928,128]{1,0:T(8,128)(2,1)S(1)} %copy-done.10, ...), custom_call_target="tpu_custom_call" | custom-call | flops 881852416 | bytes 3712000 | tf_op jit(solution)/shard_map/pallas_call | solution.py:58
  161.5 2.8 %all-to-all-done.7 = bf16[8,464,128]{2,1,0:T(8,128)(2,1)} async-done(((bf16[8,464,128]{2,1,0:T(8,128)(2,1)}), bf16[8,464,128]{2,1,0:T(8,128)(2,1)}, u32[]{:S(2)}, u32[]{:S(2)}) %all-to-all-start.7) | async-done | bytes 950304 | tf_op jit(solution)/shard_map/all_to_all | solution.py:146
  164.2 2.0 %reduce_sum.45 = bf16[464,128]{1,0:T(8,128)(2,1)} reduce(bf16[8,464,128]{2,1,0:T(8,128)(2,1)} %all-to-all-done.7, bf16[]{:T(256)} %constant.35.clone.1), dimensions={0}, to_apply=%region_3.0 | reduce | flops 415744 | bytes 1069058 | tf_op jit(solution)/shard_map/reduce_sum | solution.py:162
  (80 shorter events, 15.2 us)
Async XLA Ops:
  2.6 6.5 %copy-start.1 = (bf16[464,928]{1,0:T(8,128)(2,1)S(1)}, bf16[464,928]{1,0:T(8,128)(2,1)}, u32[]{:S(2)}) copy-start(bf16[464,928]{1,0:T(8,128)(2,1)} %refs_8_.1) | copy-start | bytes 2583556
  2.6 20.1 %all-to-all-start = ((bf16[8,464,128]{2,1,0:T(8,128)(2,1)}), bf16[8,464,128]{2,1,0:T(8,128)(2,1)S(1)}, u32[]{:S(2)}, u32[]{:S(2)}) async-start(bf16[8,464,128]{2,1,0:T(8,128)(2,1)} %broadcast_in_dim.8), calls=%async_computation | async-start | bytes 1900544 | tf_op jit(solution)/shard_map/all_to_all | solution.py:146
  22.7 1.2 copy-start.22
  23.9 1.2 copy-start.6
  25.1 22.9 %all-to-all-start.4 = ((bf16[8,464,128]{2,1,0:T(8,128)(2,1)}), bf16[8,464,128]{2,1,0:T(8,128)(2,1)S(1)}, u32[]{:S(2)}, u32[]{:S(2)}) async-start(bf16[8,464,128]{2,1,0:T(8,128)(2,1)} %broadcast_in_dim.10), calls=%async_computation.4 | async-start | bytes 1900544 | tf_op jit(solution)/shard_map/all_to_all | solution.py:146
  29.1 3.2 %collective-permute-start = (bf16[4,928,128]{2,1,0:T(8,128)(2,1)}, bf16[4,928,128]{2,1,0:T(8,128)(2,1)S(1)}, u32[]{:S(2)}, u32[]{:S(2)}) collective-permute-start(bf16[4,928,128]{2,1,0:T(8,128)(2,1)} %copy-done.6), channel_id=1, source_target_pairs={{0,1},{1,0},{2,3},{3,2},{4,5},{5,4},{6,7},{7,6},{8,9},{9,8},{10,11... | collective-permute-start | bytes 2850824 | tf_op jit(solution)/shard_map/ppermute | solution.py:154
  33.5 14.5 %copy-start = (bf16[928,464]{1,0:T(8,128)(2,1)S(1)}, bf16[928,464]{1,0:T(8,128)(2,1)}, u32[]{:S(2)}) copy-start(bf16[928,464]{1,0:T(8,128)(2,1)} %weight_ref.3) | copy-start | bytes 2583556
  33.5 8.3 %collective-permute-start.1 = (bf16[928,128]{1,0:T(8,128)(2,1)S(1)}, bf16[928,128]{1,0:T(8,128)(2,1)S(1)}, u32[]{:S(2)}, u32[]{:S(2)}) collective-permute-start(bf16[928,128]{1,0:T(8,128)(2,1)S(1)} %get-tuple-element.23), channel_id=1, source_target_pairs={{0,8},{1,9},{2,10},{3,11},{4,12},{5,13},{6,14},{7,15},{8,16},{9,17... | collective-permute-start | bytes 712712 | tf_op jit(solution)/shard_map/ppermute | solution.py:158
  34.8 13.1 %collective-permute-start.2 = (bf16[928,128]{1,0:T(8,128)(2,1)S(1)}, bf16[928,128]{1,0:T(8,128)(2,1)S(1)}, u32[]{:S(2)}, u32[]{:S(2)}) collective-permute-start(bf16[928,128]{1,0:T(8,128)(2,1)S(1)} %get-tuple-element.24), channel_id=1, source_target_pairs={{0,16},{1,17},{2,18},{3,19},{4,20},{5,21},{6,22},{7,23},{8,24},{9,... | collective-permute-start | bytes 712712 | tf_op jit(solution)/shard_map/ppermute | solution.py:158
  37.3 10.6 %collective-permute-start.3 = (bf16[928,128]{1,0:T(8,128)(2,1)S(1)}, bf16[928,128]{1,0:T(8,128)(2,1)S(1)}, u32[]{:S(2)}, u32[]{:S(2)}) collective-permute-start(bf16[928,128]{1,0:T(8,128)(2,1)S(1)} %get-tuple-element.25), channel_id=1, source_target_pairs={{0,24},{1,25},{2,26},{3,27},{4,28},{5,29},{6,30},{7,31},{8,0},{9,1... | collective-permute-start | bytes 712712 | tf_op jit(solution)/shard_map/ppermute | solution.py:158
  49.2 17.5 %collective-permute-start.11 = (bf16[4,928,128]{2,1,0:T(8,128)(2,1)S(1)}, bf16[4,928,128]{2,1,0:T(8,128)(2,1)S(1)}, u32[]{:S(2)}, u32[]{:S(2)}) collective-permute-start(bf16[4,928,128]{2,1,0:T(8,128)(2,1)S(1)} %shard_map.78), channel_id=1, source_target_pairs={{0,1},{1,0},{2,3},{3,2},{4,5},{5,4},{6,7},{7,6},{8,9},{9,8},{10,11... | collective-permute-start | bytes 2850824 | tf_op jit(solution)/shard_map/ppermute | solution.py:154
  68.8 0.8 copy-start.21
  69.6 9.1 %collective-permute-start.12 = (bf16[928,128]{1,0:T(8,128)(2,1)}, bf16[928,128]{1,0:T(8,128)(2,1)}, u32[]{:S(2)}, u32[]{:S(2)}) collective-permute-start(bf16[928,128]{1,0:T(8,128)(2,1)} %get-tuple-element.33), channel_id=1, source_target_pairs={{0,8},{1,9},{2,10},{3,11},{4,12},{5,13},{6,14},{7,15},{8,16},{9,17... | collective-permute-start | bytes 712712 | tf_op jit(solution)/shard_map/ppermute | solution.py:158
  70.6 10.2 %collective-permute-start.13 = (bf16[928,128]{1,0:T(8,128)(2,1)}, bf16[928,128]{1,0:T(8,128)(2,1)}, u32[]{:S(2)}, u32[]{:S(2)}) collective-permute-start(bf16[928,128]{1,0:T(8,128)(2,1)} %get-tuple-element.34), channel_id=1, source_target_pairs={{0,16},{1,17},{2,18},{3,19},{4,20},{5,21},{6,22},{7,23},{8,24},{9,... | collective-permute-start | bytes 712712 | tf_op jit(solution)/shard_map/ppermute | solution.py:158
  72.7 8.6 %collective-permute-start.14 = (bf16[928,128]{1,0:T(8,128)(2,1)S(1)}, bf16[928,128]{1,0:T(8,128)(2,1)}, u32[]{:S(2)}, u32[]{:S(2)}) collective-permute-start(bf16[928,128]{1,0:T(8,128)(2,1)S(1)} %get-tuple-element.35), channel_id=1, source_target_pairs={{0,24},{1,25},{2,26},{3,27},{4,28},{5,29},{6,30},{7,31},{8,0},{9,1... | collective-permute-start | bytes 712712 | tf_op jit(solution)/shard_map/ppermute | solution.py:158
  75.0 12.2 %all-to-all-start.2 = ((bf16[4,232,128]{2,1,0:T(8,128)(2,1)}), bf16[4,232,128]{2,1,0:T(8,128)(2,1)S(1)}, u32[]{:S(2)}, u32[]{:S(2)}) async-start(bf16[4,232,128]{2,1,0:T(8,128)(2,1)} %broadcast_in_dim.9), calls=%async_computation.2 | async-start | bytes 475136 | tf_op jit(solution)/shard_map/all_to_all | solution.py:146
  87.2 11.8 %all-to-all-start.5 = ((bf16[4,232,128]{2,1,0:T(8,128)(2,1)}), bf16[4,232,128]{2,1,0:T(8,128)(2,1)S(1)}, u32[]{:S(2)}, u32[]{:S(2)}) async-start(bf16[4,232,128]{2,1,0:T(8,128)(2,1)} %bitcast.27), calls=%async_computation.5 | async-start | bytes 475136 | tf_op jit(solution)/shard_map/all_to_all | solution.py:146
  90.6 18.0 %collective-permute-start.6 = (bf16[928,128]{1,0:T(8,128)(2,1)S(1)}, bf16[928,128]{1,0:T(8,128)(2,1)}, u32[]{:S(2)}, u32[]{:S(2)}) collective-permute-start(bf16[928,128]{1,0:T(8,128)(2,1)S(1)} %bitcast.15), channel_id=1, source_target_pairs={{0,8},{1,9},{2,10},{3,11},{4,12},{5,13},{6,14},{7,15},{8,16},{9,17... | collective-permute-start | bytes 712712 | tf_op jit(solution)/shard_map/ppermute | solution.py:158
  91.0 17.7 %collective-permute-start.5 = (bf16[928,128]{1,0:T(8,128)(2,1)S(1)}, bf16[928,128]{1,0:T(8,128)(2,1)}, u32[]{:S(2)}, u32[]{:S(2)}) collective-permute-start(bf16[928,128]{1,0:T(8,128)(2,1)S(1)} %bitcast.16), channel_id=1, source_target_pairs={{0,16},{1,17},{2,18},{3,19},{4,20},{5,21},{6,22},{7,23},{8,24},{9,... | collective-permute-start | bytes 712712 | tf_op jit(solution)/shard_map/ppermute | solution.py:158
  93.9 15.2 %collective-permute-start.4 = (bf16[928,128]{1,0:T(8,128)(2,1)S(1)}, bf16[928,128]{1,0:T(8,128)(2,1)}, u32[]{:S(2)}, u32[]{:S(2)}) collective-permute-start(bf16[928,128]{1,0:T(8,128)(2,1)S(1)} %bitcast.17), channel_id=1, source_target_pairs={{0,24},{1,25},{2,26},{3,27},{4,28},{5,29},{6,30},{7,31},{8,0},{9,1... | collective-permute-start | bytes 712712 | tf_op jit(solution)/shard_map/ppermute | solution.py:158
  99.9 16.1 %all-to-all-start.6 = ((bf16[4,232,128]{2,1,0:T(8,128)(2,1)}), bf16[4,232,128]{2,1,0:T(8,128)(2,1)S(1)}, u32[]{:S(2)}, u32[]{:S(2)}) async-start(bf16[4,232,128]{2,1,0:T(8,128)(2,1)} %broadcast_in_dim.11), calls=%async_computation.6 | async-start | bytes 475136 | tf_op jit(solution)/shard_map/all_to_all | solution.py:146
  103.3 7.4 %collective-permute-start.7 = (bf16[928,128]{1,0:T(8,128)(2,1)S(1)}, bf16[928,128]{1,0:T(8,128)(2,1)}, u32[]{:S(2)}, u32[]{:S(2)}) collective-permute-start(bf16[928,128]{1,0:T(8,128)(2,1)S(1)} %bitcast.18), channel_id=1, source_target_pairs={{0,1},{1,0},{2,3},{3,2},{4,5},{5,4},{6,7},{7,6},{8,9},{9,8},{10,11... | collective-permute-start | bytes 712712 | tf_op jit(solution)/shard_map/ppermute | solution.py:154
  108.6 2.0 %collective-permute-start.10 = (bf16[928,128]{1,0:T(8,128)(2,1)}, bf16[928,128]{1,0:T(8,128)(2,1)}, u32[]{:S(2)}, u32[]{:S(2)}) collective-permute-start(bf16[928,128]{1,0:T(8,128)(2,1)} %collective-permute-done.6.refs_3_), channel_id=1, source_target_pairs={{0,1},{1,0},{2,3},{3,2},{4,5},{5,4},{6,7},{7,6},{8,9},{9,8},{10,11... | collective-permute-start | bytes 712712 | tf_op jit(solution)/shard_map/ppermute | solution.py:154
  108.7 2.1 %collective-permute-start.9 = (bf16[928,128]{1,0:T(8,128)(2,1)}, bf16[928,128]{1,0:T(8,128)(2,1)}, u32[]{:S(2)}, u32[]{:S(2)}) collective-permute-start(bf16[928,128]{1,0:T(8,128)(2,1)} %collective-permute-done.5.refs_2_), channel_id=1, source_target_pairs={{0,1},{1,0},{2,3},{3,2},{4,5},{5,4},{6,7},{7,6},{8,9},{9,8},{10,11... | collective-permute-start | bytes 712712 | tf_op jit(solution)/shard_map/ppermute | solution.py:154
  109.1 2.0 %collective-permute-start.8 = (bf16[928,128]{1,0:T(8,128)(2,1)}, bf16[928,128]{1,0:T(8,128)(2,1)}, u32[]{:S(2)}, u32[]{:S(2)}) collective-permute-start(bf16[928,128]{1,0:T(8,128)(2,1)} %collective-permute-done.4.refs_1_), channel_id=1, source_target_pairs={{0,1},{1,0},{2,3},{3,2},{4,5},{5,4},{6,7},{7,6},{8,9},{9,8},{10,11... | collective-permute-start | bytes 712712 | tf_op jit(solution)/shard_map/ppermute | solution.py:154
  111.1 1.2 copy-start.5
  115.1 0.9 copy-start.3
  116.0 21.5 %copy-start.2 = (bf16[464,928]{1,0:T(8,128)(2,1)S(1)}, bf16[464,928]{1,0:T(8,128)(2,1)}, u32[]{:S(2)}) copy-start(bf16[464,928]{1,0:T(8,128)(2,1)} %refs_8_.1) | copy-start | bytes 2583556
  116.0 29.1 %all-to-all-start.3 = ((bf16[8,464,128]{2,1,0:T(8,128)(2,1)}), bf16[8,464,128]{2,1,0:T(8,128)(2,1)}, u32[]{:S(2)}, u32[]{:S(2)}) async-start(bf16[8,464,128]{2,1,0:T(8,128)(2,1)} %copy-done.3), calls=%async_computation.3 | async-start | bytes 1900544 | tf_op jit(solution)/shard_map/all_to_all | solution.py:146
  121.2 12.7 %collective-permute-start.17 = (bf16[928,128]{1,0:T(8,128)(2,1)S(1)}, bf16[928,128]{1,0:T(8,128)(2,1)S(1)}, u32[]{:S(2)}, u32[]{:S(2)}) collective-permute-start(bf16[928,128]{1,0:T(8,128)(2,1)S(1)} %bitcast.21), channel_id=1, source_target_pairs={{0,8},{1,9},{2,10},{3,11},{4,12},{5,13},{6,14},{7,15},{8,16},{9,17... | collective-permute-start | bytes 712712 | tf_op jit(solution)/shard_map/ppermute | solution.py:158
  121.4 14.2 %collective-permute-start.16 = (bf16[928,128]{1,0:T(8,128)(2,1)S(1)}, bf16[928,128]{1,0:T(8,128)(2,1)S(1)}, u32[]{:S(2)}, u32[]{:S(2)}) collective-permute-start(bf16[928,128]{1,0:T(8,128)(2,1)S(1)} %bitcast.22), channel_id=1, source_target_pairs={{0,16},{1,17},{2,18},{3,19},{4,20},{5,21},{6,22},{7,23},{8,24},{9,... | collective-permute-start | bytes 712712 | tf_op jit(solution)/shard_map/ppermute | solution.py:158
  122.2 13.4 %collective-permute-start.15 = (bf16[928,128]{1,0:T(8,128)(2,1)S(1)}, bf16[928,128]{1,0:T(8,128)(2,1)S(1)}, u32[]{:S(2)}, u32[]{:S(2)}) collective-permute-start(bf16[928,128]{1,0:T(8,128)(2,1)S(1)} %bitcast.23), channel_id=1, source_target_pairs={{0,24},{1,25},{2,26},{3,27},{4,28},{5,29},{6,30},{7,31},{8,0},{9,1... | collective-permute-start | bytes 712712 | tf_op jit(solution)/shard_map/ppermute | solution.py:158
  123.9 12.4 %collective-permute-start.18 = (bf16[928,128]{1,0:T(8,128)(2,1)S(1)}, bf16[928,128]{1,0:T(8,128)(2,1)S(1)}, u32[]{:S(2)}, u32[]{:S(2)}) collective-permute-start(bf16[928,128]{1,0:T(8,128)(2,1)S(1)} %bitcast.24), channel_id=1, source_target_pairs={{0,1},{1,0},{2,3},{3,2},{4,5},{5,4},{6,7},{7,6},{8,9},{9,8},{10,11... | collective-permute-start | bytes 712712 | tf_op jit(solution)/shard_map/ppermute | solution.py:154
  133.9 2.9 %collective-permute-start.21 = (bf16[928,128]{1,0:T(8,128)(2,1)S(1)}, bf16[928,128]{1,0:T(8,128)(2,1)S(1)}, u32[]{:S(2)}, u32[]{:S(2)}) collective-permute-start(bf16[928,128]{1,0:T(8,128)(2,1)S(1)} %collective-permute-done.17.refs_3_), channel_id=1, source_target_pairs={{0,1},{1,0},{2,3},{3,2},{4,5},{5,4},{6,7},{7,6},{8,9},{9,8},{10,11... | collective-permute-start | bytes 712712 | tf_op jit(solution)/shard_map/ppermute | solution.py:154
  135.7 1.5 collective-permute-start.20
  135.7 1.8 %collective-permute-start.19 = (bf16[928,128]{1,0:T(8,128)(2,1)S(1)}, bf16[928,128]{1,0:T(8,128)(2,1)S(1)}, u32[]{:S(2)}, u32[]{:S(2)}) collective-permute-start(bf16[928,128]{1,0:T(8,128)(2,1)S(1)} %collective-permute-done.15.refs_1_), channel_id=1, source_target_pairs={{0,1},{1,0},{2,3},{3,2},{4,5},{5,4},{6,7},{7,6},{8,9},{9,8},{10,11... | collective-permute-start | bytes 712712 | tf_op jit(solution)/shard_map/ppermute | solution.py:154
  139.3 1.0 copy-start.4
  140.9 0.7 copy-start.9
  142.3 0.7 copy-start.13
  143.7 0.7 copy-start.17
  145.1 19.1 %all-to-all-start.7 = ((bf16[8,464,128]{2,1,0:T(8,128)(2,1)}), bf16[8,464,128]{2,1,0:T(8,128)(2,1)}, u32[]{:S(2)}, u32[]{:S(2)}) async-start(bf16[8,464,128]{2,1,0:T(8,128)(2,1)} %copy-done.4), calls=%async_computation.7 | async-start | bytes 1900544 | tf_op jit(solution)/shard_map/all_to_all | solution.py:146
  153.9 2.1 %copy-start.8 = (bf16[928,128]{1,0:T(8,128)(2,1)S(1)}, bf16[928,128]{1,0:T(8,128)(2,1)}, u32[]{:S(2)}) copy-start(bf16[928,128]{1,0:T(8,128)(2,1)} %copy-done.7) | copy-start | bytes 712708
  153.9 2.1 %copy-start.10 = (bf16[928,128]{1,0:T(8,128)(2,1)S(1)}, bf16[928,128]{1,0:T(8,128)(2,1)}, u32[]{:S(2)}) copy-start(bf16[928,128]{1,0:T(8,128)(2,1)} %copy-done.9) | copy-start | bytes 712708
  153.9 2.1 %copy-start.12 = (bf16[928,128]{1,0:T(8,128)(2,1)S(1)}, bf16[928,128]{1,0:T(8,128)(2,1)}, u32[]{:S(2)}) copy-start(bf16[928,128]{1,0:T(8,128)(2,1)} %copy-done.11) | copy-start | bytes 712708
  153.9 2.1 %copy-start.14 = (bf16[928,128]{1,0:T(8,128)(2,1)S(1)}, bf16[928,128]{1,0:T(8,128)(2,1)}, u32[]{:S(2)}) copy-start(bf16[928,128]{1,0:T(8,128)(2,1)} %copy-done.13) | copy-start | bytes 712708
  156.0 0.9 copy-start.16
  156.9 0.9 copy-start.18
  157.9 0.9 copy-start.20
  (4 other events, 2.8 us)

commit v3 on v2

--- a/solution.py
+++ b/solution.py
@@ -18,9 +18,9 @@
     return (x * Z + z) * C + c
 
 
-def rep_pairs(dx, dc):
+def rep_pairs(dx, dz, dc):
     return [
-        (rep_index(x, z, c), rep_index((x + dx) % X, z, (c + dc) % C))
+        (rep_index(x, z, c), rep_index((x + dx) % X, (z + dz) % Z, (c + dc) % C))
         for x in range(X)
         for z in range(Z)
         for c in range(C)
@@ -52,16 +52,18 @@
     return jax.ShapeDtypeStruct(shape, dtype)
 
 
-def kernel_call(kernel, outs, flops, pos, operands, scratch=()):
+def kernel_call(kernel, outs, flops, pos, operands, scratch=(), far=()):
     moved = sum(math.prod(o.shape) * o.dtype.itemsize for o in [*operands, *outs])
     vmem = pl.BlockSpec(memory_space=pltpu.VMEM)
     return pl.pallas_call(
         kernel,
-        out_shape=outs,
+        out_shape=[pltpu.HBM(o.shape, o.dtype) if i in far else o for i, o in enumerate(outs)],
         in_specs=[pl.BlockSpec(memory_space=pltpu.SMEM)] + [vmem] * len(operands),
-        out_specs=[vmem] * len(outs),
+        out_specs=[
+            pl.BlockSpec(memory_space=pltpu.HBM) if i in far else vmem for i in range(len(outs))
+        ],
         scratch_shapes=scratch,
-        compiler_params=pltpu.CompilerParams(vmem_limit_bytes=24 * 1024 * 1024),
+        compiler_params=pltpu.CompilerParams(vmem_limit_bytes=16 * 1024 * 1024),
         cost_estimate=pl.CostEstimate(flops=flops, bytes_accessed=moved, transcendentals=0),
     )(pos, *operands)
 
@@ -111,35 +113,45 @@
 
 def both_halves(pos, blocks, weight):
     depth, width = weight.shape
+    count = 2 * X
 
     def kernel(pos_ref, *refs):
-        weight_ref, out_ref = refs[-2:]
+        weight_ref, out_ref, kept_ref, sems = refs[-4:]
+        kept = [
+            pltpu.make_async_copy(refs[index], kept_ref.at[index], sems.at[index])
+            for index in range(count)
+        ]
+        for copy in kept:
+            copy.start()
         x, c = pos_ref[0], pos_ref[1]
-        for part, half in ((refs[:X], c), (refs[X : 2 * X], 1 - c)):
+        for part, half in ((refs[:X], c), (refs[X:count], 1 - c)):
             product = dot(weight_ref[...], wide(part), PLAIN).astype(BF)
             for d in range(X):
                 out_ref[half * X + ((x + d) & 3)] = block(product, d)
-
-    outs = [shaped((2 * X, depth, LANES), BF)]
-    flops = 2 * depth * width * 2 * X * LANES
-    return kernel_call(kernel, outs, flops, pos, [*blocks, weight])[0]
+        for copy in kept:
+            copy.wait()
+
+    outs = [shaped((count, depth, LANES), BF), shaped((count, width, LANES), BF)]
+    flops = 2 * depth * width * count * LANES
+    scratch = [pltpu.SemaphoreType.DMA((count,))]
+    return kernel_call(kernel, outs, flops, pos, [*blocks, weight], scratch, (1,))
 
 
 def weight_grad(pos, factor, rows, blocks, rows_first):
-    width, depth = rows.shape[1], blocks[0].shape[0]
-
-    def kernel(pos_ref, rows_ref, *refs):
-        out_ref, total = refs[-1], None
+    width, depth = rows.shape[1], blocks.shape[1]
+
+    def kernel(pos_ref, rows_ref, blocks_ref, out_ref):
         x, c = pos_ref[0], pos_ref[1]
-        for part, half in ((refs[:X], c), (refs[X : 2 * X], 1 - c)):
-            pair = half_of(rows_ref, half, x), wide(part)
+        total = None
+        for part, half in ((0, c), (1, 1 - c)):
+            pair = half_of(rows_ref, half, x), half_of(blocks_ref, part, 0)
             term = dot(*(pair if rows_first else pair[::-1]), LAST)
             total = term if total is None else total + term
         out_ref[...] = (factor * total).astype(BF)
 
     outs = [shaped((width, depth) if rows_first else (depth, width), BF)]
     flops = 2 * depth * width * 2 * X * LANES
-    return kernel_call(kernel, outs, flops, pos, [rows, *blocks])[0]
+    return kernel_call(kernel, outs, flops, pos, [rows, blocks])[0]
 
 
 def exchange(value, axis, groups=None):
@@ -150,12 +162,42 @@
     return jnp.broadcast_to(value[None], (count,) + value.shape)
 
 
+def many(pos, value, count):
+    def kernel(pos_ref, value_ref, out_ref):
+        for index in range(count):
+            out_ref[index] = value_ref[...]
+
+    return kernel_call(kernel, [shaped((count,) + value.shape, BF)], 0, pos, [value])[0]
+
+
+def added(pos, value):
+    def kernel(pos_ref, value_ref, out_ref):
+        total = value_ref[0].astype(F32)
+        for index in range(1, value.shape[0]):
+            total = total + value_ref[index].astype(F32)
+        out_ref[...] = total.astype(BF)
+
+    return kernel_call(kernel, [shaped(value.shape[1:], BF)], value.size, pos, [value])[0]
+
+
+def in_order(pos, chunks):
+    def kernel(pos_ref, *refs):
+        for d in range(Z):
+            refs[-1][(pos_ref[2] + d) & 3] = refs[d][...]
+
+    return kernel_call(kernel, [shaped((Z,) + chunks[0].shape, BF)], 0, pos, chunks)[0]
+
+
 def swap_cores(value):
-    return lax.ppermute(value, "rep", rep_pairs(0, 1))
+    return lax.ppermute(value, "rep", rep_pairs(0, 0, 1))
 
 
 def move_x(value, d):
-    return lax.ppermute(value, "rep", rep_pairs(d, 0))
+    return lax.ppermute(value, "rep", rep_pairs(d, 0, 0))
+
+
+def move_z(value, d):
+    return lax.ppermute(value, "rep", rep_pairs(0, d, 0))
 
 
 def total_of(value):
@@ -169,13 +211,16 @@
     return keep.astype(BF)
 
 
-def sum_z(value):
+def scatter_z(value):
     value = value.reshape(Z, value.shape[0] // Z, LANES)
-    return total_of(exchange(value, "rep", Z_GROUPS))
-
-
-def spread_z(value):
-    whole = exchange(copies(value, Z), "rep", Z_GROUPS)
+    return exchange(value, "rep", Z_GROUPS)
+
+
+def spread_z(pos, value, by_permutes):
+    if by_permutes:
+        whole = in_order(pos, [value] + [move_z(value, -d) for d in range(1, Z)])
+    else:
+        whole = exchange(copies(value, Z), "rep", Z_GROUPS)
     return whole.reshape(Z * value.shape[0], LANES)
 
 
@@ -187,30 +232,36 @@
 def body(tokens, first_weight, second_weight, cotangent):
     factor = float(GRP * tokens.shape[0]) ** (-0.5)
     rep = lax.axis_index("rep")
-    pos = jnp.stack([rep >> 3, rep & 1]).astype(jnp.int32)
-
-    tok = exchange(copies(tokens.T, GRP), "grp")
-    first_turned, second_turned = first_weight.T, second_weight.T
+    pos = jnp.stack([rep >> 3, rep & 1, (rep >> 1) & 3]).astype(jnp.int32)
+
+    tok = exchange(many(pos, tokens.T, GRP), "grp")
+    first_turned, second_turned, tok = lax.optimization_barrier(
+        (first_weight.T, second_weight.T, tok)
+    )
     sent = other_half(pos, tok, first_turned)
-    cot = exchange(copies(after(cotangent.T, sent), GRP), "grp")
+    cot = exchange(many(pos, after(cotangent.T, sent), GRP), "grp")
     keep, sent = own_half(pos, tok, first_turned, swap_cores(sent))
     value = sum_x(keep, sent)
-    hidden = sum_z(value)
+
+    sent = other_half(pos, after(cot, value), second_weight)
+    keep, sent = own_half(pos, cot, second_weight, swap_cores(sent))
+
+    hidden = total_of(after(scatter_z(value), keep))
     active = jax.nn.gelu(hidden, approximate=False).astype(BF)
     active, hidden = lax.optimization_barrier((active, hidden))
-
-    sent = other_half(pos, after(cot, value), second_weight)
-    keep, sent = own_half(pos, cot, second_weight, swap_cores(sent))
-    upward = sum_z(sum_x(keep, sent))
+    upward = total_of(scatter_z(sum_x(keep, sent)))
     deltas = (upward * slope(hidden)).astype(BF)
 
-    act = spread_x(spread_z(active))
-    dlt = spread_x(spread_z(deltas))
-    out = exchange(both_halves(pos, act, second_turned), "grp")
-    back = exchange(both_halves(pos, dlt, first_weight), "grp")
+    act = spread_x(spread_z(pos, active, True))
+    dlt = spread_x(spread_z(pos, deltas, False))
+    out, act = both_halves(pos, act, second_turned)
+    out = exchange(out, "grp")
     second_grad = weight_grad(pos, factor, cot, act, False)
+    dlt[0] = after(dlt[0], second_grad)
+    back, dlt = both_halves(pos, dlt, first_weight)
+    back = exchange(back, "grp")
     first_grad = weight_grad(pos, factor, tok, dlt, True)
-    return (total_of(out).astype(BF).T, total_of(back).astype(BF).T, first_grad, second_grad)
+    return (added(pos, out).T, added(pos, back).T, first_grad, second_grad)
 
 
 def solution(mesh):

time: 167 us -> 176 us (1.054)
  starting transfers between devices: 59.4 us -> 80.3 us
  blocking collectives: 16.2 us -> 0 us
  Pallas kernels: 16.4 us -> 24.3 us
  local copies, waits for them, and re-layouts: 18.3 us -> 12.7 us
  waiting for transfers between devices: 48.3 us -> 51.5 us
    all_to_all x1 -> x0, blocking collectives: 16.2 us -> none  [exchange(): return lax.all_to_all(value, axis, 0, 0, axis_index_groups=groups)]
    ppermute x22 -> x25, starting transfers between devices: 28.1 us -> 41 us  [the longest x12 17.1 us: move_x(): return lax.ppermute(value, 'rep', rep_pairs(d, 0, 0))]
    all_to_all x7, starting transfers between devices: 31.2 us -> 39.3 us  [exchange(): return lax.all_to_all(value, axis, 0, 0, axis_index_groups=groups)]
    pallas_call x8 -> x13, Pallas kernels: 16.4 us -> 24.3 us  [kernel_call(): pl.pallas_call(kernel, out_shape=[pltpu.HBM(o.shape, o.dtype) if i in far...]
    ppermute x22 -> x25, waiting for transfers between devices: 23.9 us -> 30.5 us  [the longest x12 22.8 us: move_x(): return lax.ppermute(value, 'rep', rep_pairs(d, 0, 0))]
    broadcast_in_dim x4 -> x1, local copies, waits for them, and re-layouts: 4.55 us -> 0.72 us  [copies(): return jnp.broadcast_to(value[None], (count,) + value.shape)]
    all_to_all x7, waiting for transfers between devices: 24.4 us -> 21 us  [exchange(): return lax.all_to_all(value, axis, 0, 0, axis_index_groups=groups)]
    reduce_sum x4 -> x2, other arithmetic: 4.13 us -> 1.97 us  [total_of(): return jnp.sum(value.astype(F32), axis=0)]
  transfers between devices with their start and end apart: 29 -> 32, of which waited for: 15 -> 13; matrix products, arithmetic and copies ran while one was open for 5% -> 4% of each run, Pallas kernels for 7% -> 10%
where the time goes in v3:
time: 176 us; the launch traced here: 175 us
  starting transfers between devices  80.3 us (46%)
  waiting for transfers between devices  51.5 us (29%)
  Pallas kernels  24.3 us (14%)
  local copies, waits for them, and re-layouts  12.7 us (7%)
  other arithmetic  5.16 us (3%)
    all_to_all x7, starting transfers between devices, exchange(): return lax.all_to_all(value, axis, 0, 0, axis_index_groups=groups)  39.3 us
    pallas_call x13, Pallas kernels, kernel_call(): pl.pallas_call(kernel, out_shape=[pltpu.HBM(o.shape, o.dtype) if i in far...  24.3 us
    ppermute x12, waiting for transfers between devices, move_x(): return lax.ppermute(value, 'rep', rep_pairs(d, 0, 0))  22.8 us
    all_to_all x7, waiting for transfers between devices, exchange(): return lax.all_to_all(value, axis, 0, 0, axis_index_groups=groups)  21 us
    ppermute x12, starting transfers between devices, move_x(): return lax.ppermute(value, 'rep', rep_pairs(d, 0, 0))  17.1 us
    ppermute x10, starting transfers between devices, swap_cores(): return lax.ppermute(value, 'rep', rep_pairs(0, 0, 1))  14.8 us
    unnamed x28, local copies, waits for them, and re-layouts  12 us
    ppermute x3, starting transfers between devices, move_z(): return lax.ppermute(value, 'rep', rep_pairs(0, d, 0))  9.02 us
  transfers between devices with their start and end apart: 32, of which 13 were waited for; matrix products, arithmetic and copies ran while one was open for 4% of the time, Pallas kernels for 10%

profile of v3, /device:TPU:1, one launch (start us, length us, event | category | flops | bytes accessed | tf_op | source)
XLA Modules:
  0.0 174.8 jit_solution(8997798516638871758)
XLA Ops:
  3.2 6.5 %all-to-all-start = ((bf16[8,464,128]{2,1,0:T(8,128)(2,1)}), bf16[8,464,128]{2,1,0:T(8,128)(2,1)S(1)}, u32[]{:S(2)}, u32[]{:S(2)}) async-start(bf16[8,464,128]{2,1,0:T(8,128)(2,1)} %copy-done.4), calls=%async_computation | async-start | bytes 1900544 | tf_op jit(solution)/shard_map/all_to_all | solution.py:158
  9.7 1.6 copy.8
  11.4 1.5 copy.9
  12.9 10.4 %all-to-all-done.rows_ref = bf16[8,464,128]{2,1,0:T(8,128)(2,1)S(1)} async-done(((bf16[8,464,128]{2,1,0:T(8,128)(2,1)}), bf16[8,464,128]{2,1,0:T(8,128)(2,1)S(1)}, u32[]{:S(2)}, u32[]{:S(2)}) %all-to-all-start) | async-done | bytes 950304 | tf_op jit(solution)/shard_map/all_to_all | solution.py:158
  27.1 4.0 %all-to-all-start.2 = ((bf16[8,464,128]{2,1,0:T(8,128)(2,1)}), bf16[8,464,128]{2,1,0:T(8,128)(2,1)S(1)}, u32[]{:S(2)}, u32[]{:S(2)}) async-start(bf16[8,464,128]{2,1,0:T(8,128)(2,1)} %copy-done.3), calls=%async_computation.2 | async-start | bytes 1900544 | tf_op jit(solution)/shard_map/all_to_all | solution.py:158
  31.9 2.4 %collective-permute-done.arrived_ref = bf16[4,928,128]{2,1,0:T(8,128)(2,1)S(1)} collective-permute-done((bf16[4,928,128]{2,1,0:T(8,128)(2,1)}, bf16[4,928,128]{2,1,0:T(8,128)(2,1)S(1)}, u32[]{:S(2)}, u32[]{:S(2)}) %collective-permute-start) | collective-permute-done | bytes 950304 | tf_op jit(solution)/shard_map/ppermute | solution.py:192
  35.4 1.2 shard_map.77
  36.7 1.3 collective-permute-start.1
  38.0 2.5 %collective-permute-start.2 = (bf16[928,128]{1,0:T(8,128)(2,1)S(1)}, bf16[928,128]{1,0:T(8,128)(2,1)S(1)}, u32[]{:S(2)}, u32[]{:S(2)}) collective-permute-start(bf16[928,128]{1,0:T(8,128)(2,1)S(1)} %get-tuple-element.35), channel_id=1, source_target_pairs={{0,16},{1,17},{2,18},{3,19},{4,20},{5,21},{6,22},{7,23},{8,24},{9,... | collective-permute-start | bytes 712712 | tf_op jit(solution)/shard_map/ppermute | solution.py:196
  41.6 3.4 %collective-permute-done.1 = bf16[928,128]{1,0:T(8,128)(2,1)S(1)} collective-permute-done((bf16[928,128]{1,0:T(8,128)(2,1)S(1)}, bf16[928,128]{1,0:T(8,128)(2,1)S(1)}, u32[]{:S(2)}, u32[]{:S(2)}) %collective-permute-start.1) | collective-permute-done | bytes 237600 | tf_op jit(solution)/shard_map/ppermute | solution.py:196
  44.9 6.1 %collective-permute-done.2 = bf16[928,128]{1,0:T(8,128)(2,1)S(1)} collective-permute-done((bf16[928,128]{1,0:T(8,128)(2,1)S(1)}, bf16[928,128]{1,0:T(8,128)(2,1)S(1)}, u32[]{:S(2)}, u32[]{:S(2)}) %collective-permute-start.2) | collective-permute-done | bytes 237600 | tf_op jit(solution)/shard_map/ppermute | solution.py:196
  51.8 2.1 %shard_map.79 = bf16[4,928,128]{2,1,0:T(8,128)(2,1)} custom-call(s32[3]{0:T(128)S(1)} %pad_add_fusion.pos_ref, bf16[8,464,128]{2,1,0:T(8,128)(2,1)S(1)} %all-to-all-done.2.rows_ref, bf16[928,464]{1,0:T(8,128)(2,1)S(1)} %copy-done), custom_call_target="tpu_custom_call" | custom-call | flops 440926208 | bytes 2761728 | tf_op jit(solution)/shard_map/pallas_call | solution.py:58
  55.2 7.3 %all-to-all-start.1 = ((bf16[4,232,128]{2,1,0:T(8,128)(2,1)}), bf16[4,232,128]{2,1,0:T(8,128)(2,1)}, u32[]{:S(2)}, u32[]{:S(2)}) async-start(bf16[4,232,128]{2,1,0:T(8,128)(2,1)} %bitcast.6), calls=%async_computation.1 | async-start | bytes 475136 | tf_op jit(solution)/shard_map/all_to_all | solution.py:158
  62.5 2.7 %shard_map.80 = (f32[928,128]{1,0:T(8,128)S(1)}, bf16[928,128]{1,0:T(8,128)(2,1)}, bf16[928,128]{1,0:T(8,128)(2,1)}, bf16[928,128]{1,0:T(8,128)(2,1)}) custom-call(s32[3]{0:T(128)S(1)} %pad_add_fusion.pos_ref, bf16[8,464,128]{2,1,0:T(8,128)(2,1)S(1)} %all-to-all-done.2.rows_ref, bf16[928,464]{1,0:T(8,128)(2,1)S(1)} %copy-done, ...), custom_call_target="tpu_custom_call" | custom-call | flops 440926208 | bytes 3949568 | tf_op jit(solution)/shard_map/pallas_call | solution.py:58
  66.2 2.1 %collective-permute-start.16 = (bf16[928,128]{1,0:T(8,128)(2,1)}, bf16[928,128]{1,0:T(8,128)(2,1)}, u32[]{:S(2)}, u32[]{:S(2)}) collective-permute-start(bf16[928,128]{1,0:T(8,128)(2,1)} %get-tuple-element.48), channel_id=1, source_target_pairs={{0,16},{1,17},{2,18},{3,19},{4,20},{5,21},{6,22},{7,23},{8,24},{9,... | collective-permute-start | bytes 712712 | tf_op jit(solution)/shard_map/ppermute | solution.py:196
  68.4 1.3 collective-permute-start.17
  69.6 2.0 %all-to-all-done.1 = bf16[4,232,128]{2,1,0:T(8,128)(2,1)} async-done(((bf16[4,232,128]{2,1,0:T(8,128)(2,1)}), bf16[4,232,128]{2,1,0:T(8,128)(2,1)}, u32[]{:S(2)}, u32[]{:S(2)}) %all-to-all-start.1) | async-done | bytes 237600 | tf_op jit(solution)/shard_map/all_to_all | solution.py:158
  71.6 2.2 %collective-permute-done.15 = bf16[928,128]{1,0:T(8,128)(2,1)} collective-permute-done((bf16[928,128]{1,0:T(8,128)(2,1)}, bf16[928,128]{1,0:T(8,128)(2,1)}, u32[]{:S(2)}, u32[]{:S(2)}) %collective-permute-start.15) | collective-permute-done | bytes 237600 | tf_op jit(solution)/shard_map/ppermute | solution.py:196
  73.8 5.6 %collective-permute-done.16 = bf16[928,128]{1,0:T(8,128)(2,1)} collective-permute-done((bf16[928,128]{1,0:T(8,128)(2,1)}, bf16[928,128]{1,0:T(8,128)(2,1)}, u32[]{:S(2)}, u32[]{:S(2)}) %collective-permute-start.16) | collective-permute-done | bytes 237600 | tf_op jit(solution)/shard_map/ppermute | solution.py:196
  79.4 2.0 %add_convert_fusion = bf16[928,128]{1,0:T(8,128)(2,1)} fusion(bf16[928,128]{1,0:T(8,128)(2,1)} %collective-permute-done.17, bf16[928,128]{1,0:T(8,128)(2,1)} %collective-permute-done.16, f32[928,128]{1,0:T(8,128)S(1)} %get-tuple-element.42, bf16[928,128]{1,0:T(8,128)(2,1)} %collective-permute-done.15), kind=kLoop, calls=%fused_computation.1 | loop fusion | flops 831488 | bytes 1425408 | tf_op jit(solution)/shard_map/convert_element_type | solution.py:211
  81.4 6.3 %all-to-all-start.4 = ((bf16[4,232,128]{2,1,0:T(8,128)(2,1)}), bf16[4,232,128]{2,1,0:T(8,128)(2,1)}, u32[]{:S(2)}, u32[]{:S(2)}) async-start(bf16[4,232,128]{2,1,0:T(8,128)(2,1)} %bitcast.28), calls=%async_computation.4 | async-start | bytes 475136 | tf_op jit(solution)/shard_map/all_to_all | solution.py:158
  88.9 2.4 %collective-permute-start.7 = (bf16[232,128]{1,0:T(8,128)(2,1)S(1)}, bf16[232,128]{1,0:T(8,128)(2,1)S(1)}, u32[]{:S(2)}, u32[]{:S(2)}) collective-permute-start(bf16[232,128]{1,0:T(8,128)(2,1)S(1)} %fusion.2.refs_0_), channel_id=1, source_target_pairs={{0,2},{1,3},{2,4},{3,5},{4,6},{5,7},{6,0},{7,1},{8,10},{9,11},{10,... | collective-permute-start | bytes 178184 | tf_op jit(solution)/shard_map/ppermute | solution.py:200
  91.4 3.3 %collective-permute-start.6 = (bf16[232,128]{1,0:T(8,128)(2,1)S(1)}, bf16[232,128]{1,0:T(8,128)(2,1)S(1)}, u32[]{:S(2)}, u32[]{:S(2)}) collective-permute-start(bf16[232,128]{1,0:T(8,128)(2,1)S(1)} %fusion.2.refs_0_), channel_id=1, source_target_pairs={{0,4},{1,5},{2,6},{3,7},{4,0},{5,1},{6,2},{7,3},{8,12},{9,13},{10,... | collective-permute-start | bytes 178184 | tf_op jit(solution)/shard_map/ppermute | solution.py:200
  94.7 3.3 %collective-permute-start.5 = (bf16[232,128]{1,0:T(8,128)(2,1)S(1)}, bf16[232,128]{1,0:T(8,128)(2,1)S(1)}, u32[]{:S(2)}, u32[]{:S(2)}) collective-permute-start(bf16[232,128]{1,0:T(8,128)(2,1)S(1)} %fusion.2.refs_0_), channel_id=1, source_target_pairs={{0,6},{1,7},{2,0},{3,1},{4,2},{5,3},{6,4},{7,5},{8,14},{9,15},{10,... | collective-permute-start | bytes 178184 | tf_op jit(solution)/shard_map/ppermute | solution.py:200
  98.0 3.6 %collective-permute-done.6.refs_2_ = bf16[232,128]{1,0:T(8,128)(2,1)S(1)} collective-permute-done((bf16[232,128]{1,0:T(8,128)(2,1)S(1)}, bf16[232,128]{1,0:T(8,128)(2,1)S(1)}, u32[]{:S(2)}, u32[]{:S(2)}) %collective-permute-start.6) | collective-permute-done | bytes 59424 | tf_op jit(solution)/shard_map/ppermute | solution.py:200
  102.1 2.6 %collective-permute-start.10 = (bf16[928,128]{1,0:T(8,128)(2,1)S(1)}, bf16[928,128]{1,0:T(8,128)(2,1)}, u32[]{:S(2)}, u32[]{:S(2)}) collective-permute-start(bf16[928,128]{1,0:T(8,128)(2,1)S(1)} %bitcast.16), channel_id=1, source_target_pairs={{0,8},{1,9},{2,10},{3,11},{4,12},{5,13},{6,14},{7,15},{8,16},{9,17... | collective-permute-start | bytes 712712 | tf_op jit(solution)/shard_map/ppermute | solution.py:196
  104.7 2.5 %collective-permute-start.9 = (bf16[928,128]{1,0:T(8,128)(2,1)S(1)}, bf16[928,128]{1,0:T(8,128)(2,1)}, u32[]{:S(2)}, u32[]{:S(2)}) collective-permute-start(bf16[928,128]{1,0:T(8,128)(2,1)S(1)} %bitcast.17), channel_id=1, source_target_pairs={{0,16},{1,17},{2,18},{3,19},{4,20},{5,21},{6,22},{7,23},{8,24},{9,... | collective-permute-start | bytes 712712 | tf_op jit(solution)/shard_map/ppermute | solution.py:196
  109.0 4.2 %all-to-all-start.5 = ((bf16[4,232,128]{2,1,0:T(8,128)(2,1)}), bf16[4,232,128]{2,1,0:T(8,128)(2,1)S(1)}, u32[]{:S(2)}, u32[]{:S(2)}) async-start(bf16[4,232,128]{2,1,0:T(8,128)(2,1)} %broadcast_in_dim.2), calls=%async_computation.5 | async-start | bytes 475136 | tf_op jit(solution)/shard_map/all_to_all | solution.py:158
  113.3 3.3 %collective-permute-start.11 = (bf16[928,128]{1,0:T(8,128)(2,1)S(1)}, bf16[928,128]{1,0:T(8,128)(2,1)S(1)}, u32[]{:S(2)}, u32[]{:S(2)}) collective-permute-start(bf16[928,128]{1,0:T(8,128)(2,1)S(1)} %bitcast.19), channel_id=1, source_target_pairs={{0,1},{1,0},{2,3},{3,2},{4,5},{5,4},{6,7},{7,6},{8,9},{9,8},{10,11... | collective-permute-start | bytes 712712 | tf_op jit(solution)/shard_map/ppermute | solution.py:192
  116.6 2.6 %collective-permute-start.13 = (bf16[928,128]{1,0:T(8,128)(2,1)}, bf16[928,128]{1,0:T(8,128)(2,1)S(1)}, u32[]{:S(2)}, u32[]{:S(2)}) collective-permute-start(bf16[928,128]{1,0:T(8,128)(2,1)} %collective-permute-done.9.refs_2_), channel_id=1, source_target_pairs={{0,1},{1,0},{2,3},{3,2},{4,5},{5,4},{6,7},{7,6},{8,9},{9,8},{10,11... | collective-permute-start | bytes 712712 | tf_op jit(solution)/shard_map/ppermute | solution.py:192
  119.2 1.3 collective-permute-done.13.refs_6_
  120.9 2.9 %shard_map.82 = (bf16[8,464,128]{2,1,0:T(8,128)(2,1)S(1)}, bf16[8,928,128]{2,1,0:T(8,128)(2,1)}) custom-call(s32[3]{0:T(128)S(1)} %pad_add_fusion.pos_ref, bf16[928,128]{1,0:T(8,128)(2,1)S(1)} %bitcast.20, bf16[928,128]{1,0:T(8,128)(2,1)} %collective-permute-done.8.refs_1_, bf16[928,128]{1,0:T(8,128)(2,1)} %collective-permute-done.9.refs_2_, ...), custom_call_target="tpu_custom_call" | custom-call | flops 881852416 | bytes 5612544 | tf_op jit(solution)/shard_map/pallas_call | solution.py:58
  124.8 5.8 %all-to-all-start.3 = ((bf16[8,464,128]{2,1,0:T(8,128)(2,1)}), bf16[8,464,128]{2,1,0:T(8,128)(2,1)S(1)}, u32[]{:S(2)}, u32[]{:S(2)}) async-start(bf16[8,464,128]{2,1,0:T(8,128)(2,1)} %copy-done.10), calls=%async_computation.3 | async-start | bytes 1900544 | tf_op jit(solution)/shard_map/all_to_all | solution.py:158
  130.6 2.7 %collective-permute-start.19 = (bf16[928,128]{1,0:T(8,128)(2,1)S(1)}, bf16[928,128]{1,0:T(8,128)(2,1)S(1)}, u32[]{:S(2)}, u32[]{:S(2)}) collective-permute-start(bf16[928,128]{1,0:T(8,128)(2,1)S(1)} %bitcast.22), channel_id=1, source_target_pairs={{0,16},{1,17},{2,18},{3,19},{4,20},{5,21},{6,22},{7,23},{8,24},{9,... | collective-permute-start | bytes 712712 | tf_op jit(solution)/shard_map/ppermute | solution.py:196
  133.3 1.8 %collective-permute-start.21 = (bf16[928,128]{1,0:T(8,128)(2,1)S(1)}, bf16[928,128]{1,0:T(8,128)(2,1)S(1)}, u32[]{:S(2)}, u32[]{:S(2)}) collective-permute-start(bf16[928,128]{1,0:T(8,128)(2,1)S(1)} %bitcast.24), channel_id=1, source_target_pairs={{0,1},{1,0},{2,3},{3,2},{4,5},{5,4},{6,7},{7,6},{8,9},{9,8},{10,11... | collective-permute-start | bytes 712712 | tf_op jit(solution)/shard_map/ppermute | solution.py:192
  135.1 3.1 %collective-permute-done.20.refs_3_ = bf16[928,128]{1,0:T(8,128)(2,1)S(1)} collective-permute-done((bf16[928,128]{1,0:T(8,128)(2,1)S(1)}, bf16[928,128]{1,0:T(8,128)(2,1)S(1)}, u32[]{:S(2)}, u32[]{:S(2)}) %collective-permute-start.20) | collective-permute-done | bytes 237600 | tf_op jit(solution)/shard_map/ppermute | solution.py:196
  138.2 2.9 %collective-permute-start.24 = (bf16[928,128]{1,0:T(8,128)(2,1)S(1)}, bf16[928,128]{1,0:T(8,128)(2,1)S(1)}, u32[]{:S(2)}, u32[]{:S(2)}) collective-permute-start(bf16[928,128]{1,0:T(8,128)(2,1)S(1)} %collective-permute-done.20.refs_3_), channel_id=1, source_target_pairs={{0,1},{1,0},{2,3},{3,2},{4,5},{5,4},{6,7},{7,6},{8,9},{9,8},{10,11... | collective-permute-start | bytes 712712 | tf_op jit(solution)/shard_map/ppermute | solution.py:192
  141.1 2.5 %collective-permute-done.19.refs_2_ = bf16[928,128]{1,0:T(8,128)(2,1)S(1)} collective-permute-done((bf16[928,128]{1,0:T(8,128)(2,1)S(1)}, bf16[928,128]{1,0:T(8,128)(2,1)S(1)}, u32[]{:S(2)}, u32[]{:S(2)}) %collective-permute-start.19) | collective-permute-done | bytes 237600 | tf_op jit(solution)/shard_map/ppermute | solution.py:196
  143.6 1.5 collective-permute-start.23
  145.7 1.5 copy-done.5
  147.2 2.6 %shard_map.84 = bf16[928,464]{1,0:T(8,128)(2,1)} custom-call(s32[3]{0:T(128)S(1)} %pad_add_fusion.pos_ref, bf16[8,464,128]{2,1,0:T(8,128)(2,1)S(1)} %all-to-all-done.2.rows_ref, bf16[8,928,128]{2,1,0:T(8,128)(2,1)S(1)} %copy-done.5), custom_call_target="tpu_custom_call" | custom-call | flops 881852416 | bytes 3712000 | tf_op jit(solution)/shard_map/pallas_call | solution.py:58
  149.9 3.6 %shard_map.85 = (bf16[8,464,128]{2,1,0:T(8,128)(2,1)}, bf16[8,928,128]{2,1,0:T(8,128)(2,1)}) custom-call(s32[3]{0:T(128)S(1)} %pad_add_fusion.pos_ref, bf16[928,128]{1,0:T(8,128)(2,1)S(1)} %bitcast.25, bf16[928,128]{1,0:T(8,128)(2,1)S(1)} %collective-permute-done.18.refs_1_, bf16[928,128]{1,0:T(8,128)(2,1)S(1)} %collective-permute-done.19.refs_2_, ...), custom_call_target="tpu_custom_call" | custom-call | flops 881852416 | bytes 5612544 | tf_op jit(solution)/shard_map/pallas_call | solution.py:58
  153.6 5.2 %all-to-all-start.6 = ((bf16[8,464,128]{2,1,0:T(8,128)(2,1)}), bf16[8,464,128]{2,1,0:T(8,128)(2,1)}, u32[]{:S(2)}, u32[]{:S(2)}) async-start(bf16[8,464,128]{2,1,0:T(8,128)(2,1)} %get-tuple-element.56), calls=%async_computation.6 | async-start | bytes 1900544 | tf_op jit(solution)/shard_map/all_to_all | solution.py:158
  158.7 1.5 copy-done.6
  160.2 2.7 %shard_map.87 = bf16[464,928]{1,0:T(8,128)(2,1)} custom-call(s32[3]{0:T(128)S(1)} %pad_add_fusion.pos_ref, bf16[8,464,128]{2,1,0:T(8,128)(2,1)S(1)} %all-to-all-done.rows_ref, bf16[8,928,128]{2,1,0:T(8,128)(2,1)S(1)} %copy-done.6), custom_call_target="tpu_custom_call" | custom-call | flops 881852416 | bytes 3712000 | tf_op jit(solution)/shard_map/pallas_call | solution.py:58
  162.9 1.3 shard_map.83
  164.2 8.6 %all-to-all-done.6.value_ref = bf16[8,464,128]{2,1,0:T(8,128)(2,1)} async-done(((bf16[8,464,128]{2,1,0:T(8,128)(2,1)}), bf16[8,464,128]{2,1,0:T(8,128)(2,1)}, u32[]{:S(2)}, u32[]{:S(2)}) %all-to-all-start.6) | async-done | bytes 950304 | tf_op jit(solution)/shard_map/all_to_all | solution.py:158
  172.8 2.0 %shard_map.86 = bf16[464,128]{1,0:T(8,128)(2,1)} custom-call(s32[3]{0:T(128)S(1)} %pad_add_fusion.pos_ref, bf16[8,464,128]{2,1,0:T(8,128)(2,1)} %all-to-all-done.6.value_ref), custom_call_target="tpu_custom_call" | custom-call | flops 475136 | bytes 1069056 | tf_op jit(solution)/shard_map/pallas_call | solution.py:58
  (65 shorter events, 18.2 us)
Async XLA Ops:
  0.7 0.9 copy-start.11
  2.3 0.9 copy-start.4
  3.2 8.2 %copy-start = (bf16[928,464]{1,0:T(8,128)(2,1)S(1)}, bf16[928,464]{1,0:T(8,128)(2,1)}, u32[]{:S(2)}) copy-start(bf16[928,464]{1,0:T(8,128)(2,1)} %weight_ref.3) | copy-start | bytes 2583556
  3.2 20.1 %all-to-all-start = ((bf16[8,464,128]{2,1,0:T(8,128)(2,1)}), bf16[8,464,128]{2,1,0:T(8,128)(2,1)S(1)}, u32[]{:S(2)}, u32[]{:S(2)}) async-start(bf16[8,464,128]{2,1,0:T(8,128)(2,1)} %copy-done.4), calls=%async_computation | async-start | bytes 1900544 | tf_op jit(solution)/shard_map/all_to_all | solution.py:158
  11.4 13.1 %copy-start.1 = (bf16[464,928]{0,1:T(8,128)(2,1)}, bf16[464,928]{0,1:T(8,128)(2,1)S(1)}, u32[]{:S(2)}) copy-start(bf16[464,928]{0,1:T(8,128)(2,1)S(1)} %copy.8) | copy-start | bytes 2583556
  12.9 12.6 %copy-start.12 = (bf16[128,464]{0,1:T(8,128)(2,1)S(1)}, bf16[128,464]{0,1:T(8,128)(2,1)}, u32[]{:S(2)}) copy-start(bf16[128,464]{0,1:T(8,128)(2,1)} %param.7) | copy-start | bytes 356356
  24.5 0.9 copy-start.7
  26.1 1.0 copy-start.3
  27.1 24.8 %all-to-all-start.2 = ((bf16[8,464,128]{2,1,0:T(8,128)(2,1)}), bf16[8,464,128]{2,1,0:T(8,128)(2,1)S(1)}, u32[]{:S(2)}, u32[]{:S(2)}) async-start(bf16[8,464,128]{2,1,0:T(8,128)(2,1)} %copy-done.3), calls=%async_computation.2 | async-start | bytes 1900544 | tf_op jit(solution)/shard_map/all_to_all | solution.py:158
  31.1 3.2 %collective-permute-start = (bf16[4,928,128]{2,1,0:T(8,128)(2,1)}, bf16[4,928,128]{2,1,0:T(8,128)(2,1)S(1)}, u32[]{:S(2)}, u32[]{:S(2)}) collective-permute-start(bf16[4,928,128]{2,1,0:T(8,128)(2,1)} %copy-done.7), channel_id=1, source_target_pairs={{0,1},{1,0},{2,3},{3,2},{4,5},{5,4},{6,7},{7,6},{8,9},{9,8},{10,11... | collective-permute-start | bytes 2850824 | tf_op jit(solution)/shard_map/ppermute | solution.py:192
  34.3 1.2 copy-start.2
  36.7 8.3 %collective-permute-start.1 = (bf16[928,128]{1,0:T(8,128)(2,1)S(1)}, bf16[928,128]{1,0:T(8,128)(2,1)S(1)}, u32[]{:S(2)}, u32[]{:S(2)}) collective-permute-start(bf16[928,128]{1,0:T(8,128)(2,1)S(1)} %get-tuple-element.34), channel_id=1, source_target_pairs={{0,8},{1,9},{2,10},{3,11},{4,12},{5,13},{6,14},{7,15},{8,16},{9,17... | collective-permute-start | bytes 712712 | tf_op jit(solution)/shard_map/ppermute | solution.py:196
  38.0 13.1 %collective-permute-start.2 = (bf16[928,128]{1,0:T(8,128)(2,1)S(1)}, bf16[928,128]{1,0:T(8,128)(2,1)S(1)}, u32[]{:S(2)}, u32[]{:S(2)}) collective-permute-start(bf16[928,128]{1,0:T(8,128)(2,1)S(1)} %get-tuple-element.35), channel_id=1, source_target_pairs={{0,16},{1,17},{2,18},{3,19},{4,20},{5,21},{6,22},{7,23},{8,24},{9,... | collective-permute-start | bytes 712712 | tf_op jit(solution)/shard_map/ppermute | solution.py:196
  40.4 10.6 %collective-permute-start.3 = (bf16[928,128]{1,0:T(8,128)(2,1)S(1)}, bf16[928,128]{1,0:T(8,128)(2,1)S(1)}, u32[]{:S(2)}, u32[]{:S(2)}) collective-permute-start(bf16[928,128]{1,0:T(8,128)(2,1)S(1)} %get-tuple-element.36), channel_id=1, source_target_pairs={{0,24},{1,25},{2,26},{3,27},{4,28},{5,29},{6,30},{7,31},{8,0},{9,1... | collective-permute-start | bytes 712712 | tf_op jit(solution)/shard_map/ppermute | solution.py:196
  54.0 8.5 %collective-permute-start.4 = (bf16[4,928,128]{2,1,0:T(8,128)(2,1)}, bf16[4,928,128]{2,1,0:T(8,128)(2,1)}, u32[]{:S(2)}, u32[]{:S(2)}) collective-permute-start(bf16[4,928,128]{2,1,0:T(8,128)(2,1)} %shard_map.79), channel_id=1, source_target_pairs={{0,1},{1,0},{2,3},{3,2},{4,5},{5,4},{6,7},{7,6},{8,9},{9,8},{10,11... | collective-permute-start | bytes 2850824 | tf_op jit(solution)/shard_map/ppermute | solution.py:192
  55.2 16.4 %all-to-all-start.1 = ((bf16[4,232,128]{2,1,0:T(8,128)(2,1)}), bf16[4,232,128]{2,1,0:T(8,128)(2,1)}, u32[]{:S(2)}, u32[]{:S(2)}) async-start(bf16[4,232,128]{2,1,0:T(8,128)(2,1)} %bitcast.6), calls=%async_computation.1 | async-start | bytes 475136 | tf_op jit(solution)/shard_map/all_to_all | solution.py:158
  65.2 8.6 %collective-permute-start.15 = (bf16[928,128]{1,0:T(8,128)(2,1)}, bf16[928,128]{1,0:T(8,128)(2,1)}, u32[]{:S(2)}, u32[]{:S(2)}) collective-permute-start(bf16[928,128]{1,0:T(8,128)(2,1)} %get-tuple-element.47), channel_id=1, source_target_pairs={{0,8},{1,9},{2,10},{3,11},{4,12},{5,13},{6,14},{7,15},{8,16},{9,17... | collective-permute-start | bytes 712712 | tf_op jit(solution)/shard_map/ppermute | solution.py:196
  66.2 13.1 %collective-permute-start.16 = (bf16[928,128]{1,0:T(8,128)(2,1)}, bf16[928,128]{1,0:T(8,128)(2,1)}, u32[]{:S(2)}, u32[]{:S(2)}) collective-permute-start(bf16[928,128]{1,0:T(8,128)(2,1)} %get-tuple-element.48), channel_id=1, source_target_pairs={{0,16},{1,17},{2,18},{3,19},{4,20},{5,21},{6,22},{7,23},{8,24},{9,... | collective-permute-start | bytes 712712 | tf_op jit(solution)/shard_map/ppermute | solution.py:196
  68.4 11.0 %collective-permute-start.17 = (bf16[928,128]{1,0:T(8,128)(2,1)}, bf16[928,128]{1,0:T(8,128)(2,1)}, u32[]{:S(2)}, u32[]{:S(2)}) collective-permute-start(bf16[928,128]{1,0:T(8,128)(2,1)} %get-tuple-element.49), channel_id=1, source_target_pairs={{0,24},{1,25},{2,26},{3,27},{4,28},{5,29},{6,30},{7,31},{8,0},{9,1... | collective-permute-start | bytes 712712 | tf_op jit(solution)/shard_map/ppermute | solution.py:196
  71.6 49.3 %copy-start.9 = (bf16[928,464]{0,1:T(8,128)(2,1)S(1)}, bf16[928,464]{0,1:T(8,128)(2,1)}, u32[]{:S(2)}) copy-start(bf16[928,464]{0,1:T(8,128)(2,1)} %copy.9) | copy-start | bytes 2583556
  81.4 25.9 %all-to-all-start.4 = ((bf16[4,232,128]{2,1,0:T(8,128)(2,1)}), bf16[4,232,128]{2,1,0:T(8,128)(2,1)}, u32[]{:S(2)}, u32[]{:S(2)}) async-start(bf16[4,232,128]{2,1,0:T(8,128)(2,1)} %bitcast.28), calls=%async_computation.4 | async-start | bytes 475136 | tf_op jit(solution)/shard_map/all_to_all | solution.py:158
  88.9 9.0 %collective-permute-start.7 = (bf16[232,128]{1,0:T(8,128)(2,1)S(1)}, bf16[232,128]{1,0:T(8,128)(2,1)S(1)}, u32[]{:S(2)}, u32[]{:S(2)}) collective-permute-start(bf16[232,128]{1,0:T(8,128)(2,1)S(1)} %fusion.2.refs_0_), channel_id=1, source_target_pairs={{0,2},{1,3},{2,4},{3,5},{4,6},{5,7},{6,0},{7,1},{8,10},{9,11},{10,... | collective-permute-start | bytes 178184 | tf_op jit(solution)/shard_map/ppermute | solution.py:200
  91.4 10.2 %collective-permute-start.6 = (bf16[232,128]{1,0:T(8,128)(2,1)S(1)}, bf16[232,128]{1,0:T(8,128)(2,1)S(1)}, u32[]{:S(2)}, u32[]{:S(2)}) collective-permute-start(bf16[232,128]{1,0:T(8,128)(2,1)S(1)} %fusion.2.refs_0_), channel_id=1, source_target_pairs={{0,4},{1,5},{2,6},{3,7},{4,0},{5,1},{6,2},{7,3},{8,12},{9,13},{10,... | collective-permute-start | bytes 178184 | tf_op jit(solution)/shard_map/ppermute | solution.py:200
  94.7 6.9 %collective-permute-start.5 = (bf16[232,128]{1,0:T(8,128)(2,1)S(1)}, bf16[232,128]{1,0:T(8,128)(2,1)S(1)}, u32[]{:S(2)}, u32[]{:S(2)}) collective-permute-start(bf16[232,128]{1,0:T(8,128)(2,1)S(1)} %fusion.2.refs_0_), channel_id=1, source_target_pairs={{0,6},{1,7},{2,0},{3,1},{4,2},{5,3},{6,4},{7,5},{8,14},{9,15},{10,... | collective-permute-start | bytes 178184 | tf_op jit(solution)/shard_map/ppermute | solution.py:200
  102.1 14.4 %collective-permute-start.10 = (bf16[928,128]{1,0:T(8,128)(2,1)S(1)}, bf16[928,128]{1,0:T(8,128)(2,1)}, u32[]{:S(2)}, u32[]{:S(2)}) collective-permute-start(bf16[928,128]{1,0:T(8,128)(2,1)S(1)} %bitcast.16), channel_id=1, source_target_pairs={{0,8},{1,9},{2,10},{3,11},{4,12},{5,13},{6,14},{7,15},{8,16},{9,17... | collective-permute-start | bytes 712712 | tf_op jit(solution)/shard_map/ppermute | solution.py:196
  104.7 11.9 %collective-permute-start.9 = (bf16[928,128]{1,0:T(8,128)(2,1)S(1)}, bf16[928,128]{1,0:T(8,128)(2,1)}, u32[]{:S(2)}, u32[]{:S(2)}) collective-permute-start(bf16[928,128]{1,0:T(8,128)(2,1)S(1)} %bitcast.17), channel_id=1, source_target_pairs={{0,16},{1,17},{2,18},{3,19},{4,20},{5,21},{6,22},{7,23},{8,24},{9,... | collective-permute-start | bytes 712712 | tf_op jit(solution)/shard_map/ppermute | solution.py:196
  107.2 12.0 %collective-permute-start.8 = (bf16[928,128]{1,0:T(8,128)(2,1)S(1)}, bf16[928,128]{1,0:T(8,128)(2,1)}, u32[]{:S(2)}, u32[]{:S(2)}) collective-permute-start(bf16[928,128]{1,0:T(8,128)(2,1)S(1)} %bitcast.18), channel_id=1, source_target_pairs={{0,24},{1,25},{2,26},{3,27},{4,28},{5,29},{6,30},{7,31},{8,0},{9,1... | collective-permute-start | bytes 712712 | tf_op jit(solution)/shard_map/ppermute | solution.py:196
  109.0 15.8 %all-to-all-start.5 = ((bf16[4,232,128]{2,1,0:T(8,128)(2,1)}), bf16[4,232,128]{2,1,0:T(8,128)(2,1)S(1)}, u32[]{:S(2)}, u32[]{:S(2)}) async-start(bf16[4,232,128]{2,1,0:T(8,128)(2,1)} %broadcast_in_dim.2), calls=%async_computation.5 | async-start | bytes 475136 | tf_op jit(solution)/shard_map/all_to_all | solution.py:158
  113.3 6.0 %collective-permute-start.11 = (bf16[928,128]{1,0:T(8,128)(2,1)S(1)}, bf16[928,128]{1,0:T(8,128)(2,1)S(1)}, u32[]{:S(2)}, u32[]{:S(2)}) collective-permute-start(bf16[928,128]{1,0:T(8,128)(2,1)S(1)} %bitcast.19), channel_id=1, source_target_pairs={{0,1},{1,0},{2,3},{3,2},{4,5},{5,4},{6,7},{7,6},{8,9},{9,8},{10,11... | collective-permute-start | bytes 712712 | tf_op jit(solution)/shard_map/ppermute | solution.py:192
  116.5 2.7 %collective-permute-start.14 = (bf16[928,128]{1,0:T(8,128)(2,1)}, bf16[928,128]{1,0:T(8,128)(2,1)S(1)}, u32[]{:S(2)}, u32[]{:S(2)}) collective-permute-start(bf16[928,128]{1,0:T(8,128)(2,1)} %collective-permute-done.10.refs_3_), channel_id=1, source_target_pairs={{0,1},{1,0},{2,3},{3,2},{4,5},{5,4},{6,7},{7,6},{8,9},{9,8},{10,11... | collective-permute-start | bytes 712712 | tf_op jit(solution)/shard_map/ppermute | solution.py:192
  116.6 3.9 %collective-permute-start.13 = (bf16[928,128]{1,0:T(8,128)(2,1)}, bf16[928,128]{1,0:T(8,128)(2,1)S(1)}, u32[]{:S(2)}, u32[]{:S(2)}) collective-permute-start(bf16[928,128]{1,0:T(8,128)(2,1)} %collective-permute-done.9.refs_2_), channel_id=1, source_target_pairs={{0,1},{1,0},{2,3},{3,2},{4,5},{5,4},{6,7},{7,6},{8,9},{9,8},{10,11... | collective-permute-start | bytes 712712 | tf_op jit(solution)/shard_map/ppermute | solution.py:192
  119.2 1.7 collective-permute-start.12
  123.9 0.9 copy-start.10
  124.8 28.7 %all-to-all-start.3 = ((bf16[8,464,128]{2,1,0:T(8,128)(2,1)}), bf16[8,464,128]{2,1,0:T(8,128)(2,1)S(1)}, u32[]{:S(2)}, u32[]{:S(2)}) async-start(bf16[8,464,128]{2,1,0:T(8,128)(2,1)} %copy-done.10), calls=%async_computation.3 | async-start | bytes 1900544 | tf_op jit(solution)/shard_map/all_to_all | solution.py:158
  130.6 7.6 %collective-permute-start.20 = (bf16[928,128]{1,0:T(8,128)(2,1)S(1)}, bf16[928,128]{1,0:T(8,128)(2,1)S(1)}, u32[]{:S(2)}, u32[]{:S(2)}) collective-permute-start(bf16[928,128]{1,0:T(8,128)(2,1)S(1)} %bitcast.21), channel_id=1, source_target_pairs={{0,8},{1,9},{2,10},{3,11},{4,12},{5,13},{6,14},{7,15},{8,16},{9,17... | collective-permute-start | bytes 712712 | tf_op jit(solution)/shard_map/ppermute | solution.py:196
  130.6 13.0 %collective-permute-start.19 = (bf16[928,128]{1,0:T(8,128)(2,1)S(1)}, bf16[928,128]{1,0:T(8,128)(2,1)S(1)}, u32[]{:S(2)}, u32[]{:S(2)}) collective-permute-start(bf16[928,128]{1,0:T(8,128)(2,1)S(1)} %bitcast.22), channel_id=1, source_target_pairs={{0,16},{1,17},{2,18},{3,19},{4,20},{5,21},{6,22},{7,23},{8,24},{9,... | collective-permute-start | bytes 712712 | tf_op jit(solution)/shard_map/ppermute | solution.py:196
  133.3 11.8 %collective-permute-start.18 = (bf16[928,128]{1,0:T(8,128)(2,1)S(1)}, bf16[928,128]{1,0:T(8,128)(2,1)S(1)}, u32[]{:S(2)}, u32[]{:S(2)}) collective-permute-start(bf16[928,128]{1,0:T(8,128)(2,1)S(1)} %bitcast.23), channel_id=1, source_target_pairs={{0,24},{1,25},{2,26},{3,27},{4,28},{5,29},{6,30},{7,31},{8,0},{9,1... | collective-permute-start | bytes 712712 | tf_op jit(solution)/shard_map/ppermute | solution.py:196
  133.3 16.6 %collective-permute-start.21 = (bf16[928,128]{1,0:T(8,128)(2,1)S(1)}, bf16[928,128]{1,0:T(8,128)(2,1)S(1)}, u32[]{:S(2)}, u32[]{:S(2)}) collective-permute-start(bf16[928,128]{1,0:T(8,128)(2,1)S(1)} %bitcast.24), channel_id=1, source_target_pairs={{0,1},{1,0},{2,3},{3,2},{4,5},{5,4},{6,7},{7,6},{8,9},{9,8},{10,11... | collective-permute-start | bytes 712712 | tf_op jit(solution)/shard_map/ppermute | solution.py:192
  138.2 11.7 %collective-permute-start.24 = (bf16[928,128]{1,0:T(8,128)(2,1)S(1)}, bf16[928,128]{1,0:T(8,128)(2,1)S(1)}, u32[]{:S(2)}, u32[]{:S(2)}) collective-permute-start(bf16[928,128]{1,0:T(8,128)(2,1)S(1)} %collective-permute-done.20.refs_3_), channel_id=1, source_target_pairs={{0,1},{1,0},{2,3},{3,2},{4,5},{5,4},{6,7},{7,6},{8,9},{9,8},{10,11... | collective-permute-start | bytes 712712 | tf_op jit(solution)/shard_map/ppermute | solution.py:192
  143.6 6.3 %collective-permute-start.23 = (bf16[928,128]{1,0:T(8,128)(2,1)S(1)}, bf16[928,128]{1,0:T(8,128)(2,1)S(1)}, u32[]{:S(2)}, u32[]{:S(2)}) collective-permute-start(bf16[928,128]{1,0:T(8,128)(2,1)S(1)} %collective-permute-done.19.refs_2_), channel_id=1, source_target_pairs={{0,1},{1,0},{2,3},{3,2},{4,5},{5,4},{6,7},{7,6},{8,9},{9,8},{10,11... | collective-permute-start | bytes 712712 | tf_op jit(solution)/shard_map/ppermute | solution.py:192
  145.1 4.8 %collective-permute-start.22 = (bf16[928,128]{1,0:T(8,128)(2,1)S(1)}, bf16[928,128]{1,0:T(8,128)(2,1)S(1)}, u32[]{:S(2)}, u32[]{:S(2)}) collective-permute-start(bf16[928,128]{1,0:T(8,128)(2,1)S(1)} %collective-permute-done.18.refs_1_), channel_id=1, source_target_pairs={{0,1},{1,0},{2,3},{3,2},{4,5},{5,4},{6,7},{7,6},{8,9},{9,8},{10,11... | collective-permute-start | bytes 712712 | tf_op jit(solution)/shard_map/ppermute | solution.py:192
  145.7 1.5 copy-start.5
  147.2 2.7 %copy-start.8 = (bf16[464,928]{1,0:T(8,128)(2,1)S(1)}, bf16[464,928]{1,0:T(8,128)(2,1)}, u32[]{:S(2)}) copy-start(bf16[464,928]{1,0:T(8,128)(2,1)} %refs_8_.1) | copy-start | bytes 2583556
  153.6 19.2 %all-to-all-start.6 = ((bf16[8,464,128]{2,1,0:T(8,128)(2,1)}), bf16[8,464,128]{2,1,0:T(8,128)(2,1)}, u32[]{:S(2)}, u32[]{:S(2)}) async-start(bf16[8,464,128]{2,1,0:T(8,128)(2,1)} %get-tuple-element.56), calls=%async_computation.6 | async-start | bytes 1900544 | tf_op jit(solution)/shard_map/all_to_all | solution.py:158
  158.7 1.5 copy-start.6

commit v4 on v3

--- a/solution.py
+++ b/solution.py
@@ -52,16 +52,16 @@
     return jax.ShapeDtypeStruct(shape, dtype)
 
 
-def kernel_call(kernel, outs, flops, pos, operands, scratch=(), far=()):
+def kernel_call(kernel, outs, flops, pos, operands, scratch=(), far=(), far_in=()):
     moved = sum(math.prod(o.shape) * o.dtype.itemsize for o in [*operands, *outs])
     vmem = pl.BlockSpec(memory_space=pltpu.VMEM)
+    hbm = pl.BlockSpec(memory_space=pltpu.HBM)
     return pl.pallas_call(
         kernel,
         out_shape=[pltpu.HBM(o.shape, o.dtype) if i in far else o for i, o in enumerate(outs)],
-        in_specs=[pl.BlockSpec(memory_space=pltpu.SMEM)] + [vmem] * len(operands),
-        out_specs=[
-            pl.BlockSpec(memory_space=pltpu.HBM) if i in far else vmem for i in range(len(outs))
-        ],
+        in_specs=[pl.BlockSpec(memory_space=pltpu.SMEM)]
+        + [hbm if i in far_in else vmem for i in range(len(operands))],
+        out_specs=[hbm if i in far else vmem for i in range(len(outs))],
         scratch_shapes=scratch,
         compiler_params=pltpu.CompilerParams(vmem_limit_bytes=16 * 1024 * 1024),
         cost_estimate=pl.CostEstimate(flops=flops, bytes_accessed=moved, transcendentals=0),
@@ -80,34 +80,64 @@
     return value[:, d * LANES : (d + 1) * LANES]
 
 
+def staged(out):
+    return [pltpu.VMEM(out.shape, out.dtype), pltpu.SemaphoreType.DMA(out.shape[:1])]
+
+
 def other_half(pos, rows, weight):
     depth, width = weight.shape
 
-    def kernel(pos_ref, rows_ref, weight_ref, out_ref):
+    def kernel(pos_ref, rows_ref, weight_ref, out_ref, held_ref, sems):
         rows = half_of(rows_ref, 1 - pos_ref[1], pos_ref[0])
-        product = dot(weight_ref[...], rows, PLAIN).astype(BF)
-        for d in range(X):
-            out_ref[d] = block(product, d)
-
-    outs = [shaped((X, depth, LANES), BF)]
-    return kernel_call(kernel, outs, 2 * depth * width * X * LANES, pos, [rows, weight])[0]
+        copies = []
+        for pair in range(X // 2):
+            here = rows[:, pair * 2 * LANES : (pair + 1) * 2 * LANES]
+            product = dot(weight_ref[...], here, PLAIN).astype(BF)
+            for d in range(2):
+                index = pair * 2 + d
+                held_ref[index] = block(product, d)
+                copies.append(
+                    pltpu.make_async_copy(held_ref.at[index], out_ref.at[index], sems.at[index])
+                )
+                copies[-1].start()
+        for copy in copies:
+            copy.wait()
+
+    out = shaped((X, depth, LANES), BF)
+    flops = 2 * depth * width * X * LANES
+    return kernel_call(kernel, [out], flops, pos, [rows, weight], staged(out), (0,))[0]
 
 
 def own_half(pos, rows, weight, arrived):
     depth, width = weight.shape
 
-    def kernel(pos_ref, rows_ref, weight_ref, arrived_ref, keep_ref, *sent):
-        product = dot(weight_ref[...], half_of(rows_ref, pos_ref[1], pos_ref[0]), PLAIN)
-        for d in range(X):
-            total = block(product, d) + arrived_ref[d].astype(F32)
-            if d == 0:
-                keep_ref[...] = total
-            else:
-                sent[d - 1][...] = total.astype(BF)
-
-    outs = [shaped((depth, LANES), F32)] + [shaped((depth, LANES), BF)] * (X - 1)
+    def kernel(pos_ref, rows_ref, weight_ref, arrived_ref, keep_ref, *refs):
+        sent, held_ref, sems = refs[: X - 1], refs[-2], refs[-1]
+        rows = half_of(rows_ref, pos_ref[1], pos_ref[0])
+        copies = []
+        for pair in (1, 0):
+            here = rows[:, pair * 2 * LANES : (pair + 1) * 2 * LANES]
+            product = dot(weight_ref[...], here, PLAIN)
+            for i in range(2):
+                d = pair * 2 + i
+                total = block(product, i) + arrived_ref[d].astype(F32)
+                if d == 0:
+                    keep_ref[...] = total
+                    continue
+                held_ref[d - 1] = total.astype(BF)
+                copies.append(
+                    pltpu.make_async_copy(held_ref.at[d - 1], sent[d - 1], sems.at[d - 1])
+                )
+                copies[-1].start()
+        for copy in copies:
+            copy.wait()
+
+    part = shaped((depth, LANES), BF)
+    outs = [shaped((depth, LANES), F32)] + [part] * (X - 1)
+    scratch = staged(shaped((X - 1,) + part.shape, BF))
     flops = 2 * depth * width * X * LANES
-    keep, *sent = kernel_call(kernel, outs, flops, pos, [rows, weight, arrived])
+    operands = [rows, weight, arrived]
+    keep, *sent = kernel_call(kernel, outs, flops, pos, operands, scratch, range(1, X))
     return keep, sent
 
 
@@ -116,7 +146,7 @@
     count = 2 * X
 
     def kernel(pos_ref, *refs):
-        weight_ref, out_ref, kept_ref, sems = refs[-4:]
+        weight_ref, out_ref, kept_ref, held_ref, out_sems, sems = refs[-6:]
         kept = [
             pltpu.make_async_copy(refs[index], kept_ref.at[index], sems.at[index])
             for index in range(count)
@@ -127,14 +157,19 @@
         for part, half in ((refs[:X], c), (refs[X:count], 1 - c)):
             product = dot(weight_ref[...], wide(part), PLAIN).astype(BF)
             for d in range(X):
-                out_ref[half * X + ((x + d) & 3)] = block(product, d)
+                index, target = len(kept) - count, half * X + ((x + d) & 3)
+                held_ref[index] = block(product, d)
+                kept.append(
+                    pltpu.make_async_copy(held_ref.at[index], out_ref.at[target], out_sems.at[index])
+                )
+                kept[-1].start()
         for copy in kept:
             copy.wait()
 
     outs = [shaped((count, depth, LANES), BF), shaped((count, width, LANES), BF)]
     flops = 2 * depth * width * count * LANES
-    scratch = [pltpu.SemaphoreType.DMA((count,))]
-    return kernel_call(kernel, outs, flops, pos, [*blocks, weight], scratch, (1,))
+    scratch = staged(outs[0]) + [pltpu.SemaphoreType.DMA((count,))]
+    return kernel_call(kernel, outs, flops, pos, [*blocks, weight], scratch, (0, 1))
 
 
 def weight_grad(pos, factor, rows, blocks, rows_first):
@@ -158,16 +193,20 @@
     return lax.all_to_all(value, axis, 0, 0, axis_index_groups=groups)
 
 
-def copies(value, count):
-    return jnp.broadcast_to(value[None], (count,) + value.shape)
-
-
 def many(pos, value, count):
-    def kernel(pos_ref, value_ref, out_ref):
-        for index in range(count):
-            out_ref[index] = value_ref[...]
-
-    return kernel_call(kernel, [shaped((count,) + value.shape, BF)], 0, pos, [value])[0]
+    def kernel(pos_ref, value_ref, out_ref, sems):
+        copies = [
+            pltpu.make_async_copy(value_ref, out_ref.at[index], sems.at[index])
+            for index in range(count)
+        ]
+        for copy in copies:
+            copy.start()
+        for copy in copies:
+            copy.wait()
+
+    outs = [shaped((count,) + value.shape, BF)]
+    scratch = [pltpu.SemaphoreType.DMA((count,))]
+    return kernel_call(kernel, outs, 0, pos, [value], scratch, (0,), (0,))[0]
 
 
 def added(pos, value):
@@ -216,16 +255,16 @@
     return exchange(value, "rep", Z_GROUPS)
 
 
-def spread_z(pos, value, by_permutes):
-    if by_permutes:
-        whole = in_order(pos, [value] + [move_z(value, -d) for d in range(1, Z)])
-    else:
-        whole = exchange(copies(value, Z), "rep", Z_GROUPS)
+def spread_z(pos, value):
+    whole = in_order(pos, [value] + [move_z(value, -d) for d in range(1, Z)])
     return whole.reshape(Z * value.shape[0], LANES)
 
 
 def spread_x(value):
-    own = [value] + [move_x(value, -d) for d in range(1, X)]
+    return [value] + [move_x(value, -d) for d in range(1, X)]
+
+
+def with_other_half(own):
     return own + [swap_cores(part) for part in own]
 
 
@@ -239,8 +278,8 @@
         (first_weight.T, second_weight.T, tok)
     )
     sent = other_half(pos, tok, first_turned)
-    cot = exchange(many(pos, after(cotangent.T, sent), GRP), "grp")
     keep, sent = own_half(pos, tok, first_turned, swap_cores(sent))
+    cot = exchange(many(pos, after(cotangent.T, keep), GRP), "grp")
     value = sum_x(keep, sent)
 
     sent = other_half(pos, after(cot, value), second_weight)
@@ -249,15 +288,16 @@
     hidden = total_of(after(scatter_z(value), keep))
     active = jax.nn.gelu(hidden, approximate=False).astype(BF)
     active, hidden = lax.optimization_barrier((active, hidden))
-    upward = total_of(scatter_z(sum_x(keep, sent)))
+    active = spread_z(pos, active)
+    upward = total_of(scatter_z(sum_x(after(keep, active), sent)))
     deltas = (upward * slope(hidden)).astype(BF)
 
-    act = spread_x(spread_z(pos, active, True))
-    dlt = spread_x(spread_z(pos, deltas, False))
+    act = with_other_half(spread_x(active))
+    dlt = spread_x(spread_z(pos, deltas))
     out, act = both_halves(pos, act, second_turned)
     out = exchange(out, "grp")
     second_grad = weight_grad(pos, factor, cot, act, False)
-    dlt[0] = after(dlt[0], second_grad)
+    dlt = with_other_half([dlt[0]] + [after(part, second_grad) for part in dlt[1:]])
     back, dlt = both_halves(pos, dlt, first_weight)
     back = exchange(back, "grp")
     first_grad = weight_grad(pos, factor, tok, dlt, True)

time: 176 us -> 174 us (0.989)
  local copies, waits for them, and re-layouts: 12.7 us -> 7 us
  Pallas kernels: 24.3 us -> 28.6 us
  waiting for transfers between devices: 51.5 us -> 55.8 us
  starting transfers between devices: 80.3 us -> 78 us
  other arithmetic: 5.16 us -> 3.04 us
    ppermute x12, waiting for transfers between devices: 22.8 us -> 9.66 us  [move_x(): return lax.ppermute(value, 'rep', rep_pairs(d, 0, 0))]
    ppermute x3 -> x6, waiting for transfers between devices: 3.6 us -> 15.9 us  [move_z(): return lax.ppermute(value, 'rep', rep_pairs(0, d, 0))]
    all_to_all x7 -> x6, starting transfers between devices: 39.3 us -> 32.5 us  [exchange(): return lax.all_to_all(value, axis, 0, 0, axis_index_groups=groups)]
    unnamed x28 -> x16, local copies, waits for them, and re-layouts: 12 us -> 7 us
    pallas_call x13 -> x14, Pallas kernels: 24.3 us -> 28.6 us  [kernel_call(): pl.pallas_call(kernel, out_shape=[pltpu.HBM(o.shape, o.dtype) if i in far...]
    all_to_all x7 -> x6, waiting for transfers between devices: 21 us -> 25.3 us  [exchange(): return lax.all_to_all(value, axis, 0, 0, axis_index_groups=groups)]
    ppermute x3 -> x6, starting transfers between devices: 9.02 us -> 11.5 us  [move_z(): return lax.ppermute(value, 'rep', rep_pairs(0, d, 0))]
    ppermute x10, starting transfers between devices: 14.8 us -> 17.1 us  [swap_cores(): return lax.ppermute(value, 'rep', rep_pairs(0, 0, 1))]
  transfers between devices with their start and end apart: 32 -> 34, of which waited for: 13 -> 17; matrix products, arithmetic and copies ran while one was open for 4% -> 3% of each run, Pallas kernels for 10% -> 10%
where the time goes in v4:
time: 174 us; the launch traced here: 173 us
  starting transfers between devices  78 us (45%)
  waiting for transfers between devices  55.8 us (32%)
  Pallas kernels  28.6 us (16%)
  local copies, waits for them, and re-layouts  7 us (4%)
  other arithmetic  3.04 us (2%)
    all_to_all x6, starting transfers between devices, exchange(): return lax.all_to_all(value, axis, 0, 0, axis_index_groups=groups)  32.5 us
    pallas_call x14, Pallas kernels, kernel_call(): pl.pallas_call(kernel, out_shape=[pltpu.HBM(o.shape, o.dtype) if i in far...  28.6 us
    all_to_all x6, waiting for transfers between devices, exchange(): return lax.all_to_all(value, axis, 0, 0, axis_index_groups=groups)  25.3 us
    ppermute x10, starting transfers between devices, swap_cores(): return lax.ppermute(value, 'rep', rep_pairs(0, 0, 1))  17.1 us
    ppermute x12, starting transfers between devices, move_x(): return lax.ppermute(value, 'rep', rep_pairs(d, 0, 0))  16.8 us
    ppermute x6, waiting for transfers between devices, move_z(): return lax.ppermute(value, 'rep', rep_pairs(0, d, 0))  15.9 us
    ppermute x6, starting transfers between devices, move_z(): return lax.ppermute(value, 'rep', rep_pairs(0, d, 0))  11.5 us
    ppermute x12, waiting for transfers between devices, move_x(): return lax.ppermute(value, 'rep', rep_pairs(d, 0, 0))  9.66 us
  transfers between devices with their start and end apart: 34, of which 17 were waited for; matrix products, arithmetic and copies ran while one was open for 3% of the time, Pallas kernels for 10%

profile of v4, /device:TPU:1, one launch (start us, length us, event | category | flops | bytes accessed | tf_op | source)
XLA Modules:
  0.0 173.2 jit_solution(7907922484147703561)
XLA Ops:
  1.6 1.5 shard_map.75
  3.2 6.5 %all-to-all-start = ((bf16[8,464,128]{2,1,0:T(8,128)(2,1)}), bf16[8,464,128]{2,1,0:T(8,128)(2,1)S(1)}, u32[]{:S(2)}, u32[]{:S(2)}) async-start(bf16[8,464,128]{2,1,0:T(8,128)(2,1)} %shard_map.75), calls=%async_computation | async-start | bytes 1900544 | tf_op jit(solution)/shard_map/all_to_all | solution.py:193
  9.7 1.6 copy.8
  11.3 1.4 copy.9
  12.7 10.5 %all-to-all-done.rows_ref = bf16[8,464,128]{2,1,0:T(8,128)(2,1)S(1)} async-done(((bf16[8,464,128]{2,1,0:T(8,128)(2,1)}), bf16[8,464,128]{2,1,0:T(8,128)(2,1)S(1)}, u32[]{:S(2)}, u32[]{:S(2)}) %all-to-all-start) | async-done | bytes 950304 | tf_op jit(solution)/shard_map/all_to_all | solution.py:193
  23.3 2.2 %shard_map.76 = bf16[4,928,128]{2,1,0:T(8,128)(2,1)} custom-call(s32[3]{0:T(128)S(1)} %pad_add_fusion.pos_ref, bf16[8,464,128]{2,1,0:T(8,128)(2,1)S(1)} %all-to-all-done.rows_ref, bf16[928,464]{1,0:T(8,128)(2,1)S(1)} %bitcast.13), custom_call_target="tpu_custom_call" | custom-call | flops 440926208 | bytes 2761728 | tf_op jit(solution)/shard_map/pallas_call | solution.py:59
  26.7 2.4 %collective-permute-done.arrived_ref = bf16[4,928,128]{2,1,0:T(8,128)(2,1)S(1)} collective-permute-done((bf16[4,928,128]{2,1,0:T(8,128)(2,1)}, bf16[4,928,128]{2,1,0:T(8,128)(2,1)S(1)}, u32[]{:S(2)}, u32[]{:S(2)}) %collective-permute-start) | collective-permute-done | bytes 950304 | tf_op jit(solution)/shard_map/ppermute | solution.py:231
  29.0 2.1 %shard_map.77 = (f32[928,128]{1,0:T(8,128)S(1)}, bf16[928,128]{1,0:T(8,128)(2,1)}, bf16[928,128]{1,0:T(8,128)(2,1)}, bf16[928,128]{1,0:T(8,128)(2,1)}) custom-call(s32[3]{0:T(128)S(1)} %pad_add_fusion.pos_ref, bf16[8,464,128]{2,1,0:T(8,128)(2,1)S(1)} %all-to-all-done.rows_ref, bf16[928,464]{1,0:T(8,128)(2,1)S(1)} %bitcast.14, ...), custom_call_target="tpu_custom_call" | custom-call | flops 440926208 | bytes 3949568 | tf_op jit(solution)/shard_map/pallas_call | solution.py:59
  31.2 1.5 shard_map.78
  32.7 3.6 %all-to-all-start.2 = ((bf16[8,464,128]{2,1,0:T(8,128)(2,1)}), bf16[8,464,128]{2,1,0:T(8,128)(2,1)S(1)}, u32[]{:S(2)}, u32[]{:S(2)}) async-start(bf16[8,464,128]{2,1,0:T(8,128)(2,1)} %shard_map.78), calls=%async_computation.2 | async-start | bytes 1900544 | tf_op jit(solution)/shard_map/all_to_all | solution.py:193
  36.3 1.3 collective-permute-start.1
  37.6 2.4 %collective-permute-start.2 = (bf16[928,128]{1,0:T(8,128)(2,1)}, bf16[928,128]{1,0:T(8,128)(2,1)S(1)}, u32[]{:S(2)}, u32[]{:S(2)}) collective-permute-start(bf16[928,128]{1,0:T(8,128)(2,1)} %get-tuple-element.38), channel_id=1, source_target_pairs={{0,16},{1,17},{2,18},{3,19},{4,20},{5,21},{6,22},{7,23},{8,24},{9,... | collective-permute-start | bytes 712712 | tf_op jit(solution)/shard_map/ppermute | solution.py:235
  41.2 3.5 %collective-permute-done.1 = bf16[928,128]{1,0:T(8,128)(2,1)S(1)} collective-permute-done((bf16[928,128]{1,0:T(8,128)(2,1)}, bf16[928,128]{1,0:T(8,128)(2,1)S(1)}, u32[]{:S(2)}, u32[]{:S(2)}) %collective-permute-start.1) | collective-permute-done | bytes 237600 | tf_op jit(solution)/shard_map/ppermute | solution.py:235
  44.7 6.1 %collective-permute-done.2 = bf16[928,128]{1,0:T(8,128)(2,1)S(1)} collective-permute-done((bf16[928,128]{1,0:T(8,128)(2,1)}, bf16[928,128]{1,0:T(8,128)(2,1)S(1)}, u32[]{:S(2)}, u32[]{:S(2)}) %collective-permute-start.2) | collective-permute-done | bytes 237600 | tf_op jit(solution)/shard_map/ppermute | solution.py:235
  51.6 2.2 %shard_map.79 = bf16[4,928,128]{2,1,0:T(8,128)(2,1)} custom-call(s32[3]{0:T(128)S(1)} %pad_add_fusion.pos_ref, bf16[8,464,128]{2,1,0:T(8,128)(2,1)S(1)} %all-to-all-done.2.rows_ref, bf16[928,464]{1,0:T(8,128)(2,1)S(1)} %copy-done), custom_call_target="tpu_custom_call" | custom-call | flops 440926208 | bytes 2761728 | tf_op jit(solution)/shard_map/pallas_call | solution.py:59
  53.8 1.3 collective-permute-start.4
  55.1 7.3 %all-to-all-start.1 = ((bf16[4,232,128]{2,1,0:T(8,128)(2,1)}), bf16[4,232,128]{2,1,0:T(8,128)(2,1)}, u32[]{:S(2)}, u32[]{:S(2)}) async-start(bf16[4,232,128]{2,1,0:T(8,128)(2,1)} %bitcast.6), calls=%async_computation.1 | async-start | bytes 475136 | tf_op jit(solution)/shard_map/all_to_all | solution.py:193
  62.4 2.8 %shard_map.80 = (f32[928,128]{1,0:T(8,128)S(1)}, bf16[928,128]{1,0:T(8,128)(2,1)}, bf16[928,128]{1,0:T(8,128)(2,1)}, bf16[928,128]{1,0:T(8,128)(2,1)}) custom-call(s32[3]{0:T(128)S(1)} %pad_add_fusion.pos_ref, bf16[8,464,128]{2,1,0:T(8,128)(2,1)S(1)} %all-to-all-done.2.rows_ref, bf16[928,464]{1,0:T(8,128)(2,1)S(1)} %copy-done, ...), custom_call_target="tpu_custom_call" | custom-call | flops 440926208 | bytes 3949568 | tf_op jit(solution)/shard_map/pallas_call | solution.py:59
  65.2 6.3 %all-to-all-done.1 = bf16[4,232,128]{2,1,0:T(8,128)(2,1)} async-done(((bf16[4,232,128]{2,1,0:T(8,128)(2,1)}), bf16[4,232,128]{2,1,0:T(8,128)(2,1)}, u32[]{:S(2)}, u32[]{:S(2)}) %all-to-all-start.1) | async-done | bytes 237600 | tf_op jit(solution)/shard_map/all_to_all | solution.py:193
  73.7 2.1 %collective-permute-start.16 = (bf16[928,128]{1,0:T(8,128)(2,1)}, bf16[928,128]{1,0:T(8,128)(2,1)S(1)}, u32[]{:S(2)}, u32[]{:S(2)}) collective-permute-start(bf16[928,128]{1,0:T(8,128)(2,1)} %get-tuple-element.52), channel_id=1, source_target_pairs={{0,16},{1,17},{2,18},{3,19},{4,20},{5,21},{6,22},{7,23},{8,24},{9,... | collective-permute-start | bytes 712712 | tf_op jit(solution)/shard_map/ppermute | solution.py:235
  75.8 1.3 collective-permute-start.17
  77.4 4.3 %collective-permute-start.6 = (bf16[232,128]{1,0:T(8,128)(2,1)S(1)}, bf16[232,128]{1,0:T(8,128)(2,1)S(1)}, u32[]{:S(2)}, u32[]{:S(2)}) collective-permute-start(bf16[232,128]{1,0:T(8,128)(2,1)S(1)} %fusion.2.refs_0_), channel_id=1, source_target_pairs={{0,4},{1,5},{2,6},{3,7},{4,0},{5,1},{6,2},{7,3},{8,12},{9,13},{10,... | collective-permute-start | bytes 178184 | tf_op jit(solution)/shard_map/ppermute | solution.py:239
  81.7 1.6 collective-permute-done.7.refs_3_
  84.7 2.8 %collective-permute-done.5.refs_1_ = bf16[232,128]{1,0:T(8,128)(2,1)S(1)} collective-permute-done((bf16[232,128]{1,0:T(8,128)(2,1)S(1)}, bf16[232,128]{1,0:T(8,128)(2,1)S(1)}, u32[]{:S(2)}, u32[]{:S(2)}) %collective-permute-start.5) | collective-permute-done | bytes 59424 | tf_op jit(solution)/shard_map/ppermute | solution.py:239
  88.9 1.3 collective-permute-start.9
  90.2 1.4 collective-permute-start.8
  92.4 4.2 %all-to-all-start.4 = ((bf16[4,232,128]{2,1,0:T(8,128)(2,1)}), bf16[4,232,128]{2,1,0:T(8,128)(2,1)S(1)}, u32[]{:S(2)}, u32[]{:S(2)}) async-start(bf16[4,232,128]{2,1,0:T(8,128)(2,1)} %bitcast.23), calls=%async_computation.4 | async-start | bytes 475136 | tf_op jit(solution)/shard_map/all_to_all | solution.py:193
  96.6 5.1 %collective-permute-start.11 = (bf16[928,128]{1,0:T(8,128)(2,1)}, bf16[928,128]{1,0:T(8,128)(2,1)S(1)}, u32[]{:S(2)}, u32[]{:S(2)}) collective-permute-start(bf16[928,128]{1,0:T(8,128)(2,1)} %bitcast.8.refs_0_), channel_id=1, source_target_pairs={{0,1},{1,0},{2,3},{3,2},{4,5},{5,4},{6,7},{7,6},{8,9},{9,8},{10,11... | collective-permute-start | bytes 712712 | tf_op jit(solution)/shard_map/ppermute | solution.py:231
  101.8 2.1 %collective-permute-start.14 = (bf16[928,128]{1,0:T(8,128)(2,1)}, bf16[928,128]{1,0:T(8,128)(2,1)S(1)}, u32[]{:S(2)}, u32[]{:S(2)}) collective-permute-start(bf16[928,128]{1,0:T(8,128)(2,1)} %collective-permute-done.10.refs_3_), channel_id=1, source_target_pairs={{0,1},{1,0},{2,3},{3,2},{4,5},{5,4},{6,7},{7,6},{8,9},{9,8},{10,11... | collective-permute-start | bytes 712712 | tf_op jit(solution)/shard_map/ppermute | solution.py:231
  106.1 3.6 %shard_map.82 = (bf16[8,464,128]{2,1,0:T(8,128)(2,1)}, bf16[8,928,128]{2,1,0:T(8,128)(2,1)}) custom-call(s32[3]{0:T(128)S(1)} %pad_add_fusion.pos_ref, bf16[928,128]{1,0:T(8,128)(2,1)} %bitcast.8.refs_0_, bf16[928,128]{1,0:T(8,128)(2,1)} %collective-permute-done.8.refs_1_, bf16[928,128]{1,0:T(8,128)(2,1)} %collective-permute-done.9.refs_2_, ...), custom_call_target="tpu_custom_call" | custom-call | flops 881852416 | bytes 5612544 | tf_op jit(solution)/shard_map/pallas_call | solution.py:59
  109.7 7.0 %all-to-all-start.3 = ((bf16[8,464,128]{2,1,0:T(8,128)(2,1)}), bf16[8,464,128]{2,1,0:T(8,128)(2,1)S(1)}, u32[]{:S(2)}, u32[]{:S(2)}) async-start(bf16[8,464,128]{2,1,0:T(8,128)(2,1)} %get-tuple-element.49), calls=%async_computation.3 | async-start | bytes 1900544 | tf_op jit(solution)/shard_map/all_to_all | solution.py:193
  116.9 2.5 %collective-permute-start.19 = (bf16[232,128]{1,0:T(8,128)(2,1)S(1)}, bf16[232,128]{1,0:T(8,128)(2,1)S(1)}, u32[]{:S(2)}, u32[]{:S(2)}) collective-permute-start(bf16[232,128]{1,0:T(8,128)(2,1)S(1)} %fusion.8.refs_0_), channel_id=1, source_target_pairs={{0,4},{1,5},{2,6},{3,7},{4,0},{5,1},{6,2},{7,3},{8,12},{9,13},{10,... | collective-permute-start | bytes 178184 | tf_op jit(solution)/shard_map/ppermute | solution.py:239
  119.5 3.3 %collective-permute-start.18 = (bf16[232,128]{1,0:T(8,128)(2,1)S(1)}, bf16[232,128]{1,0:T(8,128)(2,1)S(1)}, u32[]{:S(2)}, u32[]{:S(2)}) collective-permute-start(bf16[232,128]{1,0:T(8,128)(2,1)S(1)} %fusion.8.refs_0_), channel_id=1, source_target_pairs={{0,6},{1,7},{2,0},{3,1},{4,2},{5,3},{6,4},{7,5},{8,14},{9,15},{10,... | collective-permute-start | bytes 178184 | tf_op jit(solution)/shard_map/ppermute | solution.py:239
  122.8 7.9 %collective-permute-done.20.refs_3_ = bf16[232,128]{1,0:T(8,128)(2,1)S(1)} collective-permute-done((bf16[232,128]{1,0:T(8,128)(2,1)S(1)}, bf16[232,128]{1,0:T(8,128)(2,1)S(1)}, u32[]{:S(2)}, u32[]{:S(2)}) %collective-permute-start.20) | collective-permute-done | bytes 59424 | tf_op jit(solution)/shard_map/ppermute | solution.py:239
  130.7 3.4 %collective-permute-done.19.refs_2_ = bf16[232,128]{1,0:T(8,128)(2,1)S(1)} collective-permute-done((bf16[232,128]{1,0:T(8,128)(2,1)S(1)}, bf16[232,128]{1,0:T(8,128)(2,1)S(1)}, u32[]{:S(2)}, u32[]{:S(2)}) %collective-permute-start.19) | collective-permute-done | bytes 59424 | tf_op jit(solution)/shard_map/ppermute | solution.py:239
  135.7 1.5 collective-permute-start.22
  137.2 2.0 %collective-permute-start.21 = (bf16[928,128]{1,0:T(8,128)(2,1)S(1)}, bf16[928,128]{1,0:T(8,128)(2,1)S(1)}, u32[]{:S(2)}, u32[]{:S(2)}) collective-permute-start(bf16[928,128]{1,0:T(8,128)(2,1)S(1)} %bitcast.18), channel_id=1, source_target_pairs={{0,24},{1,25},{2,26},{3,27},{4,28},{5,29},{6,30},{7,31},{8,0},{9,1... | collective-permute-start | bytes 712712 | tf_op jit(solution)/shard_map/ppermute | solution.py:235
  139.2 1.5 copy-done.1
  140.7 2.6 %shard_map.85 = bf16[928,464]{1,0:T(8,128)(2,1)} custom-call(s32[3]{0:T(128)S(1)} %pad_add_fusion.pos_ref, bf16[8,464,128]{2,1,0:T(8,128)(2,1)S(1)} %all-to-all-done.2.rows_ref, bf16[8,928,128]{2,1,0:T(8,128)(2,1)S(1)} %copy-done.1), custom_call_target="tpu_custom_call" | custom-call | flops 881852416 | bytes 3712000 | tf_op jit(solution)/shard_map/pallas_call | solution.py:59
  143.3 2.6 %collective-permute-start.24 = (bf16[928,128]{1,0:T(8,128)(2,1)S(1)}, bf16[928,128]{1,0:T(8,128)(2,1)S(1)}, u32[]{:S(2)}, u32[]{:S(2)}) collective-permute-start(bf16[928,128]{1,0:T(8,128)(2,1)S(1)} %bitcast.19), channel_id=1, source_target_pairs={{0,1},{1,0},{2,3},{3,2},{4,5},{5,4},{6,7},{7,6},{8,9},{9,8},{10,11... | collective-permute-start | bytes 712712 | tf_op jit(solution)/shard_map/ppermute | solution.py:231
  146.0 3.2 %collective-permute-start.27 = (bf16[928,128]{1,0:T(8,128)(2,1)S(1)}, bf16[928,128]{1,0:T(8,128)(2,1)S(1)}, u32[]{:S(2)}, u32[]{:S(2)}) collective-permute-start(bf16[928,128]{1,0:T(8,128)(2,1)S(1)} %collective-permute-done.23.refs_3_), channel_id=1, source_target_pairs={{0,1},{1,0},{2,3},{3,2},{4,5},{5,4},{6,7},{7,6},{8,9},{9,8},{10,11... | collective-permute-start | bytes 712712 | tf_op jit(solution)/shard_map/ppermute | solution.py:231
  151.1 2.9 %shard_map.86 = (bf16[8,464,128]{2,1,0:T(8,128)(2,1)}, bf16[8,928,128]{2,1,0:T(8,128)(2,1)}) custom-call(s32[3]{0:T(128)S(1)} %pad_add_fusion.pos_ref, bf16[928,128]{1,0:T(8,128)(2,1)S(1)} %bitcast.20, bf16[928,128]{1,0:T(8,128)(2,1)S(1)} %collective-permute-done.21.refs_1_, bf16[928,128]{1,0:T(8,128)(2,1)S(1)} %collective-permute-done.22.refs_2_, ...), custom_call_target="tpu_custom_call" | custom-call | flops 881852416 | bytes 5612544 | tf_op jit(solution)/shard_map/pallas_call | solution.py:59
  154.0 3.9 %all-to-all-start.5 = ((bf16[8,464,128]{2,1,0:T(8,128)(2,1)}), bf16[8,464,128]{2,1,0:T(8,128)(2,1)S(1)}, u32[]{:S(2)}, u32[]{:S(2)}) async-start(bf16[8,464,128]{2,1,0:T(8,128)(2,1)} %get-tuple-element.62), calls=%async_computation.5 | async-start | bytes 1900544 | tf_op jit(solution)/shard_map/all_to_all | solution.py:193
  158.0 1.5 copy-done.2
  159.5 2.7 %shard_map.88 = bf16[464,928]{1,0:T(8,128)(2,1)} custom-call(s32[3]{0:T(128)S(1)} %pad_add_fusion.pos_ref, bf16[8,464,128]{2,1,0:T(8,128)(2,1)S(1)} %all-to-all-done.rows_ref, bf16[8,928,128]{2,1,0:T(8,128)(2,1)S(1)} %copy-done.2), custom_call_target="tpu_custom_call" | custom-call | flops 881852416 | bytes 3712000 | tf_op jit(solution)/shard_map/pallas_call | solution.py:59
  162.1 1.3 shard_map.83
  163.4 8.4 %all-to-all-done.5.value_ref = bf16[8,464,128]{2,1,0:T(8,128)(2,1)S(1)} async-done(((bf16[8,464,128]{2,1,0:T(8,128)(2,1)}), bf16[8,464,128]{2,1,0:T(8,128)(2,1)S(1)}, u32[]{:S(2)}, u32[]{:S(2)}) %all-to-all-start.5) | async-done | bytes 950304 | tf_op jit(solution)/shard_map/all_to_all | solution.py:193
  171.9 1.3 shard_map.87
  (57 shorter events, 16.3 us)
Async XLA Ops:
  0.7 0.9 copy-start.5
  3.2 8.2 %copy-start = (bf16[928,464]{1,0:T(8,128)(2,1)S(1)}, bf16[928,464]{1,0:T(8,128)(2,1)}, u32[]{:S(2)}) copy-start(bf16[928,464]{1,0:T(8,128)(2,1)} %weight_ref.3) | copy-start | bytes 2583556
  3.2 20.1 %all-to-all-start = ((bf16[8,464,128]{2,1,0:T(8,128)(2,1)}), bf16[8,464,128]{2,1,0:T(8,128)(2,1)S(1)}, u32[]{:S(2)}, u32[]{:S(2)}) async-start(bf16[8,464,128]{2,1,0:T(8,128)(2,1)} %shard_map.75), calls=%async_computation | async-start | bytes 1900544 | tf_op jit(solution)/shard_map/all_to_all | solution.py:193
  25.4 5.7 %copy-start.6 = (bf16[128,464]{0,1:T(8,128)(2,1)S(1)}, bf16[128,464]{0,1:T(8,128)(2,1)}, u32[]{:S(2)}) copy-start(bf16[128,464]{0,1:T(8,128)(2,1)} %param.7) | copy-start | bytes 356356
  25.5 3.6 %collective-permute-start = (bf16[4,928,128]{2,1,0:T(8,128)(2,1)}, bf16[4,928,128]{2,1,0:T(8,128)(2,1)S(1)}, u32[]{:S(2)}, u32[]{:S(2)}) collective-permute-start(bf16[4,928,128]{2,1,0:T(8,128)(2,1)} %shard_map.76), channel_id=1, source_target_pairs={{0,1},{1,0},{2,3},{3,2},{4,5},{5,4},{6,7},{7,6},{8,9},{9,8},{10,11... | collective-permute-start | bytes 2850824 | tf_op jit(solution)/shard_map/ppermute | solution.py:231
  32.7 18.9 %all-to-all-start.2 = ((bf16[8,464,128]{2,1,0:T(8,128)(2,1)}), bf16[8,464,128]{2,1,0:T(8,128)(2,1)S(1)}, u32[]{:S(2)}, u32[]{:S(2)}) async-start(bf16[8,464,128]{2,1,0:T(8,128)(2,1)} %shard_map.78), calls=%async_computation.2 | async-start | bytes 1900544 | tf_op jit(solution)/shard_map/all_to_all | solution.py:193
  36.3 8.4 %collective-permute-start.1 = (bf16[928,128]{1,0:T(8,128)(2,1)}, bf16[928,128]{1,0:T(8,128)(2,1)S(1)}, u32[]{:S(2)}, u32[]{:S(2)}) collective-permute-start(bf16[928,128]{1,0:T(8,128)(2,1)} %get-tuple-element.37), channel_id=1, source_target_pairs={{0,8},{1,9},{2,10},{3,11},{4,12},{5,13},{6,14},{7,15},{8,16},{9,17... | collective-permute-start | bytes 712712 | tf_op jit(solution)/shard_map/ppermute | solution.py:235
  37.6 13.2 %collective-permute-start.2 = (bf16[928,128]{1,0:T(8,128)(2,1)}, bf16[928,128]{1,0:T(8,128)(2,1)S(1)}, u32[]{:S(2)}, u32[]{:S(2)}) collective-permute-start(bf16[928,128]{1,0:T(8,128)(2,1)} %get-tuple-element.38), channel_id=1, source_target_pairs={{0,16},{1,17},{2,18},{3,19},{4,20},{5,21},{6,22},{7,23},{8,24},{9,... | collective-permute-start | bytes 712712 | tf_op jit(solution)/shard_map/ppermute | solution.py:235
  40.0 10.8 %collective-permute-start.3 = (bf16[928,128]{1,0:T(8,128)(2,1)}, bf16[928,128]{1,0:T(8,128)(2,1)S(1)}, u32[]{:S(2)}, u32[]{:S(2)}) collective-permute-start(bf16[928,128]{1,0:T(8,128)(2,1)} %get-tuple-element.39), channel_id=1, source_target_pairs={{0,24},{1,25},{2,26},{3,27},{4,28},{5,29},{6,30},{7,31},{8,0},{9,1... | collective-permute-start | bytes 712712 | tf_op jit(solution)/shard_map/ppermute | solution.py:235
  53.8 8.6 %collective-permute-start.4 = (bf16[4,928,128]{2,1,0:T(8,128)(2,1)}, bf16[4,928,128]{2,1,0:T(8,128)(2,1)}, u32[]{:S(2)}, u32[]{:S(2)}) collective-permute-start(bf16[4,928,128]{2,1,0:T(8,128)(2,1)} %shard_map.79), channel_id=1, source_target_pairs={{0,1},{1,0},{2,3},{3,2},{4,5},{5,4},{6,7},{7,6},{8,9},{9,8},{10,11... | collective-permute-start | bytes 2850824 | tf_op jit(solution)/shard_map/ppermute | solution.py:231
  55.1 16.4 %all-to-all-start.1 = ((bf16[4,232,128]{2,1,0:T(8,128)(2,1)}), bf16[4,232,128]{2,1,0:T(8,128)(2,1)}, u32[]{:S(2)}, u32[]{:S(2)}) async-start(bf16[4,232,128]{2,1,0:T(8,128)(2,1)} %bitcast.6), calls=%async_computation.1 | async-start | bytes 475136 | tf_op jit(solution)/shard_map/all_to_all | solution.py:193
  65.2 40.9 %copy-start.4 = (bf16[928,464]{0,1:T(8,128)(2,1)S(1)}, bf16[928,464]{0,1:T(8,128)(2,1)}, u32[]{:S(2)}) copy-start(bf16[928,464]{0,1:T(8,128)(2,1)} %copy.9) | copy-start | bytes 2583556
  72.5 17.6 %collective-permute-start.15 = (bf16[928,128]{1,0:T(8,128)(2,1)}, bf16[928,128]{1,0:T(8,128)(2,1)S(1)}, u32[]{:S(2)}, u32[]{:S(2)}) collective-permute-start(bf16[928,128]{1,0:T(8,128)(2,1)} %get-tuple-element.51), channel_id=1, source_target_pairs={{0,8},{1,9},{2,10},{3,11},{4,12},{5,13},{6,14},{7,15},{8,16},{9,17... | collective-permute-start | bytes 712712 | tf_op jit(solution)/shard_map/ppermute | solution.py:235
  73.7 17.9 %collective-permute-start.16 = (bf16[928,128]{1,0:T(8,128)(2,1)}, bf16[928,128]{1,0:T(8,128)(2,1)S(1)}, u32[]{:S(2)}, u32[]{:S(2)}) collective-permute-start(bf16[928,128]{1,0:T(8,128)(2,1)} %get-tuple-element.52), channel_id=1, source_target_pairs={{0,16},{1,17},{2,18},{3,19},{4,20},{5,21},{6,22},{7,23},{8,24},{9,... | collective-permute-start | bytes 712712 | tf_op jit(solution)/shard_map/ppermute | solution.py:235
  75.8 15.8 %collective-permute-start.17 = (bf16[928,128]{1,0:T(8,128)(2,1)}, bf16[928,128]{1,0:T(8,128)(2,1)S(1)}, u32[]{:S(2)}, u32[]{:S(2)}) collective-permute-start(bf16[928,128]{1,0:T(8,128)(2,1)} %get-tuple-element.53), channel_id=1, source_target_pairs={{0,24},{1,25},{2,26},{3,27},{4,28},{5,29},{6,30},{7,31},{8,0},{9,1... | collective-permute-start | bytes 712712 | tf_op jit(solution)/shard_map/ppermute | solution.py:235
  77.3 6.0 %collective-permute-start.7 = (bf16[232,128]{1,0:T(8,128)(2,1)S(1)}, bf16[232,128]{1,0:T(8,128)(2,1)S(1)}, u32[]{:S(2)}, u32[]{:S(2)}) collective-permute-start(bf16[232,128]{1,0:T(8,128)(2,1)S(1)} %fusion.2.refs_0_), channel_id=1, source_target_pairs={{0,2},{1,3},{2,4},{3,5},{4,6},{5,7},{6,0},{7,1},{8,10},{9,11},{10,... | collective-permute-start | bytes 178184 | tf_op jit(solution)/shard_map/ppermute | solution.py:239
  77.4 7.2 %collective-permute-start.6 = (bf16[232,128]{1,0:T(8,128)(2,1)S(1)}, bf16[232,128]{1,0:T(8,128)(2,1)S(1)}, u32[]{:S(2)}, u32[]{:S(2)}) collective-permute-start(bf16[232,128]{1,0:T(8,128)(2,1)S(1)} %fusion.2.refs_0_), channel_id=1, source_target_pairs={{0,4},{1,5},{2,6},{3,7},{4,0},{5,1},{6,2},{7,3},{8,12},{9,13},{10,... | collective-permute-start | bytes 178184 | tf_op jit(solution)/shard_map/ppermute | solution.py:239
  83.3 4.1 %collective-permute-start.5 = (bf16[232,128]{1,0:T(8,128)(2,1)S(1)}, bf16[232,128]{1,0:T(8,128)(2,1)S(1)}, u32[]{:S(2)}, u32[]{:S(2)}) collective-permute-start(bf16[232,128]{1,0:T(8,128)(2,1)S(1)} %fusion.2.refs_0_), channel_id=1, source_target_pairs={{0,6},{1,7},{2,0},{3,1},{4,2},{5,3},{6,4},{7,5},{8,14},{9,15},{10,... | collective-permute-start | bytes 178184 | tf_op jit(solution)/shard_map/ppermute | solution.py:239
  88.7 13.0 %collective-permute-start.10 = (bf16[928,128]{1,0:T(8,128)(2,1)}, bf16[928,128]{1,0:T(8,128)(2,1)}, u32[]{:S(2)}, u32[]{:S(2)}) collective-permute-start(bf16[928,128]{1,0:T(8,128)(2,1)} %bitcast.8.refs_0_), channel_id=1, source_target_pairs={{0,8},{1,9},{2,10},{3,11},{4,12},{5,13},{6,14},{7,15},{8,16},{9,17... | collective-permute-start | bytes 712712 | tf_op jit(solution)/shard_map/ppermute | solution.py:235
  88.9 14.9 %collective-permute-start.9 = (bf16[928,128]{1,0:T(8,128)(2,1)}, bf16[928,128]{1,0:T(8,128)(2,1)}, u32[]{:S(2)}, u32[]{:S(2)}) collective-permute-start(bf16[928,128]{1,0:T(8,128)(2,1)} %bitcast.8.refs_0_), channel_id=1, source_target_pairs={{0,16},{1,17},{2,18},{3,19},{4,20},{5,21},{6,22},{7,23},{8,24},{9,... | collective-permute-start | bytes 712712 | tf_op jit(solution)/shard_map/ppermute | solution.py:235
  90.2 13.6 %collective-permute-start.8 = (bf16[928,128]{1,0:T(8,128)(2,1)}, bf16[928,128]{1,0:T(8,128)(2,1)}, u32[]{:S(2)}, u32[]{:S(2)}) collective-permute-start(bf16[928,128]{1,0:T(8,128)(2,1)} %bitcast.8.refs_0_), channel_id=1, source_target_pairs={{0,24},{1,25},{2,26},{3,27},{4,28},{5,29},{6,30},{7,31},{8,0},{9,1... | collective-permute-start | bytes 712712 | tf_op jit(solution)/shard_map/ppermute | solution.py:235
  92.4 17.2 %all-to-all-start.4 = ((bf16[4,232,128]{2,1,0:T(8,128)(2,1)}), bf16[4,232,128]{2,1,0:T(8,128)(2,1)S(1)}, u32[]{:S(2)}, u32[]{:S(2)}) async-start(bf16[4,232,128]{2,1,0:T(8,128)(2,1)} %bitcast.23), calls=%async_computation.4 | async-start | bytes 475136 | tf_op jit(solution)/shard_map/all_to_all | solution.py:193
  96.6 8.1 %collective-permute-start.11 = (bf16[928,128]{1,0:T(8,128)(2,1)}, bf16[928,128]{1,0:T(8,128)(2,1)S(1)}, u32[]{:S(2)}, u32[]{:S(2)}) collective-permute-start(bf16[928,128]{1,0:T(8,128)(2,1)} %bitcast.8.refs_0_), channel_id=1, source_target_pairs={{0,1},{1,0},{2,3},{3,2},{4,5},{5,4},{6,7},{7,6},{8,9},{9,8},{10,11... | collective-permute-start | bytes 712712 | tf_op jit(solution)/shard_map/ppermute | solution.py:231
  101.8 3.4 %collective-permute-start.14 = (bf16[928,128]{1,0:T(8,128)(2,1)}, bf16[928,128]{1,0:T(8,128)(2,1)S(1)}, u32[]{:S(2)}, u32[]{:S(2)}) collective-permute-start(bf16[928,128]{1,0:T(8,128)(2,1)} %collective-permute-done.10.refs_3_), channel_id=1, source_target_pairs={{0,1},{1,0},{2,3},{3,2},{4,5},{5,4},{6,7},{7,6},{8,9},{9,8},{10,11... | collective-permute-start | bytes 712712 | tf_op jit(solution)/shard_map/ppermute | solution.py:231
  103.8 1.7 collective-permute-start.13
  103.8 2.2 %collective-permute-start.12 = (bf16[928,128]{1,0:T(8,128)(2,1)}, bf16[928,128]{1,0:T(8,128)(2,1)S(1)}, u32[]{:S(2)}, u32[]{:S(2)}) collective-permute-start(bf16[928,128]{1,0:T(8,128)(2,1)} %collective-permute-done.8.refs_1_), channel_id=1, source_target_pairs={{0,1},{1,0},{2,3},{3,2},{4,5},{5,4},{6,7},{7,6},{8,9},{9,8},{10,11... | collective-permute-start | bytes 712712 | tf_op jit(solution)/shard_map/ppermute | solution.py:231
  109.7 44.3 %all-to-all-start.3 = ((bf16[8,464,128]{2,1,0:T(8,128)(2,1)}), bf16[8,464,128]{2,1,0:T(8,128)(2,1)S(1)}, u32[]{:S(2)}, u32[]{:S(2)}) async-start(bf16[8,464,128]{2,1,0:T(8,128)(2,1)} %get-tuple-element.49), calls=%async_computation.3 | async-start | bytes 1900544 | tf_op jit(solution)/shard_map/all_to_all | solution.py:193
  116.8 13.9 %collective-permute-start.20 = (bf16[232,128]{1,0:T(8,128)(2,1)S(1)}, bf16[232,128]{1,0:T(8,128)(2,1)S(1)}, u32[]{:S(2)}, u32[]{:S(2)}) collective-permute-start(bf16[232,128]{1,0:T(8,128)(2,1)S(1)} %fusion.8.refs_0_), channel_id=1, source_target_pairs={{0,2},{1,3},{2,4},{3,5},{4,6},{5,7},{6,0},{7,1},{8,10},{9,11},{10,... | collective-permute-start | bytes 178184 | tf_op jit(solution)/shard_map/ppermute | solution.py:239
  116.9 17.1 %collective-permute-start.19 = (bf16[232,128]{1,0:T(8,128)(2,1)S(1)}, bf16[232,128]{1,0:T(8,128)(2,1)S(1)}, u32[]{:S(2)}, u32[]{:S(2)}) collective-permute-start(bf16[232,128]{1,0:T(8,128)(2,1)S(1)} %fusion.8.refs_0_), channel_id=1, source_target_pairs={{0,4},{1,5},{2,6},{3,7},{4,0},{5,1},{6,2},{7,3},{8,12},{9,13},{10,... | collective-permute-start | bytes 178184 | tf_op jit(solution)/shard_map/ppermute | solution.py:239
  119.5 14.6 %collective-permute-start.18 = (bf16[232,128]{1,0:T(8,128)(2,1)S(1)}, bf16[232,128]{1,0:T(8,128)(2,1)S(1)}, u32[]{:S(2)}, u32[]{:S(2)}) collective-permute-start(bf16[232,128]{1,0:T(8,128)(2,1)S(1)} %fusion.8.refs_0_), channel_id=1, source_target_pairs={{0,6},{1,7},{2,0},{3,1},{4,2},{5,3},{6,4},{7,5},{8,14},{9,15},{10,... | collective-permute-start | bytes 178184 | tf_op jit(solution)/shard_map/ppermute | solution.py:239
  134.6 11.3 %collective-permute-start.23 = (bf16[928,128]{1,0:T(8,128)(2,1)S(1)}, bf16[928,128]{1,0:T(8,128)(2,1)S(1)}, u32[]{:S(2)}, u32[]{:S(2)}) collective-permute-start(bf16[928,128]{1,0:T(8,128)(2,1)S(1)} %bitcast.16), channel_id=1, source_target_pairs={{0,8},{1,9},{2,10},{3,11},{4,12},{5,13},{6,14},{7,15},{8,16},{9,17... | collective-permute-start | bytes 712712 | tf_op jit(solution)/shard_map/ppermute | solution.py:235
  135.7 13.5 %collective-permute-start.22 = (bf16[928,128]{1,0:T(8,128)(2,1)S(1)}, bf16[928,128]{1,0:T(8,128)(2,1)S(1)}, u32[]{:S(2)}, u32[]{:S(2)}) collective-permute-start(bf16[928,128]{1,0:T(8,128)(2,1)S(1)} %bitcast.17), channel_id=1, source_target_pairs={{0,16},{1,17},{2,18},{3,19},{4,20},{5,21},{6,22},{7,23},{8,24},{9,... | collective-permute-start | bytes 712712 | tf_op jit(solution)/shard_map/ppermute | solution.py:235
  137.2 12.0 %collective-permute-start.21 = (bf16[928,128]{1,0:T(8,128)(2,1)S(1)}, bf16[928,128]{1,0:T(8,128)(2,1)S(1)}, u32[]{:S(2)}, u32[]{:S(2)}) collective-permute-start(bf16[928,128]{1,0:T(8,128)(2,1)S(1)} %bitcast.18), channel_id=1, source_target_pairs={{0,24},{1,25},{2,26},{3,27},{4,28},{5,29},{6,30},{7,31},{8,0},{9,1... | collective-permute-start | bytes 712712 | tf_op jit(solution)/shard_map/ppermute | solution.py:235
  139.2 1.5 copy-start.1
  140.7 10.4 %copy-start.3 = (bf16[464,928]{1,0:T(8,128)(2,1)S(1)}, bf16[464,928]{1,0:T(8,128)(2,1)}, u32[]{:S(2)}) copy-start(bf16[464,928]{1,0:T(8,128)(2,1)} %refs_8_.1) | copy-start | bytes 2583556
  143.3 6.5 %collective-permute-start.24 = (bf16[928,128]{1,0:T(8,128)(2,1)S(1)}, bf16[928,128]{1,0:T(8,128)(2,1)S(1)}, u32[]{:S(2)}, u32[]{:S(2)}) collective-permute-start(bf16[928,128]{1,0:T(8,128)(2,1)S(1)} %bitcast.19), channel_id=1, source_target_pairs={{0,1},{1,0},{2,3},{3,2},{4,5},{5,4},{6,7},{7,6},{8,9},{9,8},{10,11... | collective-permute-start | bytes 712712 | tf_op jit(solution)/shard_map/ppermute | solution.py:231
  146.0 4.4 %collective-permute-start.27 = (bf16[928,128]{1,0:T(8,128)(2,1)S(1)}, bf16[928,128]{1,0:T(8,128)(2,1)S(1)}, u32[]{:S(2)}, u32[]{:S(2)}) collective-permute-start(bf16[928,128]{1,0:T(8,128)(2,1)S(1)} %collective-permute-done.23.refs_3_), channel_id=1, source_target_pairs={{0,1},{1,0},{2,3},{3,2},{4,5},{5,4},{6,7},{7,6},{8,9},{9,8},{10,11... | collective-permute-start | bytes 712712 | tf_op jit(solution)/shard_map/ppermute | solution.py:231
  149.2 1.5 collective-permute-start.26
  149.2 1.8 %collective-permute-start.25 = (bf16[928,128]{1,0:T(8,128)(2,1)S(1)}, bf16[928,128]{1,0:T(8,128)(2,1)S(1)}, u32[]{:S(2)}, u32[]{:S(2)}) collective-permute-start(bf16[928,128]{1,0:T(8,128)(2,1)S(1)} %collective-permute-done.21.refs_1_), channel_id=1, source_target_pairs={{0,1},{1,0},{2,3},{3,2},{4,5},{5,4},{6,7},{7,6},{8,9},{9,8},{10,11... | collective-permute-start | bytes 712712 | tf_op jit(solution)/shard_map/ppermute | solution.py:231
  154.0 17.8 %all-to-all-start.5 = ((bf16[8,464,128]{2,1,0:T(8,128)(2,1)}), bf16[8,464,128]{2,1,0:T(8,128)(2,1)S(1)}, u32[]{:S(2)}, u32[]{:S(2)}) async-start(bf16[8,464,128]{2,1,0:T(8,128)(2,1)} %get-tuple-element.62), calls=%async_computation.5 | async-start | bytes 1900544 | tf_op jit(solution)/shard_map/all_to_all | solution.py:193
  158.0 1.5 copy-start.2

commit v5 on v4

--- a/solution.py
+++ b/solution.py
@@ -35,7 +35,7 @@
 
 
 def slope(hidden):
-    normal_cdf = 0.5 * (1.0 + jax.scipy.special.erf(hidden * (1.0 / math.sqrt(2.0))))
+    normal_cdf = 0.5 * (1.0 + lax.erf(hidden * (1.0 / math.sqrt(2.0))))
     density = jnp.exp(-0.5 * hidden * hidden) * (1.0 / math.sqrt(2.0 * math.pi))
     return normal_cdf + hidden * density
 
@@ -209,6 +209,42 @@
     return kernel_call(kernel, outs, 0, pos, [value], scratch, (0,), (0,))[0]
 
 
+def fan_out(value, held_ref, out_ref, sems):
+    held_ref[...] = value
+    copies = [
+        pltpu.make_async_copy(held_ref, out_ref.at[index], sems.at[index]) for index in range(Z)
+    ]
+    for copy in copies:
+        copy.start()
+    return copies
+
+
+def activated(pos, arrived):
+    def kernel(pos_ref, arrived_ref, hidden_ref, out_ref, held_ref, sems):
+        hidden = total_of(arrived_ref[...])
+        cdf = 0.5 * (1.0 + lax.erf(hidden * (1.0 / math.sqrt(2.0))))
+        copies = fan_out((hidden * cdf).astype(BF), held_ref, out_ref, sems)
+        hidden_ref[...] = hidden
+        for copy in copies:
+            copy.wait()
+
+    part = arrived.shape[1:]
+    outs = [shaped(part, F32), shaped(arrived.shape, BF)]
+    scratch = [pltpu.VMEM(part, BF), pltpu.SemaphoreType.DMA((Z,))]
+    return kernel_call(kernel, outs, arrived.size, pos, [arrived], scratch, (1,))
+
+
+def sloped(pos, arrived, hidden):
+    def kernel(pos_ref, arrived_ref, hidden_ref, out_ref, held_ref, sems):
+        deltas = total_of(arrived_ref[...]) * slope(hidden_ref[...])
+        for copy in fan_out(deltas.astype(BF), held_ref, out_ref, sems):
+            copy.wait()
+
+    outs = [shaped(arrived.shape, BF)]
+    scratch = [pltpu.VMEM(hidden.shape, BF), pltpu.SemaphoreType.DMA((Z,))]
+    return kernel_call(kernel, outs, arrived.size, pos, [arrived, hidden], scratch, (0,))[0]
+
+
 def added(pos, value):
     def kernel(pos_ref, value_ref, out_ref):
         total = value_ref[0].astype(F32)
@@ -219,24 +255,12 @@
     return kernel_call(kernel, [shaped(value.shape[1:], BF)], value.size, pos, [value])[0]
 
 
-def in_order(pos, chunks):
-    def kernel(pos_ref, *refs):
-        for d in range(Z):
-            refs[-1][(pos_ref[2] + d) & 3] = refs[d][...]
-
-    return kernel_call(kernel, [shaped((Z,) + chunks[0].shape, BF)], 0, pos, chunks)[0]
-
-
 def swap_cores(value):
     return lax.ppermute(value, "rep", rep_pairs(0, 0, 1))
 
 
 def move_x(value, d):
     return lax.ppermute(value, "rep", rep_pairs(d, 0, 0))
-
-
-def move_z(value, d):
-    return lax.ppermute(value, "rep", rep_pairs(0, d, 0))
 
 
 def total_of(value):
@@ -255,9 +279,8 @@
     return exchange(value, "rep", Z_GROUPS)
 
 
-def spread_z(pos, value):
-    whole = in_order(pos, [value] + [move_z(value, -d) for d in range(1, Z)])
-    return whole.reshape(Z * value.shape[0], LANES)
+def spread_z(value):
+    return exchange(value, "rep", Z_GROUPS).reshape(-1, LANES)
 
 
 def spread_x(value):
@@ -285,15 +308,11 @@
     sent = other_half(pos, after(cot, value), second_weight)
     keep, sent = own_half(pos, cot, second_weight, swap_cores(sent))
 
-    hidden = total_of(after(scatter_z(value), keep))
-    active = jax.nn.gelu(hidden, approximate=False).astype(BF)
-    active, hidden = lax.optimization_barrier((active, hidden))
-    active = spread_z(pos, active)
-    upward = total_of(scatter_z(sum_x(after(keep, active), sent)))
-    deltas = (upward * slope(hidden)).astype(BF)
-
-    act = with_other_half(spread_x(active))
-    dlt = spread_x(spread_z(pos, deltas))
+    hidden, active = activated(pos, after(scatter_z(value), keep))
+    deltas = sloped(pos, scatter_z(sum_x(keep, sent)), hidden)
+
+    act = with_other_half(spread_x(spread_z(active)))
+    dlt = spread_x(spread_z(deltas))
     out, act = both_halves(pos, act, second_turned)
     out = exchange(out, "grp")
     second_grad = weight_grad(pos, factor, cot, act, False)

time: 174 us -> 159 us (0.914)
  waiting for transfers between devices: 55.8 us -> 46.5 us
  starting transfers between devices: 78 us -> 70.4 us
    ppermute x6 -> x0, waiting for transfers between devices: 15.9 us -> none  [move_z(): return lax.ppermute(value, 'rep', rep_pairs(0, d, 0))]
    ppermute x6 -> x0, starting transfers between devices: 11.5 us -> none  [move_z(): return lax.ppermute(value, 'rep', rep_pairs(0, d, 0))]
    all_to_all x6 -> x8, starting transfers between devices: 32.5 us -> 39.4 us  [exchange(): return lax.all_to_all(value, axis, 0, 0, axis_index_groups=groups)]
    all_to_all x6 -> x8, waiting for transfers between devices: 25.3 us -> 29.9 us  [exchange(): return lax.all_to_all(value, axis, 0, 0, axis_index_groups=groups)]
    ppermute x12, starting transfers between devices: 16.8 us -> 15 us  [move_x(): return lax.ppermute(value, 'rep', rep_pairs(d, 0, 0))]
    unnamed x16 -> x18, local copies, waits for them, and re-layouts: 7 us -> 7.76 us
  transfers between devices with their start and end apart: 34 -> 30, of which waited for: 17 -> 16; matrix products, arithmetic and copies ran while one was open for 3% -> 4% of each run, Pallas kernels for 10% -> 12%
where the time goes in v5:
time: 159 us; the launch traced here: 158 us
  starting transfers between devices  70.4 us (44%)
  waiting for transfers between devices  46.5 us (29%)
  Pallas kernels  29.3 us (18%)
  local copies, waits for them, and re-layouts  7.76 us (5%)
  other arithmetic  3.03 us (2%)
    all_to_all x8, starting transfers between devices, exchange(): return lax.all_to_all(value, axis, 0, 0, axis_index_groups=groups)  39.4 us
    all_to_all x8, waiting for transfers between devices, exchange(): return lax.all_to_all(value, axis, 0, 0, axis_index_groups=groups)  29.9 us
    pallas_call x14, Pallas kernels, kernel_call(): pl.pallas_call(kernel, out_shape=[pltpu.HBM(o.shape, o.dtype) if i in far...  29.3 us
    ppermute x10, starting transfers between devices, swap_cores(): return lax.ppermute(value, 'rep', rep_pairs(0, 0, 1))  16 us
    ppermute x12, starting transfers between devices, move_x(): return lax.ppermute(value, 'rep', rep_pairs(d, 0, 0))  15 us
    ppermute x12, waiting for transfers between devices, move_x(): return lax.ppermute(value, 'rep', rep_pairs(d, 0, 0))  11.4 us
    unnamed x18, local copies, waits for them, and re-layouts  7.76 us
    ppermute x10, waiting for transfers between devices, swap_cores(): return lax.ppermute(value, 'rep', rep_pairs(0, 0, 1))  5.3 us
  transfers between devices with their start and end apart: 30, of which 16 were waited for; matrix products, arithmetic and copies ran while one was open for 4% of the time, Pallas kernels for 12%

profile of v5, /device:TPU:1, one launch (start us, length us, event | category | flops | bytes accessed | tf_op | source)
XLA Modules:
  0.0 157.9 jit_solution(17845063838843918287)
XLA Ops:
  1.6 1.5 shard_map.75
  3.2 6.5 %all-to-all-start = ((bf16[8,464,128]{2,1,0:T(8,128)(2,1)}), bf16[8,464,128]{2,1,0:T(8,128)(2,1)S(1)}, u32[]{:S(2)}, u32[]{:S(2)}) async-start(bf16[8,464,128]{2,1,0:T(8,128)(2,1)} %shard_map.75), calls=%async_computation | async-start | bytes 1900544 | tf_op jit(solution)/shard_map/all_to_all | solution.py:193
  9.7 1.6 %copy.8 = bf16[464,928]{0,1:T(8,128)(2,1)S(1)} copy(bf16[464,928]{1,0:T(8,128)(2,1)} %refs_8_.1) | data formatting | bytes 1722368 | tf_op args[1]
  11.3 1.4 copy.9
  12.7 10.5 %all-to-all-done.rows_ref = bf16[8,464,128]{2,1,0:T(8,128)(2,1)S(1)} async-done(((bf16[8,464,128]{2,1,0:T(8,128)(2,1)}), bf16[8,464,128]{2,1,0:T(8,128)(2,1)S(1)}, u32[]{:S(2)}, u32[]{:S(2)}) %all-to-all-start) | async-done | bytes 950304 | tf_op jit(solution)/shard_map/all_to_all | solution.py:193
  23.3 2.2 %shard_map.76 = bf16[4,928,128]{2,1,0:T(8,128)(2,1)} custom-call(s32[3]{0:T(128)S(1)} %pad_add_fusion.pos_ref, bf16[8,464,128]{2,1,0:T(8,128)(2,1)S(1)} %all-to-all-done.rows_ref, bf16[928,464]{1,0:T(8,128)(2,1)S(1)} %bitcast.13), custom_call_target="tpu_custom_call" | custom-call | flops 440926208 | bytes 2761728 | tf_op jit(solution)/shard_map/pallas_call | solution.py:59
  25.5 1.2 collective-permute-start
  26.7 2.4 %collective-permute-done.arrived_ref = bf16[4,928,128]{2,1,0:T(8,128)(2,1)S(1)} collective-permute-done((bf16[4,928,128]{2,1,0:T(8,128)(2,1)}, bf16[4,928,128]{2,1,0:T(8,128)(2,1)S(1)}, u32[]{:S(2)}, u32[]{:S(2)}) %collective-permute-start) | collective-permute-done | bytes 950304 | tf_op jit(solution)/shard_map/ppermute | solution.py:259
  29.0 2.1 %shard_map.77 = (f32[928,128]{1,0:T(8,128)S(1)}, bf16[928,128]{1,0:T(8,128)(2,1)}, bf16[928,128]{1,0:T(8,128)(2,1)}, bf16[928,128]{1,0:T(8,128)(2,1)}) custom-call(s32[3]{0:T(128)S(1)} %pad_add_fusion.pos_ref, bf16[8,464,128]{2,1,0:T(8,128)(2,1)S(1)} %all-to-all-done.rows_ref, bf16[928,464]{1,0:T(8,128)(2,1)S(1)} %bitcast.14, ...), custom_call_target="tpu_custom_call" | custom-call | flops 440926208 | bytes 3949568 | tf_op jit(solution)/shard_map/pallas_call | solution.py:59
  31.1 1.5 shard_map.78
  32.7 3.6 %all-to-all-start.2 = ((bf16[8,464,128]{2,1,0:T(8,128)(2,1)}), bf16[8,464,128]{2,1,0:T(8,128)(2,1)S(1)}, u32[]{:S(2)}, u32[]{:S(2)}) async-start(bf16[8,464,128]{2,1,0:T(8,128)(2,1)} %shard_map.78), calls=%async_computation.2 | async-start | bytes 1900544 | tf_op jit(solution)/shard_map/all_to_all | solution.py:193
  36.3 1.3 collective-permute-start.1
  37.6 2.4 %collective-permute-start.2 = (bf16[928,128]{1,0:T(8,128)(2,1)}, bf16[928,128]{1,0:T(8,128)(2,1)S(1)}, u32[]{:S(2)}, u32[]{:S(2)}) collective-permute-start(bf16[928,128]{1,0:T(8,128)(2,1)} %get-tuple-element.37), channel_id=1, source_target_pairs={{0,16},{1,17},{2,18},{3,19},{4,20},{5,21},{6,22},{7,23},{8,24},{9,... | collective-permute-start | bytes 712712 | tf_op jit(solution)/shard_map/ppermute | solution.py:263
  40.0 1.2 collective-permute-start.3
  41.2 3.5 %collective-permute-done.1 = bf16[928,128]{1,0:T(8,128)(2,1)S(1)} collective-permute-done((bf16[928,128]{1,0:T(8,128)(2,1)}, bf16[928,128]{1,0:T(8,128)(2,1)S(1)}, u32[]{:S(2)}, u32[]{:S(2)}) %collective-permute-start.1) | collective-permute-done | bytes 237600 | tf_op jit(solution)/shard_map/ppermute | solution.py:263
  44.7 6.1 %collective-permute-done.2 = bf16[928,128]{1,0:T(8,128)(2,1)S(1)} collective-permute-done((bf16[928,128]{1,0:T(8,128)(2,1)}, bf16[928,128]{1,0:T(8,128)(2,1)S(1)}, u32[]{:S(2)}, u32[]{:S(2)}) %collective-permute-start.2) | collective-permute-done | bytes 237600 | tf_op jit(solution)/shard_map/ppermute | solution.py:263
  51.6 2.2 %shard_map.79 = bf16[4,928,128]{2,1,0:T(8,128)(2,1)} custom-call(s32[3]{0:T(128)S(1)} %pad_add_fusion.pos_ref, bf16[8,464,128]{2,1,0:T(8,128)(2,1)S(1)} %all-to-all-done.2.rows_ref, bf16[928,464]{1,0:T(8,128)(2,1)S(1)} %copy-done), custom_call_target="tpu_custom_call" | custom-call | flops 440926208 | bytes 2761728 | tf_op jit(solution)/shard_map/pallas_call | solution.py:59
  53.8 1.3 collective-permute-start.4
  55.1 7.3 %all-to-all-start.1 = ((bf16[4,232,128]{2,1,0:T(8,128)(2,1)}), bf16[4,232,128]{2,1,0:T(8,128)(2,1)S(1)}, u32[]{:S(2)}, u32[]{:S(2)}) async-start(bf16[4,232,128]{2,1,0:T(8,128)(2,1)} %bitcast.6), calls=%async_computation.1 | async-start | bytes 475136 | tf_op jit(solution)/shard_map/all_to_all | solution.py:193
  62.4 2.8 %shard_map.80 = (f32[928,128]{1,0:T(8,128)S(1)}, bf16[928,128]{1,0:T(8,128)(2,1)}, bf16[928,128]{1,0:T(8,128)(2,1)}, bf16[928,128]{1,0:T(8,128)(2,1)}) custom-call(s32[3]{0:T(128)S(1)} %pad_add_fusion.pos_ref, bf16[8,464,128]{2,1,0:T(8,128)(2,1)S(1)} %all-to-all-done.2.rows_ref, bf16[928,464]{1,0:T(8,128)(2,1)S(1)} %copy-done, ...), custom_call_target="tpu_custom_call" | custom-call | flops 440926208 | bytes 3949568 | tf_op jit(solution)/shard_map/pallas_call | solution.py:59
  66.0 1.1 collective-permute-start.12
  67.0 2.1 %collective-permute-start.13 = (bf16[928,128]{1,0:T(8,128)(2,1)}, bf16[928,128]{1,0:T(8,128)(2,1)}, u32[]{:S(2)}, u32[]{:S(2)}) collective-permute-start(bf16[928,128]{1,0:T(8,128)(2,1)} %get-tuple-element.50), channel_id=1, source_target_pairs={{0,16},{1,17},{2,18},{3,19},{4,20},{5,21},{6,22},{7,23},{8,24},{9,... | collective-permute-start | bytes 712712 | tf_op jit(solution)/shard_map/ppermute | solution.py:263
  69.1 1.3 collective-permute-start.14
  71.4 1.3 shard_map.81
  72.8 5.6 %all-to-all-start.3 = ((bf16[4,232,128]{2,1,0:T(8,128)(2,1)}), bf16[4,232,128]{2,1,0:T(8,128)(2,1)S(1)}, u32[]{:S(2)}, u32[]{:S(2)}) async-start(bf16[4,232,128]{2,1,0:T(8,128)(2,1)} %get-tuple-element.46), calls=%async_computation.3 | async-start | bytes 475136 | tf_op jit(solution)/shard_map/all_to_all | solution.py:193
  78.4 1.7 %collective-permute-done.13 = bf16[928,128]{1,0:T(8,128)(2,1)} collective-permute-done((bf16[928,128]{1,0:T(8,128)(2,1)}, bf16[928,128]{1,0:T(8,128)(2,1)}, u32[]{:S(2)}, u32[]{:S(2)}) %collective-permute-start.13) | collective-permute-done | bytes 237600 | tf_op jit(solution)/shard_map/ppermute | solution.py:263
  80.1 2.1 %add_convert_fusion = bf16[928,128]{1,0:T(8,128)(2,1)} fusion(bf16[928,128]{1,0:T(8,128)(2,1)} %collective-permute-done.14, bf16[928,128]{1,0:T(8,128)(2,1)} %collective-permute-done.13, f32[928,128]{1,0:T(8,128)} %copy-done.5, bf16[928,128]{1,0:T(8,128)(2,1)} %collective-permute-done.12), kind=kLoop, calls=%fused_computation | loop fusion | flops 831488 | bytes 1425408 | tf_op jit(solution)/shard_map/convert_element_type | solution.py:274
  82.3 4.7 %all-to-all-done.3 = bf16[4,232,128]{2,1,0:T(8,128)(2,1)S(1)} async-done(((bf16[4,232,128]{2,1,0:T(8,128)(2,1)}), bf16[4,232,128]{2,1,0:T(8,128)(2,1)S(1)}, u32[]{:S(2)}, u32[]{:S(2)}) %all-to-all-start.3) | async-done | bytes 237600 | tf_op jit(solution)/shard_map/all_to_all | solution.py:193
  87.0 3.7 %all-to-all-start.5 = ((bf16[4,232,128]{2,1,0:T(8,128)(2,1)}), bf16[4,232,128]{2,1,0:T(8,128)(2,1)S(1)}, u32[]{:S(2)}, u32[]{:S(2)}) async-start(bf16[4,232,128]{2,1,0:T(8,128)(2,1)} %bitcast.28), calls=%async_computation.5 | async-start | bytes 475136 | tf_op jit(solution)/shard_map/all_to_all | solution.py:193
  90.9 2.3 %collective-permute-start.6 = (bf16[928,128]{1,0:T(8,128)(2,1)S(1)}, bf16[928,128]{1,0:T(8,128)(2,1)}, u32[]{:S(2)}, u32[]{:S(2)}) collective-permute-start(bf16[928,128]{1,0:T(8,128)(2,1)S(1)} %bitcast.22), channel_id=1, source_target_pairs={{0,16},{1,17},{2,18},{3,19},{4,20},{5,21},{6,22},{7,23},{8,24},{9,... | collective-permute-start | bytes 712712 | tf_op jit(solution)/shard_map/ppermute | solution.py:263
  93.4 5.2 %all-to-all-done.5.arrived_ref = bf16[4,232,128]{2,1,0:T(8,128)(2,1)S(1)} async-done(((bf16[4,232,128]{2,1,0:T(8,128)(2,1)}), bf16[4,232,128]{2,1,0:T(8,128)(2,1)S(1)}, u32[]{:S(2)}, u32[]{:S(2)}) %all-to-all-start.5) | async-done | bytes 237600 | tf_op jit(solution)/shard_map/all_to_all | solution.py:193
  98.6 1.3 shard_map.84
  100.0 3.4 %all-to-all-start.6 = ((bf16[4,232,128]{2,1,0:T(8,128)(2,1)}), bf16[4,232,128]{2,1,0:T(8,128)(2,1)S(1)}, u32[]{:S(2)}, u32[]{:S(2)}) async-start(bf16[4,232,128]{2,1,0:T(8,128)(2,1)} %shard_map.84), calls=%async_computation.6 | async-start | bytes 475136 | tf_op jit(solution)/shard_map/all_to_all | solution.py:193
  103.4 4.9 %collective-permute-start.8 = (bf16[928,128]{1,0:T(8,128)(2,1)S(1)}, bf16[928,128]{1,0:T(8,128)(2,1)S(1)}, u32[]{:S(2)}, u32[]{:S(2)}) collective-permute-start(bf16[928,128]{1,0:T(8,128)(2,1)S(1)} %bitcast.24), channel_id=1, source_target_pairs={{0,1},{1,0},{2,3},{3,2},{4,5},{5,4},{6,7},{7,6},{8,9},{9,8},{10,11... | collective-permute-start | bytes 712712 | tf_op jit(solution)/shard_map/ppermute | solution.py:259
  110.6 3.5 %shard_map.82 = (bf16[8,464,128]{2,1,0:T(8,128)(2,1)}, bf16[8,928,128]{2,1,0:T(8,128)(2,1)}) custom-call(s32[3]{0:T(128)S(1)} %pad_add_fusion.pos_ref, bf16[928,128]{1,0:T(8,128)(2,1)S(1)} %bitcast.25, bf16[928,128]{1,0:T(8,128)(2,1)} %collective-permute-done.5.refs_1_, bf16[928,128]{1,0:T(8,128)(2,1)} %collective-permute-done.6.refs_2_, ...), custom_call_target="tpu_custom_call" | custom-call | flops 881852416 | bytes 5612544 | tf_op jit(solution)/shard_map/pallas_call | solution.py:59
  114.2 4.1 %all-to-all-start.4 = ((bf16[8,464,128]{2,1,0:T(8,128)(2,1)}), bf16[8,464,128]{2,1,0:T(8,128)(2,1)S(1)}, u32[]{:S(2)}, u32[]{:S(2)}) async-start(bf16[8,464,128]{2,1,0:T(8,128)(2,1)} %get-tuple-element.48), calls=%async_computation.4 | async-start | bytes 1900544 | tf_op jit(solution)/shard_map/all_to_all | solution.py:193
  118.5 2.2 %collective-permute-start.16 = (bf16[928,128]{1,0:T(8,128)(2,1)S(1)}, bf16[928,128]{1,0:T(8,128)(2,1)S(1)}, u32[]{:S(2)}, u32[]{:S(2)}) collective-permute-start(bf16[928,128]{1,0:T(8,128)(2,1)S(1)} %bitcast.17), channel_id=1, source_target_pairs={{0,16},{1,17},{2,18},{3,19},{4,20},{5,21},{6,22},{7,23},{8,24},{9,... | collective-permute-start | bytes 712712 | tf_op jit(solution)/shard_map/ppermute | solution.py:263
  121.2 1.5 copy-done.1
  122.8 2.7 %shard_map.85 = bf16[928,464]{1,0:T(8,128)(2,1)} custom-call(s32[3]{0:T(128)S(1)} %pad_add_fusion.pos_ref, bf16[8,464,128]{2,1,0:T(8,128)(2,1)S(1)} %all-to-all-done.2.rows_ref, bf16[8,928,128]{2,1,0:T(8,128)(2,1)S(1)} %copy-done.1), custom_call_target="tpu_custom_call" | custom-call | flops 881852416 | bytes 3712000 | tf_op jit(solution)/shard_map/pallas_call | solution.py:59
  125.4 3.9 %collective-permute-start.18 = (bf16[928,128]{1,0:T(8,128)(2,1)S(1)}, bf16[928,128]{1,0:T(8,128)(2,1)S(1)}, u32[]{:S(2)}, u32[]{:S(2)}) collective-permute-start(bf16[928,128]{1,0:T(8,128)(2,1)S(1)} %bitcast.19), channel_id=1, source_target_pairs={{0,1},{1,0},{2,3},{3,2},{4,5},{5,4},{6,7},{7,6},{8,9},{9,8},{10,11... | collective-permute-start | bytes 712712 | tf_op jit(solution)/shard_map/ppermute | solution.py:259
  129.3 3.4 %collective-permute-start.21 = (bf16[928,128]{1,0:T(8,128)(2,1)S(1)}, bf16[928,128]{1,0:T(8,128)(2,1)S(1)}, u32[]{:S(2)}, u32[]{:S(2)}) collective-permute-start(bf16[928,128]{1,0:T(8,128)(2,1)S(1)} %collective-permute-done.17.refs_3_), channel_id=1, source_target_pairs={{0,1},{1,0},{2,3},{3,2},{4,5},{5,4},{6,7},{7,6},{8,9},{9,8},{10,11... | collective-permute-start | bytes 712712 | tf_op jit(solution)/shard_map/ppermute | solution.py:259
  134.6 2.9 %shard_map.86 = (bf16[8,464,128]{2,1,0:T(8,128)(2,1)}, bf16[8,928,128]{2,1,0:T(8,128)(2,1)}) custom-call(s32[3]{0:T(128)S(1)} %pad_add_fusion.pos_ref, bf16[928,128]{1,0:T(8,128)(2,1)S(1)} %bitcast.20, bf16[928,128]{1,0:T(8,128)(2,1)S(1)} %collective-permute-done.15.refs_1_, bf16[928,128]{1,0:T(8,128)(2,1)S(1)} %collective-permute-done.16.refs_2_, ...), custom_call_target="tpu_custom_call" | custom-call | flops 881852416 | bytes 5612544 | tf_op jit(solution)/shard_map/pallas_call | solution.py:59
  137.5 5.2 %all-to-all-start.7 = ((bf16[8,464,128]{2,1,0:T(8,128)(2,1)}), bf16[8,464,128]{2,1,0:T(8,128)(2,1)S(1)}, u32[]{:S(2)}, u32[]{:S(2)}) async-start(bf16[8,464,128]{2,1,0:T(8,128)(2,1)} %get-tuple-element.60), calls=%async_computation.7 | async-start | bytes 1900544 | tf_op jit(solution)/shard_map/all_to_all | solution.py:193
  142.7 1.5 copy-done.2
  144.2 2.7 %shard_map.88 = bf16[464,928]{1,0:T(8,128)(2,1)} custom-call(s32[3]{0:T(128)S(1)} %pad_add_fusion.pos_ref, bf16[8,464,128]{2,1,0:T(8,128)(2,1)S(1)} %all-to-all-done.rows_ref, bf16[8,928,128]{2,1,0:T(8,128)(2,1)S(1)} %copy-done.2), custom_call_target="tpu_custom_call" | custom-call | flops 881852416 | bytes 3712000 | tf_op jit(solution)/shard_map/pallas_call | solution.py:59
  146.8 1.3 shard_map.83
  148.2 8.4 %all-to-all-done.7.value_ref = bf16[8,464,128]{2,1,0:T(8,128)(2,1)S(1)} async-done(((bf16[8,464,128]{2,1,0:T(8,128)(2,1)}), bf16[8,464,128]{2,1,0:T(8,128)(2,1)S(1)}, u32[]{:S(2)}, u32[]{:S(2)}) %all-to-all-start.7) | async-done | bytes 950304 | tf_op jit(solution)/shard_map/all_to_all | solution.py:193
  156.6 1.3 shard_map.87
  (47 shorter events, 9.0 us)
Async XLA Ops:
  0.7 0.9 copy-start.6
  3.2 8.2 %copy-start = (bf16[928,464]{1,0:T(8,128)(2,1)S(1)}, bf16[928,464]{1,0:T(8,128)(2,1)}, u32[]{:S(2)}) copy-start(bf16[928,464]{1,0:T(8,128)(2,1)} %weight_ref.3) | copy-start | bytes 2583556
  3.2 20.1 %all-to-all-start = ((bf16[8,464,128]{2,1,0:T(8,128)(2,1)}), bf16[8,464,128]{2,1,0:T(8,128)(2,1)S(1)}, u32[]{:S(2)}, u32[]{:S(2)}) async-start(bf16[8,464,128]{2,1,0:T(8,128)(2,1)} %shard_map.75), calls=%async_computation | async-start | bytes 1900544 | tf_op jit(solution)/shard_map/all_to_all | solution.py:193
  25.4 5.7 %copy-start.7 = (bf16[128,464]{0,1:T(8,128)(2,1)S(1)}, bf16[128,464]{0,1:T(8,128)(2,1)}, u32[]{:S(2)}) copy-start(bf16[128,464]{0,1:T(8,128)(2,1)} %param.7) | copy-start | bytes 356356
  25.5 3.6 %collective-permute-start = (bf16[4,928,128]{2,1,0:T(8,128)(2,1)}, bf16[4,928,128]{2,1,0:T(8,128)(2,1)S(1)}, u32[]{:S(2)}, u32[]{:S(2)}) collective-permute-start(bf16[4,928,128]{2,1,0:T(8,128)(2,1)} %shard_map.76), channel_id=1, source_target_pairs={{0,1},{1,0},{2,3},{3,2},{4,5},{5,4},{6,7},{7,6},{8,9},{9,8},{10,11... | collective-permute-start | bytes 2850824 | tf_op jit(solution)/shard_map/ppermute | solution.py:259
  32.7 18.9 %all-to-all-start.2 = ((bf16[8,464,128]{2,1,0:T(8,128)(2,1)}), bf16[8,464,128]{2,1,0:T(8,128)(2,1)S(1)}, u32[]{:S(2)}, u32[]{:S(2)}) async-start(bf16[8,464,128]{2,1,0:T(8,128)(2,1)} %shard_map.78), calls=%async_computation.2 | async-start | bytes 1900544 | tf_op jit(solution)/shard_map/all_to_all | solution.py:193
  36.3 8.4 %collective-permute-start.1 = (bf16[928,128]{1,0:T(8,128)(2,1)}, bf16[928,128]{1,0:T(8,128)(2,1)S(1)}, u32[]{:S(2)}, u32[]{:S(2)}) collective-permute-start(bf16[928,128]{1,0:T(8,128)(2,1)} %get-tuple-element.36), channel_id=1, source_target_pairs={{0,8},{1,9},{2,10},{3,11},{4,12},{5,13},{6,14},{7,15},{8,16},{9,17... | collective-permute-start | bytes 712712 | tf_op jit(solution)/shard_map/ppermute | solution.py:263
  37.6 13.2 %collective-permute-start.2 = (bf16[928,128]{1,0:T(8,128)(2,1)}, bf16[928,128]{1,0:T(8,128)(2,1)S(1)}, u32[]{:S(2)}, u32[]{:S(2)}) collective-permute-start(bf16[928,128]{1,0:T(8,128)(2,1)} %get-tuple-element.37), channel_id=1, source_target_pairs={{0,16},{1,17},{2,18},{3,19},{4,20},{5,21},{6,22},{7,23},{8,24},{9,... | collective-permute-start | bytes 712712 | tf_op jit(solution)/shard_map/ppermute | solution.py:263
  40.0 10.8 %collective-permute-start.3 = (bf16[928,128]{1,0:T(8,128)(2,1)}, bf16[928,128]{1,0:T(8,128)(2,1)S(1)}, u32[]{:S(2)}, u32[]{:S(2)}) collective-permute-start(bf16[928,128]{1,0:T(8,128)(2,1)} %get-tuple-element.38), channel_id=1, source_target_pairs={{0,24},{1,25},{2,26},{3,27},{4,28},{5,29},{6,30},{7,31},{8,0},{9,1... | collective-permute-start | bytes 712712 | tf_op jit(solution)/shard_map/ppermute | solution.py:263
  53.8 8.6 %collective-permute-start.4 = (bf16[4,928,128]{2,1,0:T(8,128)(2,1)}, bf16[4,928,128]{2,1,0:T(8,128)(2,1)}, u32[]{:S(2)}, u32[]{:S(2)}) collective-permute-start(bf16[4,928,128]{2,1,0:T(8,128)(2,1)} %shard_map.79), channel_id=1, source_target_pairs={{0,1},{1,0},{2,3},{3,2},{4,5},{5,4},{6,7},{7,6},{8,9},{9,8},{10,11... | collective-permute-start | bytes 2850824 | tf_op jit(solution)/shard_map/ppermute | solution.py:259
  55.1 16.3 %all-to-all-start.1 = ((bf16[4,232,128]{2,1,0:T(8,128)(2,1)}), bf16[4,232,128]{2,1,0:T(8,128)(2,1)S(1)}, u32[]{:S(2)}, u32[]{:S(2)}) async-start(bf16[4,232,128]{2,1,0:T(8,128)(2,1)} %bitcast.6), calls=%async_computation.1 | async-start | bytes 475136 | tf_op jit(solution)/shard_map/all_to_all | solution.py:193
  65.2 0.8 copy-start.5
  66.0 44.7 %copy-start.4 = (bf16[928,464]{0,1:T(8,128)(2,1)S(1)}, bf16[928,464]{0,1:T(8,128)(2,1)}, u32[]{:S(2)}) copy-start(bf16[928,464]{0,1:T(8,128)(2,1)} %copy.9) | copy-start | bytes 2583556
  66.0 12.4 %collective-permute-start.12 = (bf16[928,128]{1,0:T(8,128)(2,1)}, bf16[928,128]{1,0:T(8,128)(2,1)}, u32[]{:S(2)}, u32[]{:S(2)}) collective-permute-start(bf16[928,128]{1,0:T(8,128)(2,1)} %get-tuple-element.49), channel_id=1, source_target_pairs={{0,8},{1,9},{2,10},{3,11},{4,12},{5,13},{6,14},{7,15},{8,16},{9,17... | collective-permute-start | bytes 712712 | tf_op jit(solution)/shard_map/ppermute | solution.py:263
  67.0 13.1 %collective-permute-start.13 = (bf16[928,128]{1,0:T(8,128)(2,1)}, bf16[928,128]{1,0:T(8,128)(2,1)}, u32[]{:S(2)}, u32[]{:S(2)}) collective-permute-start(bf16[928,128]{1,0:T(8,128)(2,1)} %get-tuple-element.50), channel_id=1, source_target_pairs={{0,16},{1,17},{2,18},{3,19},{4,20},{5,21},{6,22},{7,23},{8,24},{9,... | collective-permute-start | bytes 712712 | tf_op jit(solution)/shard_map/ppermute | solution.py:263
  69.1 11.0 %collective-permute-start.14 = (bf16[928,128]{1,0:T(8,128)(2,1)}, bf16[928,128]{1,0:T(8,128)(2,1)}, u32[]{:S(2)}, u32[]{:S(2)}) collective-permute-start(bf16[928,128]{1,0:T(8,128)(2,1)} %get-tuple-element.51), channel_id=1, source_target_pairs={{0,24},{1,25},{2,26},{3,27},{4,28},{5,29},{6,30},{7,31},{8,0},{9,1... | collective-permute-start | bytes 712712 | tf_op jit(solution)/shard_map/ppermute | solution.py:263
  72.8 14.2 %all-to-all-start.3 = ((bf16[4,232,128]{2,1,0:T(8,128)(2,1)}), bf16[4,232,128]{2,1,0:T(8,128)(2,1)S(1)}, u32[]{:S(2)}, u32[]{:S(2)}) async-start(bf16[4,232,128]{2,1,0:T(8,128)(2,1)} %get-tuple-element.46), calls=%async_computation.3 | async-start | bytes 475136 | tf_op jit(solution)/shard_map/all_to_all | solution.py:193
  87.0 11.7 %all-to-all-start.5 = ((bf16[4,232,128]{2,1,0:T(8,128)(2,1)}), bf16[4,232,128]{2,1,0:T(8,128)(2,1)S(1)}, u32[]{:S(2)}, u32[]{:S(2)}) async-start(bf16[4,232,128]{2,1,0:T(8,128)(2,1)} %bitcast.28), calls=%async_computation.5 | async-start | bytes 475136 | tf_op jit(solution)/shard_map/all_to_all | solution.py:193
  90.7 17.6 %collective-permute-start.7 = (bf16[928,128]{1,0:T(8,128)(2,1)S(1)}, bf16[928,128]{1,0:T(8,128)(2,1)}, u32[]{:S(2)}, u32[]{:S(2)}) collective-permute-start(bf16[928,128]{1,0:T(8,128)(2,1)S(1)} %bitcast.21), channel_id=1, source_target_pairs={{0,8},{1,9},{2,10},{3,11},{4,12},{5,13},{6,14},{7,15},{8,16},{9,17... | collective-permute-start | bytes 712712 | tf_op jit(solution)/shard_map/ppermute | solution.py:263
  90.9 17.5 %collective-permute-start.6 = (bf16[928,128]{1,0:T(8,128)(2,1)S(1)}, bf16[928,128]{1,0:T(8,128)(2,1)}, u32[]{:S(2)}, u32[]{:S(2)}) collective-permute-start(bf16[928,128]{1,0:T(8,128)(2,1)S(1)} %bitcast.22), channel_id=1, source_target_pairs={{0,16},{1,17},{2,18},{3,19},{4,20},{5,21},{6,22},{7,23},{8,24},{9,... | collective-permute-start | bytes 712712 | tf_op jit(solution)/shard_map/ppermute | solution.py:263
  93.2 15.5 %collective-permute-start.5 = (bf16[928,128]{1,0:T(8,128)(2,1)S(1)}, bf16[928,128]{1,0:T(8,128)(2,1)}, u32[]{:S(2)}, u32[]{:S(2)}) collective-permute-start(bf16[928,128]{1,0:T(8,128)(2,1)S(1)} %bitcast.23), channel_id=1, source_target_pairs={{0,24},{1,25},{2,26},{3,27},{4,28},{5,29},{6,30},{7,31},{8,0},{9,1... | collective-permute-start | bytes 712712 | tf_op jit(solution)/shard_map/ppermute | solution.py:263
  100.0 14.2 %all-to-all-start.6 = ((bf16[4,232,128]{2,1,0:T(8,128)(2,1)}), bf16[4,232,128]{2,1,0:T(8,128)(2,1)S(1)}, u32[]{:S(2)}, u32[]{:S(2)}) async-start(bf16[4,232,128]{2,1,0:T(8,128)(2,1)} %shard_map.84), calls=%async_computation.6 | async-start | bytes 475136 | tf_op jit(solution)/shard_map/all_to_all | solution.py:193
  103.4 6.0 %collective-permute-start.8 = (bf16[928,128]{1,0:T(8,128)(2,1)S(1)}, bf16[928,128]{1,0:T(8,128)(2,1)S(1)}, u32[]{:S(2)}, u32[]{:S(2)}) collective-permute-start(bf16[928,128]{1,0:T(8,128)(2,1)S(1)} %bitcast.24), channel_id=1, source_target_pairs={{0,1},{1,0},{2,3},{3,2},{4,5},{5,4},{6,7},{7,6},{8,9},{9,8},{10,11... | collective-permute-start | bytes 712712 | tf_op jit(solution)/shard_map/ppermute | solution.py:259
  108.2 1.7 %collective-permute-start.11 = (bf16[928,128]{1,0:T(8,128)(2,1)}, bf16[928,128]{1,0:T(8,128)(2,1)S(1)}, u32[]{:S(2)}, u32[]{:S(2)}) collective-permute-start(bf16[928,128]{1,0:T(8,128)(2,1)} %collective-permute-done.7.refs_3_), channel_id=1, source_target_pairs={{0,1},{1,0},{2,3},{3,2},{4,5},{5,4},{6,7},{7,6},{8,9},{9,8},{10,11... | collective-permute-start | bytes 712712 | tf_op jit(solution)/shard_map/ppermute | solution.py:259
  108.4 1.9 %collective-permute-start.10 = (bf16[928,128]{1,0:T(8,128)(2,1)}, bf16[928,128]{1,0:T(8,128)(2,1)S(1)}, u32[]{:S(2)}, u32[]{:S(2)}) collective-permute-start(bf16[928,128]{1,0:T(8,128)(2,1)} %collective-permute-done.6.refs_2_), channel_id=1, source_target_pairs={{0,1},{1,0},{2,3},{3,2},{4,5},{5,4},{6,7},{7,6},{8,9},{9,8},{10,11... | collective-permute-start | bytes 712712 | tf_op jit(solution)/shard_map/ppermute | solution.py:259
  108.8 1.9 %collective-permute-start.9 = (bf16[928,128]{1,0:T(8,128)(2,1)}, bf16[928,128]{1,0:T(8,128)(2,1)S(1)}, u32[]{:S(2)}, u32[]{:S(2)}) collective-permute-start(bf16[928,128]{1,0:T(8,128)(2,1)} %collective-permute-done.5.refs_1_), channel_id=1, source_target_pairs={{0,1},{1,0},{2,3},{3,2},{4,5},{5,4},{6,7},{7,6},{8,9},{9,8},{10,11... | collective-permute-start | bytes 712712 | tf_op jit(solution)/shard_map/ppermute | solution.py:259
  114.2 23.3 %all-to-all-start.4 = ((bf16[8,464,128]{2,1,0:T(8,128)(2,1)}), bf16[8,464,128]{2,1,0:T(8,128)(2,1)S(1)}, u32[]{:S(2)}, u32[]{:S(2)}) async-start(bf16[8,464,128]{2,1,0:T(8,128)(2,1)} %get-tuple-element.48), calls=%async_computation.4 | async-start | bytes 1900544 | tf_op jit(solution)/shard_map/all_to_all | solution.py:193
  118.3 11.1 %collective-permute-start.17 = (bf16[928,128]{1,0:T(8,128)(2,1)S(1)}, bf16[928,128]{1,0:T(8,128)(2,1)S(1)}, u32[]{:S(2)}, u32[]{:S(2)}) collective-permute-start(bf16[928,128]{1,0:T(8,128)(2,1)S(1)} %bitcast.16), channel_id=1, source_target_pairs={{0,8},{1,9},{2,10},{3,11},{4,12},{5,13},{6,14},{7,15},{8,16},{9,17... | collective-permute-start | bytes 712712 | tf_op jit(solution)/shard_map/ppermute | solution.py:263
  118.5 14.2 %collective-permute-start.16 = (bf16[928,128]{1,0:T(8,128)(2,1)S(1)}, bf16[928,128]{1,0:T(8,128)(2,1)S(1)}, u32[]{:S(2)}, u32[]{:S(2)}) collective-permute-start(bf16[928,128]{1,0:T(8,128)(2,1)S(1)} %bitcast.17), channel_id=1, source_target_pairs={{0,16},{1,17},{2,18},{3,19},{4,20},{5,21},{6,22},{7,23},{8,24},{9,... | collective-permute-start | bytes 712712 | tf_op jit(solution)/shard_map/ppermute | solution.py:263
  120.7 12.0 %collective-permute-start.15 = (bf16[928,128]{1,0:T(8,128)(2,1)S(1)}, bf16[928,128]{1,0:T(8,128)(2,1)S(1)}, u32[]{:S(2)}, u32[]{:S(2)}) collective-permute-start(bf16[928,128]{1,0:T(8,128)(2,1)S(1)} %bitcast.18), channel_id=1, source_target_pairs={{0,24},{1,25},{2,26},{3,27},{4,28},{5,29},{6,30},{7,31},{8,0},{9,1... | collective-permute-start | bytes 712712 | tf_op jit(solution)/shard_map/ppermute | solution.py:263
  121.2 1.5 copy-start.1
  122.8 11.8 %copy-start.3 = (bf16[464,928]{1,0:T(8,128)(2,1)S(1)}, bf16[464,928]{1,0:T(8,128)(2,1)}, u32[]{:S(2)}) copy-start(bf16[464,928]{1,0:T(8,128)(2,1)} %refs_8_.1) | copy-start | bytes 2583556
  125.4 8.0 %collective-permute-start.18 = (bf16[928,128]{1,0:T(8,128)(2,1)S(1)}, bf16[928,128]{1,0:T(8,128)(2,1)S(1)}, u32[]{:S(2)}, u32[]{:S(2)}) collective-permute-start(bf16[928,128]{1,0:T(8,128)(2,1)S(1)} %bitcast.19), channel_id=1, source_target_pairs={{0,1},{1,0},{2,3},{3,2},{4,5},{5,4},{6,7},{7,6},{8,9},{9,8},{10,11... | collective-permute-start | bytes 712712 | tf_op jit(solution)/shard_map/ppermute | solution.py:259
  129.3 4.5 %collective-permute-start.21 = (bf16[928,128]{1,0:T(8,128)(2,1)S(1)}, bf16[928,128]{1,0:T(8,128)(2,1)S(1)}, u32[]{:S(2)}, u32[]{:S(2)}) collective-permute-start(bf16[928,128]{1,0:T(8,128)(2,1)S(1)} %collective-permute-done.17.refs_3_), channel_id=1, source_target_pairs={{0,1},{1,0},{2,3},{3,2},{4,5},{5,4},{6,7},{7,6},{8,9},{9,8},{10,11... | collective-permute-start | bytes 712712 | tf_op jit(solution)/shard_map/ppermute | solution.py:259
  132.8 1.5 collective-permute-start.20
  132.8 1.8 %collective-permute-start.19 = (bf16[928,128]{1,0:T(8,128)(2,1)S(1)}, bf16[928,128]{1,0:T(8,128)(2,1)S(1)}, u32[]{:S(2)}, u32[]{:S(2)}) collective-permute-start(bf16[928,128]{1,0:T(8,128)(2,1)S(1)} %collective-permute-done.15.refs_1_), channel_id=1, source_target_pairs={{0,1},{1,0},{2,3},{3,2},{4,5},{5,4},{6,7},{7,6},{8,9},{9,8},{10,11... | collective-permute-start | bytes 712712 | tf_op jit(solution)/shard_map/ppermute | solution.py:259
  137.5 19.1 %all-to-all-start.7 = ((bf16[8,464,128]{2,1,0:T(8,128)(2,1)}), bf16[8,464,128]{2,1,0:T(8,128)(2,1)S(1)}, u32[]{:S(2)}, u32[]{:S(2)}) async-start(bf16[8,464,128]{2,1,0:T(8,128)(2,1)} %get-tuple-element.60), calls=%async_computation.7 | async-start | bytes 1900544 | tf_op jit(solution)/shard_map/all_to_all | solution.py:193
  142.7 1.5 copy-start.2

commit v6 on v5

--- a/solution.py
+++ b/solution.py
@@ -206,6 +206,7 @@
 
     outs = [shaped((count,) + value.shape, BF)]
     scratch = [pltpu.SemaphoreType.DMA((count,))]
+    value = pltpu.with_memory_space_constraint(value, pltpu.HBM)
     return kernel_call(kernel, outs, 0, pos, [value], scratch, (0,), (0,))[0]
 
 
@@ -297,12 +298,12 @@
     pos = jnp.stack([rep >> 3, rep & 1, (rep >> 1) & 3]).astype(jnp.int32)
 
     tok = exchange(many(pos, tokens.T, GRP), "grp")
-    first_turned, second_turned, tok = lax.optimization_barrier(
-        (first_weight.T, second_weight.T, tok)
+    first_turned, second_turned, cots, tok = lax.optimization_barrier(
+        (first_weight.T, second_weight.T, many(pos, cotangent.T, GRP), tok)
     )
     sent = other_half(pos, tok, first_turned)
     keep, sent = own_half(pos, tok, first_turned, swap_cores(sent))
-    cot = exchange(many(pos, after(cotangent.T, keep), GRP), "grp")
+    cot = exchange(after(cots, keep), "grp")
     value = sum_x(keep, sent)
 
     sent = other_half(pos, after(cot, value), second_weight)

time: 159 us -> 207 us (1.30)
  Pallas kernels: 29.3 us -> 87.2 us
  waiting for transfers between devices: 46.5 us -> 35.7 us
    pallas_call x14, Pallas kernels: 29.3 us -> 87.2 us  [kernel_call(): pl.pallas_call(kernel, out_shape=[pltpu.HBM(o.shape, o.dtype) if i in far...]
    all_to_all x8, waiting for transfers between devices: 29.9 us -> 19.3 us  [exchange(): return lax.all_to_all(value, axis, 0, 0, axis_index_groups=groups)]
    unnamed x18 -> x14, local copies, waits for them, and re-layouts: 7.76 us -> 6.86 us
  transfers between devices with their start and end apart: 30 -> 30, of which waited for: 16 -> 15; matrix products, arithmetic and copies ran while one was open for 4% -> 3% of each run, Pallas kernels for 12% -> 24%
where the time goes in v6:
time: 207 us; the launch traced here: 206 us
  Pallas kernels  87.2 us (42%)
  starting transfers between devices  72.4 us (35%)
  waiting for transfers between devices  35.7 us (17%)
  local copies, waits for them, and re-layouts  6.86 us (3%)
  other arithmetic  3.02 us (1%)
    pallas_call x14, Pallas kernels, kernel_call(): pl.pallas_call(kernel, out_shape=[pltpu.HBM(o.shape, o.dtype) if i in far...  87.2 us
    all_to_all x8, starting transfers between devices, exchange(): return lax.all_to_all(value, axis, 0, 0, axis_index_groups=groups)  41.3 us
    all_to_all x8, waiting for transfers between devices, exchange(): return lax.all_to_all(value, axis, 0, 0, axis_index_groups=groups)  19.3 us
    ppermute x10, starting transfers between devices, swap_cores(): return lax.ppermute(value, 'rep', rep_pairs(0, 0, 1))  16.2 us
    ppermute x12, starting transfers between devices, move_x(): return lax.ppermute(value, 'rep', rep_pairs(d, 0, 0))  14.9 us
    ppermute x12, waiting for transfers between devices, move_x(): return lax.ppermute(value, 'rep', rep_pairs(d, 0, 0))  11.1 us
    unnamed x14, local copies, waits for them, and re-layouts  6.86 us
    ppermute x10, waiting for transfers between devices, swap_cores(): return lax.ppermute(value, 'rep', rep_pairs(0, 0, 1))  5.3 us
  transfers between devices with their start and end apart: 30, of which 15 were waited for; matrix products, arithmetic and copies ran while one was open for 3% of the time, Pallas kernels for 24%

profile of v6, /device:TPU:1, one launch (start us, length us, event | category | flops | bytes accessed | tf_op | source)
XLA Modules:
  0.0 205.9 jit_solution(1009544345931344082)
XLA Ops:
  0.7 30.5 %shard_map.76 = bf16[8,464,128]{2,1,0:T(8,128)(2,1)} custom-call(s32[3]{0:T(128)S(1)} %pad_add_fusion.pos_ref, bf16[464,128]{1,0:T(8,128)(2,1)} %bitcast.27), custom_call_target="tpu_custom_call" | custom-call | bytes 1069056 | tf_op jit(solution)/shard_map/pallas_call | solution.py:59
  31.2 6.4 %all-to-all-start = ((bf16[8,464,128]{2,1,0:T(8,128)(2,1)}), bf16[8,464,128]{2,1,0:T(8,128)(2,1)S(1)}, u32[]{:S(2)}, u32[]{:S(2)}) async-start(bf16[8,464,128]{2,1,0:T(8,128)(2,1)} %shard_map.76), calls=%async_computation | async-start | bytes 1900544 | tf_op jit(solution)/shard_map/all_to_all | solution.py:193
  37.6 30.5 %shard_map.75 = bf16[8,464,128]{2,1,0:T(8,128)(2,1)} custom-call(s32[3]{0:T(128)S(1)} %pad_add_fusion.pos_ref, bf16[464,128]{1,0:T(8,128)(2,1)} %bitcast.28), custom_call_target="tpu_custom_call" | custom-call | bytes 1069056 | tf_op jit(solution)/shard_map/pallas_call | solution.py:59
  68.1 1.6 copy.8
  69.8 1.4 copy.9
  71.2 2.2 %shard_map.77 = bf16[4,928,128]{2,1,0:T(8,128)(2,1)} custom-call(s32[3]{0:T(128)S(1)} %pad_add_fusion.pos_ref, bf16[8,464,128]{2,1,0:T(8,128)(2,1)S(1)} %all-to-all-done.rows_ref, bf16[928,464]{1,0:T(8,128)(2,1)S(1)} %bitcast.13), custom_call_target="tpu_custom_call" | custom-call | flops 440926208 | bytes 2761728 | tf_op jit(solution)/shard_map/pallas_call | solution.py:59
  73.4 1.0 collective-permute-start
  74.4 2.4 %collective-permute-done.arrived_ref = bf16[4,928,128]{2,1,0:T(8,128)(2,1)S(1)} collective-permute-done((bf16[4,928,128]{2,1,0:T(8,128)(2,1)}, bf16[4,928,128]{2,1,0:T(8,128)(2,1)S(1)}, u32[]{:S(2)}, u32[]{:S(2)}) %collective-permute-start) | collective-permute-done | bytes 950304 | tf_op jit(solution)/shard_map/ppermute | solution.py:260
  76.8 2.1 %shard_map.78 = (f32[928,128]{1,0:T(8,128)S(1)}, bf16[928,128]{1,0:T(8,128)(2,1)}, bf16[928,128]{1,0:T(8,128)(2,1)}, bf16[928,128]{1,0:T(8,128)(2,1)}) custom-call(s32[3]{0:T(128)S(1)} %pad_add_fusion.pos_ref, bf16[8,464,128]{2,1,0:T(8,128)(2,1)S(1)} %all-to-all-done.rows_ref, bf16[928,464]{1,0:T(8,128)(2,1)S(1)} %bitcast.14, ...), custom_call_target="tpu_custom_call" | custom-call | flops 440926208 | bytes 3949568 | tf_op jit(solution)/shard_map/pallas_call | solution.py:59
  78.8 5.4 %all-to-all-start.2 = ((bf16[8,464,128]{2,1,0:T(8,128)(2,1)}), bf16[8,464,128]{2,1,0:T(8,128)(2,1)S(1)}, u32[]{:S(2)}, u32[]{:S(2)}) async-start(bf16[8,464,128]{2,1,0:T(8,128)(2,1)} %shard_map.75), calls=%async_computation.2 | async-start | bytes 1900544 | tf_op jit(solution)/shard_map/all_to_all | solution.py:193
  84.3 1.2 collective-permute-start.1
  85.5 2.5 %collective-permute-start.2 = (bf16[928,128]{1,0:T(8,128)(2,1)}, bf16[928,128]{1,0:T(8,128)(2,1)S(1)}, u32[]{:S(2)}, u32[]{:S(2)}) collective-permute-start(bf16[928,128]{1,0:T(8,128)(2,1)} %get-tuple-element.38), channel_id=1, source_target_pairs={{0,16},{1,17},{2,18},{3,19},{4,20},{5,21},{6,22},{7,23},{8,24},{9,... | collective-permute-start | bytes 712712 | tf_op jit(solution)/shard_map/ppermute | solution.py:264
  87.9 1.2 collective-permute-start.3
  89.1 3.3 %collective-permute-done.1 = bf16[928,128]{1,0:T(8,128)(2,1)S(1)} collective-permute-done((bf16[928,128]{1,0:T(8,128)(2,1)}, bf16[928,128]{1,0:T(8,128)(2,1)S(1)}, u32[]{:S(2)}, u32[]{:S(2)}) %collective-permute-start.1) | collective-permute-done | bytes 237600 | tf_op jit(solution)/shard_map/ppermute | solution.py:264
  92.4 6.1 %collective-permute-done.2 = bf16[928,128]{1,0:T(8,128)(2,1)S(1)} collective-permute-done((bf16[928,128]{1,0:T(8,128)(2,1)}, bf16[928,128]{1,0:T(8,128)(2,1)S(1)}, u32[]{:S(2)}, u32[]{:S(2)}) %collective-permute-start.2) | collective-permute-done | bytes 237600 | tf_op jit(solution)/shard_map/ppermute | solution.py:264
  99.3 2.2 %shard_map.79 = bf16[4,928,128]{2,1,0:T(8,128)(2,1)} custom-call(s32[3]{0:T(128)S(1)} %pad_add_fusion.pos_ref, bf16[8,464,128]{2,1,0:T(8,128)(2,1)S(1)} %all-to-all-done.2.rows_ref, bf16[928,464]{1,0:T(8,128)(2,1)S(1)} %copy-done), custom_call_target="tpu_custom_call" | custom-call | flops 440926208 | bytes 2761728 | tf_op jit(solution)/shard_map/pallas_call | solution.py:59
  101.4 1.6 collective-permute-start.4
  103.0 7.3 %all-to-all-start.1 = ((bf16[4,232,128]{2,1,0:T(8,128)(2,1)}), bf16[4,232,128]{2,1,0:T(8,128)(2,1)S(1)}, u32[]{:S(2)}, u32[]{:S(2)}) async-start(bf16[4,232,128]{2,1,0:T(8,128)(2,1)} %bitcast.7), calls=%async_computation.1 | async-start | bytes 475136 | tf_op jit(solution)/shard_map/all_to_all | solution.py:193
  110.3 2.8 %shard_map.80 = (f32[928,128]{1,0:T(8,128)S(1)}, bf16[928,128]{1,0:T(8,128)(2,1)}, bf16[928,128]{1,0:T(8,128)(2,1)}, bf16[928,128]{1,0:T(8,128)(2,1)}) custom-call(s32[3]{0:T(128)S(1)} %pad_add_fusion.pos_ref, bf16[8,464,128]{2,1,0:T(8,128)(2,1)S(1)} %all-to-all-done.2.rows_ref, bf16[928,464]{1,0:T(8,128)(2,1)S(1)} %copy-done, ...), custom_call_target="tpu_custom_call" | custom-call | flops 440926208 | bytes 3949568 | tf_op jit(solution)/shard_map/pallas_call | solution.py:59
  113.9 1.0 collective-permute-start.12
  114.9 2.1 %collective-permute-start.13 = (bf16[928,128]{1,0:T(8,128)(2,1)}, bf16[928,128]{1,0:T(8,128)(2,1)}, u32[]{:S(2)}, u32[]{:S(2)}) collective-permute-start(bf16[928,128]{1,0:T(8,128)(2,1)} %get-tuple-element.52), channel_id=1, source_target_pairs={{0,16},{1,17},{2,18},{3,19},{4,20},{5,21},{6,22},{7,23},{8,24},{9,... | collective-permute-start | bytes 712712 | tf_op jit(solution)/shard_map/ppermute | solution.py:264
  117.0 1.3 collective-permute-start.14
  118.3 1.0 all-to-all-done.1.arrived_ref
  119.4 1.3 shard_map.81
  120.7 5.6 %all-to-all-start.3 = ((bf16[4,232,128]{2,1,0:T(8,128)(2,1)}), bf16[4,232,128]{2,1,0:T(8,128)(2,1)S(1)}, u32[]{:S(2)}, u32[]{:S(2)}) async-start(bf16[4,232,128]{2,1,0:T(8,128)(2,1)} %get-tuple-element.48), calls=%async_computation.3 | async-start | bytes 475136 | tf_op jit(solution)/shard_map/all_to_all | solution.py:193
  126.3 1.7 collective-permute-done.13
  128.0 2.1 %add_convert_fusion = bf16[928,128]{1,0:T(8,128)(2,1)} fusion(bf16[928,128]{1,0:T(8,128)(2,1)} %collective-permute-done.14, bf16[928,128]{1,0:T(8,128)(2,1)} %collective-permute-done.13, f32[928,128]{1,0:T(8,128)} %copy-done.5, bf16[928,128]{1,0:T(8,128)(2,1)} %collective-permute-done.12), kind=kLoop, calls=%fused_computation | loop fusion | flops 831488 | bytes 1425408 | tf_op jit(solution)/shard_map/convert_element_type | solution.py:275
  130.2 4.6 %all-to-all-done.3 = bf16[4,232,128]{2,1,0:T(8,128)(2,1)S(1)} async-done(((bf16[4,232,128]{2,1,0:T(8,128)(2,1)}), bf16[4,232,128]{2,1,0:T(8,128)(2,1)S(1)}, u32[]{:S(2)}, u32[]{:S(2)}) %all-to-all-start.3) | async-done | bytes 237600 | tf_op jit(solution)/shard_map/all_to_all | solution.py:193
  134.8 3.8 %all-to-all-start.5 = ((bf16[4,232,128]{2,1,0:T(8,128)(2,1)}), bf16[4,232,128]{2,1,0:T(8,128)(2,1)S(1)}, u32[]{:S(2)}, u32[]{:S(2)}) async-start(bf16[4,232,128]{2,1,0:T(8,128)(2,1)} %bitcast.26), calls=%async_computation.5 | async-start | bytes 475136 | tf_op jit(solution)/shard_map/all_to_all | solution.py:193
  138.8 2.4 %collective-permute-start.6 = (bf16[928,128]{1,0:T(8,128)(2,1)S(1)}, bf16[928,128]{1,0:T(8,128)(2,1)}, u32[]{:S(2)}, u32[]{:S(2)}) collective-permute-start(bf16[928,128]{1,0:T(8,128)(2,1)S(1)} %bitcast.22), channel_id=1, source_target_pairs={{0,16},{1,17},{2,18},{3,19},{4,20},{5,21},{6,22},{7,23},{8,24},{9,... | collective-permute-start | bytes 712712 | tf_op jit(solution)/shard_map/ppermute | solution.py:264
  141.3 5.2 %all-to-all-done.5.arrived_ref = bf16[4,232,128]{2,1,0:T(8,128)(2,1)S(1)} async-done(((bf16[4,232,128]{2,1,0:T(8,128)(2,1)}), bf16[4,232,128]{2,1,0:T(8,128)(2,1)S(1)}, u32[]{:S(2)}, u32[]{:S(2)}) %all-to-all-start.5) | async-done | bytes 237600 | tf_op jit(solution)/shard_map/all_to_all | solution.py:193
  146.5 1.3 shard_map.84
  147.9 3.4 %all-to-all-start.6 = ((bf16[4,232,128]{2,1,0:T(8,128)(2,1)}), bf16[4,232,128]{2,1,0:T(8,128)(2,1)S(1)}, u32[]{:S(2)}, u32[]{:S(2)}) async-start(bf16[4,232,128]{2,1,0:T(8,128)(2,1)} %shard_map.84), calls=%async_computation.6 | async-start | bytes 475136 | tf_op jit(solution)/shard_map/all_to_all | solution.py:193
  151.3 4.9 %collective-permute-start.8 = (bf16[928,128]{1,0:T(8,128)(2,1)S(1)}, bf16[928,128]{1,0:T(8,128)(2,1)S(1)}, u32[]{:S(2)}, u32[]{:S(2)}) collective-permute-start(bf16[928,128]{1,0:T(8,128)(2,1)S(1)} %bitcast.24), channel_id=1, source_target_pairs={{0,1},{1,0},{2,3},{3,2},{4,5},{5,4},{6,7},{7,6},{8,9},{9,8},{10,11... | collective-permute-start | bytes 712712 | tf_op jit(solution)/shard_map/ppermute | solution.py:260
  158.6 3.5 %shard_map.82 = (bf16[8,464,128]{2,1,0:T(8,128)(2,1)}, bf16[8,928,128]{2,1,0:T(8,128)(2,1)}) custom-call(s32[3]{0:T(128)S(1)} %pad_add_fusion.pos_ref, bf16[928,128]{1,0:T(8,128)(2,1)S(1)} %bitcast.25, bf16[928,128]{1,0:T(8,128)(2,1)} %collective-permute-done.5.refs_1_, bf16[928,128]{1,0:T(8,128)(2,1)} %collective-permute-done.6.refs_2_, ...), custom_call_target="tpu_custom_call" | custom-call | flops 881852416 | bytes 5612544 | tf_op jit(solution)/shard_map/pallas_call | solution.py:59
  162.1 4.2 %all-to-all-start.4 = ((bf16[8,464,128]{2,1,0:T(8,128)(2,1)}), bf16[8,464,128]{2,1,0:T(8,128)(2,1)S(1)}, u32[]{:S(2)}, u32[]{:S(2)}) async-start(bf16[8,464,128]{2,1,0:T(8,128)(2,1)} %get-tuple-element.50), calls=%async_computation.4 | async-start | bytes 1900544 | tf_op jit(solution)/shard_map/all_to_all | solution.py:193
  166.5 2.3 %collective-permute-start.16 = (bf16[928,128]{1,0:T(8,128)(2,1)S(1)}, bf16[928,128]{1,0:T(8,128)(2,1)S(1)}, u32[]{:S(2)}, u32[]{:S(2)}) collective-permute-start(bf16[928,128]{1,0:T(8,128)(2,1)S(1)} %bitcast.17), channel_id=1, source_target_pairs={{0,16},{1,17},{2,18},{3,19},{4,20},{5,21},{6,22},{7,23},{8,24},{9,... | collective-permute-start | bytes 712712 | tf_op jit(solution)/shard_map/ppermute | solution.py:264
  169.2 1.5 copy-done.1
  170.7 2.7 %shard_map.85 = bf16[928,464]{1,0:T(8,128)(2,1)} custom-call(s32[3]{0:T(128)S(1)} %pad_add_fusion.pos_ref, bf16[8,464,128]{2,1,0:T(8,128)(2,1)S(1)} %all-to-all-done.2.rows_ref, bf16[8,928,128]{2,1,0:T(8,128)(2,1)S(1)} %copy-done.1), custom_call_target="tpu_custom_call" | custom-call | flops 881852416 | bytes 3712000 | tf_op jit(solution)/shard_map/pallas_call | solution.py:59
  173.4 4.0 %collective-permute-start.18 = (bf16[928,128]{1,0:T(8,128)(2,1)S(1)}, bf16[928,128]{1,0:T(8,128)(2,1)S(1)}, u32[]{:S(2)}, u32[]{:S(2)}) collective-permute-start(bf16[928,128]{1,0:T(8,128)(2,1)S(1)} %bitcast.19), channel_id=1, source_target_pairs={{0,1},{1,0},{2,3},{3,2},{4,5},{5,4},{6,7},{7,6},{8,9},{9,8},{10,11... | collective-permute-start | bytes 712712 | tf_op jit(solution)/shard_map/ppermute | solution.py:260
  177.4 3.4 %collective-permute-start.21 = (bf16[928,128]{1,0:T(8,128)(2,1)S(1)}, bf16[928,128]{1,0:T(8,128)(2,1)S(1)}, u32[]{:S(2)}, u32[]{:S(2)}) collective-permute-start(bf16[928,128]{1,0:T(8,128)(2,1)S(1)} %collective-permute-done.17.refs_3_), channel_id=1, source_target_pairs={{0,1},{1,0},{2,3},{3,2},{4,5},{5,4},{6,7},{7,6},{8,9},{9,8},{10,11... | collective-permute-start | bytes 712712 | tf_op jit(solution)/shard_map/ppermute | solution.py:260
  182.7 2.9 %shard_map.86 = (bf16[8,464,128]{2,1,0:T(8,128)(2,1)}, bf16[8,928,128]{2,1,0:T(8,128)(2,1)}) custom-call(s32[3]{0:T(128)S(1)} %pad_add_fusion.pos_ref, bf16[928,128]{1,0:T(8,128)(2,1)S(1)} %bitcast.20, bf16[928,128]{1,0:T(8,128)(2,1)S(1)} %collective-permute-done.15.refs_1_, bf16[928,128]{1,0:T(8,128)(2,1)S(1)} %collective-permute-done.16.refs_2_, ...), custom_call_target="tpu_custom_call" | custom-call | flops 881852416 | bytes 5612544 | tf_op jit(solution)/shard_map/pallas_call | solution.py:59
  185.6 5.2 %all-to-all-start.7 = ((bf16[8,464,128]{2,1,0:T(8,128)(2,1)}), bf16[8,464,128]{2,1,0:T(8,128)(2,1)S(1)}, u32[]{:S(2)}, u32[]{:S(2)}) async-start(bf16[8,464,128]{2,1,0:T(8,128)(2,1)} %get-tuple-element.62), calls=%async_computation.7 | async-start | bytes 1900544 | tf_op jit(solution)/shard_map/all_to_all | solution.py:193
  190.7 1.5 copy-done.2
  192.2 2.7 %shard_map.88 = bf16[464,928]{1,0:T(8,128)(2,1)} custom-call(s32[3]{0:T(128)S(1)} %pad_add_fusion.pos_ref, bf16[8,464,128]{2,1,0:T(8,128)(2,1)S(1)} %all-to-all-done.rows_ref, bf16[8,928,128]{2,1,0:T(8,128)(2,1)S(1)} %copy-done.2), custom_call_target="tpu_custom_call" | custom-call | flops 881852416 | bytes 3712000 | tf_op jit(solution)/shard_map/pallas_call | solution.py:59
  194.9 1.3 shard_map.83
  196.2 8.4 %all-to-all-done.7.value_ref = bf16[8,464,128]{2,1,0:T(8,128)(2,1)S(1)} async-done(((bf16[8,464,128]{2,1,0:T(8,128)(2,1)}), bf16[8,464,128]{2,1,0:T(8,128)(2,1)S(1)}, u32[]{:S(2)}, u32[]{:S(2)}) %all-to-all-start.7) | async-done | bytes 950304 | tf_op jit(solution)/shard_map/all_to_all | solution.py:193
  204.6 1.3 shard_map.87
  (43 shorter events, 6.9 us)
Async XLA Ops:
  31.2 40.0 %all-to-all-start = ((bf16[8,464,128]{2,1,0:T(8,128)(2,1)}), bf16[8,464,128]{2,1,0:T(8,128)(2,1)S(1)}, u32[]{:S(2)}, u32[]{:S(2)}) async-start(bf16[8,464,128]{2,1,0:T(8,128)(2,1)} %shard_map.76), calls=%async_computation | async-start | bytes 1900544 | tf_op jit(solution)/shard_map/all_to_all | solution.py:193
  37.6 32.2 %copy-start = (bf16[928,464]{1,0:T(8,128)(2,1)S(1)}, bf16[928,464]{1,0:T(8,128)(2,1)}, u32[]{:S(2)}) copy-start(bf16[928,464]{1,0:T(8,128)(2,1)} %weight_ref.3) | copy-start | bytes 2583556
  73.4 3.4 %collective-permute-start = (bf16[4,928,128]{2,1,0:T(8,128)(2,1)}, bf16[4,928,128]{2,1,0:T(8,128)(2,1)S(1)}, u32[]{:S(2)}, u32[]{:S(2)}) collective-permute-start(bf16[4,928,128]{2,1,0:T(8,128)(2,1)} %shard_map.77), channel_id=1, source_target_pairs={{0,1},{1,0},{2,3},{3,2},{4,5},{5,4},{6,7},{7,6},{8,9},{9,8},{10,11... | collective-permute-start | bytes 2850824 | tf_op jit(solution)/shard_map/ppermute | solution.py:260
  78.8 20.4 %all-to-all-start.2 = ((bf16[8,464,128]{2,1,0:T(8,128)(2,1)}), bf16[8,464,128]{2,1,0:T(8,128)(2,1)S(1)}, u32[]{:S(2)}, u32[]{:S(2)}) async-start(bf16[8,464,128]{2,1,0:T(8,128)(2,1)} %shard_map.75), calls=%async_computation.2 | async-start | bytes 1900544 | tf_op jit(solution)/shard_map/all_to_all | solution.py:193
  84.3 8.1 %collective-permute-start.1 = (bf16[928,128]{1,0:T(8,128)(2,1)}, bf16[928,128]{1,0:T(8,128)(2,1)S(1)}, u32[]{:S(2)}, u32[]{:S(2)}) collective-permute-start(bf16[928,128]{1,0:T(8,128)(2,1)} %get-tuple-element.37), channel_id=1, source_target_pairs={{0,8},{1,9},{2,10},{3,11},{4,12},{5,13},{6,14},{7,15},{8,16},{9,17... | collective-permute-start | bytes 712712 | tf_op jit(solution)/shard_map/ppermute | solution.py:264
  85.5 13.0 %collective-permute-start.2 = (bf16[928,128]{1,0:T(8,128)(2,1)}, bf16[928,128]{1,0:T(8,128)(2,1)S(1)}, u32[]{:S(2)}, u32[]{:S(2)}) collective-permute-start(bf16[928,128]{1,0:T(8,128)(2,1)} %get-tuple-element.38), channel_id=1, source_target_pairs={{0,16},{1,17},{2,18},{3,19},{4,20},{5,21},{6,22},{7,23},{8,24},{9,... | collective-permute-start | bytes 712712 | tf_op jit(solution)/shard_map/ppermute | solution.py:264
  87.9 10.5 %collective-permute-start.3 = (bf16[928,128]{1,0:T(8,128)(2,1)}, bf16[928,128]{1,0:T(8,128)(2,1)S(1)}, u32[]{:S(2)}, u32[]{:S(2)}) collective-permute-start(bf16[928,128]{1,0:T(8,128)(2,1)} %get-tuple-element.39), channel_id=1, source_target_pairs={{0,24},{1,25},{2,26},{3,27},{4,28},{5,29},{6,30},{7,31},{8,0},{9,1... | collective-permute-start | bytes 712712 | tf_op jit(solution)/shard_map/ppermute | solution.py:264
  101.4 8.9 %collective-permute-start.4 = (bf16[4,928,128]{2,1,0:T(8,128)(2,1)}, bf16[4,928,128]{2,1,0:T(8,128)(2,1)}, u32[]{:S(2)}, u32[]{:S(2)}) collective-permute-start(bf16[4,928,128]{2,1,0:T(8,128)(2,1)} %shard_map.79), channel_id=1, source_target_pairs={{0,1},{1,0},{2,3},{3,2},{4,5},{5,4},{6,7},{7,6},{8,9},{9,8},{10,11... | collective-permute-start | bytes 2850824 | tf_op jit(solution)/shard_map/ppermute | solution.py:260
  103.0 16.3 %all-to-all-start.1 = ((bf16[4,232,128]{2,1,0:T(8,128)(2,1)}), bf16[4,232,128]{2,1,0:T(8,128)(2,1)S(1)}, u32[]{:S(2)}, u32[]{:S(2)}) async-start(bf16[4,232,128]{2,1,0:T(8,128)(2,1)} %bitcast.7), calls=%async_computation.1 | async-start | bytes 475136 | tf_op jit(solution)/shard_map/all_to_all | solution.py:193
  113.1 0.8 copy-start.5
  113.9 44.7 %copy-start.4 = (bf16[928,464]{0,1:T(8,128)(2,1)S(1)}, bf16[928,464]{0,1:T(8,128)(2,1)}, u32[]{:S(2)}) copy-start(bf16[928,464]{0,1:T(8,128)(2,1)} %copy.9) | copy-start | bytes 2583556
  113.9 12.5 %collective-permute-start.12 = (bf16[928,128]{1,0:T(8,128)(2,1)}, bf16[928,128]{1,0:T(8,128)(2,1)}, u32[]{:S(2)}, u32[]{:S(2)}) collective-permute-start(bf16[928,128]{1,0:T(8,128)(2,1)} %get-tuple-element.51), channel_id=1, source_target_pairs={{0,8},{1,9},{2,10},{3,11},{4,12},{5,13},{6,14},{7,15},{8,16},{9,17... | collective-permute-start | bytes 712712 | tf_op jit(solution)/shard_map/ppermute | solution.py:264
  114.9 13.1 %collective-permute-start.13 = (bf16[928,128]{1,0:T(8,128)(2,1)}, bf16[928,128]{1,0:T(8,128)(2,1)}, u32[]{:S(2)}, u32[]{:S(2)}) collective-permute-start(bf16[928,128]{1,0:T(8,128)(2,1)} %get-tuple-element.52), channel_id=1, source_target_pairs={{0,16},{1,17},{2,18},{3,19},{4,20},{5,21},{6,22},{7,23},{8,24},{9,... | collective-permute-start | bytes 712712 | tf_op jit(solution)/shard_map/ppermute | solution.py:264
  117.0 11.0 %collective-permute-start.14 = (bf16[928,128]{1,0:T(8,128)(2,1)}, bf16[928,128]{1,0:T(8,128)(2,1)}, u32[]{:S(2)}, u32[]{:S(2)}) collective-permute-start(bf16[928,128]{1,0:T(8,128)(2,1)} %get-tuple-element.53), channel_id=1, source_target_pairs={{0,24},{1,25},{2,26},{3,27},{4,28},{5,29},{6,30},{7,31},{8,0},{9,1... | collective-permute-start | bytes 712712 | tf_op jit(solution)/shard_map/ppermute | solution.py:264
  120.7 14.1 %all-to-all-start.3 = ((bf16[4,232,128]{2,1,0:T(8,128)(2,1)}), bf16[4,232,128]{2,1,0:T(8,128)(2,1)S(1)}, u32[]{:S(2)}, u32[]{:S(2)}) async-start(bf16[4,232,128]{2,1,0:T(8,128)(2,1)} %get-tuple-element.48), calls=%async_computation.3 | async-start | bytes 475136 | tf_op jit(solution)/shard_map/all_to_all | solution.py:193
  134.8 11.8 %all-to-all-start.5 = ((bf16[4,232,128]{2,1,0:T(8,128)(2,1)}), bf16[4,232,128]{2,1,0:T(8,128)(2,1)S(1)}, u32[]{:S(2)}, u32[]{:S(2)}) async-start(bf16[4,232,128]{2,1,0:T(8,128)(2,1)} %bitcast.26), calls=%async_computation.5 | async-start | bytes 475136 | tf_op jit(solution)/shard_map/all_to_all | solution.py:193
  138.6 17.6 %collective-permute-start.7 = (bf16[928,128]{1,0:T(8,128)(2,1)S(1)}, bf16[928,128]{1,0:T(8,128)(2,1)}, u32[]{:S(2)}, u32[]{:S(2)}) collective-permute-start(bf16[928,128]{1,0:T(8,128)(2,1)S(1)} %bitcast.21), channel_id=1, source_target_pairs={{0,8},{1,9},{2,10},{3,11},{4,12},{5,13},{6,14},{7,15},{8,16},{9,17... | collective-permute-start | bytes 712712 | tf_op jit(solution)/shard_map/ppermute | solution.py:264
  138.8 17.5 %collective-permute-start.6 = (bf16[928,128]{1,0:T(8,128)(2,1)S(1)}, bf16[928,128]{1,0:T(8,128)(2,1)}, u32[]{:S(2)}, u32[]{:S(2)}) collective-permute-start(bf16[928,128]{1,0:T(8,128)(2,1)S(1)} %bitcast.22), channel_id=1, source_target_pairs={{0,16},{1,17},{2,18},{3,19},{4,20},{5,21},{6,22},{7,23},{8,24},{9,... | collective-permute-start | bytes 712712 | tf_op jit(solution)/shard_map/ppermute | solution.py:264
  141.1 15.6 %collective-permute-start.5 = (bf16[928,128]{1,0:T(8,128)(2,1)S(1)}, bf16[928,128]{1,0:T(8,128)(2,1)}, u32[]{:S(2)}, u32[]{:S(2)}) collective-permute-start(bf16[928,128]{1,0:T(8,128)(2,1)S(1)} %bitcast.23), channel_id=1, source_target_pairs={{0,24},{1,25},{2,26},{3,27},{4,28},{5,29},{6,30},{7,31},{8,0},{9,1... | collective-permute-start | bytes 712712 | tf_op jit(solution)/shard_map/ppermute | solution.py:264
  147.9 14.3 %all-to-all-start.6 = ((bf16[4,232,128]{2,1,0:T(8,128)(2,1)}), bf16[4,232,128]{2,1,0:T(8,128)(2,1)S(1)}, u32[]{:S(2)}, u32[]{:S(2)}) async-start(bf16[4,232,128]{2,1,0:T(8,128)(2,1)} %shard_map.84), calls=%async_computation.6 | async-start | bytes 475136 | tf_op jit(solution)/shard_map/all_to_all | solution.py:193
  151.3 6.0 %collective-permute-start.8 = (bf16[928,128]{1,0:T(8,128)(2,1)S(1)}, bf16[928,128]{1,0:T(8,128)(2,1)S(1)}, u32[]{:S(2)}, u32[]{:S(2)}) collective-permute-start(bf16[928,128]{1,0:T(8,128)(2,1)S(1)} %bitcast.24), channel_id=1, source_target_pairs={{0,1},{1,0},{2,3},{3,2},{4,5},{5,4},{6,7},{7,6},{8,9},{9,8},{10,11... | collective-permute-start | bytes 712712 | tf_op jit(solution)/shard_map/ppermute | solution.py:260
  156.2 1.7 collective-permute-start.11
  156.3 1.9 collective-permute-start.10
  156.7 1.9 collective-permute-start.9
  162.1 23.4 %all-to-all-start.4 = ((bf16[8,464,128]{2,1,0:T(8,128)(2,1)}), bf16[8,464,128]{2,1,0:T(8,128)(2,1)S(1)}, u32[]{:S(2)}, u32[]{:S(2)}) async-start(bf16[8,464,128]{2,1,0:T(8,128)(2,1)} %get-tuple-element.50), calls=%async_computation.4 | async-start | bytes 1900544 | tf_op jit(solution)/shard_map/all_to_all | solution.py:193
  166.3 11.1 %collective-permute-start.17 = (bf16[928,128]{1,0:T(8,128)(2,1)S(1)}, bf16[928,128]{1,0:T(8,128)(2,1)S(1)}, u32[]{:S(2)}, u32[]{:S(2)}) collective-permute-start(bf16[928,128]{1,0:T(8,128)(2,1)S(1)} %bitcast.16), channel_id=1, source_target_pairs={{0,8},{1,9},{2,10},{3,11},{4,12},{5,13},{6,14},{7,15},{8,16},{9,17... | collective-permute-start | bytes 712712 | tf_op jit(solution)/shard_map/ppermute | solution.py:264
  166.5 14.3 %collective-permute-start.16 = (bf16[928,128]{1,0:T(8,128)(2,1)S(1)}, bf16[928,128]{1,0:T(8,128)(2,1)S(1)}, u32[]{:S(2)}, u32[]{:S(2)}) collective-permute-start(bf16[928,128]{1,0:T(8,128)(2,1)S(1)} %bitcast.17), channel_id=1, source_target_pairs={{0,16},{1,17},{2,18},{3,19},{4,20},{5,21},{6,22},{7,23},{8,24},{9,... | collective-permute-start | bytes 712712 | tf_op jit(solution)/shard_map/ppermute | solution.py:264
  168.8 12.0 %collective-permute-start.15 = (bf16[928,128]{1,0:T(8,128)(2,1)S(1)}, bf16[928,128]{1,0:T(8,128)(2,1)S(1)}, u32[]{:S(2)}, u32[]{:S(2)}) collective-permute-start(bf16[928,128]{1,0:T(8,128)(2,1)S(1)} %bitcast.18), channel_id=1, source_target_pairs={{0,24},{1,25},{2,26},{3,27},{4,28},{5,29},{6,30},{7,31},{8,0},{9,1... | collective-permute-start | bytes 712712 | tf_op jit(solution)/shard_map/ppermute | solution.py:264
  169.2 1.5 copy-start.1
  170.7 11.9 %copy-start.3 = (bf16[464,928]{1,0:T(8,128)(2,1)S(1)}, bf16[464,928]{1,0:T(8,128)(2,1)}, u32[]{:S(2)}) copy-start(bf16[464,928]{1,0:T(8,128)(2,1)} %refs_8_.1) | copy-start | bytes 2583556
  173.4 8.1 %collective-permute-start.18 = (bf16[928,128]{1,0:T(8,128)(2,1)S(1)}, bf16[928,128]{1,0:T(8,128)(2,1)S(1)}, u32[]{:S(2)}, u32[]{:S(2)}) collective-permute-start(bf16[928,128]{1,0:T(8,128)(2,1)S(1)} %bitcast.19), channel_id=1, source_target_pairs={{0,1},{1,0},{2,3},{3,2},{4,5},{5,4},{6,7},{7,6},{8,9},{9,8},{10,11... | collective-permute-start | bytes 712712 | tf_op jit(solution)/shard_map/ppermute | solution.py:260
  177.4 4.5 %collective-permute-start.21 = (bf16[928,128]{1,0:T(8,128)(2,1)S(1)}, bf16[928,128]{1,0:T(8,128)(2,1)S(1)}, u32[]{:S(2)}, u32[]{:S(2)}) collective-permute-start(bf16[928,128]{1,0:T(8,128)(2,1)S(1)} %collective-permute-done.17.refs_3_), channel_id=1, source_target_pairs={{0,1},{1,0},{2,3},{3,2},{4,5},{5,4},{6,7},{7,6},{8,9},{9,8},{10,11... | collective-permute-start | bytes 712712 | tf_op jit(solution)/shard_map/ppermute | solution.py:260
  180.8 1.5 collective-permute-start.20
  180.8 1.8 collective-permute-start.19
  185.6 19.1 %all-to-all-start.7 = ((bf16[8,464,128]{2,1,0:T(8,128)(2,1)}), bf16[8,464,128]{2,1,0:T(8,128)(2,1)S(1)}, u32[]{:S(2)}, u32[]{:S(2)}) async-start(bf16[8,464,128]{2,1,0:T(8,128)(2,1)} %get-tuple-element.62), calls=%async_computation.7 | async-start | bytes 1900544 | tf_op jit(solution)/shard_map/all_to_all | solution.py:193
  190.7 1.5 copy-start.2

commit v7 on v6

--- a/solution.py
+++ b/solution.py
@@ -12,6 +12,7 @@
 GRP = 8
 X, Z, C = 4, 4, 2
 LANES = 128
+PIECES = 2
 
 
 def rep_index(x, z, c):
@@ -86,8 +87,10 @@
 
 def other_half(pos, rows, weight):
     depth, width = weight.shape
-
-    def kernel(pos_ref, rows_ref, weight_ref, out_ref, held_ref, sems):
+    each = X // PIECES
+
+    def kernel(pos_ref, rows_ref, weight_ref, *refs):
+        outs, held_ref, sems = refs[:PIECES], refs[-2], refs[-1]
         rows = half_of(rows_ref, 1 - pos_ref[1], pos_ref[0])
         copies = []
         for pair in range(X // 2):
@@ -96,23 +99,24 @@
             for d in range(2):
                 index = pair * 2 + d
                 held_ref[index] = block(product, d)
-                copies.append(
-                    pltpu.make_async_copy(held_ref.at[index], out_ref.at[index], sems.at[index])
-                )
+                target = outs[index // each].at[index % each]
+                copies.append(pltpu.make_async_copy(held_ref.at[index], target, sems.at[index]))
                 copies[-1].start()
         for copy in copies:
             copy.wait()
 
-    out = shaped((X, depth, LANES), BF)
+    outs = [shaped((each, depth, LANES), BF)] * PIECES
     flops = 2 * depth * width * X * LANES
-    return kernel_call(kernel, [out], flops, pos, [rows, weight], staged(out), (0,))[0]
+    scratch = staged(shaped((X, depth, LANES), BF))
+    return kernel_call(kernel, outs, flops, pos, [rows, weight], scratch, range(PIECES))
 
 
 def own_half(pos, rows, weight, arrived):
     depth, width = weight.shape
 
-    def kernel(pos_ref, rows_ref, weight_ref, arrived_ref, keep_ref, *refs):
-        sent, held_ref, sems = refs[: X - 1], refs[-2], refs[-1]
+    def kernel(pos_ref, rows_ref, weight_ref, *refs):
+        arrived, keep_ref = refs[:PIECES], refs[PIECES]
+        sent, held_ref, sems = refs[PIECES + 1 : -2], refs[-2], refs[-1]
         rows = half_of(rows_ref, pos_ref[1], pos_ref[0])
         copies = []
         for pair in (1, 0):
@@ -120,7 +124,8 @@
             product = dot(weight_ref[...], here, PLAIN)
             for i in range(2):
                 d = pair * 2 + i
-                total = block(product, i) + arrived_ref[d].astype(F32)
+                other = arrived[d * PIECES // X][d % (X // PIECES)]
+                total = block(product, i) + other.astype(F32)
                 if d == 0:
                     keep_ref[...] = total
                     continue
@@ -136,7 +141,7 @@
     outs = [shaped((depth, LANES), F32)] + [part] * (X - 1)
     scratch = staged(shaped((X - 1,) + part.shape, BF))
     flops = 2 * depth * width * X * LANES
-    operands = [rows, weight, arrived]
+    operands = [rows, weight, *arrived]
     keep, *sent = kernel_call(kernel, outs, flops, pos, operands, scratch, range(1, X))
     return keep, sent
 
@@ -206,8 +211,7 @@
 
     outs = [shaped((count,) + value.shape, BF)]
     scratch = [pltpu.SemaphoreType.DMA((count,))]
-    value = pltpu.with_memory_space_constraint(value, pltpu.HBM)
-    return kernel_call(kernel, outs, 0, pos, [value], scratch, (0,), (0,))[0]
+    return kernel_call(kernel, outs, 0, pos, [value], scratch, (0,))[0]
 
 
 def fan_out(value, held_ref, out_ref, sems):
@@ -302,12 +306,12 @@
         (first_weight.T, second_weight.T, many(pos, cotangent.T, GRP), tok)
     )
     sent = other_half(pos, tok, first_turned)
-    keep, sent = own_half(pos, tok, first_turned, swap_cores(sent))
+    keep, sent = own_half(pos, tok, first_turned, [swap_cores(part) for part in sent])
     cot = exchange(after(cots, keep), "grp")
     value = sum_x(keep, sent)
 
-    sent = other_half(pos, after(cot, value), second_weight)
-    keep, sent = own_half(pos, cot, second_weight, swap_cores(sent))
+    sent = other_half(pos, after(cot, keep), second_weight)
+    keep, sent = own_half(pos, cot, second_weight, [swap_cores(part) for part in sent])
 
     hidden, active = activated(pos, after(scatter_z(value), keep))
     deltas = sloped(pos, scatter_z(sum_x(keep, sent)), hidden)

time: 207 us -> 156 us (0.75)
  Pallas kernels: 87.2 us -> 29.4 us
  waiting for transfers between devices: 35.7 us -> 42.9 us
  starting transfers between devices: 72.4 us -> 70.2 us
    pallas_call x14, Pallas kernels: 87.2 us -> 29.4 us  [kernel_call(): pl.pallas_call(kernel, out_shape=[pltpu.HBM(o.shape, o.dtype) if i in far...]
    all_to_all x8, waiting for transfers between devices: 19.3 us -> 36.3 us  [exchange(): return lax.all_to_all(value, axis, 0, 0, axis_index_groups=groups)]
    ppermute x12, waiting for transfers between devices: 11.1 us -> 1.44 us  [move_x(): return lax.ppermute(value, 'rep', rep_pairs(d, 0, 0))]
    ppermute x10 -> x12, starting transfers between devices: 16.2 us -> 15.3 us  [swap_cores(): return lax.ppermute(value, 'rep', rep_pairs(0, 0, 1))]
    unnamed x14 -> x18, local copies, waits for them, and re-layouts: 6.86 us -> 7.76 us
    ppermute x10 -> x12, waiting for transfers between devices: 5.3 us -> 5.2 us  [swap_cores(): return lax.ppermute(value, 'rep', rep_pairs(0, 0, 1))]
  transfers between devices with their start and end apart: 30 -> 32, of which waited for: 15 -> 15; matrix products, arithmetic and copies ran while one was open for 3% -> 5% of each run, Pallas kernels for 24% -> 14%
where the time goes in v7:
time: 156 us; the launch traced here: 155 us
  starting transfers between devices  70.2 us (45%)
  waiting for transfers between devices  42.9 us (28%)
  Pallas kernels  29.4 us (19%)
  local copies, waits for them, and re-layouts  7.76 us (5%)
  other arithmetic  4.16 us (3%)
    all_to_all x8, starting transfers between devices, exchange(): return lax.all_to_all(value, axis, 0, 0, axis_index_groups=groups)  39.3 us
    all_to_all x8, waiting for transfers between devices, exchange(): return lax.all_to_all(value, axis, 0, 0, axis_index_groups=groups)  36.3 us
    pallas_call x14, Pallas kernels, kernel_call(): pl.pallas_call(kernel, out_shape=[pltpu.HBM(o.shape, o.dtype) if i in far...  29.4 us
    ppermute x12, starting transfers between devices, move_x(): return lax.ppermute(value, 'rep', rep_pairs(d, 0, 0))  15.7 us
    ppermute x12, starting transfers between devices, swap_cores(): return lax.ppermute(value, 'rep', rep_pairs(0, 0, 1))  15.3 us
    unnamed x18, local copies, waits for them, and re-layouts  7.76 us
    ppermute x12, waiting for transfers between devices, swap_cores(): return lax.ppermute(value, 'rep', rep_pairs(0, 0, 1))  5.2 us
    convert_element_type x2, other arithmetic, sum_x(): return keep.astype(BF)  4.08 us
  transfers between devices with their start and end apart: 32, of which 15 were waited for; matrix products, arithmetic and copies ran while one was open for 5% of the time, Pallas kernels for 14%

profile of v7, /device:TPU:1, one launch (start us, length us, event | category | flops | bytes accessed | tf_op | source)
XLA Modules:
  0.0 155.3 jit_solution(10369377918152793788)
XLA Ops:
  1.6 1.5 shard_map.76
  3.2 6.4 %all-to-all-start = ((bf16[8,464,128]{2,1,0:T(8,128)(2,1)}), bf16[8,464,128]{2,1,0:T(8,128)(2,1)S(1)}, u32[]{:S(2)}, u32[]{:S(2)}) async-start(bf16[8,464,128]{2,1,0:T(8,128)(2,1)} %shard_map.76), calls=%async_computation | async-start | bytes 1900544 | tf_op jit(solution)/shard_map/all_to_all | solution.py:198
  9.6 1.6 %shard_map.75 = bf16[8,464,128]{2,1,0:T(8,128)(2,1)} custom-call(s32[3]{0:T(128)S(1)} %pad_add_fusion.pos_ref, bf16[464,128]{1,0:T(8,128)(2,1)S(1)} %bitcast.27), custom_call_target="tpu_custom_call" | custom-call | bytes 1069056 | tf_op jit(solution)/shard_map/pallas_call | solution.py:60
  11.1 1.6 %copy.8 = bf16[464,928]{0,1:T(8,128)(2,1)S(1)} copy(bf16[464,928]{1,0:T(8,128)(2,1)} %refs_8_.1) | data formatting | bytes 1722368 | tf_op args[1]
  12.8 1.4 copy.9
  14.2 8.9 %all-to-all-done.rows_ref = bf16[8,464,128]{2,1,0:T(8,128)(2,1)S(1)} async-done(((bf16[8,464,128]{2,1,0:T(8,128)(2,1)}), bf16[8,464,128]{2,1,0:T(8,128)(2,1)S(1)}, u32[]{:S(2)}, u32[]{:S(2)}) %all-to-all-start) | async-done | bytes 950304 | tf_op jit(solution)/shard_map/all_to_all | solution.py:198
  23.1 2.2 %shard_map.77 = (bf16[2,928,128]{2,1,0:T(8,128)(2,1)}, bf16[2,928,128]{2,1,0:T(8,128)(2,1)}) custom-call(s32[3]{0:T(128)S(1)} %pad_add_fusion.pos_ref, bf16[8,464,128]{2,1,0:T(8,128)(2,1)S(1)} %all-to-all-done.rows_ref, bf16[928,464]{1,0:T(8,128)(2,1)S(1)} %bitcast.13), custom_call_target="tpu_custom_call" | custom-call | flops 440926208 | bytes 2761728 | tf_op jit(solution)/shard_map/pallas_call | solution.py:60
  25.3 1.2 collective-permute-start
  26.6 1.6 %collective-permute-done.refs_0_ = bf16[2,928,128]{2,1,0:T(8,128)(2,1)S(1)} collective-permute-done((bf16[2,928,128]{2,1,0:T(8,128)(2,1)}, bf16[2,928,128]{2,1,0:T(8,128)(2,1)S(1)}, u32[]{:S(2)}, u32[]{:S(2)}) %collective-permute-start) | collective-permute-done | bytes 475168 | tf_op jit(solution)/shard_map/ppermute | solution.py:264
  28.9 2.1 %shard_map.78 = (f32[928,128]{1,0:T(8,128)S(1)}, bf16[928,128]{1,0:T(8,128)(2,1)}, bf16[928,128]{1,0:T(8,128)(2,1)}, bf16[928,128]{1,0:T(8,128)(2,1)}) custom-call(s32[3]{0:T(128)S(1)} %pad_add_fusion.pos_ref, bf16[8,464,128]{2,1,0:T(8,128)(2,1)S(1)} %all-to-all-done.rows_ref, bf16[928,464]{1,0:T(8,128)(2,1)S(1)} %bitcast.14, ...), custom_call_target="tpu_custom_call" | custom-call | flops 440926208 | bytes 3949568 | tf_op jit(solution)/shard_map/pallas_call | solution.py:60
  31.0 3.6 %all-to-all-start.2 = ((bf16[8,464,128]{2,1,0:T(8,128)(2,1)}), bf16[8,464,128]{2,1,0:T(8,128)(2,1)S(1)}, u32[]{:S(2)}, u32[]{:S(2)}) async-start(bf16[8,464,128]{2,1,0:T(8,128)(2,1)} %shard_map.75), calls=%async_computation.2 | async-start | bytes 1900544 | tf_op jit(solution)/shard_map/all_to_all | solution.py:198
  34.6 1.3 collective-permute-start.2
  35.8 2.5 %collective-permute-start.3 = (bf16[928,128]{1,0:T(8,128)(2,1)}, bf16[928,128]{1,0:T(8,128)(2,1)}, u32[]{:S(2)}, u32[]{:S(2)}) collective-permute-start(bf16[928,128]{1,0:T(8,128)(2,1)} %get-tuple-element.44), channel_id=1, source_target_pairs={{0,16},{1,17},{2,18},{3,19},{4,20},{5,21},{6,22},{7,23},{8,24},{9,... | collective-permute-start | bytes 712712 | tf_op jit(solution)/shard_map/ppermute | solution.py:268
  38.3 1.2 collective-permute-start.4
  39.5 9.0 %all-to-all-done.2.rows_ref = bf16[8,464,128]{2,1,0:T(8,128)(2,1)S(1)} async-done(((bf16[8,464,128]{2,1,0:T(8,128)(2,1)}), bf16[8,464,128]{2,1,0:T(8,128)(2,1)S(1)}, u32[]{:S(2)}, u32[]{:S(2)}) %all-to-all-start.2) | async-done | bytes 950304 | tf_op jit(solution)/shard_map/all_to_all | solution.py:198
  48.5 2.2 %shard_map.79 = (bf16[2,928,128]{2,1,0:T(8,128)(2,1)}, bf16[2,928,128]{2,1,0:T(8,128)(2,1)}) custom-call(s32[3]{0:T(128)S(1)} %pad_add_fusion.pos_ref, bf16[8,464,128]{2,1,0:T(8,128)(2,1)S(1)} %all-to-all-done.2.rows_ref, bf16[928,464]{1,0:T(8,128)(2,1)S(1)} %copy-done), custom_call_target="tpu_custom_call" | custom-call | flops 440926208 | bytes 2761728 | tf_op jit(solution)/shard_map/pallas_call | solution.py:60
  51.6 2.0 %add_convert_fusion.1 = bf16[928,128]{1,0:T(8,128)(2,1)} fusion(bf16[928,128]{1,0:T(8,128)(2,1)} %collective-permute-done.4, bf16[928,128]{1,0:T(8,128)(2,1)} %collective-permute-done.3, f32[928,128]{1,0:T(8,128)S(1)} %get-tuple-element.42, bf16[928,128]{1,0:T(8,128)(2,1)} %collective-permute-done.2), kind=kLoop, calls=%fused_computation.1 | loop fusion | flops 831488 | bytes 1425408 | tf_op jit(solution)/shard_map/convert_element_type | solution.py:279
  53.5 7.3 %all-to-all-start.1 = ((bf16[4,232,128]{2,1,0:T(8,128)(2,1)}), bf16[4,232,128]{2,1,0:T(8,128)(2,1)S(1)}, u32[]{:S(2)}, u32[]{:S(2)}) async-start(bf16[4,232,128]{2,1,0:T(8,128)(2,1)} %bitcast.28), calls=%async_computation.1 | async-start | bytes 475136 | tf_op jit(solution)/shard_map/all_to_all | solution.py:198
  60.8 2.8 %shard_map.80 = (f32[928,128]{1,0:T(8,128)S(1)}, bf16[928,128]{1,0:T(8,128)(2,1)}, bf16[928,128]{1,0:T(8,128)(2,1)}, bf16[928,128]{1,0:T(8,128)(2,1)}) custom-call(s32[3]{0:T(128)S(1)} %pad_add_fusion.pos_ref, bf16[8,464,128]{2,1,0:T(8,128)(2,1)S(1)} %all-to-all-done.2.rows_ref, bf16[928,464]{1,0:T(8,128)(2,1)S(1)} %copy-done, ...), custom_call_target="tpu_custom_call" | custom-call | flops 440926208 | bytes 3949568 | tf_op jit(solution)/shard_map/pallas_call | solution.py:60
  64.4 1.2 collective-permute-start.14
  65.6 2.5 %collective-permute-start.15 = (bf16[928,128]{1,0:T(8,128)(2,1)}, bf16[928,128]{1,0:T(8,128)(2,1)}, u32[]{:S(2)}, u32[]{:S(2)}) collective-permute-start(bf16[928,128]{1,0:T(8,128)(2,1)} %get-tuple-element.60), channel_id=1, source_target_pairs={{0,16},{1,17},{2,18},{3,19},{4,20},{5,21},{6,22},{7,23},{8,24},{9,... | collective-permute-start | bytes 712712 | tf_op jit(solution)/shard_map/ppermute | solution.py:268
  68.0 1.2 collective-permute-start.16
  69.2 1.3 shard_map.81
  70.5 6.6 %all-to-all-start.3 = ((bf16[4,232,128]{2,1,0:T(8,128)(2,1)}), bf16[4,232,128]{2,1,0:T(8,128)(2,1)S(1)}, u32[]{:S(2)}, u32[]{:S(2)}) async-start(bf16[4,232,128]{2,1,0:T(8,128)(2,1)} %get-tuple-element.56), calls=%async_computation.3 | async-start | bytes 475136 | tf_op jit(solution)/shard_map/all_to_all | solution.py:198
  77.2 1.4 collective-permute-done.15
  78.6 2.1 %add_convert_fusion = bf16[928,128]{1,0:T(8,128)(2,1)} fusion(bf16[928,128]{1,0:T(8,128)(2,1)} %collective-permute-done.16, bf16[928,128]{1,0:T(8,128)(2,1)} %collective-permute-done.15, f32[928,128]{1,0:T(8,128)} %copy-done.5, bf16[928,128]{1,0:T(8,128)(2,1)} %collective-permute-done.14), kind=kLoop, calls=%fused_computation | loop fusion | flops 831488 | bytes 1425408 | tf_op jit(solution)/shard_map/convert_element_type | solution.py:279
  80.7 5.0 %all-to-all-done.3 = bf16[4,232,128]{2,1,0:T(8,128)(2,1)S(1)} async-done(((bf16[4,232,128]{2,1,0:T(8,128)(2,1)}), bf16[4,232,128]{2,1,0:T(8,128)(2,1)S(1)}, u32[]{:S(2)}, u32[]{:S(2)}) %all-to-all-start.3) | async-done | bytes 237600 | tf_op jit(solution)/shard_map/all_to_all | solution.py:198
  85.7 3.4 %all-to-all-start.5 = ((bf16[4,232,128]{2,1,0:T(8,128)(2,1)}), bf16[4,232,128]{2,1,0:T(8,128)(2,1)S(1)}, u32[]{:S(2)}, u32[]{:S(2)}) async-start(bf16[4,232,128]{2,1,0:T(8,128)(2,1)} %bitcast.29), calls=%async_computation.5 | async-start | bytes 475136 | tf_op jit(solution)/shard_map/all_to_all | solution.py:198
  89.5 2.0 %collective-permute-start.8 = (bf16[928,128]{1,0:T(8,128)(2,1)S(1)}, bf16[928,128]{1,0:T(8,128)(2,1)}, u32[]{:S(2)}, u32[]{:S(2)}) collective-permute-start(bf16[928,128]{1,0:T(8,128)(2,1)S(1)} %bitcast.22), channel_id=1, source_target_pairs={{0,16},{1,17},{2,18},{3,19},{4,20},{5,21},{6,22},{7,23},{8,24},{9,... | collective-permute-start | bytes 712712 | tf_op jit(solution)/shard_map/ppermute | solution.py:268
  92.0 4.9 %all-to-all-done.5.arrived_ref = bf16[4,232,128]{2,1,0:T(8,128)(2,1)S(1)} async-done(((bf16[4,232,128]{2,1,0:T(8,128)(2,1)}), bf16[4,232,128]{2,1,0:T(8,128)(2,1)S(1)}, u32[]{:S(2)}, u32[]{:S(2)}) %all-to-all-start.5) | async-done | bytes 237600 | tf_op jit(solution)/shard_map/all_to_all | solution.py:198
  96.9 1.3 shard_map.84
  98.3 3.4 %all-to-all-start.6 = ((bf16[4,232,128]{2,1,0:T(8,128)(2,1)}), bf16[4,232,128]{2,1,0:T(8,128)(2,1)S(1)}, u32[]{:S(2)}, u32[]{:S(2)}) async-start(bf16[4,232,128]{2,1,0:T(8,128)(2,1)} %shard_map.84), calls=%async_computation.6 | async-start | bytes 475136 | tf_op jit(solution)/shard_map/all_to_all | solution.py:198
  101.7 4.6 %collective-permute-start.10 = (bf16[928,128]{1,0:T(8,128)(2,1)S(1)}, bf16[928,128]{1,0:T(8,128)(2,1)S(1)}, u32[]{:S(2)}, u32[]{:S(2)}) collective-permute-start(bf16[928,128]{1,0:T(8,128)(2,1)S(1)} %bitcast.24), channel_id=1, source_target_pairs={{0,1},{1,0},{2,3},{3,2},{4,5},{5,4},{6,7},{7,6},{8,9},{9,8},{10,11... | collective-permute-start | bytes 712712 | tf_op jit(solution)/shard_map/ppermute | solution.py:264
  108.6 3.5 %shard_map.82 = (bf16[8,464,128]{2,1,0:T(8,128)(2,1)}, bf16[8,928,128]{2,1,0:T(8,128)(2,1)}) custom-call(s32[3]{0:T(128)S(1)} %pad_add_fusion.pos_ref, bf16[928,128]{1,0:T(8,128)(2,1)S(1)} %bitcast.25, bf16[928,128]{1,0:T(8,128)(2,1)} %collective-permute-done.7.refs_1_, bf16[928,128]{1,0:T(8,128)(2,1)} %collective-permute-done.8.refs_2_, ...), custom_call_target="tpu_custom_call" | custom-call | flops 881852416 | bytes 5612544 | tf_op jit(solution)/shard_map/pallas_call | solution.py:60
  112.2 3.6 %all-to-all-start.4 = ((bf16[8,464,128]{2,1,0:T(8,128)(2,1)}), bf16[8,464,128]{2,1,0:T(8,128)(2,1)S(1)}, u32[]{:S(2)}, u32[]{:S(2)}) async-start(bf16[8,464,128]{2,1,0:T(8,128)(2,1)} %get-tuple-element.58), calls=%async_computation.4 | async-start | bytes 1900544 | tf_op jit(solution)/shard_map/all_to_all | solution.py:198
  116.1 1.4 collective-permute-start.18
  117.5 1.4 collective-permute-start.17
  118.9 1.5 copy-done.1
  120.4 2.6 %shard_map.85 = bf16[928,464]{1,0:T(8,128)(2,1)} custom-call(s32[3]{0:T(128)S(1)} %pad_add_fusion.pos_ref, bf16[8,464,128]{2,1,0:T(8,128)(2,1)S(1)} %all-to-all-done.2.rows_ref, bf16[8,928,128]{2,1,0:T(8,128)(2,1)S(1)} %copy-done.1), custom_call_target="tpu_custom_call" | custom-call | flops 881852416 | bytes 3712000 | tf_op jit(solution)/shard_map/pallas_call | solution.py:60
  123.1 4.1 %collective-permute-start.20 = (bf16[928,128]{1,0:T(8,128)(2,1)S(1)}, bf16[928,128]{1,0:T(8,128)(2,1)S(1)}, u32[]{:S(2)}, u32[]{:S(2)}) collective-permute-start(bf16[928,128]{1,0:T(8,128)(2,1)S(1)} %bitcast.19), channel_id=1, source_target_pairs={{0,1},{1,0},{2,3},{3,2},{4,5},{5,4},{6,7},{7,6},{8,9},{9,8},{10,11... | collective-permute-start | bytes 712712 | tf_op jit(solution)/shard_map/ppermute | solution.py:264
  127.1 3.2 %collective-permute-start.23 = (bf16[928,128]{1,0:T(8,128)(2,1)S(1)}, bf16[928,128]{1,0:T(8,128)(2,1)S(1)}, u32[]{:S(2)}, u32[]{:S(2)}) collective-permute-start(bf16[928,128]{1,0:T(8,128)(2,1)S(1)} %collective-permute-done.19.refs_3_), channel_id=1, source_target_pairs={{0,1},{1,0},{2,3},{3,2},{4,5},{5,4},{6,7},{7,6},{8,9},{9,8},{10,11... | collective-permute-start | bytes 712712 | tf_op jit(solution)/shard_map/ppermute | solution.py:264
  132.2 2.9 %shard_map.86 = (bf16[8,464,128]{2,1,0:T(8,128)(2,1)}, bf16[8,928,128]{2,1,0:T(8,128)(2,1)}) custom-call(s32[3]{0:T(128)S(1)} %pad_add_fusion.pos_ref, bf16[928,128]{1,0:T(8,128)(2,1)S(1)} %bitcast.20, bf16[928,128]{1,0:T(8,128)(2,1)S(1)} %collective-permute-done.17.refs_1_, bf16[928,128]{1,0:T(8,128)(2,1)S(1)} %collective-permute-done.18.refs_2_, ...), custom_call_target="tpu_custom_call" | custom-call | flops 881852416 | bytes 5612544 | tf_op jit(solution)/shard_map/pallas_call | solution.py:60
  135.1 5.0 %all-to-all-start.7 = ((bf16[8,464,128]{2,1,0:T(8,128)(2,1)}), bf16[8,464,128]{2,1,0:T(8,128)(2,1)S(1)}, u32[]{:S(2)}, u32[]{:S(2)}) async-start(bf16[8,464,128]{2,1,0:T(8,128)(2,1)} %get-tuple-element.70), calls=%async_computation.7 | async-start | bytes 1900544 | tf_op jit(solution)/shard_map/all_to_all | solution.py:198
  140.1 1.5 copy-done.2
  141.6 2.7 %shard_map.88 = bf16[464,928]{1,0:T(8,128)(2,1)} custom-call(s32[3]{0:T(128)S(1)} %pad_add_fusion.pos_ref, bf16[8,464,128]{2,1,0:T(8,128)(2,1)S(1)} %all-to-all-done.rows_ref, bf16[8,928,128]{2,1,0:T(8,128)(2,1)S(1)} %copy-done.2), custom_call_target="tpu_custom_call" | custom-call | flops 881852416 | bytes 3712000 | tf_op jit(solution)/shard_map/pallas_call | solution.py:60
  144.3 1.3 shard_map.83
  145.6 8.4 %all-to-all-done.7.value_ref = bf16[8,464,128]{2,1,0:T(8,128)(2,1)S(1)} async-done(((bf16[8,464,128]{2,1,0:T(8,128)(2,1)}), bf16[8,464,128]{2,1,0:T(8,128)(2,1)S(1)}, u32[]{:S(2)}, u32[]{:S(2)}) %all-to-all-start.7) | async-done | bytes 950304 | tf_op jit(solution)/shard_map/all_to_all | solution.py:198
  154.0 1.3 shard_map.87
  (51 shorter events, 9.0 us)
Async XLA Ops:
  0.7 0.9 copy-start.6
  1.6 7.9 %copy-start.7 = (bf16[128,464]{0,1:T(8,128)(2,1)S(1)}, bf16[128,464]{0,1:T(8,128)(2,1)}, u32[]{:S(2)}) copy-start(bf16[128,464]{0,1:T(8,128)(2,1)} %param.7) | copy-start | bytes 356356
  3.2 20.0 %all-to-all-start = ((bf16[8,464,128]{2,1,0:T(8,128)(2,1)}), bf16[8,464,128]{2,1,0:T(8,128)(2,1)S(1)}, u32[]{:S(2)}, u32[]{:S(2)}) async-start(bf16[8,464,128]{2,1,0:T(8,128)(2,1)} %shard_map.76), calls=%async_computation | async-start | bytes 1900544 | tf_op jit(solution)/shard_map/all_to_all | solution.py:198
  9.5 3.3 %copy-start = (bf16[928,464]{1,0:T(8,128)(2,1)S(1)}, bf16[928,464]{1,0:T(8,128)(2,1)}, u32[]{:S(2)}) copy-start(bf16[928,464]{1,0:T(8,128)(2,1)} %weight_ref.3) | copy-start | bytes 2583556
  25.3 2.9 %collective-permute-start = (bf16[2,928,128]{2,1,0:T(8,128)(2,1)}, bf16[2,928,128]{2,1,0:T(8,128)(2,1)S(1)}, u32[]{:S(2)}, u32[]{:S(2)}) collective-permute-start(bf16[2,928,128]{2,1,0:T(8,128)(2,1)} %get-tuple-element.40), channel_id=1, source_target_pairs={{0,1},{1,0},{2,3},{3,2},{4,5},{5,4},{6,7},{7,6},{8,9},{9,8},{10,11... | collective-permute-start | bytes 1425416 | tf_op jit(solution)/shard_map/ppermute | solution.py:264
  26.5 2.4 %collective-permute-start.1 = (bf16[2,928,128]{2,1,0:T(8,128)(2,1)}, bf16[2,928,128]{2,1,0:T(8,128)(2,1)S(1)}, u32[]{:S(2)}, u32[]{:S(2)}) collective-permute-start(bf16[2,928,128]{2,1,0:T(8,128)(2,1)} %get-tuple-element.41), channel_id=1, source_target_pairs={{0,1},{1,0},{2,3},{3,2},{4,5},{5,4},{6,7},{7,6},{8,9},{9,8},{10,11... | collective-permute-start | bytes 1425416 | tf_op jit(solution)/shard_map/ppermute | solution.py:264
  31.0 17.5 %all-to-all-start.2 = ((bf16[8,464,128]{2,1,0:T(8,128)(2,1)}), bf16[8,464,128]{2,1,0:T(8,128)(2,1)S(1)}, u32[]{:S(2)}, u32[]{:S(2)}) async-start(bf16[8,464,128]{2,1,0:T(8,128)(2,1)} %shard_map.75), calls=%async_computation.2 | async-start | bytes 1900544 | tf_op jit(solution)/shard_map/all_to_all | solution.py:198
  34.6 17.0 %collective-permute-start.2 = (bf16[928,128]{1,0:T(8,128)(2,1)}, bf16[928,128]{1,0:T(8,128)(2,1)}, u32[]{:S(2)}, u32[]{:S(2)}) collective-permute-start(bf16[928,128]{1,0:T(8,128)(2,1)} %get-tuple-element.43), channel_id=1, source_target_pairs={{0,8},{1,9},{2,10},{3,11},{4,12},{5,13},{6,14},{7,15},{8,16},{9,17... | collective-permute-start | bytes 712712 | tf_op jit(solution)/shard_map/ppermute | solution.py:268
  35.8 15.7 %collective-permute-start.3 = (bf16[928,128]{1,0:T(8,128)(2,1)}, bf16[928,128]{1,0:T(8,128)(2,1)}, u32[]{:S(2)}, u32[]{:S(2)}) collective-permute-start(bf16[928,128]{1,0:T(8,128)(2,1)} %get-tuple-element.44), channel_id=1, source_target_pairs={{0,16},{1,17},{2,18},{3,19},{4,20},{5,21},{6,22},{7,23},{8,24},{9,... | collective-permute-start | bytes 712712 | tf_op jit(solution)/shard_map/ppermute | solution.py:268
  38.3 13.3 %collective-permute-start.4 = (bf16[928,128]{1,0:T(8,128)(2,1)}, bf16[928,128]{1,0:T(8,128)(2,1)}, u32[]{:S(2)}, u32[]{:S(2)}) collective-permute-start(bf16[928,128]{1,0:T(8,128)(2,1)} %get-tuple-element.45), channel_id=1, source_target_pairs={{0,24},{1,25},{2,26},{3,27},{4,28},{5,29},{6,30},{7,31},{8,0},{9,1... | collective-permute-start | bytes 712712 | tf_op jit(solution)/shard_map/ppermute | solution.py:268
  50.7 10.1 %collective-permute-start.5 = (bf16[2,928,128]{2,1,0:T(8,128)(2,1)}, bf16[2,928,128]{2,1,0:T(8,128)(2,1)}, u32[]{:S(2)}, u32[]{:S(2)}) collective-permute-start(bf16[2,928,128]{2,1,0:T(8,128)(2,1)} %get-tuple-element.52), channel_id=1, source_target_pairs={{0,1},{1,0},{2,3},{3,2},{4,5},{5,4},{6,7},{7,6},{8,9},{9,8},{10,11... | collective-permute-start | bytes 1425416 | tf_op jit(solution)/shard_map/ppermute | solution.py:264
  51.5 9.4 %collective-permute-start.6 = (bf16[2,928,128]{2,1,0:T(8,128)(2,1)}, bf16[2,928,128]{2,1,0:T(8,128)(2,1)}, u32[]{:S(2)}, u32[]{:S(2)}) collective-permute-start(bf16[2,928,128]{2,1,0:T(8,128)(2,1)} %get-tuple-element.53), channel_id=1, source_target_pairs={{0,1},{1,0},{2,3},{3,2},{4,5},{5,4},{6,7},{7,6},{8,9},{9,8},{10,11... | collective-permute-start | bytes 1425416 | tf_op jit(solution)/shard_map/ppermute | solution.py:264
  53.5 15.7 %all-to-all-start.1 = ((bf16[4,232,128]{2,1,0:T(8,128)(2,1)}), bf16[4,232,128]{2,1,0:T(8,128)(2,1)S(1)}, u32[]{:S(2)}, u32[]{:S(2)}) async-start(bf16[4,232,128]{2,1,0:T(8,128)(2,1)} %bitcast.28), calls=%async_computation.1 | async-start | bytes 475136 | tf_op jit(solution)/shard_map/all_to_all | solution.py:198
  63.6 0.8 copy-start.5
  64.4 44.3 %copy-start.4 = (bf16[928,464]{0,1:T(8,128)(2,1)S(1)}, bf16[928,464]{0,1:T(8,128)(2,1)}, u32[]{:S(2)}) copy-start(bf16[928,464]{0,1:T(8,128)(2,1)} %copy.9) | copy-start | bytes 2583556
  64.4 12.8 %collective-permute-start.14 = (bf16[928,128]{1,0:T(8,128)(2,1)}, bf16[928,128]{1,0:T(8,128)(2,1)}, u32[]{:S(2)}, u32[]{:S(2)}) collective-permute-start(bf16[928,128]{1,0:T(8,128)(2,1)} %get-tuple-element.59), channel_id=1, source_target_pairs={{0,8},{1,9},{2,10},{3,11},{4,12},{5,13},{6,14},{7,15},{8,16},{9,17... | collective-permute-start | bytes 712712 | tf_op jit(solution)/shard_map/ppermute | solution.py:268
  65.6 13.0 %collective-permute-start.15 = (bf16[928,128]{1,0:T(8,128)(2,1)}, bf16[928,128]{1,0:T(8,128)(2,1)}, u32[]{:S(2)}, u32[]{:S(2)}) collective-permute-start(bf16[928,128]{1,0:T(8,128)(2,1)} %get-tuple-element.60), channel_id=1, source_target_pairs={{0,16},{1,17},{2,18},{3,19},{4,20},{5,21},{6,22},{7,23},{8,24},{9,... | collective-permute-start | bytes 712712 | tf_op jit(solution)/shard_map/ppermute | solution.py:268
  68.0 10.6 %collective-permute-start.16 = (bf16[928,128]{1,0:T(8,128)(2,1)}, bf16[928,128]{1,0:T(8,128)(2,1)}, u32[]{:S(2)}, u32[]{:S(2)}) collective-permute-start(bf16[928,128]{1,0:T(8,128)(2,1)} %get-tuple-element.61), channel_id=1, source_target_pairs={{0,24},{1,25},{2,26},{3,27},{4,28},{5,29},{6,30},{7,31},{8,0},{9,1... | collective-permute-start | bytes 712712 | tf_op jit(solution)/shard_map/ppermute | solution.py:268
  70.5 15.2 %all-to-all-start.3 = ((bf16[4,232,128]{2,1,0:T(8,128)(2,1)}), bf16[4,232,128]{2,1,0:T(8,128)(2,1)S(1)}, u32[]{:S(2)}, u32[]{:S(2)}) async-start(bf16[4,232,128]{2,1,0:T(8,128)(2,1)} %get-tuple-element.56), calls=%async_computation.3 | async-start | bytes 475136 | tf_op jit(solution)/shard_map/all_to_all | solution.py:198
  85.7 11.2 %all-to-all-start.5 = ((bf16[4,232,128]{2,1,0:T(8,128)(2,1)}), bf16[4,232,128]{2,1,0:T(8,128)(2,1)S(1)}, u32[]{:S(2)}, u32[]{:S(2)}) async-start(bf16[4,232,128]{2,1,0:T(8,128)(2,1)} %bitcast.29), calls=%async_computation.5 | async-start | bytes 475136 | tf_op jit(solution)/shard_map/all_to_all | solution.py:198
  89.1 17.1 %collective-permute-start.9 = (bf16[928,128]{1,0:T(8,128)(2,1)S(1)}, bf16[928,128]{1,0:T(8,128)(2,1)}, u32[]{:S(2)}, u32[]{:S(2)}) collective-permute-start(bf16[928,128]{1,0:T(8,128)(2,1)S(1)} %bitcast.21), channel_id=1, source_target_pairs={{0,8},{1,9},{2,10},{3,11},{4,12},{5,13},{6,14},{7,15},{8,16},{9,17... | collective-permute-start | bytes 712712 | tf_op jit(solution)/shard_map/ppermute | solution.py:268
  89.5 16.9 %collective-permute-start.8 = (bf16[928,128]{1,0:T(8,128)(2,1)S(1)}, bf16[928,128]{1,0:T(8,128)(2,1)}, u32[]{:S(2)}, u32[]{:S(2)}) collective-permute-start(bf16[928,128]{1,0:T(8,128)(2,1)S(1)} %bitcast.22), channel_id=1, source_target_pairs={{0,16},{1,17},{2,18},{3,19},{4,20},{5,21},{6,22},{7,23},{8,24},{9,... | collective-permute-start | bytes 712712 | tf_op jit(solution)/shard_map/ppermute | solution.py:268
  91.5 15.3 %collective-permute-start.7 = (bf16[928,128]{1,0:T(8,128)(2,1)S(1)}, bf16[928,128]{1,0:T(8,128)(2,1)}, u32[]{:S(2)}, u32[]{:S(2)}) collective-permute-start(bf16[928,128]{1,0:T(8,128)(2,1)S(1)} %bitcast.23), channel_id=1, source_target_pairs={{0,24},{1,25},{2,26},{3,27},{4,28},{5,29},{6,30},{7,31},{8,0},{9,1... | collective-permute-start | bytes 712712 | tf_op jit(solution)/shard_map/ppermute | solution.py:268
  98.3 13.9 %all-to-all-start.6 = ((bf16[4,232,128]{2,1,0:T(8,128)(2,1)}), bf16[4,232,128]{2,1,0:T(8,128)(2,1)S(1)}, u32[]{:S(2)}, u32[]{:S(2)}) async-start(bf16[4,232,128]{2,1,0:T(8,128)(2,1)} %shard_map.84), calls=%async_computation.6 | async-start | bytes 475136 | tf_op jit(solution)/shard_map/all_to_all | solution.py:198
  101.7 5.7 %collective-permute-start.10 = (bf16[928,128]{1,0:T(8,128)(2,1)S(1)}, bf16[928,128]{1,0:T(8,128)(2,1)S(1)}, u32[]{:S(2)}, u32[]{:S(2)}) collective-permute-start(bf16[928,128]{1,0:T(8,128)(2,1)S(1)} %bitcast.24), channel_id=1, source_target_pairs={{0,1},{1,0},{2,3},{3,2},{4,5},{5,4},{6,7},{7,6},{8,9},{9,8},{10,11... | collective-permute-start | bytes 712712 | tf_op jit(solution)/shard_map/ppermute | solution.py:264
  106.2 1.7 %collective-permute-start.13 = (bf16[928,128]{1,0:T(8,128)(2,1)}, bf16[928,128]{1,0:T(8,128)(2,1)S(1)}, u32[]{:S(2)}, u32[]{:S(2)}) collective-permute-start(bf16[928,128]{1,0:T(8,128)(2,1)} %collective-permute-done.9.refs_3_), channel_id=1, source_target_pairs={{0,1},{1,0},{2,3},{3,2},{4,5},{5,4},{6,7},{7,6},{8,9},{9,8},{10,11... | collective-permute-start | bytes 712712 | tf_op jit(solution)/shard_map/ppermute | solution.py:264
  106.4 1.9 %collective-permute-start.12 = (bf16[928,128]{1,0:T(8,128)(2,1)}, bf16[928,128]{1,0:T(8,128)(2,1)S(1)}, u32[]{:S(2)}, u32[]{:S(2)}) collective-permute-start(bf16[928,128]{1,0:T(8,128)(2,1)} %collective-permute-done.8.refs_2_), channel_id=1, source_target_pairs={{0,1},{1,0},{2,3},{3,2},{4,5},{5,4},{6,7},{7,6},{8,9},{9,8},{10,11... | collective-permute-start | bytes 712712 | tf_op jit(solution)/shard_map/ppermute | solution.py:264
  106.8 1.9 %collective-permute-start.11 = (bf16[928,128]{1,0:T(8,128)(2,1)}, bf16[928,128]{1,0:T(8,128)(2,1)S(1)}, u32[]{:S(2)}, u32[]{:S(2)}) collective-permute-start(bf16[928,128]{1,0:T(8,128)(2,1)} %collective-permute-done.7.refs_1_), channel_id=1, source_target_pairs={{0,1},{1,0},{2,3},{3,2},{4,5},{5,4},{6,7},{7,6},{8,9},{9,8},{10,11... | collective-permute-start | bytes 712712 | tf_op jit(solution)/shard_map/ppermute | solution.py:264
  112.2 22.9 %all-to-all-start.4 = ((bf16[8,464,128]{2,1,0:T(8,128)(2,1)}), bf16[8,464,128]{2,1,0:T(8,128)(2,1)S(1)}, u32[]{:S(2)}, u32[]{:S(2)}) async-start(bf16[8,464,128]{2,1,0:T(8,128)(2,1)} %get-tuple-element.58), calls=%async_computation.4 | async-start | bytes 1900544 | tf_op jit(solution)/shard_map/all_to_all | solution.py:198
  115.8 11.4 %collective-permute-start.19 = (bf16[928,128]{1,0:T(8,128)(2,1)S(1)}, bf16[928,128]{1,0:T(8,128)(2,1)S(1)}, u32[]{:S(2)}, u32[]{:S(2)}) collective-permute-start(bf16[928,128]{1,0:T(8,128)(2,1)S(1)} %bitcast.16), channel_id=1, source_target_pairs={{0,8},{1,9},{2,10},{3,11},{4,12},{5,13},{6,14},{7,15},{8,16},{9,17... | collective-permute-start | bytes 712712 | tf_op jit(solution)/shard_map/ppermute | solution.py:268
  116.1 14.2 %collective-permute-start.18 = (bf16[928,128]{1,0:T(8,128)(2,1)S(1)}, bf16[928,128]{1,0:T(8,128)(2,1)S(1)}, u32[]{:S(2)}, u32[]{:S(2)}) collective-permute-start(bf16[928,128]{1,0:T(8,128)(2,1)S(1)} %bitcast.17), channel_id=1, source_target_pairs={{0,16},{1,17},{2,18},{3,19},{4,20},{5,21},{6,22},{7,23},{8,24},{9,... | collective-permute-start | bytes 712712 | tf_op jit(solution)/shard_map/ppermute | solution.py:268
  117.5 12.8 %collective-permute-start.17 = (bf16[928,128]{1,0:T(8,128)(2,1)S(1)}, bf16[928,128]{1,0:T(8,128)(2,1)S(1)}, u32[]{:S(2)}, u32[]{:S(2)}) collective-permute-start(bf16[928,128]{1,0:T(8,128)(2,1)S(1)} %bitcast.18), channel_id=1, source_target_pairs={{0,24},{1,25},{2,26},{3,27},{4,28},{5,29},{6,30},{7,31},{8,0},{9,1... | collective-permute-start | bytes 712712 | tf_op jit(solution)/shard_map/ppermute | solution.py:268
  118.9 1.5 copy-start.1
  120.4 11.7 %copy-start.3 = (bf16[464,928]{1,0:T(8,128)(2,1)S(1)}, bf16[464,928]{1,0:T(8,128)(2,1)}, u32[]{:S(2)}) copy-start(bf16[464,928]{1,0:T(8,128)(2,1)} %refs_8_.1) | copy-start | bytes 2583556
  123.1 7.9 %collective-permute-start.20 = (bf16[928,128]{1,0:T(8,128)(2,1)S(1)}, bf16[928,128]{1,0:T(8,128)(2,1)S(1)}, u32[]{:S(2)}, u32[]{:S(2)}) collective-permute-start(bf16[928,128]{1,0:T(8,128)(2,1)S(1)} %bitcast.19), channel_id=1, source_target_pairs={{0,1},{1,0},{2,3},{3,2},{4,5},{5,4},{6,7},{7,6},{8,9},{9,8},{10,11... | collective-permute-start | bytes 712712 | tf_op jit(solution)/shard_map/ppermute | solution.py:264
  127.1 4.3 %collective-permute-start.23 = (bf16[928,128]{1,0:T(8,128)(2,1)S(1)}, bf16[928,128]{1,0:T(8,128)(2,1)S(1)}, u32[]{:S(2)}, u32[]{:S(2)}) collective-permute-start(bf16[928,128]{1,0:T(8,128)(2,1)S(1)} %collective-permute-done.19.refs_3_), channel_id=1, source_target_pairs={{0,1},{1,0},{2,3},{3,2},{4,5},{5,4},{6,7},{7,6},{8,9},{9,8},{10,11... | collective-permute-start | bytes 712712 | tf_op jit(solution)/shard_map/ppermute | solution.py:264
  130.3 1.5 collective-permute-start.22
  130.3 1.8 %collective-permute-start.21 = (bf16[928,128]{1,0:T(8,128)(2,1)S(1)}, bf16[928,128]{1,0:T(8,128)(2,1)S(1)}, u32[]{:S(2)}, u32[]{:S(2)}) collective-permute-start(bf16[928,128]{1,0:T(8,128)(2,1)S(1)} %collective-permute-done.17.refs_1_), channel_id=1, source_target_pairs={{0,1},{1,0},{2,3},{3,2},{4,5},{5,4},{6,7},{7,6},{8,9},{9,8},{10,11... | collective-permute-start | bytes 712712 | tf_op jit(solution)/shard_map/ppermute | solution.py:264
  135.1 18.9 %all-to-all-start.7 = ((bf16[8,464,128]{2,1,0:T(8,128)(2,1)}), bf16[8,464,128]{2,1,0:T(8,128)(2,1)S(1)}, u32[]{:S(2)}, u32[]{:S(2)}) async-start(bf16[8,464,128]{2,1,0:T(8,128)(2,1)} %get-tuple-element.70), calls=%async_computation.7 | async-start | bytes 1900544 | tf_op jit(solution)/shard_map/all_to_all | solution.py:198
  140.1 1.5 copy-start.2

commit v8 on v1

v8 whole, which is shorter than its diff:
```python
import math

import jax
import jax.numpy as jnp
from jax import lax
from jax.experimental import pallas as pl
from jax.experimental.pallas import tpu as pltpu
from jax.sharding import PartitionSpec as P

BF = jnp.bfloat16
F32 = jnp.float32
GRP = 8
X, Z, C = 4, 4, 2
LANES = 128
TILE = 16


def rep_index(x, z, c):
    return (x * Z + z) * C + c


XZ_GROUPS = [[rep_index(x, z, c) for x in range(X) for z in range(Z)] for c in range(C)]
CORE_PAIRS = [
    (rep_index(x, z, c), rep_index(x, z, 1 - c))
    for x in range(X)
    for z in range(Z)
    for c in range(C)
]
PLAIN = ((1,), (0,))
LAST = ((1,), (1,))


def slope(hidden):
    normal_cdf = 0.5 * (1.0 + lax.erf(hidden * (1.0 / math.sqrt(2.0))))
    density = jnp.exp(-0.5 * hidden * hidden) * (1.0 / math.sqrt(2.0 * math.pi))
    return normal_cdf + hidden * density


def dot(left, right, dims):
    return lax.dot_general(left, right, (dims, ((), ())), preferred_element_type=F32)


def shaped(shape, dtype=BF):
    return jax.ShapeDtypeStruct(shape, dtype)


def room(shape, *copies):
    return [pltpu.VMEM(shape, BF), pltpu.SemaphoreType.DMA(copies)]


def kernel_call(kernel, outs, flops, core, operands, scratch=(), far=(), alias=None):
    moved = sum(math.prod(o.shape) * o.dtype.itemsize for o in [*operands, *outs])
    vmem = pl.BlockSpec(memory_space=pltpu.VMEM)
    hbm = pl.BlockSpec(memory_space=pltpu.HBM)
    return pl.pallas_call(
        kernel,
        out_shape=[pltpu.HBM(o.shape, o.dtype) if i in far else o for i, o in enumerate(outs)],
        in_specs=[pl.BlockSpec(memory_space=pltpu.SMEM)]
        + [hbm if i == alias else vmem for i in range(len(operands))],
        out_specs=[hbm if i in far else vmem for i in range(len(outs))],
        scratch_shapes=scratch,
        input_output_aliases={} if alias is None else {alias + 1: 0},
        compiler_params=pltpu.CompilerParams(vmem_limit_bytes=24 * 1024 * 1024),
        cost_estimate=pl.CostEstimate(flops=flops, bytes_accessed=moved, transcendentals=0),
    )(core, *operands)


def start(copies, source, target, sem):
    copies.append(pltpu.make_async_copy(source, target, sem))
    copies[-1].start()


def finish(copies):
    for copy in copies:
        copy.wait()


def half_of(ref, half, here):
    return jnp.concatenate([ref[half * X + k, here] for k in range(X)], axis=1)


def block(value, k):
    return value[:, k * LANES : (k + 1) * LANES]


def many(core, first, second):
    rows = first.shape[0]

    def kernel(core_ref, first_ref, second_ref, out_ref, sems):
        copies = []
        for index in range(GRP):
            for part, ref in enumerate((first_ref, second_ref)):
                target = out_ref.at[index, pl.ds(part * rows, rows)]
                start(copies, ref, target, sems.at[index, part])
        finish(copies)

    outs = [shaped((GRP, 2 * rows, LANES))]
    scratch = [pltpu.SemaphoreType.DMA((GRP, 2))]
    return kernel_call(kernel, outs, 0, core, [first, second], scratch, (0,))[0]


def other_half(core, rows, here, weight):
    depth, width = weight.shape

    def kernel(core_ref, rows_ref, weight_ref, out_ref, held_ref, sems):
        rows = half_of(rows_ref, 1 - core_ref[0], here)
        copies = []
        for pair in range(X // 2):
            two = rows[:, pair * 2 * LANES : (pair + 1) * 2 * LANES]
            product = dot(weight_ref[...], two, PLAIN).astype(BF)
            for i in range(2):
                k = pair * 2 + i
                held_ref[k] = block(product, i)
                start(copies, held_ref.at[k], out_ref.at[k], sems.at[k])
        finish(copies)

    shape = (X, depth, LANES)
    flops = 2 * depth * width * X * LANES
    return kernel_call(kernel, [shaped(shape)], flops, core, [rows, weight], room(shape, X), (0,))[0]


def own_half(core, rows, here, weight, arrived, part, chunk, before=None):
    depth, width = weight.shape

    def kernel(core_ref, rows_ref, weight_ref, arrived_ref, *refs):
        out_ref, held_ref, sems = refs[-3:]
        rows = half_of(rows_ref, core_ref[0], here)
        copies = []
        for pair in range(X // 2):
            two = rows[:, pair * 2 * LANES : (pair + 1) * 2 * LANES]
            product = dot(weight_ref[...], two, PLAIN)
            for i in range(2):
                k = pair * 2 + i
                total = block(product, i) + arrived_ref[k].astype(F32)
                for z in range(Z):
                    index, lower = k * Z + z, z * chunk
                    count = min(chunk, depth - lower)
                    held_ref[index, :count] = total[lower : lower + count].astype(BF)
                    if count < chunk:
                        held_ref[index, count:] = jnp.zeros((chunk - count, LANES), BF)
                    start(copies, held_ref.at[index], out_ref.at[index, part], sems.at[index])
        finish(copies)

    outs = [shaped((X * Z, 2, chunk, LANES))]
    flops = 2 * depth * width * X * LANES
    operands = [rows, weight, arrived] + ([] if before is None else [before])
    scratch = room((X * Z, chunk, LANES), X * Z)
    alias = None if before is None else 3
    return kernel_call(kernel, outs, flops, core, operands, scratch, (0,), alias)[0]


def middle(core, arrived):
    count, _, chunk, _ = arrived.shape

    def kernel(core_ref, arrived_ref, out_ref, held_ref, sems):
        hidden, upward = arrived_ref[0, 0].astype(F32), arrived_ref[0, 1].astype(F32)
        for index in range(1, count):
            hidden = hidden + arrived_ref[index, 0].astype(F32)
            upward = upward + arrived_ref[index, 1].astype(F32)
        cdf = 0.5 * (1.0 + lax.erf(hidden * (1.0 / math.sqrt(2.0))))
        held_ref[0] = (hidden * cdf).astype(BF)
        held_ref[1] = (upward * slope(hidden)).astype(BF)
        copies = []
        for index in range(count):
            start(copies, held_ref, out_ref.at[index], sems.at[index])
        finish(copies)

    outs = [shaped(arrived.shape)]
    scratch = room(arrived.shape[1:], count)
    return kernel_call(kernel, outs, arrived.size, core, [arrived], scratch, (0,))[0]


def gathered(ref, part, wide_ref):
    depth, chunk = wide_ref.shape[0], ref.shape[2]
    for k in range(X):
        for z in range(Z):
            lower = z * chunk
            count = min(chunk, depth - lower)
            wide_ref[lower : lower + count, k * LANES : (k + 1) * LANES] = ref[k * Z + z, part, :count]
    return wide_ref[...]


def back_products(core, chunks, own, weights, before=None):
    width, depth = weights[0].shape

    def kernel(core_ref, chunks_ref, first_ref, second_ref, *refs):
        out_ref, kept_ref, wide_ref, held_ref, sems, kept_sem = refs[-6:]
        copies = []
        start(copies, chunks_ref, kept_ref, kept_sem)
        half = core_ref[0] if own else 1 - core_ref[0]
        for part, weight_ref in enumerate((first_ref, second_ref)):
            product = dot(weight_ref[...], gathered(chunks_ref, part, wide_ref), PLAIN).astype(BF)
            for k in range(X):
                held_ref[part, k] = block(product, k)
                target = out_ref.at[half * X + k, pl.ds(part * width, width)]
                start(copies, held_ref.at[part, k], target, sems.at[part, k])
        finish(copies)

    outs = [shaped((GRP, 2 * width, LANES)), shaped(chunks.shape)]
    flops = 4 * depth * width * X * LANES
    scratch = [pltpu.VMEM((depth, X * LANES), BF)] + room((2, X, width, LANES), 2, X)
    scratch += [pltpu.SemaphoreType.DMA]
    operands = [chunks, *weights] + ([] if before is None else [before])
    alias = None if before is None else 3
    return kernel_call(kernel, outs, flops, core, operands, scratch, (0, 1), alias)


def weight_grad(core, factor, rows, here, own, other, part, depth, rows_first):
    width = here.stop - here.start

    def kernel(core_ref, rows_ref, own_ref, other_ref, out_ref, wide_ref):
        total = None
        for ref, half in ((own_ref, core_ref[0]), (other_ref, 1 - core_ref[0])):
            pair = half_of(rows_ref, half, here), gathered(ref, part, wide_ref)
            term = dot(*(pair if rows_first else pair[::-1]), LAST)
            total = term if total is None else total + term
        out_ref[...] = (factor * total).astype(BF)

    outs = [shaped((width, depth) if rows_first else (depth, width))]
    flops = 4 * depth * width * X * LANES
    scratch = [pltpu.VMEM((depth, X * LANES), BF)]
    return kernel_call(kernel, outs, flops, core, [rows, own, other], scratch)[0]


def added(core, value):
    rows = value.shape[1] // 2

    def kernel(core_ref, value_ref, *outs):
        for part, out_ref in enumerate(outs):
            here = slice(part * rows, (part + 1) * rows)
            total = value_ref[0, here].astype(F32)
            for index in range(1, value.shape[0]):
                total = total + value_ref[index, here].astype(F32)
            out_ref[...] = total.astype(BF)

    return kernel_call(kernel, [shaped((rows, LANES))] * 2, value.size, core, [value])


def over_grp(value):
    return lax.all_to_all(value, "grp", 0, 0)


def over_xz(value):
    return lax.all_to_all(value, "rep", 0, 0, axis_index_groups=XZ_GROUPS)


def swap_cores(value):
    return lax.ppermute(value, "rep", CORE_PAIRS)


def body(tokens, first_weight, second_weight, cotangent):
    factor = float(GRP * tokens.shape[0]) ** (-0.5)
    width, depth = first_weight.shape
    chunk = -(-depth // (Z * TILE)) * TILE
    core = (lax.axis_index("rep") & 1).astype(jnp.int32).reshape(1)
    tok, cot = slice(0, width), slice(width, 2 * width)

    rows = over_grp(many(core, tokens.T, cotangent.T))
    first_turned, second_turned, rows = lax.optimization_barrier(
        (first_weight.T, second_weight.T, rows)
    )
    sent = other_half(core, rows, tok, first_turned), other_half(core, rows, cot, second_weight)
    sent = [swap_cores(part) for part in sent]
    sums = own_half(core, rows, tok, first_turned, sent[0], 0, chunk)
    sums = own_half(core, rows, cot, second_weight, sent[1], 1, chunk, sums)

    own = over_xz(middle(core, over_xz(sums)))
    other = swap_cores(own)
    weights = [second_turned, first_weight]
    outs, own = back_products(core, own, True, weights)
    outs, other = back_products(core, other, False, weights, outs)
    out, back = added(core, over_grp(outs))
    first_grad = weight_grad(core, factor, rows, tok, own, other, 1, depth, True)
    second_grad = weight_grad(core, factor, rows, cot, own, other, 0, depth, False)
    return (out.T, back.T, first_grad, second_grad)


def solution(mesh):
    in_specs = (P("grp", "rep"), P("rep", "grp"), P("grp", "rep"), P("grp", "rep"))
    out_specs = (P("grp", "rep"), P("grp", "rep"), P("rep", "grp"), P("grp", "rep"))
    return jax.shard_map(body, mesh=mesh, in_specs=in_specs, out_specs=out_specs, check_vma=False)
```

time: 203 us -> 196 us (0.966)
  blocking collectives: 146 us -> 89.8 us
  starting transfers between devices: 4.5 us -> 34 us
  waiting for transfers between devices: 17.9 us -> 39.8 us
  Pallas kernels: 0 us -> 21.4 us
  other arithmetic: 11.2 us -> 0 us
  matrix products: 10.7 us -> 0 us
  local copies, waits for them, and re-layouts: 12 us -> 9.75 us
    all_to_all x7 -> x2, blocking collectives: 146 us -> 89.8 us  [over_xz(): return lax.all_to_all(value, 'rep', 0, 0, axis_index_groups=XZ_GROUPS)]
    pallas_call x0 -> x11, Pallas kernels: none -> 21.4 us  [kernel_call(): pl.pallas_call(kernel, out_shape=[pltpu.HBM(o.shape, o.dtype) if i in far...]
    all_to_all x1 -> x2, starting transfers between devices: 4.5 us -> 24.4 us  [over_grp(): return lax.all_to_all(value, 'grp', 0, 0)]
    all_to_all x1 -> x2, waiting for transfers between devices: 17.9 us -> 37.5 us  [over_grp(): return lax.all_to_all(value, 'grp', 0, 0)]
    dot_general x6 -> x0, matrix products: 10.7 us -> none  [dot(): lax.dot_general(left, right, (dims, ((), ())), preferred_element_type=F32)]
    ppermute x0 -> x3, starting transfers between devices: none -> 9.56 us  [swap_cores(): return lax.ppermute(value, 'rep', CORE_PAIRS)]
    reduce_sum x4 -> x0, other arithmetic: 9.19 us -> none  [scatter_sum(): return jnp.sum(exchange(value.astype(BF), groups, axis).astype(F32), axis=0)]
    unnamed x16 -> x20, local copies, waits for them, and re-layouts: 1.81 us -> 9.75 us
  transfers between devices with their start and end apart: 1 -> 5, of which waited for: 1 -> 5; matrix products, arithmetic and copies ran while one was open for 2% -> 2% of each run, Pallas kernels for 0% -> 5%
where the time goes in v8:
time: 196 us
  blocking collectives  89.8 us (46%)
  waiting for transfers between devices  39.8 us (20%)
  starting transfers between devices  34 us (17%)
  Pallas kernels  21.4 us (11%)
  local copies, waits for them, and re-layouts  9.75 us (5%)
    all_to_all x2, blocking collectives, over_xz(): return lax.all_to_all(value, 'rep', 0, 0, axis_index_groups=XZ_GROUPS)  89.8 us
    all_to_all x2, waiting for transfers between devices, over_grp(): return lax.all_to_all(value, 'grp', 0, 0)  37.5 us
    all_to_all x2, starting transfers between devices, over_grp(): return lax.all_to_all(value, 'grp', 0, 0)  24.4 us
    pallas_call x11, Pallas kernels, kernel_call(): pl.pallas_call(kernel, out_shape=[pltpu.HBM(o.shape, o.dtype) if i in far...  21.4 us
    unnamed x20, local copies, waits for them, and re-layouts  9.75 us
    ppermute x3, starting transfers between devices, swap_cores(): return lax.ppermute(value, 'rep', CORE_PAIRS)  9.56 us
  transfers between devices with their start and end apart: 5, of which 5 were waited for; matrix products, arithmetic and copies ran while one was open for 2% of the time, Pallas kernels for 5%

profile of v8, /device:TPU:1, one launch (start us, length us, event | category | flops | bytes accessed | tf_op | source)
XLA Modules:
  0.0 195.6 jit_solution(10927588525372257183)
XLA Ops:
  0.6 0.0 copy-start.7
  0.6 0.9 copy-done.7
  1.5 0.0 copy-start.8
  1.5 0.9 copy-done.8
  2.4 1.4 shard_map.75
  3.9 0.0 copy-start
  3.9 6.5 %all-to-all-start = ((bf16[8,928,128]{2,1,0:T(8,128)(2,1)}), bf16[8,928,128]{2,1,0:T(8,128)(2,1)S(1)}, u32[]{:S(2)}, u32[]{:S(2)}) async-start(bf16[8,928,128]{2,1,0:T(8,128)(2,1)} %shard_map.75), calls=%async_computation | async-start | bytes 3801088 | tf_op jit(solution)/shard_map/all_to_all | solution.py:240
  10.4 2.2 %copy.10 = bf16[464,928]{0,1:T(8,128)(2,1)} copy(bf16[464,928]{1,0:T(8,128)(2,1)} %second_ref.3) | data formatting | bytes 1722368 | tf_op args[1]
  12.6 0.0 copy-done
  12.6 1.4 copy.11
  14.1 20.4 %all-to-all-done.rows_ref = bf16[8,928,128]{2,1,0:T(8,128)(2,1)S(1)} async-done(((bf16[8,928,128]{2,1,0:T(8,128)(2,1)}), bf16[8,928,128]{2,1,0:T(8,128)(2,1)S(1)}, u32[]{:S(2)}, u32[]{:S(2)}) %all-to-all-start) | async-done | bytes 1900576 | tf_op jit(solution)/shard_map/all_to_all | solution.py:240
  34.5 0.0 copy-start.3
  34.5 1.2 copy-done.3
  35.6 1.6 shard_map.77
  37.3 0.0 copy-start.4
  37.3 0.9 collective-permute-start.1
  38.2 1.6 shard_map.76
  39.9 0.1 collective-permute-start
  40.0 0.6 collective-permute-done.1.arrived_ref
  40.6 0.0 copy-done.4
  40.6 1.7 shard_map.78.refs_0_
  42.3 0.4 collective-permute-done.arrived_ref
  42.7 1.7 shard_map.79
  44.4 49.4 %all_to_all.20.arrived_ref = bf16[16,2,240,128]{3,2,1,0:T(8,128)(2,1)S(1)} all-to-all(bf16[16,2,240,128]{3,2,1,0:T(8,128)(2,1)} %shard_map.79), channel_id=1, replica_groups={{0,2,4,6,8,10,12,14,16,18,20,22,24,26,28,30},{1,3,5,7,9,11,13,15,17,19,..., dimensions={0} | all-to-all | bytes 3932160 | tf_op jit(solution)/shard_map/all_to_all | solution.py:244
  93.8 1.7 shard_map.80
  95.5 0.0 copy-start.1
  95.6 0.0 copy-start.2
  95.6 40.4 %all_to_all.21.chunks_ref = bf16[16,2,240,128]{3,2,1,0:T(8,128)(2,1)S(1)} all-to-all(bf16[16,2,240,128]{3,2,1,0:T(8,128)(2,1)} %shard_map.80), channel_id=1, replica_groups={{0,2,4,6,8,10,12,14,16,18,20,22,24,26,28,30},{1,3,5,7,9,11,13,15,17,19,..., dimensions={0} | all-to-all | bytes 3932160 | tf_op jit(solution)/shard_map/all_to_all | solution.py:244
  136.0 8.5 %collective-permute-start.2 = (bf16[16,2,240,128]{3,2,1,0:T(8,128)(2,1)S(1)}, bf16[16,2,240,128]{3,2,1,0:T(8,128)(2,1)S(1)}, u32[]{:S(2)}, u32[]{:S(2)}) collective-permute-start(bf16[16,2,240,128]{3,2,1,0:T(8,128)(2,1)S(1)} %all_to_all.21.chunks_ref), channel_id=1, source_target_pairs={{0,1},{1,0},{2,3},{3,2},{4,5},{5,4},{6,7},{7,6},{8,9},{9,8},{10,11... | collective-permute-start | bytes 5898248 | tf_op jit(solution)/shard_map/ppermute | solution.py:248
  144.5 0.0 copy-done.1
  144.5 0.0 copy-done.2
  144.5 2.3 %shard_map.81 = (bf16[8,928,128]{2,1,0:T(8,128)(2,1)}, bf16[16,2,240,128]{3,2,1,0:T(8,128)(2,1)}) custom-call(s32[1]{0:T(128)} %bitcast.core_ref, bf16[16,2,240,128]{3,2,1,0:T(8,128)(2,1)S(1)} %all_to_all.21.chunks_ref, bf16[464,928]{1,0:T(8,128)(2,1)S(1)} %bitcast.7, bf16[464,928]{1,0:T(8,128)(2,1)S(1)} %copy-done.1), custom_call_target="tpu_custom_call" | custom-call | flops 881852416 | bytes 7555072 | tf_op jit(solution)/shard_map/pallas_call | solution.py:55
  146.8 1.3 collective-permute-done.2.chunks_ref
  148.1 2.3 %shard_map.82 = (bf16[8,928,128]{2,1,0:T(8,128)(2,1)}, bf16[16,2,240,128]{3,2,1,0:T(8,128)(2,1)}) custom-call(s32[1]{0:T(128)} %bitcast.core_ref, bf16[16,2,240,128]{3,2,1,0:T(8,128)(2,1)S(1)} %collective-permute-done.2.chunks_ref, bf16[464,928]{1,0:T(8,128)(2,1)S(1)} %bitcast.8, bf16[464,928]{1,0:T(8,128)(2,1)S(1)} %copy-done.1, ...), custom_call_target="tpu_custom_call", output_to_operand_aliasing={{0}: (4, {})} | custom-call | flops 881852416 | bytes 9455616 | tf_op jit(solution)/shard_map/pallas_call | solution.py:55
  150.5 17.9 %all-to-all-start.3 = ((bf16[8,928,128]{2,1,0:T(8,128)(2,1)}), bf16[8,928,128]{2,1,0:T(8,128)(2,1)}, u32[]{:S(2)}, u32[]{:S(2)}) async-start(bf16[8,928,128]{2,1,0:T(8,128)(2,1)} %get-tuple-element.17), calls=%async_computation.3 | async-start | bytes 3801088 | tf_op jit(solution)/shard_map/all_to_all | solution.py:240
  168.4 0.0 copy-start.5
  168.4 1.5 copy-done.5
  169.9 0.0 copy-start.6
  169.9 1.5 copy-done.6
  171.4 2.2 %shard_map.85 = bf16[928,464]{1,0:T(8,128)(2,1)} custom-call(s32[1]{0:T(128)} %bitcast.core_ref, bf16[8,928,128]{2,1,0:T(8,128)(2,1)S(1)} %all-to-all-done.rows_ref, bf16[16,2,240,128]{3,2,1,0:T(8,128)(2,1)S(1)} %copy-done.5, bf16[16,2,240,128]{3,2,1,0:T(8,128)(2,1)S(1)} %copy-done.6), custom_call_target="tpu_custom_call" | custom-call | flops 881852416 | bytes 6693888 | tf_op jit(solution)/shard_map/pallas_call | solution.py:55
  173.7 2.3 %shard_map.84 = bf16[464,928]{1,0:T(8,128)(2,1)} custom-call(s32[1]{0:T(128)} %bitcast.core_ref, bf16[8,928,128]{2,1,0:T(8,128)(2,1)S(1)} %all-to-all-done.rows_ref, bf16[16,2,240,128]{3,2,1,0:T(8,128)(2,1)S(1)} %copy-done.5, bf16[16,2,240,128]{3,2,1,0:T(8,128)(2,1)S(1)} %copy-done.6), custom_call_target="tpu_custom_call" | custom-call | flops 881852416 | bytes 6693888 | tf_op jit(solution)/shard_map/pallas_call | solution.py:55
  176.0 17.1 %all-to-all-done.3.value_ref = bf16[8,928,128]{2,1,0:T(8,128)(2,1)} async-done(((bf16[8,928,128]{2,1,0:T(8,128)(2,1)}), bf16[8,928,128]{2,1,0:T(8,128)(2,1)}, u32[]{:S(2)}, u32[]{:S(2)}) %all-to-all-start.3) | async-done | bytes 1900576 | tf_op jit(solution)/shard_map/all_to_all | solution.py:240
  193.2 2.4 %shard_map.83 = (bf16[464,128]{1,0:T(8,128)(2,1)}, bf16[464,128]{1,0:T(8,128)(2,1)}) custom-call(s32[1]{0:T(128)} %bitcast.core_ref, bf16[8,928,128]{2,1,0:T(8,128)(2,1)} %all-to-all-done.3.value_ref), custom_call_target="tpu_custom_call" | custom-call | flops 950272 | bytes 2138112 | tf_op jit(solution)/shard_map/pallas_call | solution.py:55
Async XLA Ops:
  0.6 0.9 copy-start.7
  1.5 0.9 copy-start.8
  3.9 8.7 %copy-start = (bf16[928,464]{1,0:T(8,128)(2,1)S(1)}, bf16[928,464]{1,0:T(8,128)(2,1)}, u32[]{:S(2)}) copy-start(bf16[928,464]{1,0:T(8,128)(2,1)} %weight_ref.3) | copy-start | bytes 2583556
  3.9 30.6 %all-to-all-start = ((bf16[8,928,128]{2,1,0:T(8,128)(2,1)}), bf16[8,928,128]{2,1,0:T(8,128)(2,1)S(1)}, u32[]{:S(2)}, u32[]{:S(2)}) async-start(bf16[8,928,128]{2,1,0:T(8,128)(2,1)} %shard_map.75), calls=%async_computation | async-start | bytes 3801088 | tf_op jit(solution)/shard_map/all_to_all | solution.py:240
  34.5 1.2 copy-start.3
  37.3 3.3 %copy-start.4 = (bf16[464,928]{0,1:T(8,128)(2,1)S(1)}, bf16[464,928]{0,1:T(8,128)(2,1)}, u32[]{:S(2)}) copy-start(bf16[464,928]{0,1:T(8,128)(2,1)} %copy.10) | copy-start | bytes 2583556
  37.3 3.3 %collective-permute-start.1 = (bf16[4,928,128]{2,1,0:T(8,128)(2,1)}, bf16[4,928,128]{2,1,0:T(8,128)(2,1)S(1)}, u32[]{:S(2)}, u32[]{:S(2)}) collective-permute-start(bf16[4,928,128]{2,1,0:T(8,128)(2,1)} %shard_map.77), channel_id=1, source_target_pairs={{0,1},{1,0},{2,3},{3,2},{4,5},{5,4},{6,7},{7,6},{8,9},{9,8},{10,11... | collective-permute-start | bytes 2850824 | tf_op jit(solution)/shard_map/ppermute | solution.py:248
  39.9 2.8 %collective-permute-start = (bf16[4,928,128]{2,1,0:T(8,128)(2,1)}, bf16[4,928,128]{2,1,0:T(8,128)(2,1)S(1)}, u32[]{:S(2)}, u32[]{:S(2)}) collective-permute-start(bf16[4,928,128]{2,1,0:T(8,128)(2,1)} %shard_map.76), channel_id=1, source_target_pairs={{0,1},{1,0},{2,3},{3,2},{4,5},{5,4},{6,7},{7,6},{8,9},{9,8},{10,11... | collective-permute-start | bytes 2850824 | tf_op jit(solution)/shard_map/ppermute | solution.py:248
  95.5 49.0 %copy-start.1 = (bf16[464,928]{1,0:T(8,128)(2,1)S(1)}, bf16[464,928]{1,0:T(8,128)(2,1)}, u32[]{:S(2)}) copy-start(bf16[464,928]{1,0:T(8,128)(2,1)} %second_ref.3) | copy-start | bytes 2583556
  95.6 49.0 %copy-start.2 = (bf16[928,464]{0,1:T(8,128)(2,1)S(1)}, bf16[928,464]{0,1:T(8,128)(2,1)}, u32[]{:S(2)}) copy-start(bf16[928,464]{0,1:T(8,128)(2,1)} %copy.11) | copy-start | bytes 2583556
  136.0 12.1 %collective-permute-start.2 = (bf16[16,2,240,128]{3,2,1,0:T(8,128)(2,1)S(1)}, bf16[16,2,240,128]{3,2,1,0:T(8,128)(2,1)S(1)}, u32[]{:S(2)}, u32[]{:S(2)}) collective-permute-start(bf16[16,2,240,128]{3,2,1,0:T(8,128)(2,1)S(1)} %all_to_all.21.chunks_ref), channel_id=1, source_target_pairs={{0,1},{1,0},{2,3},{3,2},{4,5},{5,4},{6,7},{7,6},{8,9},{9,8},{10,11... | collective-permute-start | bytes 5898248 | tf_op jit(solution)/shard_map/ppermute | solution.py:248
  150.5 42.7 %all-to-all-start.3 = ((bf16[8,928,128]{2,1,0:T(8,128)(2,1)}), bf16[8,928,128]{2,1,0:T(8,128)(2,1)}, u32[]{:S(2)}, u32[]{:S(2)}) async-start(bf16[8,928,128]{2,1,0:T(8,128)(2,1)} %get-tuple-element.17), calls=%async_computation.3 | async-start | bytes 3801088 | tf_op jit(solution)/shard_map/all_to_all | solution.py:240
  168.4 1.5 copy-start.5
  169.9 1.5 copy-start.6

commit v9 on v7

--- a/solution.py
+++ b/solution.py
@@ -57,11 +57,12 @@
     moved = sum(math.prod(o.shape) * o.dtype.itemsize for o in [*operands, *outs])
     vmem = pl.BlockSpec(memory_space=pltpu.VMEM)
     hbm = pl.BlockSpec(memory_space=pltpu.HBM)
+    anywhere = pl.BlockSpec(memory_space=pl.ANY)
     return pl.pallas_call(
         kernel,
         out_shape=[pltpu.HBM(o.shape, o.dtype) if i in far else o for i, o in enumerate(outs)],
         in_specs=[pl.BlockSpec(memory_space=pltpu.SMEM)]
-        + [hbm if i in far_in else vmem for i in range(len(operands))],
+        + [anywhere if i in far_in else vmem for i in range(len(operands))],
         out_specs=[hbm if i in far else vmem for i in range(len(outs))],
         scratch_shapes=scratch,
         compiler_params=pltpu.CompilerParams(vmem_limit_bytes=16 * 1024 * 1024),
@@ -71,10 +72,6 @@
 
 def half_of(ref, half, x):
     return jnp.concatenate([ref[half * X + ((x + d) & 3)] for d in range(X)], axis=1)
-
-
-def wide(refs):
-    return jnp.concatenate([ref[...] for ref in refs], axis=1)
 
 
 def block(value, d):
@@ -151,30 +148,39 @@
     count = 2 * X
 
     def kernel(pos_ref, *refs):
-        weight_ref, out_ref, kept_ref, held_ref, out_sems, sems = refs[-6:]
-        kept = [
-            pltpu.make_async_copy(refs[index], kept_ref.at[index], sems.at[index])
-            for index in range(count)
-        ]
-        for copy in kept:
-            copy.start()
+        weight_ref, out_ref, kept_ref, held_ref, out_sems, wide_ref, in_sems, sems = refs[-8:]
         x, c = pos_ref[0], pos_ref[1]
-        for part, half in ((refs[:X], c), (refs[X:count], 1 - c)):
-            product = dot(weight_ref[...], wide(part), PLAIN).astype(BF)
+        arriving, leaving = [], []
+        for index in range(count):
+            part, d = divmod(index, X)
+            here = wide_ref.at[part, :, pl.ds(d * LANES, LANES)]
+            arriving.append(pltpu.make_async_copy(refs[index], here, in_sems.at[index]))
+            arriving[-1].start()
+        for part, half in ((0, c), (1, 1 - c)):
+            for copy in arriving[part * X : (part + 1) * X]:
+                copy.wait()
+            kept = pltpu.make_async_copy(wide_ref.at[part], kept_ref.at[part], sems.at[part])
+            kept.start()
+            product = dot(weight_ref[...], wide_ref[part], PLAIN).astype(BF)
             for d in range(X):
-                index, target = len(kept) - count, half * X + ((x + d) & 3)
+                index, target = part * X + d, half * X + ((x + d) & 3)
                 held_ref[index] = block(product, d)
-                kept.append(
-                    pltpu.make_async_copy(held_ref.at[index], out_ref.at[target], out_sems.at[index])
+                copy = pltpu.make_async_copy(
+                    held_ref.at[index], out_ref.at[target], out_sems.at[index]
                 )
-                kept[-1].start()
-        for copy in kept:
-            copy.wait()
-
-    outs = [shaped((count, depth, LANES), BF), shaped((count, width, LANES), BF)]
+                copy.start()
+                leaving.append(copy)
+            leaving.append(kept)
+        for copy in leaving:
+            copy.wait()
+
+    outs = [shaped((count, depth, LANES), BF), shaped((2, width, X * LANES), BF)]
     flops = 2 * depth * width * count * LANES
-    scratch = staged(outs[0]) + [pltpu.SemaphoreType.DMA((count,))]
-    return kernel_call(kernel, outs, flops, pos, [*blocks, weight], scratch, (0, 1))
+    scratch = staged(outs[0]) + [pltpu.VMEM(outs[1].shape, BF)]
+    scratch += [pltpu.SemaphoreType.DMA((count,)), pltpu.SemaphoreType.DMA((2,))]
+    return kernel_call(
+        kernel, outs, flops, pos, [*blocks, weight], scratch, (0, 1), range(count)
+    )
 
 
 def weight_grad(pos, factor, rows, blocks, rows_first):
@@ -184,7 +190,7 @@
         x, c = pos_ref[0], pos_ref[1]
         total = None
         for part, half in ((0, c), (1, 1 - c)):
-            pair = half_of(rows_ref, half, x), half_of(blocks_ref, part, 0)
+            pair = half_of(rows_ref, half, x), blocks_ref[part]
             term = dot(*(pair if rows_first else pair[::-1]), LAST)
             total = term if total is None else total + term
         out_ref[...] = (factor * total).astype(BF)
@@ -199,9 +205,12 @@
 
 
 def many(pos, value, count):
-    def kernel(pos_ref, value_ref, out_ref, sems):
+    def kernel(pos_ref, value_ref, out_ref, held_ref, sems):
+        copy = pltpu.make_async_copy(value_ref, held_ref, sems.at[count])
+        copy.start()
+        copy.wait()
         copies = [
-            pltpu.make_async_copy(value_ref, out_ref.at[index], sems.at[index])
+            pltpu.make_async_copy(held_ref, out_ref.at[index], sems.at[index])
             for index in range(count)
         ]
         for copy in copies:
@@ -210,8 +219,8 @@
             copy.wait()
 
     outs = [shaped((count,) + value.shape, BF)]
-    scratch = [pltpu.SemaphoreType.DMA((count,))]
-    return kernel_call(kernel, outs, 0, pos, [value], scratch, (0,))[0]
+    scratch = [pltpu.VMEM(value.shape, BF), pltpu.SemaphoreType.DMA((count + 1,))]
+    return kernel_call(kernel, outs, 0, pos, [value], scratch, (0,), (0,))[0]
 
 
 def fan_out(value, held_ref, out_ref, sems):

time: 156 us -> 157 us (level)
  transfers between devices with their start and end apart: 32 -> 32, of which waited for: 15 -> 15; matrix products, arithmetic and copies ran while one was open for 5% -> 5% of each run, Pallas kernels for 14% -> 15%
where the time goes in v9:
time: 157 us; the launch traced here: 156 us
  starting transfers between devices  70.2 us (45%)
  waiting for transfers between devices  42.8 us (27%)
  Pallas kernels  30.5 us (19%)
  local copies, waits for them, and re-layouts  7.76 us (5%)
  other arithmetic  4.16 us (3%)
    all_to_all x8, starting transfers between devices, exchange(): return lax.all_to_all(value, axis, 0, 0, axis_index_groups=groups)  39.2 us
    all_to_all x8, waiting for transfers between devices, exchange(): return lax.all_to_all(value, axis, 0, 0, axis_index_groups=groups)  36.1 us
    pallas_call x14, Pallas kernels, kernel_call(): pl.pallas_call(kernel, out_shape=[pltpu.HBM(o.shape, o.dtype) if i in far...  30.5 us
    ppermute x12, starting transfers between devices, move_x(): return lax.ppermute(value, 'rep', rep_pairs(d, 0, 0))  15.7 us
    ppermute x12, starting transfers between devices, swap_cores(): return lax.ppermute(value, 'rep', rep_pairs(0, 0, 1))  15.2 us
    unnamed x18, local copies, waits for them, and re-layouts  7.76 us
    ppermute x12, waiting for transfers between devices, swap_cores(): return lax.ppermute(value, 'rep', rep_pairs(0, 0, 1))  5.25 us
    convert_element_type x2, other arithmetic, sum_x(): return keep.astype(BF)  4.08 us
  transfers between devices with their start and end apart: 32, of which 15 were waited for; matrix products, arithmetic and copies ran while one was open for 5% of the time, Pallas kernels for 15%

profile of v9, /device:TPU:1, one launch (start us, length us, event | category | flops | bytes accessed | tf_op | source)
XLA Modules:
  0.0 156.3 jit_solution(15088506652726713909)
XLA Ops:
  1.6 1.7 %shard_map.76 = bf16[8,464,128]{2,1,0:T(8,128)(2,1)} custom-call(s32[3]{0:T(128)S(1)} %pad_add_fusion.pos_ref, bf16[464,128]{1,0:T(8,128)(2,1)S(1)} %bitcast.26), custom_call_target="tpu_custom_call" | custom-call | bytes 1069056 | tf_op jit(solution)/shard_map/pallas_call | solution.py:61
  3.3 6.4 %all-to-all-start = ((bf16[8,464,128]{2,1,0:T(8,128)(2,1)}), bf16[8,464,128]{2,1,0:T(8,128)(2,1)S(1)}, u32[]{:S(2)}, u32[]{:S(2)}) async-start(bf16[8,464,128]{2,1,0:T(8,128)(2,1)} %shard_map.76), calls=%async_computation | async-start | bytes 1900544 | tf_op jit(solution)/shard_map/all_to_all | solution.py:204
  9.7 1.7 %shard_map.75 = bf16[8,464,128]{2,1,0:T(8,128)(2,1)} custom-call(s32[3]{0:T(128)S(1)} %pad_add_fusion.pos_ref, bf16[464,128]{1,0:T(8,128)(2,1)S(1)} %bitcast.27), custom_call_target="tpu_custom_call" | custom-call | bytes 1069056 | tf_op jit(solution)/shard_map/pallas_call | solution.py:61
  11.5 1.6 %copy.8 = bf16[464,928]{0,1:T(8,128)(2,1)S(1)} copy(bf16[464,928]{1,0:T(8,128)(2,1)} %refs_8_.1) | data formatting | bytes 1722368 | tf_op args[1]
  13.1 1.4 copy.9
  14.5 8.7 %all-to-all-done.rows_ref = bf16[8,464,128]{2,1,0:T(8,128)(2,1)S(1)} async-done(((bf16[8,464,128]{2,1,0:T(8,128)(2,1)}), bf16[8,464,128]{2,1,0:T(8,128)(2,1)S(1)}, u32[]{:S(2)}, u32[]{:S(2)}) %all-to-all-start) | async-done | bytes 950304 | tf_op jit(solution)/shard_map/all_to_all | solution.py:204
  23.3 2.2 %shard_map.77 = (bf16[2,928,128]{2,1,0:T(8,128)(2,1)}, bf16[2,928,128]{2,1,0:T(8,128)(2,1)}) custom-call(s32[3]{0:T(128)S(1)} %pad_add_fusion.pos_ref, bf16[8,464,128]{2,1,0:T(8,128)(2,1)S(1)} %all-to-all-done.rows_ref, bf16[928,464]{1,0:T(8,128)(2,1)S(1)} %bitcast.13), custom_call_target="tpu_custom_call" | custom-call | flops 440926208 | bytes 2761728 | tf_op jit(solution)/shard_map/pallas_call | solution.py:61
  25.5 1.2 collective-permute-start
  26.8 1.6 %collective-permute-done.refs_0_ = bf16[2,928,128]{2,1,0:T(8,128)(2,1)S(1)} collective-permute-done((bf16[2,928,128]{2,1,0:T(8,128)(2,1)}, bf16[2,928,128]{2,1,0:T(8,128)(2,1)S(1)}, u32[]{:S(2)}, u32[]{:S(2)}) %collective-permute-start) | collective-permute-done | bytes 475168 | tf_op jit(solution)/shard_map/ppermute | solution.py:273
  29.1 2.1 %shard_map.78 = (f32[928,128]{1,0:T(8,128)S(1)}, bf16[928,128]{1,0:T(8,128)(2,1)}, bf16[928,128]{1,0:T(8,128)(2,1)}, bf16[928,128]{1,0:T(8,128)(2,1)}) custom-call(s32[3]{0:T(128)S(1)} %pad_add_fusion.pos_ref, bf16[8,464,128]{2,1,0:T(8,128)(2,1)S(1)} %all-to-all-done.rows_ref, bf16[928,464]{1,0:T(8,128)(2,1)S(1)} %bitcast.14, ...), custom_call_target="tpu_custom_call" | custom-call | flops 440926208 | bytes 3949568 | tf_op jit(solution)/shard_map/pallas_call | solution.py:61
  31.1 3.6 %all-to-all-start.2 = ((bf16[8,464,128]{2,1,0:T(8,128)(2,1)}), bf16[8,464,128]{2,1,0:T(8,128)(2,1)S(1)}, u32[]{:S(2)}, u32[]{:S(2)}) async-start(bf16[8,464,128]{2,1,0:T(8,128)(2,1)} %shard_map.75), calls=%async_computation.2 | async-start | bytes 1900544 | tf_op jit(solution)/shard_map/all_to_all | solution.py:204
  34.7 1.3 collective-permute-start.2
  36.0 2.5 %collective-permute-start.3 = (bf16[928,128]{1,0:T(8,128)(2,1)}, bf16[928,128]{1,0:T(8,128)(2,1)}, u32[]{:S(2)}, u32[]{:S(2)}) collective-permute-start(bf16[928,128]{1,0:T(8,128)(2,1)} %get-tuple-element.44), channel_id=1, source_target_pairs={{0,16},{1,17},{2,18},{3,19},{4,20},{5,21},{6,22},{7,23},{8,24},{9,... | collective-permute-start | bytes 712712 | tf_op jit(solution)/shard_map/ppermute | solution.py:277
  38.5 1.2 collective-permute-start.4
  39.6 9.1 %all-to-all-done.2.rows_ref = bf16[8,464,128]{2,1,0:T(8,128)(2,1)S(1)} async-done(((bf16[8,464,128]{2,1,0:T(8,128)(2,1)}), bf16[8,464,128]{2,1,0:T(8,128)(2,1)S(1)}, u32[]{:S(2)}, u32[]{:S(2)}) %all-to-all-start.2) | async-done | bytes 950304 | tf_op jit(solution)/shard_map/all_to_all | solution.py:204
  48.7 2.2 %shard_map.79 = (bf16[2,928,128]{2,1,0:T(8,128)(2,1)}, bf16[2,928,128]{2,1,0:T(8,128)(2,1)}) custom-call(s32[3]{0:T(128)S(1)} %pad_add_fusion.pos_ref, bf16[8,464,128]{2,1,0:T(8,128)(2,1)S(1)} %all-to-all-done.2.rows_ref, bf16[928,464]{1,0:T(8,128)(2,1)S(1)} %copy-done), custom_call_target="tpu_custom_call" | custom-call | flops 440926208 | bytes 2761728 | tf_op jit(solution)/shard_map/pallas_call | solution.py:61
  51.7 2.0 %add_convert_fusion.1 = bf16[928,128]{1,0:T(8,128)(2,1)} fusion(bf16[928,128]{1,0:T(8,128)(2,1)} %collective-permute-done.4, bf16[928,128]{1,0:T(8,128)(2,1)} %collective-permute-done.3, f32[928,128]{1,0:T(8,128)S(1)} %get-tuple-element.42, bf16[928,128]{1,0:T(8,128)(2,1)} %collective-permute-done.2), kind=kLoop, calls=%fused_computation.1 | loop fusion | flops 831488 | bytes 1425408 | tf_op jit(solution)/shard_map/convert_element_type | solution.py:288
  53.7 7.3 %all-to-all-start.1 = ((bf16[4,232,128]{2,1,0:T(8,128)(2,1)}), bf16[4,232,128]{2,1,0:T(8,128)(2,1)S(1)}, u32[]{:S(2)}, u32[]{:S(2)}) async-start(bf16[4,232,128]{2,1,0:T(8,128)(2,1)} %bitcast.28), calls=%async_computation.1 | async-start | bytes 475136 | tf_op jit(solution)/shard_map/all_to_all | solution.py:204
  61.0 2.8 %shard_map.80 = (f32[928,128]{1,0:T(8,128)S(1)}, bf16[928,128]{1,0:T(8,128)(2,1)}, bf16[928,128]{1,0:T(8,128)(2,1)}, bf16[928,128]{1,0:T(8,128)(2,1)}) custom-call(s32[3]{0:T(128)S(1)} %pad_add_fusion.pos_ref, bf16[8,464,128]{2,1,0:T(8,128)(2,1)S(1)} %all-to-all-done.2.rows_ref, bf16[928,464]{1,0:T(8,128)(2,1)S(1)} %copy-done, ...), custom_call_target="tpu_custom_call" | custom-call | flops 440926208 | bytes 3949568 | tf_op jit(solution)/shard_map/pallas_call | solution.py:61
  64.5 1.2 collective-permute-start.14
  65.7 2.5 %collective-permute-start.15 = (bf16[928,128]{1,0:T(8,128)(2,1)}, bf16[928,128]{1,0:T(8,128)(2,1)}, u32[]{:S(2)}, u32[]{:S(2)}) collective-permute-start(bf16[928,128]{1,0:T(8,128)(2,1)} %get-tuple-element.60), channel_id=1, source_target_pairs={{0,16},{1,17},{2,18},{3,19},{4,20},{5,21},{6,22},{7,23},{8,24},{9,... | collective-permute-start | bytes 712712 | tf_op jit(solution)/shard_map/ppermute | solution.py:277
  68.2 1.2 collective-permute-start.16
  69.4 1.3 shard_map.81
  70.7 6.6 %all-to-all-start.3 = ((bf16[4,232,128]{2,1,0:T(8,128)(2,1)}), bf16[4,232,128]{2,1,0:T(8,128)(2,1)S(1)}, u32[]{:S(2)}, u32[]{:S(2)}) async-start(bf16[4,232,128]{2,1,0:T(8,128)(2,1)} %get-tuple-element.56), calls=%async_computation.3 | async-start | bytes 475136 | tf_op jit(solution)/shard_map/all_to_all | solution.py:204
  77.4 1.4 collective-permute-done.15
  78.8 2.1 %add_convert_fusion = bf16[928,128]{1,0:T(8,128)(2,1)} fusion(bf16[928,128]{1,0:T(8,128)(2,1)} %collective-permute-done.16, bf16[928,128]{1,0:T(8,128)(2,1)} %collective-permute-done.15, f32[928,128]{1,0:T(8,128)} %copy-done.5, bf16[928,128]{1,0:T(8,128)(2,1)} %collective-permute-done.14), kind=kLoop, calls=%fused_computation | loop fusion | flops 831488 | bytes 1425408 | tf_op jit(solution)/shard_map/convert_element_type | solution.py:288
  80.9 5.0 %all-to-all-done.3 = bf16[4,232,128]{2,1,0:T(8,128)(2,1)S(1)} async-done(((bf16[4,232,128]{2,1,0:T(8,128)(2,1)}), bf16[4,232,128]{2,1,0:T(8,128)(2,1)S(1)}, u32[]{:S(2)}, u32[]{:S(2)}) %all-to-all-start.3) | async-done | bytes 237600 | tf_op jit(solution)/shard_map/all_to_all | solution.py:204
  85.9 3.4 %all-to-all-start.5 = ((bf16[4,232,128]{2,1,0:T(8,128)(2,1)}), bf16[4,232,128]{2,1,0:T(8,128)(2,1)S(1)}, u32[]{:S(2)}, u32[]{:S(2)}) async-start(bf16[4,232,128]{2,1,0:T(8,128)(2,1)} %bitcast.29), calls=%async_computation.5 | async-start | bytes 475136 | tf_op jit(solution)/shard_map/all_to_all | solution.py:204
  89.7 1.9 %collective-permute-start.8 = (bf16[928,128]{1,0:T(8,128)(2,1)S(1)}, bf16[928,128]{1,0:T(8,128)(2,1)}, u32[]{:S(2)}, u32[]{:S(2)}) collective-permute-start(bf16[928,128]{1,0:T(8,128)(2,1)S(1)} %bitcast.22), channel_id=1, source_target_pairs={{0,16},{1,17},{2,18},{3,19},{4,20},{5,21},{6,22},{7,23},{8,24},{9,... | collective-permute-start | bytes 712712 | tf_op jit(solution)/shard_map/ppermute | solution.py:277
  92.2 4.9 %all-to-all-done.5.arrived_ref = bf16[4,232,128]{2,1,0:T(8,128)(2,1)S(1)} async-done(((bf16[4,232,128]{2,1,0:T(8,128)(2,1)}), bf16[4,232,128]{2,1,0:T(8,128)(2,1)S(1)}, u32[]{:S(2)}, u32[]{:S(2)}) %all-to-all-start.5) | async-done | bytes 237600 | tf_op jit(solution)/shard_map/all_to_all | solution.py:204
  97.1 1.3 shard_map.84
  98.4 3.4 %all-to-all-start.6 = ((bf16[4,232,128]{2,1,0:T(8,128)(2,1)}), bf16[4,232,128]{2,1,0:T(8,128)(2,1)S(1)}, u32[]{:S(2)}, u32[]{:S(2)}) async-start(bf16[4,232,128]{2,1,0:T(8,128)(2,1)} %shard_map.84), calls=%async_computation.6 | async-start | bytes 475136 | tf_op jit(solution)/shard_map/all_to_all | solution.py:204
  101.9 4.5 %collective-permute-start.10 = (bf16[928,128]{1,0:T(8,128)(2,1)S(1)}, bf16[928,128]{1,0:T(8,128)(2,1)S(1)}, u32[]{:S(2)}, u32[]{:S(2)}) collective-permute-start(bf16[928,128]{1,0:T(8,128)(2,1)S(1)} %bitcast.24), channel_id=1, source_target_pairs={{0,1},{1,0},{2,3},{3,2},{4,5},{5,4},{6,7},{7,6},{8,9},{9,8},{10,11... | collective-permute-start | bytes 712712 | tf_op jit(solution)/shard_map/ppermute | solution.py:273
  108.8 4.0 %shard_map.82 = (bf16[8,464,128]{2,1,0:T(8,128)(2,1)}, bf16[2,928,512]{2,1,0:T(8,128)(2,1)}) custom-call(s32[3]{0:T(128)S(1)} %pad_add_fusion.pos_ref, bf16[928,128]{1,0:T(8,128)(2,1)S(1)} %bitcast.25, bf16[928,128]{1,0:T(8,128)(2,1)} %collective-permute-done.7.refs_1_, bf16[928,128]{1,0:T(8,128)(2,1)} %collective-permute-done.8.refs_2_, ...), custom_call_target="tpu_custom_call" | custom-call | flops 881852416 | bytes 5612544 | tf_op jit(solution)/shard_map/pallas_call | solution.py:61
  112.8 3.6 %all-to-all-start.4 = ((bf16[8,464,128]{2,1,0:T(8,128)(2,1)}), bf16[8,464,128]{2,1,0:T(8,128)(2,1)S(1)}, u32[]{:S(2)}, u32[]{:S(2)}) async-start(bf16[8,464,128]{2,1,0:T(8,128)(2,1)} %get-tuple-element.58), calls=%async_computation.4 | async-start | bytes 1900544 | tf_op jit(solution)/shard_map/all_to_all | solution.py:204
  116.8 1.3 collective-permute-start.18
  118.1 1.5 collective-permute-start.17
  119.6 1.5 copy-done.1
  121.1 2.7 %shard_map.85 = bf16[928,464]{1,0:T(8,128)(2,1)} custom-call(s32[3]{0:T(128)S(1)} %pad_add_fusion.pos_ref, bf16[8,464,128]{2,1,0:T(8,128)(2,1)S(1)} %all-to-all-done.2.rows_ref, bf16[2,928,512]{2,1,0:T(8,128)(2,1)S(1)} %copy-done.1), custom_call_target="tpu_custom_call" | custom-call | flops 881852416 | bytes 3712000 | tf_op jit(solution)/shard_map/pallas_call | solution.py:61
  123.7 3.7 %collective-permute-start.20 = (bf16[928,128]{1,0:T(8,128)(2,1)S(1)}, bf16[928,128]{1,0:T(8,128)(2,1)S(1)}, u32[]{:S(2)}, u32[]{:S(2)}) collective-permute-start(bf16[928,128]{1,0:T(8,128)(2,1)S(1)} %bitcast.19), channel_id=1, source_target_pairs={{0,1},{1,0},{2,3},{3,2},{4,5},{5,4},{6,7},{7,6},{8,9},{9,8},{10,11... | collective-permute-start | bytes 712712 | tf_op jit(solution)/shard_map/ppermute | solution.py:273
  127.4 3.6 %collective-permute-start.23 = (bf16[928,128]{1,0:T(8,128)(2,1)S(1)}, bf16[928,128]{1,0:T(8,128)(2,1)S(1)}, u32[]{:S(2)}, u32[]{:S(2)}) collective-permute-start(bf16[928,128]{1,0:T(8,128)(2,1)S(1)} %collective-permute-done.19.refs_3_), channel_id=1, source_target_pairs={{0,1},{1,0},{2,3},{3,2},{4,5},{5,4},{6,7},{7,6},{8,9},{9,8},{10,11... | collective-permute-start | bytes 712712 | tf_op jit(solution)/shard_map/ppermute | solution.py:273
  132.8 3.2 %shard_map.86 = (bf16[8,464,128]{2,1,0:T(8,128)(2,1)}, bf16[2,928,512]{2,1,0:T(8,128)(2,1)}) custom-call(s32[3]{0:T(128)S(1)} %pad_add_fusion.pos_ref, bf16[928,128]{1,0:T(8,128)(2,1)S(1)} %bitcast.20, bf16[928,128]{1,0:T(8,128)(2,1)S(1)} %collective-permute-done.17.refs_1_, bf16[928,128]{1,0:T(8,128)(2,1)S(1)} %collective-permute-done.18.refs_2_, ...), custom_call_target="tpu_custom_call" | custom-call | flops 881852416 | bytes 5612544 | tf_op jit(solution)/shard_map/pallas_call | solution.py:61
  136.0 5.0 %all-to-all-start.7 = ((bf16[8,464,128]{2,1,0:T(8,128)(2,1)}), bf16[8,464,128]{2,1,0:T(8,128)(2,1)S(1)}, u32[]{:S(2)}, u32[]{:S(2)}) async-start(bf16[8,464,128]{2,1,0:T(8,128)(2,1)} %get-tuple-element.70), calls=%async_computation.7 | async-start | bytes 1900544 | tf_op jit(solution)/shard_map/all_to_all | solution.py:204
  141.1 1.5 copy-done.2
  142.6 2.7 %shard_map.88 = bf16[464,928]{1,0:T(8,128)(2,1)} custom-call(s32[3]{0:T(128)S(1)} %pad_add_fusion.pos_ref, bf16[8,464,128]{2,1,0:T(8,128)(2,1)S(1)} %all-to-all-done.rows_ref, bf16[2,928,512]{2,1,0:T(8,128)(2,1)S(1)} %copy-done.2), custom_call_target="tpu_custom_call" | custom-call | flops 881852416 | bytes 3712000 | tf_op jit(solution)/shard_map/pallas_call | solution.py:61
  145.2 1.3 shard_map.83
  146.5 8.4 %all-to-all-done.7.value_ref = bf16[8,464,128]{2,1,0:T(8,128)(2,1)S(1)} async-done(((bf16[8,464,128]{2,1,0:T(8,128)(2,1)}), bf16[8,464,128]{2,1,0:T(8,128)(2,1)S(1)}, u32[]{:S(2)}, u32[]{:S(2)}) %all-to-all-start.7) | async-done | bytes 950304 | tf_op jit(solution)/shard_map/all_to_all | solution.py:204
  155.0 1.3 shard_map.87
  (51 shorter events, 9.0 us)
Async XLA Ops:
  0.7 0.9 copy-start.6
  1.6 8.1 %copy-start.7 = (bf16[128,464]{0,1:T(8,128)(2,1)S(1)}, bf16[128,464]{0,1:T(8,128)(2,1)}, u32[]{:S(2)}) copy-start(bf16[128,464]{0,1:T(8,128)(2,1)} %param.7) | copy-start | bytes 356356
  3.3 20.0 %all-to-all-start = ((bf16[8,464,128]{2,1,0:T(8,128)(2,1)}), bf16[8,464,128]{2,1,0:T(8,128)(2,1)S(1)}, u32[]{:S(2)}, u32[]{:S(2)}) async-start(bf16[8,464,128]{2,1,0:T(8,128)(2,1)} %shard_map.76), calls=%async_computation | async-start | bytes 1900544 | tf_op jit(solution)/shard_map/all_to_all | solution.py:204
  9.7 3.4 %copy-start = (bf16[928,464]{1,0:T(8,128)(2,1)S(1)}, bf16[928,464]{1,0:T(8,128)(2,1)}, u32[]{:S(2)}) copy-start(bf16[928,464]{1,0:T(8,128)(2,1)} %weight_ref.3) | copy-start | bytes 2583556
  25.5 2.9 %collective-permute-start = (bf16[2,928,128]{2,1,0:T(8,128)(2,1)}, bf16[2,928,128]{2,1,0:T(8,128)(2,1)S(1)}, u32[]{:S(2)}, u32[]{:S(2)}) collective-permute-start(bf16[2,928,128]{2,1,0:T(8,128)(2,1)} %get-tuple-element.40), channel_id=1, source_target_pairs={{0,1},{1,0},{2,3},{3,2},{4,5},{5,4},{6,7},{7,6},{8,9},{9,8},{10,11... | collective-permute-start | bytes 1425416 | tf_op jit(solution)/shard_map/ppermute | solution.py:273
  26.7 2.4 %collective-permute-start.1 = (bf16[2,928,128]{2,1,0:T(8,128)(2,1)}, bf16[2,928,128]{2,1,0:T(8,128)(2,1)S(1)}, u32[]{:S(2)}, u32[]{:S(2)}) collective-permute-start(bf16[2,928,128]{2,1,0:T(8,128)(2,1)} %get-tuple-element.41), channel_id=1, source_target_pairs={{0,1},{1,0},{2,3},{3,2},{4,5},{5,4},{6,7},{7,6},{8,9},{9,8},{10,11... | collective-permute-start | bytes 1425416 | tf_op jit(solution)/shard_map/ppermute | solution.py:273
  31.1 17.5 %all-to-all-start.2 = ((bf16[8,464,128]{2,1,0:T(8,128)(2,1)}), bf16[8,464,128]{2,1,0:T(8,128)(2,1)S(1)}, u32[]{:S(2)}, u32[]{:S(2)}) async-start(bf16[8,464,128]{2,1,0:T(8,128)(2,1)} %shard_map.75), calls=%async_computation.2 | async-start | bytes 1900544 | tf_op jit(solution)/shard_map/all_to_all | solution.py:204
  34.7 17.0 %collective-permute-start.2 = (bf16[928,128]{1,0:T(8,128)(2,1)}, bf16[928,128]{1,0:T(8,128)(2,1)}, u32[]{:S(2)}, u32[]{:S(2)}) collective-permute-start(bf16[928,128]{1,0:T(8,128)(2,1)} %get-tuple-element.43), channel_id=1, source_target_pairs={{0,8},{1,9},{2,10},{3,11},{4,12},{5,13},{6,14},{7,15},{8,16},{9,17... | collective-permute-start | bytes 712712 | tf_op jit(solution)/shard_map/ppermute | solution.py:277
  36.0 15.7 %collective-permute-start.3 = (bf16[928,128]{1,0:T(8,128)(2,1)}, bf16[928,128]{1,0:T(8,128)(2,1)}, u32[]{:S(2)}, u32[]{:S(2)}) collective-permute-start(bf16[928,128]{1,0:T(8,128)(2,1)} %get-tuple-element.44), channel_id=1, source_target_pairs={{0,16},{1,17},{2,18},{3,19},{4,20},{5,21},{6,22},{7,23},{8,24},{9,... | collective-permute-start | bytes 712712 | tf_op jit(solution)/shard_map/ppermute | solution.py:277
  38.5 13.3 %collective-permute-start.4 = (bf16[928,128]{1,0:T(8,128)(2,1)}, bf16[928,128]{1,0:T(8,128)(2,1)}, u32[]{:S(2)}, u32[]{:S(2)}) collective-permute-start(bf16[928,128]{1,0:T(8,128)(2,1)} %get-tuple-element.45), channel_id=1, source_target_pairs={{0,24},{1,25},{2,26},{3,27},{4,28},{5,29},{6,30},{7,31},{8,0},{9,1... | collective-permute-start | bytes 712712 | tf_op jit(solution)/shard_map/ppermute | solution.py:277
  50.9 10.1 %collective-permute-start.5 = (bf16[2,928,128]{2,1,0:T(8,128)(2,1)}, bf16[2,928,128]{2,1,0:T(8,128)(2,1)}, u32[]{:S(2)}, u32[]{:S(2)}) collective-permute-start(bf16[2,928,128]{2,1,0:T(8,128)(2,1)} %get-tuple-element.52), channel_id=1, source_target_pairs={{0,1},{1,0},{2,3},{3,2},{4,5},{5,4},{6,7},{7,6},{8,9},{9,8},{10,11... | collective-permute-start | bytes 1425416 | tf_op jit(solution)/shard_map/ppermute | solution.py:273
  51.6 9.4 %collective-permute-start.6 = (bf16[2,928,128]{2,1,0:T(8,128)(2,1)}, bf16[2,928,128]{2,1,0:T(8,128)(2,1)}, u32[]{:S(2)}, u32[]{:S(2)}) collective-permute-start(bf16[2,928,128]{2,1,0:T(8,128)(2,1)} %get-tuple-element.53), channel_id=1, source_target_pairs={{0,1},{1,0},{2,3},{3,2},{4,5},{5,4},{6,7},{7,6},{8,9},{9,8},{10,11... | collective-permute-start | bytes 1425416 | tf_op jit(solution)/shard_map/ppermute | solution.py:273
  53.7 15.7 %all-to-all-start.1 = ((bf16[4,232,128]{2,1,0:T(8,128)(2,1)}), bf16[4,232,128]{2,1,0:T(8,128)(2,1)S(1)}, u32[]{:S(2)}, u32[]{:S(2)}) async-start(bf16[4,232,128]{2,1,0:T(8,128)(2,1)} %bitcast.28), calls=%async_computation.1 | async-start | bytes 475136 | tf_op jit(solution)/shard_map/all_to_all | solution.py:204
  63.8 0.8 copy-start.5
  64.5 44.3 %copy-start.4 = (bf16[928,464]{0,1:T(8,128)(2,1)S(1)}, bf16[928,464]{0,1:T(8,128)(2,1)}, u32[]{:S(2)}) copy-start(bf16[928,464]{0,1:T(8,128)(2,1)} %copy.9) | copy-start | bytes 2583556
  64.5 12.8 %collective-permute-start.14 = (bf16[928,128]{1,0:T(8,128)(2,1)}, bf16[928,128]{1,0:T(8,128)(2,1)}, u32[]{:S(2)}, u32[]{:S(2)}) collective-permute-start(bf16[928,128]{1,0:T(8,128)(2,1)} %get-tuple-element.59), channel_id=1, source_target_pairs={{0,8},{1,9},{2,10},{3,11},{4,12},{5,13},{6,14},{7,15},{8,16},{9,17... | collective-permute-start | bytes 712712 | tf_op jit(solution)/shard_map/ppermute | solution.py:277
  65.7 13.0 %collective-permute-start.15 = (bf16[928,128]{1,0:T(8,128)(2,1)}, bf16[928,128]{1,0:T(8,128)(2,1)}, u32[]{:S(2)}, u32[]{:S(2)}) collective-permute-start(bf16[928,128]{1,0:T(8,128)(2,1)} %get-tuple-element.60), channel_id=1, source_target_pairs={{0,16},{1,17},{2,18},{3,19},{4,20},{5,21},{6,22},{7,23},{8,24},{9,... | collective-permute-start | bytes 712712 | tf_op jit(solution)/shard_map/ppermute | solution.py:277
  68.2 10.6 %collective-permute-start.16 = (bf16[928,128]{1,0:T(8,128)(2,1)}, bf16[928,128]{1,0:T(8,128)(2,1)}, u32[]{:S(2)}, u32[]{:S(2)}) collective-permute-start(bf16[928,128]{1,0:T(8,128)(2,1)} %get-tuple-element.61), channel_id=1, source_target_pairs={{0,24},{1,25},{2,26},{3,27},{4,28},{5,29},{6,30},{7,31},{8,0},{9,1... | collective-permute-start | bytes 712712 | tf_op jit(solution)/shard_map/ppermute | solution.py:277
  70.7 15.2 %all-to-all-start.3 = ((bf16[4,232,128]{2,1,0:T(8,128)(2,1)}), bf16[4,232,128]{2,1,0:T(8,128)(2,1)S(1)}, u32[]{:S(2)}, u32[]{:S(2)}) async-start(bf16[4,232,128]{2,1,0:T(8,128)(2,1)} %get-tuple-element.56), calls=%async_computation.3 | async-start | bytes 475136 | tf_op jit(solution)/shard_map/all_to_all | solution.py:204
  85.9 11.2 %all-to-all-start.5 = ((bf16[4,232,128]{2,1,0:T(8,128)(2,1)}), bf16[4,232,128]{2,1,0:T(8,128)(2,1)S(1)}, u32[]{:S(2)}, u32[]{:S(2)}) async-start(bf16[4,232,128]{2,1,0:T(8,128)(2,1)} %bitcast.29), calls=%async_computation.5 | async-start | bytes 475136 | tf_op jit(solution)/shard_map/all_to_all | solution.py:204
  89.3 17.1 %collective-permute-start.9 = (bf16[928,128]{1,0:T(8,128)(2,1)S(1)}, bf16[928,128]{1,0:T(8,128)(2,1)}, u32[]{:S(2)}, u32[]{:S(2)}) collective-permute-start(bf16[928,128]{1,0:T(8,128)(2,1)S(1)} %bitcast.21), channel_id=1, source_target_pairs={{0,8},{1,9},{2,10},{3,11},{4,12},{5,13},{6,14},{7,15},{8,16},{9,17... | collective-permute-start | bytes 712712 | tf_op jit(solution)/shard_map/ppermute | solution.py:277
  89.7 16.8 %collective-permute-start.8 = (bf16[928,128]{1,0:T(8,128)(2,1)S(1)}, bf16[928,128]{1,0:T(8,128)(2,1)}, u32[]{:S(2)}, u32[]{:S(2)}) collective-permute-start(bf16[928,128]{1,0:T(8,128)(2,1)S(1)} %bitcast.22), channel_id=1, source_target_pairs={{0,16},{1,17},{2,18},{3,19},{4,20},{5,21},{6,22},{7,23},{8,24},{9,... | collective-permute-start | bytes 712712 | tf_op jit(solution)/shard_map/ppermute | solution.py:277
  91.6 15.3 %collective-permute-start.7 = (bf16[928,128]{1,0:T(8,128)(2,1)S(1)}, bf16[928,128]{1,0:T(8,128)(2,1)}, u32[]{:S(2)}, u32[]{:S(2)}) collective-permute-start(bf16[928,128]{1,0:T(8,128)(2,1)S(1)} %bitcast.23), channel_id=1, source_target_pairs={{0,24},{1,25},{2,26},{3,27},{4,28},{5,29},{6,30},{7,31},{8,0},{9,1... | collective-permute-start | bytes 712712 | tf_op jit(solution)/shard_map/ppermute | solution.py:277
  98.4 14.4 %all-to-all-start.6 = ((bf16[4,232,128]{2,1,0:T(8,128)(2,1)}), bf16[4,232,128]{2,1,0:T(8,128)(2,1)S(1)}, u32[]{:S(2)}, u32[]{:S(2)}) async-start(bf16[4,232,128]{2,1,0:T(8,128)(2,1)} %shard_map.84), calls=%async_computation.6 | async-start | bytes 475136 | tf_op jit(solution)/shard_map/all_to_all | solution.py:204
  101.9 5.7 %collective-permute-start.10 = (bf16[928,128]{1,0:T(8,128)(2,1)S(1)}, bf16[928,128]{1,0:T(8,128)(2,1)S(1)}, u32[]{:S(2)}, u32[]{:S(2)}) collective-permute-start(bf16[928,128]{1,0:T(8,128)(2,1)S(1)} %bitcast.24), channel_id=1, source_target_pairs={{0,1},{1,0},{2,3},{3,2},{4,5},{5,4},{6,7},{7,6},{8,9},{9,8},{10,11... | collective-permute-start | bytes 712712 | tf_op jit(solution)/shard_map/ppermute | solution.py:273
  106.4 1.7 %collective-permute-start.13 = (bf16[928,128]{1,0:T(8,128)(2,1)}, bf16[928,128]{1,0:T(8,128)(2,1)S(1)}, u32[]{:S(2)}, u32[]{:S(2)}) collective-permute-start(bf16[928,128]{1,0:T(8,128)(2,1)} %collective-permute-done.9.refs_3_), channel_id=1, source_target_pairs={{0,1},{1,0},{2,3},{3,2},{4,5},{5,4},{6,7},{7,6},{8,9},{9,8},{10,11... | collective-permute-start | bytes 712712 | tf_op jit(solution)/shard_map/ppermute | solution.py:273
  106.5 1.9 %collective-permute-start.12 = (bf16[928,128]{1,0:T(8,128)(2,1)}, bf16[928,128]{1,0:T(8,128)(2,1)S(1)}, u32[]{:S(2)}, u32[]{:S(2)}) collective-permute-start(bf16[928,128]{1,0:T(8,128)(2,1)} %collective-permute-done.8.refs_2_), channel_id=1, source_target_pairs={{0,1},{1,0},{2,3},{3,2},{4,5},{5,4},{6,7},{7,6},{8,9},{9,8},{10,11... | collective-permute-start | bytes 712712 | tf_op jit(solution)/shard_map/ppermute | solution.py:273
  106.9 1.9 %collective-permute-start.11 = (bf16[928,128]{1,0:T(8,128)(2,1)}, bf16[928,128]{1,0:T(8,128)(2,1)S(1)}, u32[]{:S(2)}, u32[]{:S(2)}) collective-permute-start(bf16[928,128]{1,0:T(8,128)(2,1)} %collective-permute-done.7.refs_1_), channel_id=1, source_target_pairs={{0,1},{1,0},{2,3},{3,2},{4,5},{5,4},{6,7},{7,6},{8,9},{9,8},{10,11... | collective-permute-start | bytes 712712 | tf_op jit(solution)/shard_map/ppermute | solution.py:273
  112.8 23.2 %all-to-all-start.4 = ((bf16[8,464,128]{2,1,0:T(8,128)(2,1)}), bf16[8,464,128]{2,1,0:T(8,128)(2,1)S(1)}, u32[]{:S(2)}, u32[]{:S(2)}) async-start(bf16[8,464,128]{2,1,0:T(8,128)(2,1)} %get-tuple-element.58), calls=%async_computation.4 | async-start | bytes 1900544 | tf_op jit(solution)/shard_map/all_to_all | solution.py:204
  116.4 11.0 %collective-permute-start.19 = (bf16[928,128]{1,0:T(8,128)(2,1)S(1)}, bf16[928,128]{1,0:T(8,128)(2,1)S(1)}, u32[]{:S(2)}, u32[]{:S(2)}) collective-permute-start(bf16[928,128]{1,0:T(8,128)(2,1)S(1)} %bitcast.16), channel_id=1, source_target_pairs={{0,8},{1,9},{2,10},{3,11},{4,12},{5,13},{6,14},{7,15},{8,16},{9,17... | collective-permute-start | bytes 712712 | tf_op jit(solution)/shard_map/ppermute | solution.py:277
  116.8 14.2 %collective-permute-start.18 = (bf16[928,128]{1,0:T(8,128)(2,1)S(1)}, bf16[928,128]{1,0:T(8,128)(2,1)S(1)}, u32[]{:S(2)}, u32[]{:S(2)}) collective-permute-start(bf16[928,128]{1,0:T(8,128)(2,1)S(1)} %bitcast.17), channel_id=1, source_target_pairs={{0,16},{1,17},{2,18},{3,19},{4,20},{5,21},{6,22},{7,23},{8,24},{9,... | collective-permute-start | bytes 712712 | tf_op jit(solution)/shard_map/ppermute | solution.py:277
  118.1 12.9 %collective-permute-start.17 = (bf16[928,128]{1,0:T(8,128)(2,1)S(1)}, bf16[928,128]{1,0:T(8,128)(2,1)S(1)}, u32[]{:S(2)}, u32[]{:S(2)}) collective-permute-start(bf16[928,128]{1,0:T(8,128)(2,1)S(1)} %bitcast.18), channel_id=1, source_target_pairs={{0,24},{1,25},{2,26},{3,27},{4,28},{5,29},{6,30},{7,31},{8,0},{9,1... | collective-permute-start | bytes 712712 | tf_op jit(solution)/shard_map/ppermute | solution.py:277
  119.6 1.5 copy-start.1
  121.1 11.8 %copy-start.3 = (bf16[464,928]{1,0:T(8,128)(2,1)S(1)}, bf16[464,928]{1,0:T(8,128)(2,1)}, u32[]{:S(2)}) copy-start(bf16[464,928]{1,0:T(8,128)(2,1)} %refs_8_.1) | copy-start | bytes 2583556
  123.7 7.9 %collective-permute-start.20 = (bf16[928,128]{1,0:T(8,128)(2,1)S(1)}, bf16[928,128]{1,0:T(8,128)(2,1)S(1)}, u32[]{:S(2)}, u32[]{:S(2)}) collective-permute-start(bf16[928,128]{1,0:T(8,128)(2,1)S(1)} %bitcast.19), channel_id=1, source_target_pairs={{0,1},{1,0},{2,3},{3,2},{4,5},{5,4},{6,7},{7,6},{8,9},{9,8},{10,11... | collective-permute-start | bytes 712712 | tf_op jit(solution)/shard_map/ppermute | solution.py:273
  127.4 4.7 %collective-permute-start.23 = (bf16[928,128]{1,0:T(8,128)(2,1)S(1)}, bf16[928,128]{1,0:T(8,128)(2,1)S(1)}, u32[]{:S(2)}, u32[]{:S(2)}) collective-permute-start(bf16[928,128]{1,0:T(8,128)(2,1)S(1)} %collective-permute-done.19.refs_3_), channel_id=1, source_target_pairs={{0,1},{1,0},{2,3},{3,2},{4,5},{5,4},{6,7},{7,6},{8,9},{9,8},{10,11... | collective-permute-start | bytes 712712 | tf_op jit(solution)/shard_map/ppermute | solution.py:273
  131.0 1.5 collective-permute-start.22
  131.0 1.8 %collective-permute-start.21 = (bf16[928,128]{1,0:T(8,128)(2,1)S(1)}, bf16[928,128]{1,0:T(8,128)(2,1)S(1)}, u32[]{:S(2)}, u32[]{:S(2)}) collective-permute-start(bf16[928,128]{1,0:T(8,128)(2,1)S(1)} %collective-permute-done.17.refs_1_), channel_id=1, source_target_pairs={{0,1},{1,0},{2,3},{3,2},{4,5},{5,4},{6,7},{7,6},{8,9},{9,8},{10,11... | collective-permute-start | bytes 712712 | tf_op jit(solution)/shard_map/ppermute | solution.py:273
  136.0 18.9 %all-to-all-start.7 = ((bf16[8,464,128]{2,1,0:T(8,128)(2,1)}), bf16[8,464,128]{2,1,0:T(8,128)(2,1)S(1)}, u32[]{:S(2)}, u32[]{:S(2)}) async-start(bf16[8,464,128]{2,1,0:T(8,128)(2,1)} %get-tuple-element.70), calls=%async_computation.7 | async-start | bytes 1900544 | tf_op jit(solution)/shard_map/all_to_all | solution.py:204
  141.0 1.5 copy-start.2

commit v10 on v7

--- a/solution.py
+++ b/solution.py
@@ -307,7 +307,7 @@
     )
     sent = other_half(pos, tok, first_turned)
     keep, sent = own_half(pos, tok, first_turned, [swap_cores(part) for part in sent])
-    cot = exchange(after(cots, keep), "grp")
+    cot = exchange(cots, "grp")
     value = sum_x(keep, sent)
 
     sent = other_half(pos, after(cot, keep), second_weight)

time: 156 us -> 157 us (level)
  starting transfers between devices: 70.2 us -> 72.5 us
  waiting for transfers between devices: 42.9 us -> 40.7 us
    all_to_all x8, waiting for transfers between devices: 36.3 us -> 27.1 us  [exchange(): return lax.all_to_all(value, axis, 0, 0, axis_index_groups=groups)]
    ppermute x12, waiting for transfers between devices: 1.44 us -> 8.41 us  [move_x(): return lax.ppermute(value, 'rep', rep_pairs(d, 0, 0))]
    unnamed x18 -> x22, local copies, waits for them, and re-layouts: 7.76 us -> 8.7 us
  transfers between devices with their start and end apart: 32 -> 32, of which waited for: 15 -> 18; matrix products, arithmetic and copies ran while one was open for 5% -> 4% of each run, Pallas kernels for 14% -> 17%
where the time goes in v10:
time: 157 us; the launch traced here: 156 us
  starting transfers between devices  72.5 us (46%)
  waiting for transfers between devices  40.7 us (26%)
  Pallas kernels  29.3 us (19%)
  local copies, waits for them, and re-layouts  8.7 us (6%)
  other arithmetic  4.19 us (3%)
    all_to_all x8, starting transfers between devices, exchange(): return lax.all_to_all(value, axis, 0, 0, axis_index_groups=groups)  40.7 us
    pallas_call x14, Pallas kernels, kernel_call(): pl.pallas_call(kernel, out_shape=[pltpu.HBM(o.shape, o.dtype) if i in far...  29.3 us
    all_to_all x8, waiting for transfers between devices, exchange(): return lax.all_to_all(value, axis, 0, 0, axis_index_groups=groups)  27.1 us
    ppermute x12, starting transfers between devices, swap_cores(): return lax.ppermute(value, 'rep', rep_pairs(0, 0, 1))  15.9 us
    ppermute x12, starting transfers between devices, move_x(): return lax.ppermute(value, 'rep', rep_pairs(d, 0, 0))  15.9 us
    unnamed x22, local copies, waits for them, and re-layouts  8.7 us
    ppermute x12, waiting for transfers between devices, move_x(): return lax.ppermute(value, 'rep', rep_pairs(d, 0, 0))  8.41 us
    ppermute x12, waiting for transfers between devices, swap_cores(): return lax.ppermute(value, 'rep', rep_pairs(0, 0, 1))  5.2 us
  transfers between devices with their start and end apart: 32, of which 18 were waited for; matrix products, arithmetic and copies ran while one was open for 4% of the time, Pallas kernels for 17%

profile of v10, /device:TPU:1, one launch (start us, length us, event | category | flops | bytes accessed | tf_op | source)
XLA Modules:
  0.0 156.2 jit_solution(9306851078992711547)
XLA Ops:
  1.6 1.5 shard_map.76
  3.2 6.4 %all-to-all-start = ((bf16[8,464,128]{2,1,0:T(8,128)(2,1)}), bf16[8,464,128]{2,1,0:T(8,128)(2,1)S(1)}, u32[]{:S(2)}, u32[]{:S(2)}) async-start(bf16[8,464,128]{2,1,0:T(8,128)(2,1)} %shard_map.76), calls=%async_computation | async-start | bytes 1900544 | tf_op jit(solution)/shard_map/all_to_all | solution.py:198
  9.6 1.6 %shard_map.75 = bf16[8,464,128]{2,1,0:T(8,128)(2,1)} custom-call(s32[3]{0:T(128)S(1)} %pad_add_fusion.pos_ref, bf16[464,128]{1,0:T(8,128)(2,1)S(1)} %bitcast.27), custom_call_target="tpu_custom_call" | custom-call | bytes 1069056 | tf_op jit(solution)/shard_map/pallas_call | solution.py:60
  11.1 1.3 copy.8
  12.5 1.4 copy.9
  13.9 9.2 %all-to-all-done.rows_ref = bf16[8,464,128]{2,1,0:T(8,128)(2,1)S(1)} async-done(((bf16[8,464,128]{2,1,0:T(8,128)(2,1)}), bf16[8,464,128]{2,1,0:T(8,128)(2,1)S(1)}, u32[]{:S(2)}, u32[]{:S(2)}) %all-to-all-start) | async-done | bytes 950304 | tf_op jit(solution)/shard_map/all_to_all | solution.py:198
  23.1 4.0 %all-to-all-start.2 = ((bf16[8,464,128]{2,1,0:T(8,128)(2,1)}), bf16[8,464,128]{2,1,0:T(8,128)(2,1)S(1)}, u32[]{:S(2)}, u32[]{:S(2)}) async-start(bf16[8,464,128]{2,1,0:T(8,128)(2,1)} %shard_map.75), calls=%async_computation.2 | async-start | bytes 1900544 | tf_op jit(solution)/shard_map/all_to_all | solution.py:198
  27.1 1.2 copy-done.1
  28.3 2.2 %shard_map.77 = (bf16[2,928,128]{2,1,0:T(8,128)(2,1)}, bf16[2,928,128]{2,1,0:T(8,128)(2,1)}) custom-call(s32[3]{0:T(128)S(1)} %pad_add_fusion.pos_ref, bf16[8,464,128]{2,1,0:T(8,128)(2,1)S(1)} %all-to-all-done.rows_ref, bf16[928,464]{1,0:T(8,128)(2,1)S(1)} %bitcast.13), custom_call_target="tpu_custom_call" | custom-call | flops 440926208 | bytes 2761728 | tf_op jit(solution)/shard_map/pallas_call | solution.py:60
  31.4 1.6 %collective-permute-done.refs_0_ = bf16[2,928,128]{2,1,0:T(8,128)(2,1)S(1)} collective-permute-done((bf16[2,928,128]{2,1,0:T(8,128)(2,1)}, bf16[2,928,128]{2,1,0:T(8,128)(2,1)S(1)}, u32[]{:S(2)}, u32[]{:S(2)}) %collective-permute-start) | collective-permute-done | bytes 475168 | tf_op jit(solution)/shard_map/ppermute | solution.py:264
  33.7 2.1 %shard_map.78 = (f32[928,128]{1,0:T(8,128)S(1)}, bf16[928,128]{1,0:T(8,128)(2,1)}, bf16[928,128]{1,0:T(8,128)(2,1)}, bf16[928,128]{1,0:T(8,128)(2,1)}) custom-call(s32[3]{0:T(128)S(1)} %pad_add_fusion.pos_ref, bf16[8,464,128]{2,1,0:T(8,128)(2,1)S(1)} %all-to-all-done.rows_ref, bf16[928,464]{1,0:T(8,128)(2,1)S(1)} %bitcast.14, ...), custom_call_target="tpu_custom_call" | custom-call | flops 440926208 | bytes 3949568 | tf_op jit(solution)/shard_map/pallas_call | solution.py:60
  35.8 1.3 collective-permute-start.2
  37.1 2.5 %collective-permute-start.3 = (bf16[928,128]{1,0:T(8,128)(2,1)}, bf16[928,128]{1,0:T(8,128)(2,1)}, u32[]{:S(2)}, u32[]{:S(2)}) collective-permute-start(bf16[928,128]{1,0:T(8,128)(2,1)} %get-tuple-element.43), channel_id=1, source_target_pairs={{0,16},{1,17},{2,18},{3,19},{4,20},{5,21},{6,22},{7,23},{8,24},{9,... | collective-permute-start | bytes 712712 | tf_op jit(solution)/shard_map/ppermute | solution.py:268
  39.5 1.2 collective-permute-start.4
  41.0 2.2 %shard_map.79 = (bf16[2,928,128]{2,1,0:T(8,128)(2,1)}, bf16[2,928,128]{2,1,0:T(8,128)(2,1)}) custom-call(s32[3]{0:T(128)S(1)} %pad_add_fusion.pos_ref, bf16[8,464,128]{2,1,0:T(8,128)(2,1)S(1)} %all-to-all-done.2.rows_ref, bf16[928,464]{1,0:T(8,128)(2,1)S(1)} %copy-done), custom_call_target="tpu_custom_call" | custom-call | flops 440926208 | bytes 2761728 | tf_op jit(solution)/shard_map/pallas_call | solution.py:60
  44.4 6.1 %collective-permute-done.3 = bf16[928,128]{1,0:T(8,128)(2,1)} collective-permute-done((bf16[928,128]{1,0:T(8,128)(2,1)}, bf16[928,128]{1,0:T(8,128)(2,1)}, u32[]{:S(2)}, u32[]{:S(2)}) %collective-permute-start.3) | collective-permute-done | bytes 237600 | tf_op jit(solution)/shard_map/ppermute | solution.py:268
  50.5 2.0 %add_convert_fusion.1 = bf16[928,128]{1,0:T(8,128)(2,1)} fusion(bf16[928,128]{1,0:T(8,128)(2,1)} %collective-permute-done.4, bf16[928,128]{1,0:T(8,128)(2,1)} %collective-permute-done.3, f32[928,128]{1,0:T(8,128)S(1)} %get-tuple-element.41, bf16[928,128]{1,0:T(8,128)(2,1)} %collective-permute-done.2), kind=kLoop, calls=%fused_computation.1 | loop fusion | flops 831488 | bytes 1425408 | tf_op jit(solution)/shard_map/convert_element_type | solution.py:279
  52.4 7.3 %all-to-all-start.1 = ((bf16[4,232,128]{2,1,0:T(8,128)(2,1)}), bf16[4,232,128]{2,1,0:T(8,128)(2,1)S(1)}, u32[]{:S(2)}, u32[]{:S(2)}) async-start(bf16[4,232,128]{2,1,0:T(8,128)(2,1)} %bitcast.28), calls=%async_computation.1 | async-start | bytes 475136 | tf_op jit(solution)/shard_map/all_to_all | solution.py:198
  59.7 2.8 %shard_map.80 = (f32[928,128]{1,0:T(8,128)S(1)}, bf16[928,128]{1,0:T(8,128)(2,1)}, bf16[928,128]{1,0:T(8,128)(2,1)}, bf16[928,128]{1,0:T(8,128)(2,1)}) custom-call(s32[3]{0:T(128)S(1)} %pad_add_fusion.pos_ref, bf16[8,464,128]{2,1,0:T(8,128)(2,1)S(1)} %all-to-all-done.2.rows_ref, bf16[928,464]{1,0:T(8,128)(2,1)S(1)} %copy-done, ...), custom_call_target="tpu_custom_call" | custom-call | flops 440926208 | bytes 3949568 | tf_op jit(solution)/shard_map/pallas_call | solution.py:60
  63.3 1.0 collective-permute-start.14
  64.3 2.8 %collective-permute-start.15 = (bf16[928,128]{1,0:T(8,128)(2,1)}, bf16[928,128]{1,0:T(8,128)(2,1)}, u32[]{:S(2)}, u32[]{:S(2)}) collective-permute-start(bf16[928,128]{1,0:T(8,128)(2,1)} %get-tuple-element.58), channel_id=1, source_target_pairs={{0,16},{1,17},{2,18},{3,19},{4,20},{5,21},{6,22},{7,23},{8,24},{9,... | collective-permute-start | bytes 712712 | tf_op jit(solution)/shard_map/ppermute | solution.py:268
  68.0 1.3 shard_map.81
  69.3 6.1 %all-to-all-start.3 = ((bf16[4,232,128]{2,1,0:T(8,128)(2,1)}), bf16[4,232,128]{2,1,0:T(8,128)(2,1)S(1)}, u32[]{:S(2)}, u32[]{:S(2)}) async-start(bf16[4,232,128]{2,1,0:T(8,128)(2,1)} %get-tuple-element.54), calls=%async_computation.3 | async-start | bytes 475136 | tf_op jit(solution)/shard_map/all_to_all | solution.py:198
  75.4 2.2 %collective-permute-done.15 = bf16[928,128]{1,0:T(8,128)(2,1)} collective-permute-done((bf16[928,128]{1,0:T(8,128)(2,1)}, bf16[928,128]{1,0:T(8,128)(2,1)}, u32[]{:S(2)}, u32[]{:S(2)}) %collective-permute-start.15) | collective-permute-done | bytes 237600 | tf_op jit(solution)/shard_map/ppermute | solution.py:268
  77.6 2.1 %add_convert_fusion = bf16[928,128]{1,0:T(8,128)(2,1)} fusion(bf16[928,128]{1,0:T(8,128)(2,1)} %collective-permute-done.16, bf16[928,128]{1,0:T(8,128)(2,1)} %collective-permute-done.15, f32[928,128]{1,0:T(8,128)} %copy-done.7, bf16[928,128]{1,0:T(8,128)(2,1)} %collective-permute-done.14), kind=kLoop, calls=%fused_computation | loop fusion | flops 831488 | bytes 1425408 | tf_op jit(solution)/shard_map/convert_element_type | solution.py:279
  79.8 4.1 %all-to-all-done.3 = bf16[4,232,128]{2,1,0:T(8,128)(2,1)S(1)} async-done(((bf16[4,232,128]{2,1,0:T(8,128)(2,1)}), bf16[4,232,128]{2,1,0:T(8,128)(2,1)S(1)}, u32[]{:S(2)}, u32[]{:S(2)}) %all-to-all-start.3) | async-done | bytes 237600 | tf_op jit(solution)/shard_map/all_to_all | solution.py:198
  83.9 3.4 %all-to-all-start.5 = ((bf16[4,232,128]{2,1,0:T(8,128)(2,1)}), bf16[4,232,128]{2,1,0:T(8,128)(2,1)S(1)}, u32[]{:S(2)}, u32[]{:S(2)}) async-start(bf16[4,232,128]{2,1,0:T(8,128)(2,1)} %bitcast.29), calls=%async_computation.5 | async-start | bytes 475136 | tf_op jit(solution)/shard_map/all_to_all | solution.py:198
  87.3 1.4 collective-permute-start.9
  88.7 1.1 collective-permute-start.8
  89.8 1.4 collective-permute-start.7
  91.2 4.5 %all-to-all-done.5.arrived_ref = bf16[4,232,128]{2,1,0:T(8,128)(2,1)S(1)} async-done(((bf16[4,232,128]{2,1,0:T(8,128)(2,1)}), bf16[4,232,128]{2,1,0:T(8,128)(2,1)S(1)}, u32[]{:S(2)}, u32[]{:S(2)}) %all-to-all-start.5) | async-done | bytes 237600 | tf_op jit(solution)/shard_map/all_to_all | solution.py:198
  95.7 1.3 shard_map.84
  97.0 3.4 %all-to-all-start.6 = ((bf16[4,232,128]{2,1,0:T(8,128)(2,1)}), bf16[4,232,128]{2,1,0:T(8,128)(2,1)S(1)}, u32[]{:S(2)}, u32[]{:S(2)}) async-start(bf16[4,232,128]{2,1,0:T(8,128)(2,1)} %shard_map.84), calls=%async_computation.6 | async-start | bytes 475136 | tf_op jit(solution)/shard_map/all_to_all | solution.py:198
  100.4 5.2 %collective-permute-start.10 = (bf16[928,128]{1,0:T(8,128)(2,1)S(1)}, bf16[928,128]{1,0:T(8,128)(2,1)S(1)}, u32[]{:S(2)}, u32[]{:S(2)}) collective-permute-start(bf16[928,128]{1,0:T(8,128)(2,1)S(1)} %bitcast.24), channel_id=1, source_target_pairs={{0,1},{1,0},{2,3},{3,2},{4,5},{5,4},{6,7},{7,6},{8,9},{9,8},{10,11... | collective-permute-start | bytes 712712 | tf_op jit(solution)/shard_map/ppermute | solution.py:264
  108.1 3.5 %shard_map.82 = (bf16[8,464,128]{2,1,0:T(8,128)(2,1)}, bf16[8,928,128]{2,1,0:T(8,128)(2,1)}) custom-call(s32[3]{0:T(128)S(1)} %pad_add_fusion.pos_ref, bf16[928,128]{1,0:T(8,128)(2,1)S(1)} %bitcast.25, bf16[928,128]{1,0:T(8,128)(2,1)} %collective-permute-done.7.refs_1_, bf16[928,128]{1,0:T(8,128)(2,1)} %collective-permute-done.8.refs_2_, ...), custom_call_target="tpu_custom_call" | custom-call | flops 881852416 | bytes 5612544 | tf_op jit(solution)/shard_map/pallas_call | solution.py:60
  111.6 5.0 %all-to-all-start.4 = ((bf16[8,464,128]{2,1,0:T(8,128)(2,1)}), bf16[8,464,128]{2,1,0:T(8,128)(2,1)S(1)}, u32[]{:S(2)}, u32[]{:S(2)}) async-start(bf16[8,464,128]{2,1,0:T(8,128)(2,1)} %get-tuple-element.56), calls=%async_computation.4 | async-start | bytes 1900544 | tf_op jit(solution)/shard_map/all_to_all | solution.py:198
  118.0 1.5 collective-permute-start.17
  119.5 1.5 copy-done.2
  121.0 2.7 %shard_map.85 = bf16[928,464]{1,0:T(8,128)(2,1)} custom-call(s32[3]{0:T(128)S(1)} %pad_add_fusion.pos_ref, bf16[8,464,128]{2,1,0:T(8,128)(2,1)S(1)} %all-to-all-done.2.rows_ref, bf16[8,928,128]{2,1,0:T(8,128)(2,1)S(1)} %copy-done.2), custom_call_target="tpu_custom_call" | custom-call | flops 881852416 | bytes 3712000 | tf_op jit(solution)/shard_map/pallas_call | solution.py:60
  123.7 4.2 %collective-permute-start.20 = (bf16[928,128]{1,0:T(8,128)(2,1)S(1)}, bf16[928,128]{1,0:T(8,128)(2,1)S(1)}, u32[]{:S(2)}, u32[]{:S(2)}) collective-permute-start(bf16[928,128]{1,0:T(8,128)(2,1)S(1)} %bitcast.19), channel_id=1, source_target_pairs={{0,1},{1,0},{2,3},{3,2},{4,5},{5,4},{6,7},{7,6},{8,9},{9,8},{10,11... | collective-permute-start | bytes 712712 | tf_op jit(solution)/shard_map/ppermute | solution.py:264
  127.8 3.2 %collective-permute-start.23 = (bf16[928,128]{1,0:T(8,128)(2,1)S(1)}, bf16[928,128]{1,0:T(8,128)(2,1)S(1)}, u32[]{:S(2)}, u32[]{:S(2)}) collective-permute-start(bf16[928,128]{1,0:T(8,128)(2,1)S(1)} %collective-permute-done.19.refs_3_), channel_id=1, source_target_pairs={{0,1},{1,0},{2,3},{3,2},{4,5},{5,4},{6,7},{7,6},{8,9},{9,8},{10,11... | collective-permute-start | bytes 712712 | tf_op jit(solution)/shard_map/ppermute | solution.py:264
  132.9 2.9 %shard_map.86 = (bf16[8,464,128]{2,1,0:T(8,128)(2,1)}, bf16[8,928,128]{2,1,0:T(8,128)(2,1)}) custom-call(s32[3]{0:T(128)S(1)} %pad_add_fusion.pos_ref, bf16[928,128]{1,0:T(8,128)(2,1)S(1)} %bitcast.20, bf16[928,128]{1,0:T(8,128)(2,1)S(1)} %collective-permute-done.17.refs_1_, bf16[928,128]{1,0:T(8,128)(2,1)S(1)} %collective-permute-done.18.refs_2_, ...), custom_call_target="tpu_custom_call" | custom-call | flops 881852416 | bytes 5612544 | tf_op jit(solution)/shard_map/pallas_call | solution.py:60
  135.8 5.2 %all-to-all-start.7 = ((bf16[8,464,128]{2,1,0:T(8,128)(2,1)}), bf16[8,464,128]{2,1,0:T(8,128)(2,1)S(1)}, u32[]{:S(2)}, u32[]{:S(2)}) async-start(bf16[8,464,128]{2,1,0:T(8,128)(2,1)} %get-tuple-element.68), calls=%async_computation.7 | async-start | bytes 1900544 | tf_op jit(solution)/shard_map/all_to_all | solution.py:198
  141.0 1.5 copy-done.3
  142.5 2.7 %shard_map.88 = bf16[464,928]{1,0:T(8,128)(2,1)} custom-call(s32[3]{0:T(128)S(1)} %pad_add_fusion.pos_ref, bf16[8,464,128]{2,1,0:T(8,128)(2,1)S(1)} %all-to-all-done.rows_ref, bf16[8,928,128]{2,1,0:T(8,128)(2,1)S(1)} %copy-done.3), custom_call_target="tpu_custom_call" | custom-call | flops 881852416 | bytes 3712000 | tf_op jit(solution)/shard_map/pallas_call | solution.py:60
  145.2 1.3 shard_map.83
  146.5 8.4 %all-to-all-done.7.value_ref = bf16[8,464,128]{2,1,0:T(8,128)(2,1)S(1)} async-done(((bf16[8,464,128]{2,1,0:T(8,128)(2,1)}), bf16[8,464,128]{2,1,0:T(8,128)(2,1)S(1)}, u32[]{:S(2)}, u32[]{:S(2)}) %all-to-all-start.7) | async-done | bytes 950304 | tf_op jit(solution)/shard_map/all_to_all | solution.py:198
  154.9 1.3 shard_map.87
  (55 shorter events, 11.4 us)
Async XLA Ops:
  0.7 0.9 copy-start.8
  1.6 7.9 %copy-start.9 = (bf16[128,464]{0,1:T(8,128)(2,1)S(1)}, bf16[128,464]{0,1:T(8,128)(2,1)}, u32[]{:S(2)}) copy-start(bf16[128,464]{0,1:T(8,128)(2,1)} %param.7) | copy-start | bytes 356356
  1.6 9.5 %copy-start.4 = (bf16[464,928]{1,0:T(8,128)(2,1)S(1)}, bf16[464,928]{1,0:T(8,128)(2,1)}, u32[]{:S(2)}) copy-start(bf16[464,928]{1,0:T(8,128)(2,1)} %refs_8_.1) | copy-start | bytes 2583556
  3.2 20.0 %all-to-all-start = ((bf16[8,464,128]{2,1,0:T(8,128)(2,1)}), bf16[8,464,128]{2,1,0:T(8,128)(2,1)S(1)}, u32[]{:S(2)}, u32[]{:S(2)}) async-start(bf16[8,464,128]{2,1,0:T(8,128)(2,1)} %shard_map.76), calls=%async_computation | async-start | bytes 1900544 | tf_op jit(solution)/shard_map/all_to_all | solution.py:198
  9.5 3.0 %copy-start = (bf16[928,464]{1,0:T(8,128)(2,1)S(1)}, bf16[928,464]{1,0:T(8,128)(2,1)}, u32[]{:S(2)}) copy-start(bf16[928,464]{1,0:T(8,128)(2,1)} %weight_ref.3) | copy-start | bytes 2583556
  23.1 17.9 %all-to-all-start.2 = ((bf16[8,464,128]{2,1,0:T(8,128)(2,1)}), bf16[8,464,128]{2,1,0:T(8,128)(2,1)S(1)}, u32[]{:S(2)}, u32[]{:S(2)}) async-start(bf16[8,464,128]{2,1,0:T(8,128)(2,1)} %shard_map.75), calls=%async_computation.2 | async-start | bytes 1900544 | tf_op jit(solution)/shard_map/all_to_all | solution.py:198
  27.1 1.2 copy-start.1
  30.5 2.5 %collective-permute-start = (bf16[2,928,128]{2,1,0:T(8,128)(2,1)}, bf16[2,928,128]{2,1,0:T(8,128)(2,1)S(1)}, u32[]{:S(2)}, u32[]{:S(2)}) collective-permute-start(bf16[2,928,128]{2,1,0:T(8,128)(2,1)} %get-tuple-element.39), channel_id=1, source_target_pairs={{0,1},{1,0},{2,3},{3,2},{4,5},{5,4},{6,7},{7,6},{8,9},{9,8},{10,11... | collective-permute-start | bytes 1425416 | tf_op jit(solution)/shard_map/ppermute | solution.py:264
  31.3 2.4 %collective-permute-start.1 = (bf16[2,928,128]{2,1,0:T(8,128)(2,1)}, bf16[2,928,128]{2,1,0:T(8,128)(2,1)S(1)}, u32[]{:S(2)}, u32[]{:S(2)}) collective-permute-start(bf16[2,928,128]{2,1,0:T(8,128)(2,1)} %get-tuple-element.40), channel_id=1, source_target_pairs={{0,1},{1,0},{2,3},{3,2},{4,5},{5,4},{6,7},{7,6},{8,9},{9,8},{10,11... | collective-permute-start | bytes 1425416 | tf_op jit(solution)/shard_map/ppermute | solution.py:264
  35.8 8.6 %collective-permute-start.2 = (bf16[928,128]{1,0:T(8,128)(2,1)}, bf16[928,128]{1,0:T(8,128)(2,1)}, u32[]{:S(2)}, u32[]{:S(2)}) collective-permute-start(bf16[928,128]{1,0:T(8,128)(2,1)} %get-tuple-element.42), channel_id=1, source_target_pairs={{0,8},{1,9},{2,10},{3,11},{4,12},{5,13},{6,14},{7,15},{8,16},{9,17... | collective-permute-start | bytes 712712 | tf_op jit(solution)/shard_map/ppermute | solution.py:268
  37.1 13.4 %collective-permute-start.3 = (bf16[928,128]{1,0:T(8,128)(2,1)}, bf16[928,128]{1,0:T(8,128)(2,1)}, u32[]{:S(2)}, u32[]{:S(2)}) collective-permute-start(bf16[928,128]{1,0:T(8,128)(2,1)} %get-tuple-element.43), channel_id=1, source_target_pairs={{0,16},{1,17},{2,18},{3,19},{4,20},{5,21},{6,22},{7,23},{8,24},{9,... | collective-permute-start | bytes 712712 | tf_op jit(solution)/shard_map/ppermute | solution.py:268
  39.5 10.9 %collective-permute-start.4 = (bf16[928,128]{1,0:T(8,128)(2,1)}, bf16[928,128]{1,0:T(8,128)(2,1)}, u32[]{:S(2)}, u32[]{:S(2)}) collective-permute-start(bf16[928,128]{1,0:T(8,128)(2,1)} %get-tuple-element.44), channel_id=1, source_target_pairs={{0,24},{1,25},{2,26},{3,27},{4,28},{5,29},{6,30},{7,31},{8,0},{9,1... | collective-permute-start | bytes 712712 | tf_op jit(solution)/shard_map/ppermute | solution.py:268
  43.2 16.5 %collective-permute-start.5 = (bf16[2,928,128]{2,1,0:T(8,128)(2,1)}, bf16[2,928,128]{2,1,0:T(8,128)(2,1)}, u32[]{:S(2)}, u32[]{:S(2)}) collective-permute-start(bf16[2,928,128]{2,1,0:T(8,128)(2,1)} %get-tuple-element.50), channel_id=1, source_target_pairs={{0,1},{1,0},{2,3},{3,2},{4,5},{5,4},{6,7},{7,6},{8,9},{9,8},{10,11... | collective-permute-start | bytes 1425416 | tf_op jit(solution)/shard_map/ppermute | solution.py:264
  44.2 15.6 %collective-permute-start.6 = (bf16[2,928,128]{2,1,0:T(8,128)(2,1)}, bf16[2,928,128]{2,1,0:T(8,128)(2,1)}, u32[]{:S(2)}, u32[]{:S(2)}) collective-permute-start(bf16[2,928,128]{2,1,0:T(8,128)(2,1)} %get-tuple-element.51), channel_id=1, source_target_pairs={{0,1},{1,0},{2,3},{3,2},{4,5},{5,4},{6,7},{7,6},{8,9},{9,8},{10,11... | collective-permute-start | bytes 1425416 | tf_op jit(solution)/shard_map/ppermute | solution.py:264
  52.4 15.5 %all-to-all-start.1 = ((bf16[4,232,128]{2,1,0:T(8,128)(2,1)}), bf16[4,232,128]{2,1,0:T(8,128)(2,1)S(1)}, u32[]{:S(2)}, u32[]{:S(2)}) async-start(bf16[4,232,128]{2,1,0:T(8,128)(2,1)} %bitcast.28), calls=%async_computation.1 | async-start | bytes 475136 | tf_op jit(solution)/shard_map/all_to_all | solution.py:198
  62.5 0.8 copy-start.7
  63.3 44.8 %copy-start.6 = (bf16[928,464]{0,1:T(8,128)(2,1)S(1)}, bf16[928,464]{0,1:T(8,128)(2,1)}, u32[]{:S(2)}) copy-start(bf16[928,464]{0,1:T(8,128)(2,1)} %copy.9) | copy-start | bytes 2583556
  63.3 12.1 %collective-permute-start.14 = (bf16[928,128]{1,0:T(8,128)(2,1)}, bf16[928,128]{1,0:T(8,128)(2,1)}, u32[]{:S(2)}, u32[]{:S(2)}) collective-permute-start(bf16[928,128]{1,0:T(8,128)(2,1)} %get-tuple-element.57), channel_id=1, source_target_pairs={{0,8},{1,9},{2,10},{3,11},{4,12},{5,13},{6,14},{7,15},{8,16},{9,17... | collective-permute-start | bytes 712712 | tf_op jit(solution)/shard_map/ppermute | solution.py:268
  64.3 13.3 %collective-permute-start.15 = (bf16[928,128]{1,0:T(8,128)(2,1)}, bf16[928,128]{1,0:T(8,128)(2,1)}, u32[]{:S(2)}, u32[]{:S(2)}) collective-permute-start(bf16[928,128]{1,0:T(8,128)(2,1)} %get-tuple-element.58), channel_id=1, source_target_pairs={{0,16},{1,17},{2,18},{3,19},{4,20},{5,21},{6,22},{7,23},{8,24},{9,... | collective-permute-start | bytes 712712 | tf_op jit(solution)/shard_map/ppermute | solution.py:268
  67.2 10.5 %collective-permute-start.16 = (bf16[928,128]{1,0:T(8,128)(2,1)}, bf16[928,128]{1,0:T(8,128)(2,1)}, u32[]{:S(2)}, u32[]{:S(2)}) collective-permute-start(bf16[928,128]{1,0:T(8,128)(2,1)} %get-tuple-element.59), channel_id=1, source_target_pairs={{0,24},{1,25},{2,26},{3,27},{4,28},{5,29},{6,30},{7,31},{8,0},{9,1... | collective-permute-start | bytes 712712 | tf_op jit(solution)/shard_map/ppermute | solution.py:268
  69.3 14.6 %all-to-all-start.3 = ((bf16[4,232,128]{2,1,0:T(8,128)(2,1)}), bf16[4,232,128]{2,1,0:T(8,128)(2,1)S(1)}, u32[]{:S(2)}, u32[]{:S(2)}) async-start(bf16[4,232,128]{2,1,0:T(8,128)(2,1)} %get-tuple-element.54), calls=%async_computation.3 | async-start | bytes 475136 | tf_op jit(solution)/shard_map/all_to_all | solution.py:198
  83.9 11.8 %all-to-all-start.5 = ((bf16[4,232,128]{2,1,0:T(8,128)(2,1)}), bf16[4,232,128]{2,1,0:T(8,128)(2,1)S(1)}, u32[]{:S(2)}, u32[]{:S(2)}) async-start(bf16[4,232,128]{2,1,0:T(8,128)(2,1)} %bitcast.29), calls=%async_computation.5 | async-start | bytes 475136 | tf_op jit(solution)/shard_map/all_to_all | solution.py:198
  87.3 18.4 %collective-permute-start.9 = (bf16[928,128]{1,0:T(8,128)(2,1)S(1)}, bf16[928,128]{1,0:T(8,128)(2,1)}, u32[]{:S(2)}, u32[]{:S(2)}) collective-permute-start(bf16[928,128]{1,0:T(8,128)(2,1)S(1)} %bitcast.21), channel_id=1, source_target_pairs={{0,8},{1,9},{2,10},{3,11},{4,12},{5,13},{6,14},{7,15},{8,16},{9,17... | collective-permute-start | bytes 712712 | tf_op jit(solution)/shard_map/ppermute | solution.py:268
  88.7 17.1 %collective-permute-start.8 = (bf16[928,128]{1,0:T(8,128)(2,1)S(1)}, bf16[928,128]{1,0:T(8,128)(2,1)}, u32[]{:S(2)}, u32[]{:S(2)}) collective-permute-start(bf16[928,128]{1,0:T(8,128)(2,1)S(1)} %bitcast.22), channel_id=1, source_target_pairs={{0,16},{1,17},{2,18},{3,19},{4,20},{5,21},{6,22},{7,23},{8,24},{9,... | collective-permute-start | bytes 712712 | tf_op jit(solution)/shard_map/ppermute | solution.py:268
  89.8 16.4 %collective-permute-start.7 = (bf16[928,128]{1,0:T(8,128)(2,1)S(1)}, bf16[928,128]{1,0:T(8,128)(2,1)}, u32[]{:S(2)}, u32[]{:S(2)}) collective-permute-start(bf16[928,128]{1,0:T(8,128)(2,1)S(1)} %bitcast.23), channel_id=1, source_target_pairs={{0,24},{1,25},{2,26},{3,27},{4,28},{5,29},{6,30},{7,31},{8,0},{9,1... | collective-permute-start | bytes 712712 | tf_op jit(solution)/shard_map/ppermute | solution.py:268
  97.0 14.6 %all-to-all-start.6 = ((bf16[4,232,128]{2,1,0:T(8,128)(2,1)}), bf16[4,232,128]{2,1,0:T(8,128)(2,1)S(1)}, u32[]{:S(2)}, u32[]{:S(2)}) async-start(bf16[4,232,128]{2,1,0:T(8,128)(2,1)} %shard_map.84), calls=%async_computation.6 | async-start | bytes 475136 | tf_op jit(solution)/shard_map/all_to_all | solution.py:198
  100.4 6.4 %collective-permute-start.10 = (bf16[928,128]{1,0:T(8,128)(2,1)S(1)}, bf16[928,128]{1,0:T(8,128)(2,1)S(1)}, u32[]{:S(2)}, u32[]{:S(2)}) collective-permute-start(bf16[928,128]{1,0:T(8,128)(2,1)S(1)} %bitcast.24), channel_id=1, source_target_pairs={{0,1},{1,0},{2,3},{3,2},{4,5},{5,4},{6,7},{7,6},{8,9},{9,8},{10,11... | collective-permute-start | bytes 712712 | tf_op jit(solution)/shard_map/ppermute | solution.py:264
  105.7 1.7 %collective-permute-start.13 = (bf16[928,128]{1,0:T(8,128)(2,1)}, bf16[928,128]{1,0:T(8,128)(2,1)S(1)}, u32[]{:S(2)}, u32[]{:S(2)}) collective-permute-start(bf16[928,128]{1,0:T(8,128)(2,1)} %collective-permute-done.9.refs_3_), channel_id=1, source_target_pairs={{0,1},{1,0},{2,3},{3,2},{4,5},{5,4},{6,7},{7,6},{8,9},{9,8},{10,11... | collective-permute-start | bytes 712712 | tf_op jit(solution)/shard_map/ppermute | solution.py:264
  105.8 1.9 %collective-permute-start.12 = (bf16[928,128]{1,0:T(8,128)(2,1)}, bf16[928,128]{1,0:T(8,128)(2,1)S(1)}, u32[]{:S(2)}, u32[]{:S(2)}) collective-permute-start(bf16[928,128]{1,0:T(8,128)(2,1)} %collective-permute-done.8.refs_2_), channel_id=1, source_target_pairs={{0,1},{1,0},{2,3},{3,2},{4,5},{5,4},{6,7},{7,6},{8,9},{9,8},{10,11... | collective-permute-start | bytes 712712 | tf_op jit(solution)/shard_map/ppermute | solution.py:264
  106.2 1.9 %collective-permute-start.11 = (bf16[928,128]{1,0:T(8,128)(2,1)}, bf16[928,128]{1,0:T(8,128)(2,1)S(1)}, u32[]{:S(2)}, u32[]{:S(2)}) collective-permute-start(bf16[928,128]{1,0:T(8,128)(2,1)} %collective-permute-done.7.refs_1_), channel_id=1, source_target_pairs={{0,1},{1,0},{2,3},{3,2},{4,5},{5,4},{6,7},{7,6},{8,9},{9,8},{10,11... | collective-permute-start | bytes 712712 | tf_op jit(solution)/shard_map/ppermute | solution.py:264
  111.6 24.2 %all-to-all-start.4 = ((bf16[8,464,128]{2,1,0:T(8,128)(2,1)}), bf16[8,464,128]{2,1,0:T(8,128)(2,1)S(1)}, u32[]{:S(2)}, u32[]{:S(2)}) async-start(bf16[8,464,128]{2,1,0:T(8,128)(2,1)} %get-tuple-element.56), calls=%async_computation.4 | async-start | bytes 1900544 | tf_op jit(solution)/shard_map/all_to_all | solution.py:198
  116.6 11.3 %collective-permute-start.19 = (bf16[928,128]{1,0:T(8,128)(2,1)S(1)}, bf16[928,128]{1,0:T(8,128)(2,1)S(1)}, u32[]{:S(2)}, u32[]{:S(2)}) collective-permute-start(bf16[928,128]{1,0:T(8,128)(2,1)S(1)} %bitcast.16), channel_id=1, source_target_pairs={{0,8},{1,9},{2,10},{3,11},{4,12},{5,13},{6,14},{7,15},{8,16},{9,17... | collective-permute-start | bytes 712712 | tf_op jit(solution)/shard_map/ppermute | solution.py:268
  117.0 14.1 %collective-permute-start.18 = (bf16[928,128]{1,0:T(8,128)(2,1)S(1)}, bf16[928,128]{1,0:T(8,128)(2,1)S(1)}, u32[]{:S(2)}, u32[]{:S(2)}) collective-permute-start(bf16[928,128]{1,0:T(8,128)(2,1)S(1)} %bitcast.17), channel_id=1, source_target_pairs={{0,16},{1,17},{2,18},{3,19},{4,20},{5,21},{6,22},{7,23},{8,24},{9,... | collective-permute-start | bytes 712712 | tf_op jit(solution)/shard_map/ppermute | solution.py:268
  118.0 13.1 %collective-permute-start.17 = (bf16[928,128]{1,0:T(8,128)(2,1)S(1)}, bf16[928,128]{1,0:T(8,128)(2,1)S(1)}, u32[]{:S(2)}, u32[]{:S(2)}) collective-permute-start(bf16[928,128]{1,0:T(8,128)(2,1)S(1)} %bitcast.18), channel_id=1, source_target_pairs={{0,24},{1,25},{2,26},{3,27},{4,28},{5,29},{6,30},{7,31},{8,0},{9,1... | collective-permute-start | bytes 712712 | tf_op jit(solution)/shard_map/ppermute | solution.py:268
  119.5 1.5 copy-start.2
  121.0 11.9 %copy-start.5 = (bf16[464,928]{1,0:T(8,128)(2,1)S(1)}, bf16[464,928]{1,0:T(8,128)(2,1)}, u32[]{:S(2)}) copy-start(bf16[464,928]{1,0:T(8,128)(2,1)} %refs_8_.1) | copy-start | bytes 2583556
  123.7 8.1 %collective-permute-start.20 = (bf16[928,128]{1,0:T(8,128)(2,1)S(1)}, bf16[928,128]{1,0:T(8,128)(2,1)S(1)}, u32[]{:S(2)}, u32[]{:S(2)}) collective-permute-start(bf16[928,128]{1,0:T(8,128)(2,1)S(1)} %bitcast.19), channel_id=1, source_target_pairs={{0,1},{1,0},{2,3},{3,2},{4,5},{5,4},{6,7},{7,6},{8,9},{9,8},{10,11... | collective-permute-start | bytes 712712 | tf_op jit(solution)/shard_map/ppermute | solution.py:264
  127.8 4.4 %collective-permute-start.23 = (bf16[928,128]{1,0:T(8,128)(2,1)S(1)}, bf16[928,128]{1,0:T(8,128)(2,1)S(1)}, u32[]{:S(2)}, u32[]{:S(2)}) collective-permute-start(bf16[928,128]{1,0:T(8,128)(2,1)S(1)} %collective-permute-done.19.refs_3_), channel_id=1, source_target_pairs={{0,1},{1,0},{2,3},{3,2},{4,5},{5,4},{6,7},{7,6},{8,9},{9,8},{10,11... | collective-permute-start | bytes 712712 | tf_op jit(solution)/shard_map/ppermute | solution.py:264
  131.1 1.5 collective-permute-start.22
  131.1 1.8 %collective-permute-start.21 = (bf16[928,128]{1,0:T(8,128)(2,1)S(1)}, bf16[928,128]{1,0:T(8,128)(2,1)S(1)}, u32[]{:S(2)}, u32[]{:S(2)}) collective-permute-start(bf16[928,128]{1,0:T(8,128)(2,1)S(1)} %collective-permute-done.17.refs_1_), channel_id=1, source_target_pairs={{0,1},{1,0},{2,3},{3,2},{4,5},{5,4},{6,7},{7,6},{8,9},{9,8},{10,11... | collective-permute-start | bytes 712712 | tf_op jit(solution)/shard_map/ppermute | solution.py:264
  135.8 19.1 %all-to-all-start.7 = ((bf16[8,464,128]{2,1,0:T(8,128)(2,1)}), bf16[8,464,128]{2,1,0:T(8,128)(2,1)S(1)}, u32[]{:S(2)}, u32[]{:S(2)}) async-start(bf16[8,464,128]{2,1,0:T(8,128)(2,1)} %get-tuple-element.68), calls=%async_computation.7 | async-start | bytes 1900544 | tf_op jit(solution)/shard_map/all_to_all | solution.py:198
  141.0 1.5 copy-start.3

commit v11 on v7

--- a/solution.py
+++ b/solution.py
@@ -12,6 +12,7 @@
 GRP = 8
 X, Z, C = 4, 4, 2
 LANES = 128
+TILE = 16
 PIECES = 2
 
 
@@ -73,8 +74,8 @@
     return jnp.concatenate([ref[half * X + ((x + d) & 3)] for d in range(X)], axis=1)
 
 
-def wide(refs):
-    return jnp.concatenate([ref[...] for ref in refs], axis=1)
+def wide(refs, rows):
+    return jnp.concatenate([ref[:rows] for ref in refs], axis=1)
 
 
 def block(value, d):
@@ -113,6 +114,7 @@
 
 def own_half(pos, rows, weight, arrived):
     depth, width = weight.shape
+    padded = -(-depth // (Z * TILE)) * Z * TILE
 
     def kernel(pos_ref, rows_ref, weight_ref, *refs):
         arrived, keep_ref = refs[:PIECES], refs[PIECES]
@@ -127,9 +129,11 @@
                 other = arrived[d * PIECES // X][d % (X // PIECES)]
                 total = block(product, i) + other.astype(F32)
                 if d == 0:
-                    keep_ref[...] = total
+                    keep_ref[:depth] = total
+                    keep_ref[depth:] = jnp.zeros((padded - depth, LANES), F32)
                     continue
-                held_ref[d - 1] = total.astype(BF)
+                held_ref[d - 1, :depth] = total.astype(BF)
+                held_ref[d - 1, depth:] = jnp.zeros((padded - depth, LANES), BF)
                 copies.append(
                     pltpu.make_async_copy(held_ref.at[d - 1], sent[d - 1], sems.at[d - 1])
                 )
@@ -137,8 +141,8 @@
         for copy in copies:
             copy.wait()
 
-    part = shaped((depth, LANES), BF)
-    outs = [shaped((depth, LANES), F32)] + [part] * (X - 1)
+    part = shaped((padded, LANES), BF)
+    outs = [shaped((padded, LANES), F32)] + [part] * (X - 1)
     scratch = staged(shaped((X - 1,) + part.shape, BF))
     flops = 2 * depth * width * X * LANES
     operands = [rows, weight, *arrived]
@@ -153,14 +157,16 @@
     def kernel(pos_ref, *refs):
         weight_ref, out_ref, kept_ref, held_ref, out_sems, sems = refs[-6:]
         kept = [
-            pltpu.make_async_copy(refs[index], kept_ref.at[index], sems.at[index])
+            pltpu.make_async_copy(
+                refs[index].at[pl.ds(0, width)], kept_ref.at[index], sems.at[index]
+            )
             for index in range(count)
         ]
         for copy in kept:
             copy.start()
         x, c = pos_ref[0], pos_ref[1]
         for part, half in ((refs[:X], c), (refs[X:count], 1 - c)):
-            product = dot(weight_ref[...], wide(part), PLAIN).astype(BF)
+            product = dot(weight_ref[...], wide(part, width), PLAIN).astype(BF)
             for d in range(X):
                 index, target = len(kept) - count, half * X + ((x + d) & 3)
                 held_ref[index] = block(product, d)
@@ -280,8 +286,7 @@
 
 
 def scatter_z(value):
-    value = value.reshape(Z, value.shape[0] // Z, LANES)
-    return exchange(value, "rep", Z_GROUPS)
+    return exchange(value.reshape(Z, value.shape[0] // Z, LANES), "rep", Z_GROUPS)
 
 
 def spread_z(value):

time: 156 us -> 157 us (level)
  no operation moved by 1% of the time
where the time goes in v11:
time: 157 us; the launch traced here: 156 us
  starting transfers between devices  71.1 us (45%)
  waiting for transfers between devices  43.1 us (27%)
  Pallas kernels  29.4 us (19%)
  local copies, waits for them, and re-layouts  7.77 us (5%)
  other arithmetic  4.2 us (3%)
    all_to_all x8, starting transfers between devices, exchange(): return lax.all_to_all(value, axis, 0, 0, axis_index_groups=groups)  39.8 us
    all_to_all x8, waiting for transfers between devices, exchange(): return lax.all_to_all(value, axis, 0, 0, axis_index_groups=groups)  36.2 us
    pallas_call x14, Pallas kernels, kernel_call(): pl.pallas_call(kernel, out_shape=[pltpu.HBM(o.shape, o.dtype) if i in far...  29.4 us
    ppermute x12, starting transfers between devices, swap_cores(): return lax.ppermute(value, 'rep', rep_pairs(0, 0, 1))  15.7 us
    ppermute x12, starting transfers between devices, move_x(): return lax.ppermute(value, 'rep', rep_pairs(d, 0, 0))  15.6 us
    unnamed x18, local copies, waits for them, and re-layouts  7.77 us
    ppermute x12, waiting for transfers between devices, swap_cores(): return lax.ppermute(value, 'rep', rep_pairs(0, 0, 1))  5.26 us
    convert_element_type x2, other arithmetic, sum_x(): return keep.astype(BF)  4.12 us
  transfers between devices with their start and end apart: 32, of which 15 were waited for; matrix products, arithmetic and copies ran while one was open for 5% of the time, Pallas kernels for 14%

profile of v11, /device:TPU:1, one launch (start us, length us, event | category | flops | bytes accessed | tf_op | source)
XLA Modules:
  0.0 156.4 jit_solution(3945926813460126778)
XLA Ops:
  1.6 1.5 shard_map.76
  3.2 6.4 %all-to-all-start = ((bf16[8,464,128]{2,1,0:T(8,128)(2,1)}), bf16[8,464,128]{2,1,0:T(8,128)(2,1)S(1)}, u32[]{:S(2)}, u32[]{:S(2)}) async-start(bf16[8,464,128]{2,1,0:T(8,128)(2,1)} %shard_map.76), calls=%async_computation | async-start | bytes 1900544 | tf_op jit(solution)/shard_map/all_to_all | solution.py:204
  9.6 1.6 %shard_map.75 = bf16[8,464,128]{2,1,0:T(8,128)(2,1)} custom-call(s32[3]{0:T(128)S(1)} %pad_add_fusion.pos_ref, bf16[464,128]{1,0:T(8,128)(2,1)S(1)} %bitcast.27), custom_call_target="tpu_custom_call" | custom-call | bytes 1069056 | tf_op jit(solution)/shard_map/pallas_call | solution.py:61
  11.1 1.6 %copy.8 = bf16[464,928]{0,1:T(8,128)(2,1)S(1)} copy(bf16[464,928]{1,0:T(8,128)(2,1)} %refs_8_.1) | data formatting | bytes 1722368 | tf_op args[1]
  12.8 1.4 copy.9
  14.2 8.9 %all-to-all-done.rows_ref = bf16[8,464,128]{2,1,0:T(8,128)(2,1)S(1)} async-done(((bf16[8,464,128]{2,1,0:T(8,128)(2,1)}), bf16[8,464,128]{2,1,0:T(8,128)(2,1)S(1)}, u32[]{:S(2)}, u32[]{:S(2)}) %all-to-all-start) | async-done | bytes 950304 | tf_op jit(solution)/shard_map/all_to_all | solution.py:204
  23.1 2.2 %shard_map.77 = (bf16[2,928,128]{2,1,0:T(8,128)(2,1)}, bf16[2,928,128]{2,1,0:T(8,128)(2,1)}) custom-call(s32[3]{0:T(128)S(1)} %pad_add_fusion.pos_ref, bf16[8,464,128]{2,1,0:T(8,128)(2,1)S(1)} %all-to-all-done.rows_ref, bf16[928,464]{1,0:T(8,128)(2,1)S(1)} %bitcast.13), custom_call_target="tpu_custom_call" | custom-call | flops 440926208 | bytes 2761728 | tf_op jit(solution)/shard_map/pallas_call | solution.py:61
  25.3 1.2 collective-permute-start
  26.6 1.6 %collective-permute-done.refs_0_ = bf16[2,928,128]{2,1,0:T(8,128)(2,1)S(1)} collective-permute-done((bf16[2,928,128]{2,1,0:T(8,128)(2,1)}, bf16[2,928,128]{2,1,0:T(8,128)(2,1)S(1)}, u32[]{:S(2)}, u32[]{:S(2)}) %collective-permute-start) | collective-permute-done | bytes 475168 | tf_op jit(solution)/shard_map/ppermute | solution.py:270
  28.9 2.1 %shard_map.78 = (f32[960,128]{1,0:T(8,128)S(1)}, bf16[960,128]{1,0:T(8,128)(2,1)}, bf16[960,128]{1,0:T(8,128)(2,1)}, bf16[960,128]{1,0:T(8,128)(2,1)}) custom-call(s32[3]{0:T(128)S(1)} %pad_add_fusion.pos_ref, bf16[8,464,128]{2,1,0:T(8,128)(2,1)S(1)} %all-to-all-done.rows_ref, bf16[928,464]{1,0:T(8,128)(2,1)S(1)} %bitcast.14, ...), custom_call_target="tpu_custom_call" | custom-call | flops 440926208 | bytes 3990528 | tf_op jit(solution)/shard_map/pallas_call | solution.py:61
  31.0 3.6 %all-to-all-start.2 = ((bf16[8,464,128]{2,1,0:T(8,128)(2,1)}), bf16[8,464,128]{2,1,0:T(8,128)(2,1)S(1)}, u32[]{:S(2)}, u32[]{:S(2)}) async-start(bf16[8,464,128]{2,1,0:T(8,128)(2,1)} %shard_map.75), calls=%async_computation.2 | async-start | bytes 1900544 | tf_op jit(solution)/shard_map/all_to_all | solution.py:204
  34.6 1.3 collective-permute-start.2
  35.8 2.5 %collective-permute-start.3 = (bf16[960,128]{1,0:T(8,128)(2,1)}, bf16[960,128]{1,0:T(8,128)(2,1)}, u32[]{:S(2)}, u32[]{:S(2)}) collective-permute-start(bf16[960,128]{1,0:T(8,128)(2,1)} %get-tuple-element.44), channel_id=1, source_target_pairs={{0,16},{1,17},{2,18},{3,19},{4,20},{5,21},{6,22},{7,23},{8,24},{9,... | collective-permute-start | bytes 737288 | tf_op jit(solution)/shard_map/ppermute | solution.py:274
  38.3 1.2 collective-permute-start.4
  39.5 9.0 %all-to-all-done.2.rows_ref = bf16[8,464,128]{2,1,0:T(8,128)(2,1)S(1)} async-done(((bf16[8,464,128]{2,1,0:T(8,128)(2,1)}), bf16[8,464,128]{2,1,0:T(8,128)(2,1)S(1)}, u32[]{:S(2)}, u32[]{:S(2)}) %all-to-all-start.2) | async-done | bytes 950304 | tf_op jit(solution)/shard_map/all_to_all | solution.py:204
  48.5 2.2 %shard_map.79 = (bf16[2,928,128]{2,1,0:T(8,128)(2,1)}, bf16[2,928,128]{2,1,0:T(8,128)(2,1)}) custom-call(s32[3]{0:T(128)S(1)} %pad_add_fusion.pos_ref, bf16[8,464,128]{2,1,0:T(8,128)(2,1)S(1)} %all-to-all-done.2.rows_ref, bf16[928,464]{1,0:T(8,128)(2,1)S(1)} %copy-done), custom_call_target="tpu_custom_call" | custom-call | flops 440926208 | bytes 2761728 | tf_op jit(solution)/shard_map/pallas_call | solution.py:61
  51.6 2.0 %add_convert_fusion.1 = bf16[960,128]{1,0:T(8,128)(2,1)} fusion(bf16[960,128]{1,0:T(8,128)(2,1)} %collective-permute-done.4, bf16[960,128]{1,0:T(8,128)(2,1)} %collective-permute-done.3, f32[960,128]{1,0:T(8,128)S(1)} %get-tuple-element.42, bf16[960,128]{1,0:T(8,128)(2,1)} %collective-permute-done.2), kind=kLoop, calls=%fused_computation.1 | loop fusion | flops 860160 | bytes 1474560 | tf_op jit(solution)/shard_map/convert_element_type | solution.py:285
  53.5 7.3 %all-to-all-start.1 = ((bf16[4,240,128]{2,1,0:T(8,128)(2,1)}), bf16[4,240,128]{2,1,0:T(8,128)(2,1)S(1)}, u32[]{:S(2)}, u32[]{:S(2)}) async-start(bf16[4,240,128]{2,1,0:T(8,128)(2,1)} %bitcast.28), calls=%async_computation.1 | async-start | bytes 491520 | tf_op jit(solution)/shard_map/all_to_all | solution.py:204
  60.9 2.8 %shard_map.80 = (f32[960,128]{1,0:T(8,128)S(1)}, bf16[960,128]{1,0:T(8,128)(2,1)}, bf16[960,128]{1,0:T(8,128)(2,1)}, bf16[960,128]{1,0:T(8,128)(2,1)}) custom-call(s32[3]{0:T(128)S(1)} %pad_add_fusion.pos_ref, bf16[8,464,128]{2,1,0:T(8,128)(2,1)S(1)} %all-to-all-done.2.rows_ref, bf16[928,464]{1,0:T(8,128)(2,1)S(1)} %copy-done, ...), custom_call_target="tpu_custom_call" | custom-call | flops 440926208 | bytes 3990528 | tf_op jit(solution)/shard_map/pallas_call | solution.py:61
  64.4 1.2 collective-permute-start.14
  65.6 2.5 %collective-permute-start.15 = (bf16[960,128]{1,0:T(8,128)(2,1)}, bf16[960,128]{1,0:T(8,128)(2,1)}, u32[]{:S(2)}, u32[]{:S(2)}) collective-permute-start(bf16[960,128]{1,0:T(8,128)(2,1)} %get-tuple-element.60), channel_id=1, source_target_pairs={{0,16},{1,17},{2,18},{3,19},{4,20},{5,21},{6,22},{7,23},{8,24},{9,... | collective-permute-start | bytes 737288 | tf_op jit(solution)/shard_map/ppermute | solution.py:274
  68.1 1.2 collective-permute-start.16
  69.2 1.3 shard_map.81
  70.6 6.8 %all-to-all-start.3 = ((bf16[4,240,128]{2,1,0:T(8,128)(2,1)}), bf16[4,240,128]{2,1,0:T(8,128)(2,1)S(1)}, u32[]{:S(2)}, u32[]{:S(2)}) async-start(bf16[4,240,128]{2,1,0:T(8,128)(2,1)} %get-tuple-element.56), calls=%async_computation.3 | async-start | bytes 491520 | tf_op jit(solution)/shard_map/all_to_all | solution.py:204
  77.4 1.6 %collective-permute-done.15 = bf16[960,128]{1,0:T(8,128)(2,1)} collective-permute-done((bf16[960,128]{1,0:T(8,128)(2,1)}, bf16[960,128]{1,0:T(8,128)(2,1)}, u32[]{:S(2)}, u32[]{:S(2)}) %collective-permute-start.15) | collective-permute-done | bytes 245792 | tf_op jit(solution)/shard_map/ppermute | solution.py:274
  79.0 2.1 %add_convert_fusion = bf16[960,128]{1,0:T(8,128)(2,1)} fusion(bf16[960,128]{1,0:T(8,128)(2,1)} %collective-permute-done.16, bf16[960,128]{1,0:T(8,128)(2,1)} %collective-permute-done.15, f32[960,128]{1,0:T(8,128)} %copy-done.5, bf16[960,128]{1,0:T(8,128)(2,1)} %collective-permute-done.14), kind=kLoop, calls=%fused_computation | loop fusion | flops 860160 | bytes 1474560 | tf_op jit(solution)/shard_map/convert_element_type | solution.py:285
  81.1 4.8 %all-to-all-done.3 = bf16[4,240,128]{2,1,0:T(8,128)(2,1)S(1)} async-done(((bf16[4,240,128]{2,1,0:T(8,128)(2,1)}), bf16[4,240,128]{2,1,0:T(8,128)(2,1)S(1)}, u32[]{:S(2)}, u32[]{:S(2)}) %all-to-all-start.3) | async-done | bytes 245792 | tf_op jit(solution)/shard_map/all_to_all | solution.py:204
  86.0 3.4 %all-to-all-start.5 = ((bf16[4,240,128]{2,1,0:T(8,128)(2,1)}), bf16[4,240,128]{2,1,0:T(8,128)(2,1)S(1)}, u32[]{:S(2)}, u32[]{:S(2)}) async-start(bf16[4,240,128]{2,1,0:T(8,128)(2,1)} %bitcast.29), calls=%async_computation.5 | async-start | bytes 491520 | tf_op jit(solution)/shard_map/all_to_all | solution.py:204
  89.8 2.2 %collective-permute-start.8 = (bf16[960,128]{1,0:T(8,128)(2,1)S(1)}, bf16[960,128]{1,0:T(8,128)(2,1)}, u32[]{:S(2)}, u32[]{:S(2)}) collective-permute-start(bf16[960,128]{1,0:T(8,128)(2,1)S(1)} %bitcast.22), channel_id=1, source_target_pairs={{0,16},{1,17},{2,18},{3,19},{4,20},{5,21},{6,22},{7,23},{8,24},{9,... | collective-permute-start | bytes 737288 | tf_op jit(solution)/shard_map/ppermute | solution.py:274
  92.3 5.0 %all-to-all-done.5.arrived_ref = bf16[4,240,128]{2,1,0:T(8,128)(2,1)S(1)} async-done(((bf16[4,240,128]{2,1,0:T(8,128)(2,1)}), bf16[4,240,128]{2,1,0:T(8,128)(2,1)S(1)}, u32[]{:S(2)}, u32[]{:S(2)}) %all-to-all-start.5) | async-done | bytes 245792 | tf_op jit(solution)/shard_map/all_to_all | solution.py:204
  97.2 1.3 shard_map.84
  98.6 3.4 %all-to-all-start.6 = ((bf16[4,240,128]{2,1,0:T(8,128)(2,1)}), bf16[4,240,128]{2,1,0:T(8,128)(2,1)S(1)}, u32[]{:S(2)}, u32[]{:S(2)}) async-start(bf16[4,240,128]{2,1,0:T(8,128)(2,1)} %shard_map.84), calls=%async_computation.6 | async-start | bytes 491520 | tf_op jit(solution)/shard_map/all_to_all | solution.py:204
  102.0 4.6 %collective-permute-start.10 = (bf16[960,128]{1,0:T(8,128)(2,1)S(1)}, bf16[960,128]{1,0:T(8,128)(2,1)S(1)}, u32[]{:S(2)}, u32[]{:S(2)}) collective-permute-start(bf16[960,128]{1,0:T(8,128)(2,1)S(1)} %bitcast.24), channel_id=1, source_target_pairs={{0,1},{1,0},{2,3},{3,2},{4,5},{5,4},{6,7},{7,6},{8,9},{9,8},{10,11... | collective-permute-start | bytes 737288 | tf_op jit(solution)/shard_map/ppermute | solution.py:270
  109.0 3.5 %shard_map.82 = (bf16[8,464,128]{2,1,0:T(8,128)(2,1)}, bf16[8,928,128]{2,1,0:T(8,128)(2,1)}) custom-call(s32[3]{0:T(128)S(1)} %pad_add_fusion.pos_ref, bf16[960,128]{1,0:T(8,128)(2,1)S(1)} %bitcast.25, bf16[960,128]{1,0:T(8,128)(2,1)} %collective-permute-done.7.refs_1_, bf16[960,128]{1,0:T(8,128)(2,1)} %collective-permute-done.8.refs_2_, ...), custom_call_target="tpu_custom_call" | custom-call | flops 881852416 | bytes 5678080 | tf_op jit(solution)/shard_map/pallas_call | solution.py:61
  112.5 3.9 %all-to-all-start.4 = ((bf16[8,464,128]{2,1,0:T(8,128)(2,1)}), bf16[8,464,128]{2,1,0:T(8,128)(2,1)S(1)}, u32[]{:S(2)}, u32[]{:S(2)}) async-start(bf16[8,464,128]{2,1,0:T(8,128)(2,1)} %get-tuple-element.58), calls=%async_computation.4 | async-start | bytes 1900544 | tf_op jit(solution)/shard_map/all_to_all | solution.py:204
  116.6 1.6 collective-permute-start.18
  118.2 1.2 collective-permute-start.17
  119.4 1.5 copy-done.1
  120.9 2.6 %shard_map.85 = bf16[928,464]{1,0:T(8,128)(2,1)} custom-call(s32[3]{0:T(128)S(1)} %pad_add_fusion.pos_ref, bf16[8,464,128]{2,1,0:T(8,128)(2,1)S(1)} %all-to-all-done.2.rows_ref, bf16[8,928,128]{2,1,0:T(8,128)(2,1)S(1)} %copy-done.1), custom_call_target="tpu_custom_call" | custom-call | flops 881852416 | bytes 3712000 | tf_op jit(solution)/shard_map/pallas_call | solution.py:61
  123.6 4.0 %collective-permute-start.20 = (bf16[960,128]{1,0:T(8,128)(2,1)S(1)}, bf16[960,128]{1,0:T(8,128)(2,1)S(1)}, u32[]{:S(2)}, u32[]{:S(2)}) collective-permute-start(bf16[960,128]{1,0:T(8,128)(2,1)S(1)} %bitcast.19), channel_id=1, source_target_pairs={{0,1},{1,0},{2,3},{3,2},{4,5},{5,4},{6,7},{7,6},{8,9},{9,8},{10,11... | collective-permute-start | bytes 737288 | tf_op jit(solution)/shard_map/ppermute | solution.py:270
  127.6 3.7 %collective-permute-start.23 = (bf16[960,128]{1,0:T(8,128)(2,1)S(1)}, bf16[960,128]{1,0:T(8,128)(2,1)S(1)}, u32[]{:S(2)}, u32[]{:S(2)}) collective-permute-start(bf16[960,128]{1,0:T(8,128)(2,1)S(1)} %collective-permute-done.19.refs_3_), channel_id=1, source_target_pairs={{0,1},{1,0},{2,3},{3,2},{4,5},{5,4},{6,7},{7,6},{8,9},{9,8},{10,11... | collective-permute-start | bytes 737288 | tf_op jit(solution)/shard_map/ppermute | solution.py:270
  133.1 2.9 %shard_map.86 = (bf16[8,464,128]{2,1,0:T(8,128)(2,1)}, bf16[8,928,128]{2,1,0:T(8,128)(2,1)}) custom-call(s32[3]{0:T(128)S(1)} %pad_add_fusion.pos_ref, bf16[960,128]{1,0:T(8,128)(2,1)S(1)} %bitcast.20, bf16[960,128]{1,0:T(8,128)(2,1)S(1)} %collective-permute-done.17.refs_1_, bf16[960,128]{1,0:T(8,128)(2,1)S(1)} %collective-permute-done.18.refs_2_, ...), custom_call_target="tpu_custom_call" | custom-call | flops 881852416 | bytes 5678080 | tf_op jit(solution)/shard_map/pallas_call | solution.py:61
  136.0 5.2 %all-to-all-start.7 = ((bf16[8,464,128]{2,1,0:T(8,128)(2,1)}), bf16[8,464,128]{2,1,0:T(8,128)(2,1)S(1)}, u32[]{:S(2)}, u32[]{:S(2)}) async-start(bf16[8,464,128]{2,1,0:T(8,128)(2,1)} %get-tuple-element.70), calls=%async_computation.7 | async-start | bytes 1900544 | tf_op jit(solution)/shard_map/all_to_all | solution.py:204
  141.2 1.5 copy-done.2
  142.7 2.7 %shard_map.88 = bf16[464,928]{1,0:T(8,128)(2,1)} custom-call(s32[3]{0:T(128)S(1)} %pad_add_fusion.pos_ref, bf16[8,464,128]{2,1,0:T(8,128)(2,1)S(1)} %all-to-all-done.rows_ref, bf16[8,928,128]{2,1,0:T(8,128)(2,1)S(1)} %copy-done.2), custom_call_target="tpu_custom_call" | custom-call | flops 881852416 | bytes 3712000 | tf_op jit(solution)/shard_map/pallas_call | solution.py:61
  145.4 1.3 shard_map.83
  146.7 8.4 %all-to-all-done.7.value_ref = bf16[8,464,128]{2,1,0:T(8,128)(2,1)S(1)} async-done(((bf16[8,464,128]{2,1,0:T(8,128)(2,1)}), bf16[8,464,128]{2,1,0:T(8,128)(2,1)S(1)}, u32[]{:S(2)}, u32[]{:S(2)}) %all-to-all-start.7) | async-done | bytes 950304 | tf_op jit(solution)/shard_map/all_to_all | solution.py:204
  155.1 1.3 shard_map.87
  (51 shorter events, 8.6 us)
Async XLA Ops:
  0.7 0.9 copy-start.6
  1.6 7.9 %copy-start.7 = (bf16[128,464]{0,1:T(8,128)(2,1)S(1)}, bf16[128,464]{0,1:T(8,128)(2,1)}, u32[]{:S(2)}) copy-start(bf16[128,464]{0,1:T(8,128)(2,1)} %param.7) | copy-start | bytes 356356
  3.2 20.0 %all-to-all-start = ((bf16[8,464,128]{2,1,0:T(8,128)(2,1)}), bf16[8,464,128]{2,1,0:T(8,128)(2,1)S(1)}, u32[]{:S(2)}, u32[]{:S(2)}) async-start(bf16[8,464,128]{2,1,0:T(8,128)(2,1)} %shard_map.76), calls=%async_computation | async-start | bytes 1900544 | tf_op jit(solution)/shard_map/all_to_all | solution.py:204
  9.5 3.3 %copy-start = (bf16[928,464]{1,0:T(8,128)(2,1)S(1)}, bf16[928,464]{1,0:T(8,128)(2,1)}, u32[]{:S(2)}) copy-start(bf16[928,464]{1,0:T(8,128)(2,1)} %weight_ref.3) | copy-start | bytes 2583556
  25.3 2.9 %collective-permute-start = (bf16[2,928,128]{2,1,0:T(8,128)(2,1)}, bf16[2,928,128]{2,1,0:T(8,128)(2,1)S(1)}, u32[]{:S(2)}, u32[]{:S(2)}) collective-permute-start(bf16[2,928,128]{2,1,0:T(8,128)(2,1)} %get-tuple-element.40), channel_id=1, source_target_pairs={{0,1},{1,0},{2,3},{3,2},{4,5},{5,4},{6,7},{7,6},{8,9},{9,8},{10,11... | collective-permute-start | bytes 1425416 | tf_op jit(solution)/shard_map/ppermute | solution.py:270
  26.5 2.4 %collective-permute-start.1 = (bf16[2,928,128]{2,1,0:T(8,128)(2,1)}, bf16[2,928,128]{2,1,0:T(8,128)(2,1)S(1)}, u32[]{:S(2)}, u32[]{:S(2)}) collective-permute-start(bf16[2,928,128]{2,1,0:T(8,128)(2,1)} %get-tuple-element.41), channel_id=1, source_target_pairs={{0,1},{1,0},{2,3},{3,2},{4,5},{5,4},{6,7},{7,6},{8,9},{9,8},{10,11... | collective-permute-start | bytes 1425416 | tf_op jit(solution)/shard_map/ppermute | solution.py:270
  31.0 17.5 %all-to-all-start.2 = ((bf16[8,464,128]{2,1,0:T(8,128)(2,1)}), bf16[8,464,128]{2,1,0:T(8,128)(2,1)S(1)}, u32[]{:S(2)}, u32[]{:S(2)}) async-start(bf16[8,464,128]{2,1,0:T(8,128)(2,1)} %shard_map.75), calls=%async_computation.2 | async-start | bytes 1900544 | tf_op jit(solution)/shard_map/all_to_all | solution.py:204
  34.6 17.0 %collective-permute-start.2 = (bf16[960,128]{1,0:T(8,128)(2,1)}, bf16[960,128]{1,0:T(8,128)(2,1)}, u32[]{:S(2)}, u32[]{:S(2)}) collective-permute-start(bf16[960,128]{1,0:T(8,128)(2,1)} %get-tuple-element.43), channel_id=1, source_target_pairs={{0,8},{1,9},{2,10},{3,11},{4,12},{5,13},{6,14},{7,15},{8,16},{9,17... | collective-permute-start | bytes 737288 | tf_op jit(solution)/shard_map/ppermute | solution.py:274
  35.8 15.7 %collective-permute-start.3 = (bf16[960,128]{1,0:T(8,128)(2,1)}, bf16[960,128]{1,0:T(8,128)(2,1)}, u32[]{:S(2)}, u32[]{:S(2)}) collective-permute-start(bf16[960,128]{1,0:T(8,128)(2,1)} %get-tuple-element.44), channel_id=1, source_target_pairs={{0,16},{1,17},{2,18},{3,19},{4,20},{5,21},{6,22},{7,23},{8,24},{9,... | collective-permute-start | bytes 737288 | tf_op jit(solution)/shard_map/ppermute | solution.py:274
  38.3 13.3 %collective-permute-start.4 = (bf16[960,128]{1,0:T(8,128)(2,1)}, bf16[960,128]{1,0:T(8,128)(2,1)}, u32[]{:S(2)}, u32[]{:S(2)}) collective-permute-start(bf16[960,128]{1,0:T(8,128)(2,1)} %get-tuple-element.45), channel_id=1, source_target_pairs={{0,24},{1,25},{2,26},{3,27},{4,28},{5,29},{6,30},{7,31},{8,0},{9,1... | collective-permute-start | bytes 737288 | tf_op jit(solution)/shard_map/ppermute | solution.py:274
  50.7 10.2 %collective-permute-start.5 = (bf16[2,928,128]{2,1,0:T(8,128)(2,1)}, bf16[2,928,128]{2,1,0:T(8,128)(2,1)}, u32[]{:S(2)}, u32[]{:S(2)}) collective-permute-start(bf16[2,928,128]{2,1,0:T(8,128)(2,1)} %get-tuple-element.52), channel_id=1, source_target_pairs={{0,1},{1,0},{2,3},{3,2},{4,5},{5,4},{6,7},{7,6},{8,9},{9,8},{10,11... | collective-permute-start | bytes 1425416 | tf_op jit(solution)/shard_map/ppermute | solution.py:270
  51.5 9.4 %collective-permute-start.6 = (bf16[2,928,128]{2,1,0:T(8,128)(2,1)}, bf16[2,928,128]{2,1,0:T(8,128)(2,1)}, u32[]{:S(2)}, u32[]{:S(2)}) collective-permute-start(bf16[2,928,128]{2,1,0:T(8,128)(2,1)} %get-tuple-element.53), channel_id=1, source_target_pairs={{0,1},{1,0},{2,3},{3,2},{4,5},{5,4},{6,7},{7,6},{8,9},{9,8},{10,11... | collective-permute-start | bytes 1425416 | tf_op jit(solution)/shard_map/ppermute | solution.py:270
  53.5 15.7 %all-to-all-start.1 = ((bf16[4,240,128]{2,1,0:T(8,128)(2,1)}), bf16[4,240,128]{2,1,0:T(8,128)(2,1)S(1)}, u32[]{:S(2)}, u32[]{:S(2)}) async-start(bf16[4,240,128]{2,1,0:T(8,128)(2,1)} %bitcast.28), calls=%async_computation.1 | async-start | bytes 491520 | tf_op jit(solution)/shard_map/all_to_all | solution.py:204
  63.6 0.8 copy-start.5
  64.4 13.0 %collective-permute-start.14 = (bf16[960,128]{1,0:T(8,128)(2,1)}, bf16[960,128]{1,0:T(8,128)(2,1)}, u32[]{:S(2)}, u32[]{:S(2)}) collective-permute-start(bf16[960,128]{1,0:T(8,128)(2,1)} %get-tuple-element.59), channel_id=1, source_target_pairs={{0,8},{1,9},{2,10},{3,11},{4,12},{5,13},{6,14},{7,15},{8,16},{9,17... | collective-permute-start | bytes 737288 | tf_op jit(solution)/shard_map/ppermute | solution.py:274
  65.6 13.4 %collective-permute-start.15 = (bf16[960,128]{1,0:T(8,128)(2,1)}, bf16[960,128]{1,0:T(8,128)(2,1)}, u32[]{:S(2)}, u32[]{:S(2)}) collective-permute-start(bf16[960,128]{1,0:T(8,128)(2,1)} %get-tuple-element.60), channel_id=1, source_target_pairs={{0,16},{1,17},{2,18},{3,19},{4,20},{5,21},{6,22},{7,23},{8,24},{9,... | collective-permute-start | bytes 737288 | tf_op jit(solution)/shard_map/ppermute | solution.py:274
  68.1 10.9 %collective-permute-start.16 = (bf16[960,128]{1,0:T(8,128)(2,1)}, bf16[960,128]{1,0:T(8,128)(2,1)}, u32[]{:S(2)}, u32[]{:S(2)}) collective-permute-start(bf16[960,128]{1,0:T(8,128)(2,1)} %get-tuple-element.61), channel_id=1, source_target_pairs={{0,24},{1,25},{2,26},{3,27},{4,28},{5,29},{6,30},{7,31},{8,0},{9,1... | collective-permute-start | bytes 737288 | tf_op jit(solution)/shard_map/ppermute | solution.py:274
  70.6 38.4 %copy-start.4 = (bf16[928,464]{0,1:T(8,128)(2,1)S(1)}, bf16[928,464]{0,1:T(8,128)(2,1)}, u32[]{:S(2)}) copy-start(bf16[928,464]{0,1:T(8,128)(2,1)} %copy.9) | copy-start | bytes 2583556
  70.6 15.4 %all-to-all-start.3 = ((bf16[4,240,128]{2,1,0:T(8,128)(2,1)}), bf16[4,240,128]{2,1,0:T(8,128)(2,1)S(1)}, u32[]{:S(2)}, u32[]{:S(2)}) async-start(bf16[4,240,128]{2,1,0:T(8,128)(2,1)} %get-tuple-element.56), calls=%async_computation.3 | async-start | bytes 491520 | tf_op jit(solution)/shard_map/all_to_all | solution.py:204
  86.0 11.2 %all-to-all-start.5 = ((bf16[4,240,128]{2,1,0:T(8,128)(2,1)}), bf16[4,240,128]{2,1,0:T(8,128)(2,1)S(1)}, u32[]{:S(2)}, u32[]{:S(2)}) async-start(bf16[4,240,128]{2,1,0:T(8,128)(2,1)} %bitcast.29), calls=%async_computation.5 | async-start | bytes 491520 | tf_op jit(solution)/shard_map/all_to_all | solution.py:204
  89.4 17.2 %collective-permute-start.9 = (bf16[960,128]{1,0:T(8,128)(2,1)S(1)}, bf16[960,128]{1,0:T(8,128)(2,1)}, u32[]{:S(2)}, u32[]{:S(2)}) collective-permute-start(bf16[960,128]{1,0:T(8,128)(2,1)S(1)} %bitcast.21), channel_id=1, source_target_pairs={{0,8},{1,9},{2,10},{3,11},{4,12},{5,13},{6,14},{7,15},{8,16},{9,17... | collective-permute-start | bytes 737288 | tf_op jit(solution)/shard_map/ppermute | solution.py:274
  89.8 16.9 %collective-permute-start.8 = (bf16[960,128]{1,0:T(8,128)(2,1)S(1)}, bf16[960,128]{1,0:T(8,128)(2,1)}, u32[]{:S(2)}, u32[]{:S(2)}) collective-permute-start(bf16[960,128]{1,0:T(8,128)(2,1)S(1)} %bitcast.22), channel_id=1, source_target_pairs={{0,16},{1,17},{2,18},{3,19},{4,20},{5,21},{6,22},{7,23},{8,24},{9,... | collective-permute-start | bytes 737288 | tf_op jit(solution)/shard_map/ppermute | solution.py:274
  92.0 15.1 %collective-permute-start.7 = (bf16[960,128]{1,0:T(8,128)(2,1)S(1)}, bf16[960,128]{1,0:T(8,128)(2,1)}, u32[]{:S(2)}, u32[]{:S(2)}) collective-permute-start(bf16[960,128]{1,0:T(8,128)(2,1)S(1)} %bitcast.23), channel_id=1, source_target_pairs={{0,24},{1,25},{2,26},{3,27},{4,28},{5,29},{6,30},{7,31},{8,0},{9,1... | collective-permute-start | bytes 737288 | tf_op jit(solution)/shard_map/ppermute | solution.py:274
  98.6 13.9 %all-to-all-start.6 = ((bf16[4,240,128]{2,1,0:T(8,128)(2,1)}), bf16[4,240,128]{2,1,0:T(8,128)(2,1)S(1)}, u32[]{:S(2)}, u32[]{:S(2)}) async-start(bf16[4,240,128]{2,1,0:T(8,128)(2,1)} %shard_map.84), calls=%async_computation.6 | async-start | bytes 491520 | tf_op jit(solution)/shard_map/all_to_all | solution.py:204
  102.0 5.7 %collective-permute-start.10 = (bf16[960,128]{1,0:T(8,128)(2,1)S(1)}, bf16[960,128]{1,0:T(8,128)(2,1)S(1)}, u32[]{:S(2)}, u32[]{:S(2)}) collective-permute-start(bf16[960,128]{1,0:T(8,128)(2,1)S(1)} %bitcast.24), channel_id=1, source_target_pairs={{0,1},{1,0},{2,3},{3,2},{4,5},{5,4},{6,7},{7,6},{8,9},{9,8},{10,11... | collective-permute-start | bytes 737288 | tf_op jit(solution)/shard_map/ppermute | solution.py:270
  106.6 1.7 %collective-permute-start.13 = (bf16[960,128]{1,0:T(8,128)(2,1)}, bf16[960,128]{1,0:T(8,128)(2,1)S(1)}, u32[]{:S(2)}, u32[]{:S(2)}) collective-permute-start(bf16[960,128]{1,0:T(8,128)(2,1)} %collective-permute-done.9.refs_3_), channel_id=1, source_target_pairs={{0,1},{1,0},{2,3},{3,2},{4,5},{5,4},{6,7},{7,6},{8,9},{9,8},{10,11... | collective-permute-start | bytes 737288 | tf_op jit(solution)/shard_map/ppermute | solution.py:270
  106.7 2.0 %collective-permute-start.12 = (bf16[960,128]{1,0:T(8,128)(2,1)}, bf16[960,128]{1,0:T(8,128)(2,1)S(1)}, u32[]{:S(2)}, u32[]{:S(2)}) collective-permute-start(bf16[960,128]{1,0:T(8,128)(2,1)} %collective-permute-done.8.refs_2_), channel_id=1, source_target_pairs={{0,1},{1,0},{2,3},{3,2},{4,5},{5,4},{6,7},{7,6},{8,9},{9,8},{10,11... | collective-permute-start | bytes 737288 | tf_op jit(solution)/shard_map/ppermute | solution.py:270
  107.1 1.9 %collective-permute-start.11 = (bf16[960,128]{1,0:T(8,128)(2,1)}, bf16[960,128]{1,0:T(8,128)(2,1)S(1)}, u32[]{:S(2)}, u32[]{:S(2)}) collective-permute-start(bf16[960,128]{1,0:T(8,128)(2,1)} %collective-permute-done.7.refs_1_), channel_id=1, source_target_pairs={{0,1},{1,0},{2,3},{3,2},{4,5},{5,4},{6,7},{7,6},{8,9},{9,8},{10,11... | collective-permute-start | bytes 737288 | tf_op jit(solution)/shard_map/ppermute | solution.py:270
  112.5 23.5 %all-to-all-start.4 = ((bf16[8,464,128]{2,1,0:T(8,128)(2,1)}), bf16[8,464,128]{2,1,0:T(8,128)(2,1)S(1)}, u32[]{:S(2)}, u32[]{:S(2)}) async-start(bf16[8,464,128]{2,1,0:T(8,128)(2,1)} %get-tuple-element.58), calls=%async_computation.4 | async-start | bytes 1900544 | tf_op jit(solution)/shard_map/all_to_all | solution.py:204
  116.4 11.2 %collective-permute-start.19 = (bf16[960,128]{1,0:T(8,128)(2,1)S(1)}, bf16[960,128]{1,0:T(8,128)(2,1)S(1)}, u32[]{:S(2)}, u32[]{:S(2)}) collective-permute-start(bf16[960,128]{1,0:T(8,128)(2,1)S(1)} %bitcast.16), channel_id=1, source_target_pairs={{0,8},{1,9},{2,10},{3,11},{4,12},{5,13},{6,14},{7,15},{8,16},{9,17... | collective-permute-start | bytes 737288 | tf_op jit(solution)/shard_map/ppermute | solution.py:274
  116.6 14.6 %collective-permute-start.18 = (bf16[960,128]{1,0:T(8,128)(2,1)S(1)}, bf16[960,128]{1,0:T(8,128)(2,1)S(1)}, u32[]{:S(2)}, u32[]{:S(2)}) collective-permute-start(bf16[960,128]{1,0:T(8,128)(2,1)S(1)} %bitcast.17), channel_id=1, source_target_pairs={{0,16},{1,17},{2,18},{3,19},{4,20},{5,21},{6,22},{7,23},{8,24},{9,... | collective-permute-start | bytes 737288 | tf_op jit(solution)/shard_map/ppermute | solution.py:274
  118.2 13.1 %collective-permute-start.17 = (bf16[960,128]{1,0:T(8,128)(2,1)S(1)}, bf16[960,128]{1,0:T(8,128)(2,1)S(1)}, u32[]{:S(2)}, u32[]{:S(2)}) collective-permute-start(bf16[960,128]{1,0:T(8,128)(2,1)S(1)} %bitcast.18), channel_id=1, source_target_pairs={{0,24},{1,25},{2,26},{3,27},{4,28},{5,29},{6,30},{7,31},{8,0},{9,1... | collective-permute-start | bytes 737288 | tf_op jit(solution)/shard_map/ppermute | solution.py:274
  119.4 1.5 copy-start.1
  120.9 12.2 %copy-start.3 = (bf16[464,928]{1,0:T(8,128)(2,1)S(1)}, bf16[464,928]{1,0:T(8,128)(2,1)}, u32[]{:S(2)}) copy-start(bf16[464,928]{1,0:T(8,128)(2,1)} %refs_8_.1) | copy-start | bytes 2583556
  123.6 8.3 %collective-permute-start.20 = (bf16[960,128]{1,0:T(8,128)(2,1)S(1)}, bf16[960,128]{1,0:T(8,128)(2,1)S(1)}, u32[]{:S(2)}, u32[]{:S(2)}) collective-permute-start(bf16[960,128]{1,0:T(8,128)(2,1)S(1)} %bitcast.19), channel_id=1, source_target_pairs={{0,1},{1,0},{2,3},{3,2},{4,5},{5,4},{6,7},{7,6},{8,9},{9,8},{10,11... | collective-permute-start | bytes 737288 | tf_op jit(solution)/shard_map/ppermute | solution.py:270
  127.6 4.8 %collective-permute-start.23 = (bf16[960,128]{1,0:T(8,128)(2,1)S(1)}, bf16[960,128]{1,0:T(8,128)(2,1)S(1)}, u32[]{:S(2)}, u32[]{:S(2)}) collective-permute-start(bf16[960,128]{1,0:T(8,128)(2,1)S(1)} %collective-permute-done.19.refs_3_), channel_id=1, source_target_pairs={{0,1},{1,0},{2,3},{3,2},{4,5},{5,4},{6,7},{7,6},{8,9},{9,8},{10,11... | collective-permute-start | bytes 737288 | tf_op jit(solution)/shard_map/ppermute | solution.py:270
  131.2 1.5 collective-permute-start.22
  131.3 1.9 %collective-permute-start.21 = (bf16[960,128]{1,0:T(8,128)(2,1)S(1)}, bf16[960,128]{1,0:T(8,128)(2,1)S(1)}, u32[]{:S(2)}, u32[]{:S(2)}) collective-permute-start(bf16[960,128]{1,0:T(8,128)(2,1)S(1)} %collective-permute-done.17.refs_1_), channel_id=1, source_target_pairs={{0,1},{1,0},{2,3},{3,2},{4,5},{5,4},{6,7},{7,6},{8,9},{9,8},{10,11... | collective-permute-start | bytes 737288 | tf_op jit(solution)/shard_map/ppermute | solution.py:270
  136.0 19.1 %all-to-all-start.7 = ((bf16[8,464,128]{2,1,0:T(8,128)(2,1)}), bf16[8,464,128]{2,1,0:T(8,128)(2,1)S(1)}, u32[]{:S(2)}, u32[]{:S(2)}) async-start(bf16[8,464,128]{2,1,0:T(8,128)(2,1)} %get-tuple-element.70), calls=%async_computation.7 | async-start | bytes 1900544 | tf_op jit(solution)/shard_map/all_to_all | solution.py:204
  141.2 1.5 copy-start.2

commit v12 on v11

--- a/solution.py
+++ b/solution.py
@@ -58,11 +58,12 @@
     moved = sum(math.prod(o.shape) * o.dtype.itemsize for o in [*operands, *outs])
     vmem = pl.BlockSpec(memory_space=pltpu.VMEM)
     hbm = pl.BlockSpec(memory_space=pltpu.HBM)
+    anywhere = pl.BlockSpec(memory_space=pl.ANY)
     return pl.pallas_call(
         kernel,
         out_shape=[pltpu.HBM(o.shape, o.dtype) if i in far else o for i, o in enumerate(outs)],
         in_specs=[pl.BlockSpec(memory_space=pltpu.SMEM)]
-        + [hbm if i in far_in else vmem for i in range(len(operands))],
+        + [anywhere if i in far_in else vmem for i in range(len(operands))],
         out_specs=[hbm if i in far else vmem for i in range(len(outs))],
         scratch_shapes=scratch,
         compiler_params=pltpu.CompilerParams(vmem_limit_bytes=16 * 1024 * 1024),
@@ -118,15 +119,22 @@
 
     def kernel(pos_ref, rows_ref, weight_ref, *refs):
         arrived, keep_ref = refs[:PIECES], refs[PIECES]
-        sent, held_ref, sems = refs[PIECES + 1 : -2], refs[-2], refs[-1]
+        sent, (held_ref, sems, near_ref, near_sems) = refs[PIECES + 1 : -4], refs[-4:]
+        arriving = [
+            pltpu.make_async_copy(arrived[p], near_ref.at[p], near_sems.at[p])
+            for p in range(PIECES)
+        ]
+        for copy in arriving[::-1]:
+            copy.start()
         rows = half_of(rows_ref, pos_ref[1], pos_ref[0])
         copies = []
         for pair in (1, 0):
             here = rows[:, pair * 2 * LANES : (pair + 1) * 2 * LANES]
             product = dot(weight_ref[...], here, PLAIN)
+            arriving[pair].wait()
             for i in range(2):
                 d = pair * 2 + i
-                other = arrived[d * PIECES // X][d % (X // PIECES)]
+                other = near_ref[pair, i]
                 total = block(product, i) + other.astype(F32)
                 if d == 0:
                     keep_ref[:depth] = total
@@ -144,9 +152,12 @@
     part = shaped((padded, LANES), BF)
     outs = [shaped((padded, LANES), F32)] + [part] * (X - 1)
     scratch = staged(shaped((X - 1,) + part.shape, BF))
+    scratch += staged(shaped((PIECES,) + arrived[0].shape, BF))
     flops = 2 * depth * width * X * LANES
     operands = [rows, weight, *arrived]
-    keep, *sent = kernel_call(kernel, outs, flops, pos, operands, scratch, range(1, X))
+    keep, *sent = kernel_call(
+        kernel, outs, flops, pos, operands, scratch, range(1, X), range(2, 2 + PIECES)
+    )
     return keep, sent
 
 

time: 157 us -> 159 us (1.013)
  Pallas kernels: 29.4 us -> 31 us
    pallas_call x14, Pallas kernels: 29.4 us -> 31 us  [kernel_call(): pl.pallas_call(kernel, out_shape=[pltpu.HBM(o.shape, o.dtype) if i in far...]
where the time goes in v12:
time: 159 us; the launch traced here: 158 us
  starting transfers between devices  71.3 us (45%)
  waiting for transfers between devices  42.9 us (27%)
  Pallas kernels  31 us (19%)
  local copies, waits for them, and re-layouts  7.77 us (5%)
  other arithmetic  4.2 us (3%)
    all_to_all x8, starting transfers between devices, exchange(): return lax.all_to_all(value, axis, 0, 0, axis_index_groups=groups)  39.8 us
    all_to_all x8, waiting for transfers between devices, exchange(): return lax.all_to_all(value, axis, 0, 0, axis_index_groups=groups)  36 us
    pallas_call x14, Pallas kernels, kernel_call(): pl.pallas_call(kernel, out_shape=[pltpu.HBM(o.shape, o.dtype) if i in far...  31 us
    ppermute x12, starting transfers between devices, swap_cores(): return lax.ppermute(value, 'rep', rep_pairs(0, 0, 1))  15.9 us
    ppermute x12, starting transfers between devices, move_x(): return lax.ppermute(value, 'rep', rep_pairs(d, 0, 0))  15.6 us
    unnamed x18, local copies, waits for them, and re-layouts  7.77 us
    ppermute x12, waiting for transfers between devices, swap_cores(): return lax.ppermute(value, 'rep', rep_pairs(0, 0, 1))  5.26 us
    convert_element_type x2, other arithmetic, sum_x(): return keep.astype(BF)  4.12 us
  transfers between devices with their start and end apart: 32, of which 15 were waited for; matrix products, arithmetic and copies ran while one was open for 5% of the time, Pallas kernels for 14%

profile of v12, /device:TPU:1, one launch (start us, length us, event | category | flops | bytes accessed | tf_op | source)
XLA Modules:
  0.0 158.0 jit_solution(5316595828763365583)
XLA Ops:
  1.6 1.5 shard_map.76
  3.2 6.4 %all-to-all-start = ((bf16[8,464,128]{2,1,0:T(8,128)(2,1)}), bf16[8,464,128]{2,1,0:T(8,128)(2,1)S(1)}, u32[]{:S(2)}, u32[]{:S(2)}) async-start(bf16[8,464,128]{2,1,0:T(8,128)(2,1)} %shard_map.76), calls=%async_computation | async-start | bytes 1900544 | tf_op jit(solution)/shard_map/all_to_all | solution.py:215
  9.6 1.6 %shard_map.75 = bf16[8,464,128]{2,1,0:T(8,128)(2,1)} custom-call(s32[3]{0:T(128)S(1)} %pad_add_fusion.pos_ref, bf16[464,128]{1,0:T(8,128)(2,1)S(1)} %bitcast.27), custom_call_target="tpu_custom_call" | custom-call | bytes 1069056 | tf_op jit(solution)/shard_map/pallas_call | solution.py:62
  11.1 1.6 %copy.8 = bf16[464,928]{0,1:T(8,128)(2,1)S(1)} copy(bf16[464,928]{1,0:T(8,128)(2,1)} %refs_8_.1) | data formatting | bytes 1722368 | tf_op args[1]
  12.8 1.4 copy.9
  14.2 8.9 %all-to-all-done.rows_ref = bf16[8,464,128]{2,1,0:T(8,128)(2,1)S(1)} async-done(((bf16[8,464,128]{2,1,0:T(8,128)(2,1)}), bf16[8,464,128]{2,1,0:T(8,128)(2,1)S(1)}, u32[]{:S(2)}, u32[]{:S(2)}) %all-to-all-start) | async-done | bytes 950304 | tf_op jit(solution)/shard_map/all_to_all | solution.py:215
  23.1 2.2 %shard_map.77 = (bf16[2,928,128]{2,1,0:T(8,128)(2,1)}, bf16[2,928,128]{2,1,0:T(8,128)(2,1)}) custom-call(s32[3]{0:T(128)S(1)} %pad_add_fusion.pos_ref, bf16[8,464,128]{2,1,0:T(8,128)(2,1)S(1)} %all-to-all-done.rows_ref, bf16[928,464]{1,0:T(8,128)(2,1)S(1)} %bitcast.13), custom_call_target="tpu_custom_call" | custom-call | flops 440926208 | bytes 2761728 | tf_op jit(solution)/shard_map/pallas_call | solution.py:62
  25.3 1.2 collective-permute-start
  26.6 1.6 collective-permute-done.refs_0_
  28.9 3.3 %shard_map.78 = (f32[960,128]{1,0:T(8,128)S(1)}, bf16[960,128]{1,0:T(8,128)(2,1)}, bf16[960,128]{1,0:T(8,128)(2,1)}, bf16[960,128]{1,0:T(8,128)(2,1)}) custom-call(s32[3]{0:T(128)S(1)} %pad_add_fusion.pos_ref, bf16[8,464,128]{2,1,0:T(8,128)(2,1)S(1)} %all-to-all-done.rows_ref, bf16[928,464]{1,0:T(8,128)(2,1)S(1)} %bitcast.14, ...), custom_call_target="tpu_custom_call" | custom-call | flops 440926208 | bytes 3990528 | tf_op jit(solution)/shard_map/pallas_call | solution.py:62
  32.2 3.6 %all-to-all-start.2 = ((bf16[8,464,128]{2,1,0:T(8,128)(2,1)}), bf16[8,464,128]{2,1,0:T(8,128)(2,1)S(1)}, u32[]{:S(2)}, u32[]{:S(2)}) async-start(bf16[8,464,128]{2,1,0:T(8,128)(2,1)} %shard_map.75), calls=%async_computation.2 | async-start | bytes 1900544 | tf_op jit(solution)/shard_map/all_to_all | solution.py:215
  35.8 1.3 collective-permute-start.2
  37.1 2.5 %collective-permute-start.3 = (bf16[960,128]{1,0:T(8,128)(2,1)}, bf16[960,128]{1,0:T(8,128)(2,1)}, u32[]{:S(2)}, u32[]{:S(2)}) collective-permute-start(bf16[960,128]{1,0:T(8,128)(2,1)} %get-tuple-element.44), channel_id=1, source_target_pairs={{0,16},{1,17},{2,18},{3,19},{4,20},{5,21},{6,22},{7,23},{8,24},{9,... | collective-permute-start | bytes 737288 | tf_op jit(solution)/shard_map/ppermute | solution.py:285
  39.5 1.2 collective-permute-start.4
  40.7 9.0 %all-to-all-done.2.rows_ref = bf16[8,464,128]{2,1,0:T(8,128)(2,1)S(1)} async-done(((bf16[8,464,128]{2,1,0:T(8,128)(2,1)}), bf16[8,464,128]{2,1,0:T(8,128)(2,1)S(1)}, u32[]{:S(2)}, u32[]{:S(2)}) %all-to-all-start.2) | async-done | bytes 950304 | tf_op jit(solution)/shard_map/all_to_all | solution.py:215
  49.7 2.2 %shard_map.79 = (bf16[2,928,128]{2,1,0:T(8,128)(2,1)}, bf16[2,928,128]{2,1,0:T(8,128)(2,1)}) custom-call(s32[3]{0:T(128)S(1)} %pad_add_fusion.pos_ref, bf16[8,464,128]{2,1,0:T(8,128)(2,1)S(1)} %all-to-all-done.2.rows_ref, bf16[928,464]{1,0:T(8,128)(2,1)S(1)} %copy-done), custom_call_target="tpu_custom_call" | custom-call | flops 440926208 | bytes 2761728 | tf_op jit(solution)/shard_map/pallas_call | solution.py:62
  52.8 2.0 %add_convert_fusion.1 = bf16[960,128]{1,0:T(8,128)(2,1)} fusion(bf16[960,128]{1,0:T(8,128)(2,1)} %collective-permute-done.4, bf16[960,128]{1,0:T(8,128)(2,1)} %collective-permute-done.3, f32[960,128]{1,0:T(8,128)S(1)} %get-tuple-element.42, bf16[960,128]{1,0:T(8,128)(2,1)} %collective-permute-done.2), kind=kLoop, calls=%fused_computation.1 | loop fusion | flops 860160 | bytes 1474560 | tf_op jit(solution)/shard_map/convert_element_type | solution.py:296
  54.8 7.3 %all-to-all-start.1 = ((bf16[4,240,128]{2,1,0:T(8,128)(2,1)}), bf16[4,240,128]{2,1,0:T(8,128)(2,1)S(1)}, u32[]{:S(2)}, u32[]{:S(2)}) async-start(bf16[4,240,128]{2,1,0:T(8,128)(2,1)} %bitcast.28), calls=%async_computation.1 | async-start | bytes 491520 | tf_op jit(solution)/shard_map/all_to_all | solution.py:215
  62.1 3.2 %shard_map.80 = (f32[960,128]{1,0:T(8,128)S(1)}, bf16[960,128]{1,0:T(8,128)(2,1)}, bf16[960,128]{1,0:T(8,128)(2,1)}, bf16[960,128]{1,0:T(8,128)(2,1)}) custom-call(s32[3]{0:T(128)S(1)} %pad_add_fusion.pos_ref, bf16[8,464,128]{2,1,0:T(8,128)(2,1)S(1)} %all-to-all-done.2.rows_ref, bf16[928,464]{1,0:T(8,128)(2,1)S(1)} %copy-done, ...), custom_call_target="tpu_custom_call" | custom-call | flops 440926208 | bytes 3990528 | tf_op jit(solution)/shard_map/pallas_call | solution.py:62
  66.0 1.2 collective-permute-start.14
  67.2 2.5 %collective-permute-start.15 = (bf16[960,128]{1,0:T(8,128)(2,1)}, bf16[960,128]{1,0:T(8,128)(2,1)}, u32[]{:S(2)}, u32[]{:S(2)}) collective-permute-start(bf16[960,128]{1,0:T(8,128)(2,1)} %get-tuple-element.60), channel_id=1, source_target_pairs={{0,16},{1,17},{2,18},{3,19},{4,20},{5,21},{6,22},{7,23},{8,24},{9,... | collective-permute-start | bytes 737288 | tf_op jit(solution)/shard_map/ppermute | solution.py:285
  69.7 1.2 collective-permute-start.16
  70.9 1.3 shard_map.81
  72.2 6.8 %all-to-all-start.3 = ((bf16[4,240,128]{2,1,0:T(8,128)(2,1)}), bf16[4,240,128]{2,1,0:T(8,128)(2,1)S(1)}, u32[]{:S(2)}, u32[]{:S(2)}) async-start(bf16[4,240,128]{2,1,0:T(8,128)(2,1)} %get-tuple-element.56), calls=%async_computation.3 | async-start | bytes 491520 | tf_op jit(solution)/shard_map/all_to_all | solution.py:215
  79.0 1.6 %collective-permute-done.15 = bf16[960,128]{1,0:T(8,128)(2,1)} collective-permute-done((bf16[960,128]{1,0:T(8,128)(2,1)}, bf16[960,128]{1,0:T(8,128)(2,1)}, u32[]{:S(2)}, u32[]{:S(2)}) %collective-permute-start.15) | collective-permute-done | bytes 245792 | tf_op jit(solution)/shard_map/ppermute | solution.py:285
  80.6 2.1 %add_convert_fusion = bf16[960,128]{1,0:T(8,128)(2,1)} fusion(bf16[960,128]{1,0:T(8,128)(2,1)} %collective-permute-done.16, bf16[960,128]{1,0:T(8,128)(2,1)} %collective-permute-done.15, f32[960,128]{1,0:T(8,128)} %copy-done.5, bf16[960,128]{1,0:T(8,128)(2,1)} %collective-permute-done.14), kind=kLoop, calls=%fused_computation | loop fusion | flops 860160 | bytes 1474560 | tf_op jit(solution)/shard_map/convert_element_type | solution.py:296
  82.8 4.8 %all-to-all-done.3 = bf16[4,240,128]{2,1,0:T(8,128)(2,1)S(1)} async-done(((bf16[4,240,128]{2,1,0:T(8,128)(2,1)}), bf16[4,240,128]{2,1,0:T(8,128)(2,1)S(1)}, u32[]{:S(2)}, u32[]{:S(2)}) %all-to-all-start.3) | async-done | bytes 245792 | tf_op jit(solution)/shard_map/all_to_all | solution.py:215
  87.6 3.4 %all-to-all-start.5 = ((bf16[4,240,128]{2,1,0:T(8,128)(2,1)}), bf16[4,240,128]{2,1,0:T(8,128)(2,1)S(1)}, u32[]{:S(2)}, u32[]{:S(2)}) async-start(bf16[4,240,128]{2,1,0:T(8,128)(2,1)} %bitcast.29), calls=%async_computation.5 | async-start | bytes 491520 | tf_op jit(solution)/shard_map/all_to_all | solution.py:215
  91.4 2.2 %collective-permute-start.8 = (bf16[960,128]{1,0:T(8,128)(2,1)S(1)}, bf16[960,128]{1,0:T(8,128)(2,1)}, u32[]{:S(2)}, u32[]{:S(2)}) collective-permute-start(bf16[960,128]{1,0:T(8,128)(2,1)S(1)} %bitcast.22), channel_id=1, source_target_pairs={{0,16},{1,17},{2,18},{3,19},{4,20},{5,21},{6,22},{7,23},{8,24},{9,... | collective-permute-start | bytes 737288 | tf_op jit(solution)/shard_map/ppermute | solution.py:285
  94.1 4.8 %all-to-all-done.5.arrived_ref = bf16[4,240,128]{2,1,0:T(8,128)(2,1)S(1)} async-done(((bf16[4,240,128]{2,1,0:T(8,128)(2,1)}), bf16[4,240,128]{2,1,0:T(8,128)(2,1)S(1)}, u32[]{:S(2)}, u32[]{:S(2)}) %all-to-all-start.5) | async-done | bytes 245792 | tf_op jit(solution)/shard_map/all_to_all | solution.py:215
  98.8 1.3 shard_map.84
  100.2 3.4 %all-to-all-start.6 = ((bf16[4,240,128]{2,1,0:T(8,128)(2,1)}), bf16[4,240,128]{2,1,0:T(8,128)(2,1)S(1)}, u32[]{:S(2)}, u32[]{:S(2)}) async-start(bf16[4,240,128]{2,1,0:T(8,128)(2,1)} %shard_map.84), calls=%async_computation.6 | async-start | bytes 491520 | tf_op jit(solution)/shard_map/all_to_all | solution.py:215
  103.6 4.6 %collective-permute-start.10 = (bf16[960,128]{1,0:T(8,128)(2,1)S(1)}, bf16[960,128]{1,0:T(8,128)(2,1)S(1)}, u32[]{:S(2)}, u32[]{:S(2)}) collective-permute-start(bf16[960,128]{1,0:T(8,128)(2,1)S(1)} %bitcast.24), channel_id=1, source_target_pairs={{0,1},{1,0},{2,3},{3,2},{4,5},{5,4},{6,7},{7,6},{8,9},{9,8},{10,11... | collective-permute-start | bytes 737288 | tf_op jit(solution)/shard_map/ppermute | solution.py:281
  110.6 3.5 %shard_map.82 = (bf16[8,464,128]{2,1,0:T(8,128)(2,1)}, bf16[8,928,128]{2,1,0:T(8,128)(2,1)}) custom-call(s32[3]{0:T(128)S(1)} %pad_add_fusion.pos_ref, bf16[960,128]{1,0:T(8,128)(2,1)S(1)} %bitcast.25, bf16[960,128]{1,0:T(8,128)(2,1)} %collective-permute-done.7.refs_1_, bf16[960,128]{1,0:T(8,128)(2,1)} %collective-permute-done.8.refs_2_, ...), custom_call_target="tpu_custom_call" | custom-call | flops 881852416 | bytes 5678080 | tf_op jit(solution)/shard_map/pallas_call | solution.py:62
  114.2 3.9 %all-to-all-start.4 = ((bf16[8,464,128]{2,1,0:T(8,128)(2,1)}), bf16[8,464,128]{2,1,0:T(8,128)(2,1)S(1)}, u32[]{:S(2)}, u32[]{:S(2)}) async-start(bf16[8,464,128]{2,1,0:T(8,128)(2,1)} %get-tuple-element.58), calls=%async_computation.4 | async-start | bytes 1900544 | tf_op jit(solution)/shard_map/all_to_all | solution.py:215
  118.2 1.6 %collective-permute-start.18 = (bf16[960,128]{1,0:T(8,128)(2,1)S(1)}, bf16[960,128]{1,0:T(8,128)(2,1)S(1)}, u32[]{:S(2)}, u32[]{:S(2)}) collective-permute-start(bf16[960,128]{1,0:T(8,128)(2,1)S(1)} %bitcast.17), channel_id=1, source_target_pairs={{0,16},{1,17},{2,18},{3,19},{4,20},{5,21},{6,22},{7,23},{8,24},{9,... | collective-permute-start | bytes 737288 | tf_op jit(solution)/shard_map/ppermute | solution.py:285
  119.9 1.0 collective-permute-start.17
  120.9 1.5 copy-done.1
  122.4 2.7 %shard_map.85 = bf16[928,464]{1,0:T(8,128)(2,1)} custom-call(s32[3]{0:T(128)S(1)} %pad_add_fusion.pos_ref, bf16[8,464,128]{2,1,0:T(8,128)(2,1)S(1)} %all-to-all-done.2.rows_ref, bf16[8,928,128]{2,1,0:T(8,128)(2,1)S(1)} %copy-done.1), custom_call_target="tpu_custom_call" | custom-call | flops 881852416 | bytes 3712000 | tf_op jit(solution)/shard_map/pallas_call | solution.py:62
  125.0 4.1 %collective-permute-start.20 = (bf16[960,128]{1,0:T(8,128)(2,1)S(1)}, bf16[960,128]{1,0:T(8,128)(2,1)S(1)}, u32[]{:S(2)}, u32[]{:S(2)}) collective-permute-start(bf16[960,128]{1,0:T(8,128)(2,1)S(1)} %bitcast.19), channel_id=1, source_target_pairs={{0,1},{1,0},{2,3},{3,2},{4,5},{5,4},{6,7},{7,6},{8,9},{9,8},{10,11... | collective-permute-start | bytes 737288 | tf_op jit(solution)/shard_map/ppermute | solution.py:281
  129.2 3.7 %collective-permute-start.23 = (bf16[960,128]{1,0:T(8,128)(2,1)S(1)}, bf16[960,128]{1,0:T(8,128)(2,1)S(1)}, u32[]{:S(2)}, u32[]{:S(2)}) collective-permute-start(bf16[960,128]{1,0:T(8,128)(2,1)S(1)} %collective-permute-done.19.refs_3_), channel_id=1, source_target_pairs={{0,1},{1,0},{2,3},{3,2},{4,5},{5,4},{6,7},{7,6},{8,9},{9,8},{10,11... | collective-permute-start | bytes 737288 | tf_op jit(solution)/shard_map/ppermute | solution.py:281
  134.7 2.9 %shard_map.86 = (bf16[8,464,128]{2,1,0:T(8,128)(2,1)}, bf16[8,928,128]{2,1,0:T(8,128)(2,1)}) custom-call(s32[3]{0:T(128)S(1)} %pad_add_fusion.pos_ref, bf16[960,128]{1,0:T(8,128)(2,1)S(1)} %bitcast.20, bf16[960,128]{1,0:T(8,128)(2,1)S(1)} %collective-permute-done.17.refs_1_, bf16[960,128]{1,0:T(8,128)(2,1)S(1)} %collective-permute-done.18.refs_2_, ...), custom_call_target="tpu_custom_call" | custom-call | flops 881852416 | bytes 5678080 | tf_op jit(solution)/shard_map/pallas_call | solution.py:62
  137.6 5.2 %all-to-all-start.7 = ((bf16[8,464,128]{2,1,0:T(8,128)(2,1)}), bf16[8,464,128]{2,1,0:T(8,128)(2,1)S(1)}, u32[]{:S(2)}, u32[]{:S(2)}) async-start(bf16[8,464,128]{2,1,0:T(8,128)(2,1)} %get-tuple-element.70), calls=%async_computation.7 | async-start | bytes 1900544 | tf_op jit(solution)/shard_map/all_to_all | solution.py:215
  142.8 1.5 copy-done.2
  144.3 2.7 %shard_map.88 = bf16[464,928]{1,0:T(8,128)(2,1)} custom-call(s32[3]{0:T(128)S(1)} %pad_add_fusion.pos_ref, bf16[8,464,128]{2,1,0:T(8,128)(2,1)S(1)} %all-to-all-done.rows_ref, bf16[8,928,128]{2,1,0:T(8,128)(2,1)S(1)} %copy-done.2), custom_call_target="tpu_custom_call" | custom-call | flops 881852416 | bytes 3712000 | tf_op jit(solution)/shard_map/pallas_call | solution.py:62
  147.0 1.3 shard_map.83
  148.3 8.4 %all-to-all-done.7.value_ref = bf16[8,464,128]{2,1,0:T(8,128)(2,1)S(1)} async-done(((bf16[8,464,128]{2,1,0:T(8,128)(2,1)}), bf16[8,464,128]{2,1,0:T(8,128)(2,1)S(1)}, u32[]{:S(2)}, u32[]{:S(2)}) %all-to-all-start.7) | async-done | bytes 950304 | tf_op jit(solution)/shard_map/all_to_all | solution.py:215
  156.7 1.3 shard_map.87
  (51 shorter events, 8.8 us)
Async XLA Ops:
  0.7 0.9 copy-start.6
  1.6 7.9 %copy-start.7 = (bf16[128,464]{0,1:T(8,128)(2,1)S(1)}, bf16[128,464]{0,1:T(8,128)(2,1)}, u32[]{:S(2)}) copy-start(bf16[128,464]{0,1:T(8,128)(2,1)} %param.7) | copy-start | bytes 356356
  3.2 20.0 %all-to-all-start = ((bf16[8,464,128]{2,1,0:T(8,128)(2,1)}), bf16[8,464,128]{2,1,0:T(8,128)(2,1)S(1)}, u32[]{:S(2)}, u32[]{:S(2)}) async-start(bf16[8,464,128]{2,1,0:T(8,128)(2,1)} %shard_map.76), calls=%async_computation | async-start | bytes 1900544 | tf_op jit(solution)/shard_map/all_to_all | solution.py:215
  9.5 3.3 %copy-start = (bf16[928,464]{1,0:T(8,128)(2,1)S(1)}, bf16[928,464]{1,0:T(8,128)(2,1)}, u32[]{:S(2)}) copy-start(bf16[928,464]{1,0:T(8,128)(2,1)} %weight_ref.3) | copy-start | bytes 2583556
  25.3 2.9 %collective-permute-start = (bf16[2,928,128]{2,1,0:T(8,128)(2,1)}, bf16[2,928,128]{2,1,0:T(8,128)(2,1)S(1)}, u32[]{:S(2)}, u32[]{:S(2)}) collective-permute-start(bf16[2,928,128]{2,1,0:T(8,128)(2,1)} %get-tuple-element.40), channel_id=1, source_target_pairs={{0,1},{1,0},{2,3},{3,2},{4,5},{5,4},{6,7},{7,6},{8,9},{9,8},{10,11... | collective-permute-start | bytes 1425416 | tf_op jit(solution)/shard_map/ppermute | solution.py:281
  26.5 2.4 %collective-permute-start.1 = (bf16[2,928,128]{2,1,0:T(8,128)(2,1)}, bf16[2,928,128]{2,1,0:T(8,128)(2,1)S(1)}, u32[]{:S(2)}, u32[]{:S(2)}) collective-permute-start(bf16[2,928,128]{2,1,0:T(8,128)(2,1)} %get-tuple-element.41), channel_id=1, source_target_pairs={{0,1},{1,0},{2,3},{3,2},{4,5},{5,4},{6,7},{7,6},{8,9},{9,8},{10,11... | collective-permute-start | bytes 1425416 | tf_op jit(solution)/shard_map/ppermute | solution.py:281
  32.2 17.5 %all-to-all-start.2 = ((bf16[8,464,128]{2,1,0:T(8,128)(2,1)}), bf16[8,464,128]{2,1,0:T(8,128)(2,1)S(1)}, u32[]{:S(2)}, u32[]{:S(2)}) async-start(bf16[8,464,128]{2,1,0:T(8,128)(2,1)} %shard_map.75), calls=%async_computation.2 | async-start | bytes 1900544 | tf_op jit(solution)/shard_map/all_to_all | solution.py:215
  35.8 17.0 %collective-permute-start.2 = (bf16[960,128]{1,0:T(8,128)(2,1)}, bf16[960,128]{1,0:T(8,128)(2,1)}, u32[]{:S(2)}, u32[]{:S(2)}) collective-permute-start(bf16[960,128]{1,0:T(8,128)(2,1)} %get-tuple-element.43), channel_id=1, source_target_pairs={{0,8},{1,9},{2,10},{3,11},{4,12},{5,13},{6,14},{7,15},{8,16},{9,17... | collective-permute-start | bytes 737288 | tf_op jit(solution)/shard_map/ppermute | solution.py:285
  37.1 15.7 %collective-permute-start.3 = (bf16[960,128]{1,0:T(8,128)(2,1)}, bf16[960,128]{1,0:T(8,128)(2,1)}, u32[]{:S(2)}, u32[]{:S(2)}) collective-permute-start(bf16[960,128]{1,0:T(8,128)(2,1)} %get-tuple-element.44), channel_id=1, source_target_pairs={{0,16},{1,17},{2,18},{3,19},{4,20},{5,21},{6,22},{7,23},{8,24},{9,... | collective-permute-start | bytes 737288 | tf_op jit(solution)/shard_map/ppermute | solution.py:285
  39.5 13.3 %collective-permute-start.4 = (bf16[960,128]{1,0:T(8,128)(2,1)}, bf16[960,128]{1,0:T(8,128)(2,1)}, u32[]{:S(2)}, u32[]{:S(2)}) collective-permute-start(bf16[960,128]{1,0:T(8,128)(2,1)} %get-tuple-element.45), channel_id=1, source_target_pairs={{0,24},{1,25},{2,26},{3,27},{4,28},{5,29},{6,30},{7,31},{8,0},{9,1... | collective-permute-start | bytes 737288 | tf_op jit(solution)/shard_map/ppermute | solution.py:285
  51.9 10.1 %collective-permute-start.5 = (bf16[2,928,128]{2,1,0:T(8,128)(2,1)}, bf16[2,928,128]{2,1,0:T(8,128)(2,1)}, u32[]{:S(2)}, u32[]{:S(2)}) collective-permute-start(bf16[2,928,128]{2,1,0:T(8,128)(2,1)} %get-tuple-element.52), channel_id=1, source_target_pairs={{0,1},{1,0},{2,3},{3,2},{4,5},{5,4},{6,7},{7,6},{8,9},{9,8},{10,11... | collective-permute-start | bytes 1425416 | tf_op jit(solution)/shard_map/ppermute | solution.py:281
  52.7 9.4 %collective-permute-start.6 = (bf16[2,928,128]{2,1,0:T(8,128)(2,1)}, bf16[2,928,128]{2,1,0:T(8,128)(2,1)}, u32[]{:S(2)}, u32[]{:S(2)}) collective-permute-start(bf16[2,928,128]{2,1,0:T(8,128)(2,1)} %get-tuple-element.53), channel_id=1, source_target_pairs={{0,1},{1,0},{2,3},{3,2},{4,5},{5,4},{6,7},{7,6},{8,9},{9,8},{10,11... | collective-permute-start | bytes 1425416 | tf_op jit(solution)/shard_map/ppermute | solution.py:281
  54.8 16.1 %all-to-all-start.1 = ((bf16[4,240,128]{2,1,0:T(8,128)(2,1)}), bf16[4,240,128]{2,1,0:T(8,128)(2,1)S(1)}, u32[]{:S(2)}, u32[]{:S(2)}) async-start(bf16[4,240,128]{2,1,0:T(8,128)(2,1)} %bitcast.28), calls=%async_computation.1 | async-start | bytes 491520 | tf_op jit(solution)/shard_map/all_to_all | solution.py:215
  65.3 0.8 copy-start.5
  66.0 13.0 %collective-permute-start.14 = (bf16[960,128]{1,0:T(8,128)(2,1)}, bf16[960,128]{1,0:T(8,128)(2,1)}, u32[]{:S(2)}, u32[]{:S(2)}) collective-permute-start(bf16[960,128]{1,0:T(8,128)(2,1)} %get-tuple-element.59), channel_id=1, source_target_pairs={{0,8},{1,9},{2,10},{3,11},{4,12},{5,13},{6,14},{7,15},{8,16},{9,17... | collective-permute-start | bytes 737288 | tf_op jit(solution)/shard_map/ppermute | solution.py:285
  67.2 13.4 %collective-permute-start.15 = (bf16[960,128]{1,0:T(8,128)(2,1)}, bf16[960,128]{1,0:T(8,128)(2,1)}, u32[]{:S(2)}, u32[]{:S(2)}) collective-permute-start(bf16[960,128]{1,0:T(8,128)(2,1)} %get-tuple-element.60), channel_id=1, source_target_pairs={{0,16},{1,17},{2,18},{3,19},{4,20},{5,21},{6,22},{7,23},{8,24},{9,... | collective-permute-start | bytes 737288 | tf_op jit(solution)/shard_map/ppermute | solution.py:285
  69.7 10.9 %collective-permute-start.16 = (bf16[960,128]{1,0:T(8,128)(2,1)}, bf16[960,128]{1,0:T(8,128)(2,1)}, u32[]{:S(2)}, u32[]{:S(2)}) collective-permute-start(bf16[960,128]{1,0:T(8,128)(2,1)} %get-tuple-element.61), channel_id=1, source_target_pairs={{0,24},{1,25},{2,26},{3,27},{4,28},{5,29},{6,30},{7,31},{8,0},{9,1... | collective-permute-start | bytes 737288 | tf_op jit(solution)/shard_map/ppermute | solution.py:285
  72.2 38.4 %copy-start.4 = (bf16[928,464]{0,1:T(8,128)(2,1)S(1)}, bf16[928,464]{0,1:T(8,128)(2,1)}, u32[]{:S(2)}) copy-start(bf16[928,464]{0,1:T(8,128)(2,1)} %copy.9) | copy-start | bytes 2583556
  72.2 15.4 %all-to-all-start.3 = ((bf16[4,240,128]{2,1,0:T(8,128)(2,1)}), bf16[4,240,128]{2,1,0:T(8,128)(2,1)S(1)}, u32[]{:S(2)}, u32[]{:S(2)}) async-start(bf16[4,240,128]{2,1,0:T(8,128)(2,1)} %get-tuple-element.56), calls=%async_computation.3 | async-start | bytes 491520 | tf_op jit(solution)/shard_map/all_to_all | solution.py:215
  87.6 11.2 %all-to-all-start.5 = ((bf16[4,240,128]{2,1,0:T(8,128)(2,1)}), bf16[4,240,128]{2,1,0:T(8,128)(2,1)S(1)}, u32[]{:S(2)}, u32[]{:S(2)}) async-start(bf16[4,240,128]{2,1,0:T(8,128)(2,1)} %bitcast.29), calls=%async_computation.5 | async-start | bytes 491520 | tf_op jit(solution)/shard_map/all_to_all | solution.py:215
  91.0 17.2 %collective-permute-start.9 = (bf16[960,128]{1,0:T(8,128)(2,1)S(1)}, bf16[960,128]{1,0:T(8,128)(2,1)}, u32[]{:S(2)}, u32[]{:S(2)}) collective-permute-start(bf16[960,128]{1,0:T(8,128)(2,1)S(1)} %bitcast.21), channel_id=1, source_target_pairs={{0,8},{1,9},{2,10},{3,11},{4,12},{5,13},{6,14},{7,15},{8,16},{9,17... | collective-permute-start | bytes 737288 | tf_op jit(solution)/shard_map/ppermute | solution.py:285
  91.4 16.9 %collective-permute-start.8 = (bf16[960,128]{1,0:T(8,128)(2,1)S(1)}, bf16[960,128]{1,0:T(8,128)(2,1)}, u32[]{:S(2)}, u32[]{:S(2)}) collective-permute-start(bf16[960,128]{1,0:T(8,128)(2,1)S(1)} %bitcast.22), channel_id=1, source_target_pairs={{0,16},{1,17},{2,18},{3,19},{4,20},{5,21},{6,22},{7,23},{8,24},{9,... | collective-permute-start | bytes 737288 | tf_op jit(solution)/shard_map/ppermute | solution.py:285
  93.6 15.1 %collective-permute-start.7 = (bf16[960,128]{1,0:T(8,128)(2,1)S(1)}, bf16[960,128]{1,0:T(8,128)(2,1)}, u32[]{:S(2)}, u32[]{:S(2)}) collective-permute-start(bf16[960,128]{1,0:T(8,128)(2,1)S(1)} %bitcast.23), channel_id=1, source_target_pairs={{0,24},{1,25},{2,26},{3,27},{4,28},{5,29},{6,30},{7,31},{8,0},{9,1... | collective-permute-start | bytes 737288 | tf_op jit(solution)/shard_map/ppermute | solution.py:285
  100.2 13.9 %all-to-all-start.6 = ((bf16[4,240,128]{2,1,0:T(8,128)(2,1)}), bf16[4,240,128]{2,1,0:T(8,128)(2,1)S(1)}, u32[]{:S(2)}, u32[]{:S(2)}) async-start(bf16[4,240,128]{2,1,0:T(8,128)(2,1)} %shard_map.84), calls=%async_computation.6 | async-start | bytes 491520 | tf_op jit(solution)/shard_map/all_to_all | solution.py:215
  103.6 5.7 %collective-permute-start.10 = (bf16[960,128]{1,0:T(8,128)(2,1)S(1)}, bf16[960,128]{1,0:T(8,128)(2,1)S(1)}, u32[]{:S(2)}, u32[]{:S(2)}) collective-permute-start(bf16[960,128]{1,0:T(8,128)(2,1)S(1)} %bitcast.24), channel_id=1, source_target_pairs={{0,1},{1,0},{2,3},{3,2},{4,5},{5,4},{6,7},{7,6},{8,9},{9,8},{10,11... | collective-permute-start | bytes 737288 | tf_op jit(solution)/shard_map/ppermute | solution.py:281
  108.2 1.7 %collective-permute-start.13 = (bf16[960,128]{1,0:T(8,128)(2,1)}, bf16[960,128]{1,0:T(8,128)(2,1)S(1)}, u32[]{:S(2)}, u32[]{:S(2)}) collective-permute-start(bf16[960,128]{1,0:T(8,128)(2,1)} %collective-permute-done.9.refs_3_), channel_id=1, source_target_pairs={{0,1},{1,0},{2,3},{3,2},{4,5},{5,4},{6,7},{7,6},{8,9},{9,8},{10,11... | collective-permute-start | bytes 737288 | tf_op jit(solution)/shard_map/ppermute | solution.py:281
  108.3 2.0 %collective-permute-start.12 = (bf16[960,128]{1,0:T(8,128)(2,1)}, bf16[960,128]{1,0:T(8,128)(2,1)S(1)}, u32[]{:S(2)}, u32[]{:S(2)}) collective-permute-start(bf16[960,128]{1,0:T(8,128)(2,1)} %collective-permute-done.8.refs_2_), channel_id=1, source_target_pairs={{0,1},{1,0},{2,3},{3,2},{4,5},{5,4},{6,7},{7,6},{8,9},{9,8},{10,11... | collective-permute-start | bytes 737288 | tf_op jit(solution)/shard_map/ppermute | solution.py:281
  108.7 1.9 %collective-permute-start.11 = (bf16[960,128]{1,0:T(8,128)(2,1)}, bf16[960,128]{1,0:T(8,128)(2,1)S(1)}, u32[]{:S(2)}, u32[]{:S(2)}) collective-permute-start(bf16[960,128]{1,0:T(8,128)(2,1)} %collective-permute-done.7.refs_1_), channel_id=1, source_target_pairs={{0,1},{1,0},{2,3},{3,2},{4,5},{5,4},{6,7},{7,6},{8,9},{9,8},{10,11... | collective-permute-start | bytes 737288 | tf_op jit(solution)/shard_map/ppermute | solution.py:281
  114.2 23.5 %all-to-all-start.4 = ((bf16[8,464,128]{2,1,0:T(8,128)(2,1)}), bf16[8,464,128]{2,1,0:T(8,128)(2,1)S(1)}, u32[]{:S(2)}, u32[]{:S(2)}) async-start(bf16[8,464,128]{2,1,0:T(8,128)(2,1)} %get-tuple-element.58), calls=%async_computation.4 | async-start | bytes 1900544 | tf_op jit(solution)/shard_map/all_to_all | solution.py:215
  118.0 11.2 %collective-permute-start.19 = (bf16[960,128]{1,0:T(8,128)(2,1)S(1)}, bf16[960,128]{1,0:T(8,128)(2,1)S(1)}, u32[]{:S(2)}, u32[]{:S(2)}) collective-permute-start(bf16[960,128]{1,0:T(8,128)(2,1)S(1)} %bitcast.16), channel_id=1, source_target_pairs={{0,8},{1,9},{2,10},{3,11},{4,12},{5,13},{6,14},{7,15},{8,16},{9,17... | collective-permute-start | bytes 737288 | tf_op jit(solution)/shard_map/ppermute | solution.py:285
  118.2 14.7 %collective-permute-start.18 = (bf16[960,128]{1,0:T(8,128)(2,1)S(1)}, bf16[960,128]{1,0:T(8,128)(2,1)S(1)}, u32[]{:S(2)}, u32[]{:S(2)}) collective-permute-start(bf16[960,128]{1,0:T(8,128)(2,1)S(1)} %bitcast.17), channel_id=1, source_target_pairs={{0,16},{1,17},{2,18},{3,19},{4,20},{5,21},{6,22},{7,23},{8,24},{9,... | collective-permute-start | bytes 737288 | tf_op jit(solution)/shard_map/ppermute | solution.py:285
  119.9 13.0 %collective-permute-start.17 = (bf16[960,128]{1,0:T(8,128)(2,1)S(1)}, bf16[960,128]{1,0:T(8,128)(2,1)S(1)}, u32[]{:S(2)}, u32[]{:S(2)}) collective-permute-start(bf16[960,128]{1,0:T(8,128)(2,1)S(1)} %bitcast.18), channel_id=1, source_target_pairs={{0,24},{1,25},{2,26},{3,27},{4,28},{5,29},{6,30},{7,31},{8,0},{9,1... | collective-permute-start | bytes 737288 | tf_op jit(solution)/shard_map/ppermute | solution.py:285
  120.9 1.5 copy-start.1
  122.4 12.4 %copy-start.3 = (bf16[464,928]{1,0:T(8,128)(2,1)S(1)}, bf16[464,928]{1,0:T(8,128)(2,1)}, u32[]{:S(2)}) copy-start(bf16[464,928]{1,0:T(8,128)(2,1)} %refs_8_.1) | copy-start | bytes 2583556
  125.0 8.5 %collective-permute-start.20 = (bf16[960,128]{1,0:T(8,128)(2,1)S(1)}, bf16[960,128]{1,0:T(8,128)(2,1)S(1)}, u32[]{:S(2)}, u32[]{:S(2)}) collective-permute-start(bf16[960,128]{1,0:T(8,128)(2,1)S(1)} %bitcast.19), channel_id=1, source_target_pairs={{0,1},{1,0},{2,3},{3,2},{4,5},{5,4},{6,7},{7,6},{8,9},{9,8},{10,11... | collective-permute-start | bytes 737288 | tf_op jit(solution)/shard_map/ppermute | solution.py:281
  129.2 4.8 %collective-permute-start.23 = (bf16[960,128]{1,0:T(8,128)(2,1)S(1)}, bf16[960,128]{1,0:T(8,128)(2,1)S(1)}, u32[]{:S(2)}, u32[]{:S(2)}) collective-permute-start(bf16[960,128]{1,0:T(8,128)(2,1)S(1)} %collective-permute-done.19.refs_3_), channel_id=1, source_target_pairs={{0,1},{1,0},{2,3},{3,2},{4,5},{5,4},{6,7},{7,6},{8,9},{9,8},{10,11... | collective-permute-start | bytes 737288 | tf_op jit(solution)/shard_map/ppermute | solution.py:281
  132.9 1.5 collective-permute-start.22
  132.9 1.9 %collective-permute-start.21 = (bf16[960,128]{1,0:T(8,128)(2,1)S(1)}, bf16[960,128]{1,0:T(8,128)(2,1)S(1)}, u32[]{:S(2)}, u32[]{:S(2)}) collective-permute-start(bf16[960,128]{1,0:T(8,128)(2,1)S(1)} %collective-permute-done.17.refs_1_), channel_id=1, source_target_pairs={{0,1},{1,0},{2,3},{3,2},{4,5},{5,4},{6,7},{7,6},{8,9},{9,8},{10,11... | collective-permute-start | bytes 737288 | tf_op jit(solution)/shard_map/ppermute | solution.py:281
  137.6 19.1 %all-to-all-start.7 = ((bf16[8,464,128]{2,1,0:T(8,128)(2,1)}), bf16[8,464,128]{2,1,0:T(8,128)(2,1)S(1)}, u32[]{:S(2)}, u32[]{:S(2)}) async-start(bf16[8,464,128]{2,1,0:T(8,128)(2,1)} %get-tuple-element.70), calls=%async_computation.7 | async-start | bytes 1900544 | tf_op jit(solution)/shard_map/all_to_all | solution.py:215
  142.8 1.5 copy-start.2

commit v13 on v11

--- a/solution.py
+++ b/solution.py
@@ -94,12 +94,11 @@
         outs, held_ref, sems = refs[:PIECES], refs[-2], refs[-1]
         rows = half_of(rows_ref, 1 - pos_ref[1], pos_ref[0])
         copies = []
+        product = dot(weight_ref[...], rows, PLAIN).astype(BF)
         for pair in range(X // 2):
-            here = rows[:, pair * 2 * LANES : (pair + 1) * 2 * LANES]
-            product = dot(weight_ref[...], here, PLAIN).astype(BF)
             for d in range(2):
                 index = pair * 2 + d
-                held_ref[index] = block(product, d)
+                held_ref[index] = block(product, index)
                 target = outs[index // each].at[index % each]
                 copies.append(pltpu.make_async_copy(held_ref.at[index], target, sems.at[index]))
                 copies[-1].start()

time: 157 us -> 157 us (level)
  no operation moved by 1% of the time
where the time goes in v13:
time: 157 us; the launch traced here: 156 us
  starting transfers between devices  71.1 us (45%)
  waiting for transfers between devices  43.1 us (27%)
  Pallas kernels  29.4 us (19%)
  local copies, waits for them, and re-layouts  7.77 us (5%)
  other arithmetic  4.2 us (3%)
    all_to_all x8, starting transfers between devices, exchange(): return lax.all_to_all(value, axis, 0, 0, axis_index_groups=groups)  39.8 us
    all_to_all x8, waiting for transfers between devices, exchange(): return lax.all_to_all(value, axis, 0, 0, axis_index_groups=groups)  36.2 us
    pallas_call x14, Pallas kernels, kernel_call(): pl.pallas_call(kernel, out_shape=[pltpu.HBM(o.shape, o.dtype) if i in far...  29.4 us
    ppermute x12, starting transfers between devices, swap_cores(): return lax.ppermute(value, 'rep', rep_pairs(0, 0, 1))  15.7 us
    ppermute x12, starting transfers between devices, move_x(): return lax.ppermute(value, 'rep', rep_pairs(d, 0, 0))  15.6 us
    unnamed x18, local copies, waits for them, and re-layouts  7.77 us
    ppermute x12, waiting for transfers between devices, swap_cores(): return lax.ppermute(value, 'rep', rep_pairs(0, 0, 1))  5.26 us
    convert_element_type x2, other arithmetic, sum_x(): return keep.astype(BF)  4.12 us
  transfers between devices with their start and end apart: 32, of which 15 were waited for; matrix products, arithmetic and copies ran while one was open for 5% of the time, Pallas kernels for 14%

profile of v13, /device:TPU:1, one launch (start us, length us, event | category | flops | bytes accessed | tf_op | source)
XLA Modules:
  0.0 156.4 jit_solution(3945926813460126778)
XLA Ops:
  1.6 1.5 shard_map.76
  3.2 6.4 %all-to-all-start = ((bf16[8,464,128]{2,1,0:T(8,128)(2,1)}), bf16[8,464,128]{2,1,0:T(8,128)(2,1)S(1)}, u32[]{:S(2)}, u32[]{:S(2)}) async-start(bf16[8,464,128]{2,1,0:T(8,128)(2,1)} %shard_map.76), calls=%async_computation | async-start | bytes 1900544 | tf_op jit(solution)/shard_map/all_to_all | solution.py:203
  9.6 1.6 %shard_map.75 = bf16[8,464,128]{2,1,0:T(8,128)(2,1)} custom-call(s32[3]{0:T(128)S(1)} %pad_add_fusion.pos_ref, bf16[464,128]{1,0:T(8,128)(2,1)S(1)} %bitcast.27), custom_call_target="tpu_custom_call" | custom-call | bytes 1069056 | tf_op jit(solution)/shard_map/pallas_call | solution.py:61
  11.1 1.6 %copy.8 = bf16[464,928]{0,1:T(8,128)(2,1)S(1)} copy(bf16[464,928]{1,0:T(8,128)(2,1)} %refs_8_.1) | data formatting | bytes 1722368 | tf_op args[1]
  12.8 1.4 copy.9
  14.2 8.9 %all-to-all-done.rows_ref = bf16[8,464,128]{2,1,0:T(8,128)(2,1)S(1)} async-done(((bf16[8,464,128]{2,1,0:T(8,128)(2,1)}), bf16[8,464,128]{2,1,0:T(8,128)(2,1)S(1)}, u32[]{:S(2)}, u32[]{:S(2)}) %all-to-all-start) | async-done | bytes 950304 | tf_op jit(solution)/shard_map/all_to_all | solution.py:203
  23.1 2.2 %shard_map.77 = (bf16[2,928,128]{2,1,0:T(8,128)(2,1)}, bf16[2,928,128]{2,1,0:T(8,128)(2,1)}) custom-call(s32[3]{0:T(128)S(1)} %pad_add_fusion.pos_ref, bf16[8,464,128]{2,1,0:T(8,128)(2,1)S(1)} %all-to-all-done.rows_ref, bf16[928,464]{1,0:T(8,128)(2,1)S(1)} %bitcast.13), custom_call_target="tpu_custom_call" | custom-call | flops 440926208 | bytes 2761728 | tf_op jit(solution)/shard_map/pallas_call | solution.py:61
  25.3 1.2 collective-permute-start
  26.6 1.6 %collective-permute-done.refs_0_ = bf16[2,928,128]{2,1,0:T(8,128)(2,1)S(1)} collective-permute-done((bf16[2,928,128]{2,1,0:T(8,128)(2,1)}, bf16[2,928,128]{2,1,0:T(8,128)(2,1)S(1)}, u32[]{:S(2)}, u32[]{:S(2)}) %collective-permute-start) | collective-permute-done | bytes 475168 | tf_op jit(solution)/shard_map/ppermute | solution.py:269
  28.9 2.1 %shard_map.78 = (f32[960,128]{1,0:T(8,128)S(1)}, bf16[960,128]{1,0:T(8,128)(2,1)}, bf16[960,128]{1,0:T(8,128)(2,1)}, bf16[960,128]{1,0:T(8,128)(2,1)}) custom-call(s32[3]{0:T(128)S(1)} %pad_add_fusion.pos_ref, bf16[8,464,128]{2,1,0:T(8,128)(2,1)S(1)} %all-to-all-done.rows_ref, bf16[928,464]{1,0:T(8,128)(2,1)S(1)} %bitcast.14, ...), custom_call_target="tpu_custom_call" | custom-call | flops 440926208 | bytes 3990528 | tf_op jit(solution)/shard_map/pallas_call | solution.py:61
  31.0 3.6 %all-to-all-start.2 = ((bf16[8,464,128]{2,1,0:T(8,128)(2,1)}), bf16[8,464,128]{2,1,0:T(8,128)(2,1)S(1)}, u32[]{:S(2)}, u32[]{:S(2)}) async-start(bf16[8,464,128]{2,1,0:T(8,128)(2,1)} %shard_map.75), calls=%async_computation.2 | async-start | bytes 1900544 | tf_op jit(solution)/shard_map/all_to_all | solution.py:203
  34.6 1.3 collective-permute-start.2
  35.8 2.5 %collective-permute-start.3 = (bf16[960,128]{1,0:T(8,128)(2,1)}, bf16[960,128]{1,0:T(8,128)(2,1)}, u32[]{:S(2)}, u32[]{:S(2)}) collective-permute-start(bf16[960,128]{1,0:T(8,128)(2,1)} %get-tuple-element.44), channel_id=1, source_target_pairs={{0,16},{1,17},{2,18},{3,19},{4,20},{5,21},{6,22},{7,23},{8,24},{9,... | collective-permute-start | bytes 737288 | tf_op jit(solution)/shard_map/ppermute | solution.py:273
  38.3 1.2 collective-permute-start.4
  39.5 9.0 %all-to-all-done.2.rows_ref = bf16[8,464,128]{2,1,0:T(8,128)(2,1)S(1)} async-done(((bf16[8,464,128]{2,1,0:T(8,128)(2,1)}), bf16[8,464,128]{2,1,0:T(8,128)(2,1)S(1)}, u32[]{:S(2)}, u32[]{:S(2)}) %all-to-all-start.2) | async-done | bytes 950304 | tf_op jit(solution)/shard_map/all_to_all | solution.py:203
  48.5 2.2 %shard_map.79 = (bf16[2,928,128]{2,1,0:T(8,128)(2,1)}, bf16[2,928,128]{2,1,0:T(8,128)(2,1)}) custom-call(s32[3]{0:T(128)S(1)} %pad_add_fusion.pos_ref, bf16[8,464,128]{2,1,0:T(8,128)(2,1)S(1)} %all-to-all-done.2.rows_ref, bf16[928,464]{1,0:T(8,128)(2,1)S(1)} %copy-done), custom_call_target="tpu_custom_call" | custom-call | flops 440926208 | bytes 2761728 | tf_op jit(solution)/shard_map/pallas_call | solution.py:61
  51.6 2.0 %add_convert_fusion.1 = bf16[960,128]{1,0:T(8,128)(2,1)} fusion(bf16[960,128]{1,0:T(8,128)(2,1)} %collective-permute-done.4, bf16[960,128]{1,0:T(8,128)(2,1)} %collective-permute-done.3, f32[960,128]{1,0:T(8,128)S(1)} %get-tuple-element.42, bf16[960,128]{1,0:T(8,128)(2,1)} %collective-permute-done.2), kind=kLoop, calls=%fused_computation.1 | loop fusion | flops 860160 | bytes 1474560 | tf_op jit(solution)/shard_map/convert_element_type | solution.py:284
  53.5 7.3 %all-to-all-start.1 = ((bf16[4,240,128]{2,1,0:T(8,128)(2,1)}), bf16[4,240,128]{2,1,0:T(8,128)(2,1)S(1)}, u32[]{:S(2)}, u32[]{:S(2)}) async-start(bf16[4,240,128]{2,1,0:T(8,128)(2,1)} %bitcast.28), calls=%async_computation.1 | async-start | bytes 491520 | tf_op jit(solution)/shard_map/all_to_all | solution.py:203
  60.9 2.8 %shard_map.80 = (f32[960,128]{1,0:T(8,128)S(1)}, bf16[960,128]{1,0:T(8,128)(2,1)}, bf16[960,128]{1,0:T(8,128)(2,1)}, bf16[960,128]{1,0:T(8,128)(2,1)}) custom-call(s32[3]{0:T(128)S(1)} %pad_add_fusion.pos_ref, bf16[8,464,128]{2,1,0:T(8,128)(2,1)S(1)} %all-to-all-done.2.rows_ref, bf16[928,464]{1,0:T(8,128)(2,1)S(1)} %copy-done, ...), custom_call_target="tpu_custom_call" | custom-call | flops 440926208 | bytes 3990528 | tf_op jit(solution)/shard_map/pallas_call | solution.py:61
  64.4 1.2 collective-permute-start.14
  65.6 2.5 %collective-permute-start.15 = (bf16[960,128]{1,0:T(8,128)(2,1)}, bf16[960,128]{1,0:T(8,128)(2,1)}, u32[]{:S(2)}, u32[]{:S(2)}) collective-permute-start(bf16[960,128]{1,0:T(8,128)(2,1)} %get-tuple-element.60), channel_id=1, source_target_pairs={{0,16},{1,17},{2,18},{3,19},{4,20},{5,21},{6,22},{7,23},{8,24},{9,... | collective-permute-start | bytes 737288 | tf_op jit(solution)/shard_map/ppermute | solution.py:273
  68.1 1.2 collective-permute-start.16
  69.2 1.3 shard_map.81
  70.6 6.8 %all-to-all-start.3 = ((bf16[4,240,128]{2,1,0:T(8,128)(2,1)}), bf16[4,240,128]{2,1,0:T(8,128)(2,1)S(1)}, u32[]{:S(2)}, u32[]{:S(2)}) async-start(bf16[4,240,128]{2,1,0:T(8,128)(2,1)} %get-tuple-element.56), calls=%async_computation.3 | async-start | bytes 491520 | tf_op jit(solution)/shard_map/all_to_all | solution.py:203
  77.4 1.6 %collective-permute-done.15 = bf16[960,128]{1,0:T(8,128)(2,1)} collective-permute-done((bf16[960,128]{1,0:T(8,128)(2,1)}, bf16[960,128]{1,0:T(8,128)(2,1)}, u32[]{:S(2)}, u32[]{:S(2)}) %collective-permute-start.15) | collective-permute-done | bytes 245792 | tf_op jit(solution)/shard_map/ppermute | solution.py:273
  79.0 2.1 %add_convert_fusion = bf16[960,128]{1,0:T(8,128)(2,1)} fusion(bf16[960,128]{1,0:T(8,128)(2,1)} %collective-permute-done.16, bf16[960,128]{1,0:T(8,128)(2,1)} %collective-permute-done.15, f32[960,128]{1,0:T(8,128)} %copy-done.5, bf16[960,128]{1,0:T(8,128)(2,1)} %collective-permute-done.14), kind=kLoop, calls=%fused_computation | loop fusion | flops 860160 | bytes 1474560 | tf_op jit(solution)/shard_map/convert_element_type | solution.py:284
  81.1 4.8 %all-to-all-done.3 = bf16[4,240,128]{2,1,0:T(8,128)(2,1)S(1)} async-done(((bf16[4,240,128]{2,1,0:T(8,128)(2,1)}), bf16[4,240,128]{2,1,0:T(8,128)(2,1)S(1)}, u32[]{:S(2)}, u32[]{:S(2)}) %all-to-all-start.3) | async-done | bytes 245792 | tf_op jit(solution)/shard_map/all_to_all | solution.py:203
  86.0 3.4 %all-to-all-start.5 = ((bf16[4,240,128]{2,1,0:T(8,128)(2,1)}), bf16[4,240,128]{2,1,0:T(8,128)(2,1)S(1)}, u32[]{:S(2)}, u32[]{:S(2)}) async-start(bf16[4,240,128]{2,1,0:T(8,128)(2,1)} %bitcast.29), calls=%async_computation.5 | async-start | bytes 491520 | tf_op jit(solution)/shard_map/all_to_all | solution.py:203
  89.8 2.2 %collective-permute-start.8 = (bf16[960,128]{1,0:T(8,128)(2,1)S(1)}, bf16[960,128]{1,0:T(8,128)(2,1)}, u32[]{:S(2)}, u32[]{:S(2)}) collective-permute-start(bf16[960,128]{1,0:T(8,128)(2,1)S(1)} %bitcast.22), channel_id=1, source_target_pairs={{0,16},{1,17},{2,18},{3,19},{4,20},{5,21},{6,22},{7,23},{8,24},{9,... | collective-permute-start | bytes 737288 | tf_op jit(solution)/shard_map/ppermute | solution.py:273
  92.3 5.0 %all-to-all-done.5.arrived_ref = bf16[4,240,128]{2,1,0:T(8,128)(2,1)S(1)} async-done(((bf16[4,240,128]{2,1,0:T(8,128)(2,1)}), bf16[4,240,128]{2,1,0:T(8,128)(2,1)S(1)}, u32[]{:S(2)}, u32[]{:S(2)}) %all-to-all-start.5) | async-done | bytes 245792 | tf_op jit(solution)/shard_map/all_to_all | solution.py:203
  97.2 1.3 shard_map.84
  98.6 3.4 %all-to-all-start.6 = ((bf16[4,240,128]{2,1,0:T(8,128)(2,1)}), bf16[4,240,128]{2,1,0:T(8,128)(2,1)S(1)}, u32[]{:S(2)}, u32[]{:S(2)}) async-start(bf16[4,240,128]{2,1,0:T(8,128)(2,1)} %shard_map.84), calls=%async_computation.6 | async-start | bytes 491520 | tf_op jit(solution)/shard_map/all_to_all | solution.py:203
  102.0 4.6 %collective-permute-start.10 = (bf16[960,128]{1,0:T(8,128)(2,1)S(1)}, bf16[960,128]{1,0:T(8,128)(2,1)S(1)}, u32[]{:S(2)}, u32[]{:S(2)}) collective-permute-start(bf16[960,128]{1,0:T(8,128)(2,1)S(1)} %bitcast.24), channel_id=1, source_target_pairs={{0,1},{1,0},{2,3},{3,2},{4,5},{5,4},{6,7},{7,6},{8,9},{9,8},{10,11... | collective-permute-start | bytes 737288 | tf_op jit(solution)/shard_map/ppermute | solution.py:269
  109.0 3.5 %shard_map.82 = (bf16[8,464,128]{2,1,0:T(8,128)(2,1)}, bf16[8,928,128]{2,1,0:T(8,128)(2,1)}) custom-call(s32[3]{0:T(128)S(1)} %pad_add_fusion.pos_ref, bf16[960,128]{1,0:T(8,128)(2,1)S(1)} %bitcast.25, bf16[960,128]{1,0:T(8,128)(2,1)} %collective-permute-done.7.refs_1_, bf16[960,128]{1,0:T(8,128)(2,1)} %collective-permute-done.8.refs_2_, ...), custom_call_target="tpu_custom_call" | custom-call | flops 881852416 | bytes 5678080 | tf_op jit(solution)/shard_map/pallas_call | solution.py:61
  112.5 3.9 %all-to-all-start.4 = ((bf16[8,464,128]{2,1,0:T(8,128)(2,1)}), bf16[8,464,128]{2,1,0:T(8,128)(2,1)S(1)}, u32[]{:S(2)}, u32[]{:S(2)}) async-start(bf16[8,464,128]{2,1,0:T(8,128)(2,1)} %get-tuple-element.58), calls=%async_computation.4 | async-start | bytes 1900544 | tf_op jit(solution)/shard_map/all_to_all | solution.py:203
  116.6 1.6 collective-permute-start.18
  118.2 1.2 collective-permute-start.17
  119.4 1.5 copy-done.1
  120.9 2.6 %shard_map.85 = bf16[928,464]{1,0:T(8,128)(2,1)} custom-call(s32[3]{0:T(128)S(1)} %pad_add_fusion.pos_ref, bf16[8,464,128]{2,1,0:T(8,128)(2,1)S(1)} %all-to-all-done.2.rows_ref, bf16[8,928,128]{2,1,0:T(8,128)(2,1)S(1)} %copy-done.1), custom_call_target="tpu_custom_call" | custom-call | flops 881852416 | bytes 3712000 | tf_op jit(solution)/shard_map/pallas_call | solution.py:61
  123.6 4.0 %collective-permute-start.20 = (bf16[960,128]{1,0:T(8,128)(2,1)S(1)}, bf16[960,128]{1,0:T(8,128)(2,1)S(1)}, u32[]{:S(2)}, u32[]{:S(2)}) collective-permute-start(bf16[960,128]{1,0:T(8,128)(2,1)S(1)} %bitcast.19), channel_id=1, source_target_pairs={{0,1},{1,0},{2,3},{3,2},{4,5},{5,4},{6,7},{7,6},{8,9},{9,8},{10,11... | collective-permute-start | bytes 737288 | tf_op jit(solution)/shard_map/ppermute | solution.py:269
  127.6 3.7 %collective-permute-start.23 = (bf16[960,128]{1,0:T(8,128)(2,1)S(1)}, bf16[960,128]{1,0:T(8,128)(2,1)S(1)}, u32[]{:S(2)}, u32[]{:S(2)}) collective-permute-start(bf16[960,128]{1,0:T(8,128)(2,1)S(1)} %collective-permute-done.19.refs_3_), channel_id=1, source_target_pairs={{0,1},{1,0},{2,3},{3,2},{4,5},{5,4},{6,7},{7,6},{8,9},{9,8},{10,11... | collective-permute-start | bytes 737288 | tf_op jit(solution)/shard_map/ppermute | solution.py:269
  133.1 2.9 %shard_map.86 = (bf16[8,464,128]{2,1,0:T(8,128)(2,1)}, bf16[8,928,128]{2,1,0:T(8,128)(2,1)}) custom-call(s32[3]{0:T(128)S(1)} %pad_add_fusion.pos_ref, bf16[960,128]{1,0:T(8,128)(2,1)S(1)} %bitcast.20, bf16[960,128]{1,0:T(8,128)(2,1)S(1)} %collective-permute-done.17.refs_1_, bf16[960,128]{1,0:T(8,128)(2,1)S(1)} %collective-permute-done.18.refs_2_, ...), custom_call_target="tpu_custom_call" | custom-call | flops 881852416 | bytes 5678080 | tf_op jit(solution)/shard_map/pallas_call | solution.py:61
  136.0 5.2 %all-to-all-start.7 = ((bf16[8,464,128]{2,1,0:T(8,128)(2,1)}), bf16[8,464,128]{2,1,0:T(8,128)(2,1)S(1)}, u32[]{:S(2)}, u32[]{:S(2)}) async-start(bf16[8,464,128]{2,1,0:T(8,128)(2,1)} %get-tuple-element.70), calls=%async_computation.7 | async-start | bytes 1900544 | tf_op jit(solution)/shard_map/all_to_all | solution.py:203
  141.2 1.5 copy-done.2
  142.7 2.7 %shard_map.88 = bf16[464,928]{1,0:T(8,128)(2,1)} custom-call(s32[3]{0:T(128)S(1)} %pad_add_fusion.pos_ref, bf16[8,464,128]{2,1,0:T(8,128)(2,1)S(1)} %all-to-all-done.rows_ref, bf16[8,928,128]{2,1,0:T(8,128)(2,1)S(1)} %copy-done.2), custom_call_target="tpu_custom_call" | custom-call | flops 881852416 | bytes 3712000 | tf_op jit(solution)/shard_map/pallas_call | solution.py:61
  145.4 1.3 shard_map.83
  146.7 8.4 %all-to-all-done.7.value_ref = bf16[8,464,128]{2,1,0:T(8,128)(2,1)S(1)} async-done(((bf16[8,464,128]{2,1,0:T(8,128)(2,1)}), bf16[8,464,128]{2,1,0:T(8,128)(2,1)S(1)}, u32[]{:S(2)}, u32[]{:S(2)}) %all-to-all-start.7) | async-done | bytes 950304 | tf_op jit(solution)/shard_map/all_to_all | solution.py:203
  155.1 1.3 shard_map.87
  (51 shorter events, 8.6 us)
Async XLA Ops:
  0.7 0.9 copy-start.6
  1.6 7.9 %copy-start.7 = (bf16[128,464]{0,1:T(8,128)(2,1)S(1)}, bf16[128,464]{0,1:T(8,128)(2,1)}, u32[]{:S(2)}) copy-start(bf16[128,464]{0,1:T(8,128)(2,1)} %param.7) | copy-start | bytes 356356
  3.2 20.0 %all-to-all-start = ((bf16[8,464,128]{2,1,0:T(8,128)(2,1)}), bf16[8,464,128]{2,1,0:T(8,128)(2,1)S(1)}, u32[]{:S(2)}, u32[]{:S(2)}) async-start(bf16[8,464,128]{2,1,0:T(8,128)(2,1)} %shard_map.76), calls=%async_computation | async-start | bytes 1900544 | tf_op jit(solution)/shard_map/all_to_all | solution.py:203
  9.5 3.3 %copy-start = (bf16[928,464]{1,0:T(8,128)(2,1)S(1)}, bf16[928,464]{1,0:T(8,128)(2,1)}, u32[]{:S(2)}) copy-start(bf16[928,464]{1,0:T(8,128)(2,1)} %weight_ref.3) | copy-start | bytes 2583556
  25.3 2.9 %collective-permute-start = (bf16[2,928,128]{2,1,0:T(8,128)(2,1)}, bf16[2,928,128]{2,1,0:T(8,128)(2,1)S(1)}, u32[]{:S(2)}, u32[]{:S(2)}) collective-permute-start(bf16[2,928,128]{2,1,0:T(8,128)(2,1)} %get-tuple-element.40), channel_id=1, source_target_pairs={{0,1},{1,0},{2,3},{3,2},{4,5},{5,4},{6,7},{7,6},{8,9},{9,8},{10,11... | collective-permute-start | bytes 1425416 | tf_op jit(solution)/shard_map/ppermute | solution.py:269
  26.5 2.4 %collective-permute-start.1 = (bf16[2,928,128]{2,1,0:T(8,128)(2,1)}, bf16[2,928,128]{2,1,0:T(8,128)(2,1)S(1)}, u32[]{:S(2)}, u32[]{:S(2)}) collective-permute-start(bf16[2,928,128]{2,1,0:T(8,128)(2,1)} %get-tuple-element.41), channel_id=1, source_target_pairs={{0,1},{1,0},{2,3},{3,2},{4,5},{5,4},{6,7},{7,6},{8,9},{9,8},{10,11... | collective-permute-start | bytes 1425416 | tf_op jit(solution)/shard_map/ppermute | solution.py:269
  31.0 17.5 %all-to-all-start.2 = ((bf16[8,464,128]{2,1,0:T(8,128)(2,1)}), bf16[8,464,128]{2,1,0:T(8,128)(2,1)S(1)}, u32[]{:S(2)}, u32[]{:S(2)}) async-start(bf16[8,464,128]{2,1,0:T(8,128)(2,1)} %shard_map.75), calls=%async_computation.2 | async-start | bytes 1900544 | tf_op jit(solution)/shard_map/all_to_all | solution.py:203
  34.6 17.0 %collective-permute-start.2 = (bf16[960,128]{1,0:T(8,128)(2,1)}, bf16[960,128]{1,0:T(8,128)(2,1)}, u32[]{:S(2)}, u32[]{:S(2)}) collective-permute-start(bf16[960,128]{1,0:T(8,128)(2,1)} %get-tuple-element.43), channel_id=1, source_target_pairs={{0,8},{1,9},{2,10},{3,11},{4,12},{5,13},{6,14},{7,15},{8,16},{9,17... | collective-permute-start | bytes 737288 | tf_op jit(solution)/shard_map/ppermute | solution.py:273
  35.8 15.7 %collective-permute-start.3 = (bf16[960,128]{1,0:T(8,128)(2,1)}, bf16[960,128]{1,0:T(8,128)(2,1)}, u32[]{:S(2)}, u32[]{:S(2)}) collective-permute-start(bf16[960,128]{1,0:T(8,128)(2,1)} %get-tuple-element.44), channel_id=1, source_target_pairs={{0,16},{1,17},{2,18},{3,19},{4,20},{5,21},{6,22},{7,23},{8,24},{9,... | collective-permute-start | bytes 737288 | tf_op jit(solution)/shard_map/ppermute | solution.py:273
  38.3 13.3 %collective-permute-start.4 = (bf16[960,128]{1,0:T(8,128)(2,1)}, bf16[960,128]{1,0:T(8,128)(2,1)}, u32[]{:S(2)}, u32[]{:S(2)}) collective-permute-start(bf16[960,128]{1,0:T(8,128)(2,1)} %get-tuple-element.45), channel_id=1, source_target_pairs={{0,24},{1,25},{2,26},{3,27},{4,28},{5,29},{6,30},{7,31},{8,0},{9,1... | collective-permute-start | bytes 737288 | tf_op jit(solution)/shard_map/ppermute | solution.py:273
  50.7 10.2 %collective-permute-start.5 = (bf16[2,928,128]{2,1,0:T(8,128)(2,1)}, bf16[2,928,128]{2,1,0:T(8,128)(2,1)}, u32[]{:S(2)}, u32[]{:S(2)}) collective-permute-start(bf16[2,928,128]{2,1,0:T(8,128)(2,1)} %get-tuple-element.52), channel_id=1, source_target_pairs={{0,1},{1,0},{2,3},{3,2},{4,5},{5,4},{6,7},{7,6},{8,9},{9,8},{10,11... | collective-permute-start | bytes 1425416 | tf_op jit(solution)/shard_map/ppermute | solution.py:269
  51.5 9.4 %collective-permute-start.6 = (bf16[2,928,128]{2,1,0:T(8,128)(2,1)}, bf16[2,928,128]{2,1,0:T(8,128)(2,1)}, u32[]{:S(2)}, u32[]{:S(2)}) collective-permute-start(bf16[2,928,128]{2,1,0:T(8,128)(2,1)} %get-tuple-element.53), channel_id=1, source_target_pairs={{0,1},{1,0},{2,3},{3,2},{4,5},{5,4},{6,7},{7,6},{8,9},{9,8},{10,11... | collective-permute-start | bytes 1425416 | tf_op jit(solution)/shard_map/ppermute | solution.py:269
  53.5 15.7 %all-to-all-start.1 = ((bf16[4,240,128]{2,1,0:T(8,128)(2,1)}), bf16[4,240,128]{2,1,0:T(8,128)(2,1)S(1)}, u32[]{:S(2)}, u32[]{:S(2)}) async-start(bf16[4,240,128]{2,1,0:T(8,128)(2,1)} %bitcast.28), calls=%async_computation.1 | async-start | bytes 491520 | tf_op jit(solution)/shard_map/all_to_all | solution.py:203
  63.6 0.8 copy-start.5
  64.4 13.0 %collective-permute-start.14 = (bf16[960,128]{1,0:T(8,128)(2,1)}, bf16[960,128]{1,0:T(8,128)(2,1)}, u32[]{:S(2)}, u32[]{:S(2)}) collective-permute-start(bf16[960,128]{1,0:T(8,128)(2,1)} %get-tuple-element.59), channel_id=1, source_target_pairs={{0,8},{1,9},{2,10},{3,11},{4,12},{5,13},{6,14},{7,15},{8,16},{9,17... | collective-permute-start | bytes 737288 | tf_op jit(solution)/shard_map/ppermute | solution.py:273
  65.6 13.4 %collective-permute-start.15 = (bf16[960,128]{1,0:T(8,128)(2,1)}, bf16[960,128]{1,0:T(8,128)(2,1)}, u32[]{:S(2)}, u32[]{:S(2)}) collective-permute-start(bf16[960,128]{1,0:T(8,128)(2,1)} %get-tuple-element.60), channel_id=1, source_target_pairs={{0,16},{1,17},{2,18},{3,19},{4,20},{5,21},{6,22},{7,23},{8,24},{9,... | collective-permute-start | bytes 737288 | tf_op jit(solution)/shard_map/ppermute | solution.py:273
  68.1 10.9 %collective-permute-start.16 = (bf16[960,128]{1,0:T(8,128)(2,1)}, bf16[960,128]{1,0:T(8,128)(2,1)}, u32[]{:S(2)}, u32[]{:S(2)}) collective-permute-start(bf16[960,128]{1,0:T(8,128)(2,1)} %get-tuple-element.61), channel_id=1, source_target_pairs={{0,24},{1,25},{2,26},{3,27},{4,28},{5,29},{6,30},{7,31},{8,0},{9,1... | collective-permute-start | bytes 737288 | tf_op jit(solution)/shard_map/ppermute | solution.py:273
  70.6 38.4 %copy-start.4 = (bf16[928,464]{0,1:T(8,128)(2,1)S(1)}, bf16[928,464]{0,1:T(8,128)(2,1)}, u32[]{:S(2)}) copy-start(bf16[928,464]{0,1:T(8,128)(2,1)} %copy.9) | copy-start | bytes 2583556
  70.6 15.4 %all-to-all-start.3 = ((bf16[4,240,128]{2,1,0:T(8,128)(2,1)}), bf16[4,240,128]{2,1,0:T(8,128)(2,1)S(1)}, u32[]{:S(2)}, u32[]{:S(2)}) async-start(bf16[4,240,128]{2,1,0:T(8,128)(2,1)} %get-tuple-element.56), calls=%async_computation.3 | async-start | bytes 491520 | tf_op jit(solution)/shard_map/all_to_all | solution.py:203
  86.0 11.2 %all-to-all-start.5 = ((bf16[4,240,128]{2,1,0:T(8,128)(2,1)}), bf16[4,240,128]{2,1,0:T(8,128)(2,1)S(1)}, u32[]{:S(2)}, u32[]{:S(2)}) async-start(bf16[4,240,128]{2,1,0:T(8,128)(2,1)} %bitcast.29), calls=%async_computation.5 | async-start | bytes 491520 | tf_op jit(solution)/shard_map/all_to_all | solution.py:203
  89.4 17.2 %collective-permute-start.9 = (bf16[960,128]{1,0:T(8,128)(2,1)S(1)}, bf16[960,128]{1,0:T(8,128)(2,1)}, u32[]{:S(2)}, u32[]{:S(2)}) collective-permute-start(bf16[960,128]{1,0:T(8,128)(2,1)S(1)} %bitcast.21), channel_id=1, source_target_pairs={{0,8},{1,9},{2,10},{3,11},{4,12},{5,13},{6,14},{7,15},{8,16},{9,17... | collective-permute-start | bytes 737288 | tf_op jit(solution)/shard_map/ppermute | solution.py:273
  89.8 16.9 %collective-permute-start.8 = (bf16[960,128]{1,0:T(8,128)(2,1)S(1)}, bf16[960,128]{1,0:T(8,128)(2,1)}, u32[]{:S(2)}, u32[]{:S(2)}) collective-permute-start(bf16[960,128]{1,0:T(8,128)(2,1)S(1)} %bitcast.22), channel_id=1, source_target_pairs={{0,16},{1,17},{2,18},{3,19},{4,20},{5,21},{6,22},{7,23},{8,24},{9,... | collective-permute-start | bytes 737288 | tf_op jit(solution)/shard_map/ppermute | solution.py:273
  92.0 15.1 %collective-permute-start.7 = (bf16[960,128]{1,0:T(8,128)(2,1)S(1)}, bf16[960,128]{1,0:T(8,128)(2,1)}, u32[]{:S(2)}, u32[]{:S(2)}) collective-permute-start(bf16[960,128]{1,0:T(8,128)(2,1)S(1)} %bitcast.23), channel_id=1, source_target_pairs={{0,24},{1,25},{2,26},{3,27},{4,28},{5,29},{6,30},{7,31},{8,0},{9,1... | collective-permute-start | bytes 737288 | tf_op jit(solution)/shard_map/ppermute | solution.py:273
  98.6 13.9 %all-to-all-start.6 = ((bf16[4,240,128]{2,1,0:T(8,128)(2,1)}), bf16[4,240,128]{2,1,0:T(8,128)(2,1)S(1)}, u32[]{:S(2)}, u32[]{:S(2)}) async-start(bf16[4,240,128]{2,1,0:T(8,128)(2,1)} %shard_map.84), calls=%async_computation.6 | async-start | bytes 491520 | tf_op jit(solution)/shard_map/all_to_all | solution.py:203
  102.0 5.7 %collective-permute-start.10 = (bf16[960,128]{1,0:T(8,128)(2,1)S(1)}, bf16[960,128]{1,0:T(8,128)(2,1)S(1)}, u32[]{:S(2)}, u32[]{:S(2)}) collective-permute-start(bf16[960,128]{1,0:T(8,128)(2,1)S(1)} %bitcast.24), channel_id=1, source_target_pairs={{0,1},{1,0},{2,3},{3,2},{4,5},{5,4},{6,7},{7,6},{8,9},{9,8},{10,11... | collective-permute-start | bytes 737288 | tf_op jit(solution)/shard_map/ppermute | solution.py:269
  106.6 1.7 %collective-permute-start.13 = (bf16[960,128]{1,0:T(8,128)(2,1)}, bf16[960,128]{1,0:T(8,128)(2,1)S(1)}, u32[]{:S(2)}, u32[]{:S(2)}) collective-permute-start(bf16[960,128]{1,0:T(8,128)(2,1)} %collective-permute-done.9.refs_3_), channel_id=1, source_target_pairs={{0,1},{1,0},{2,3},{3,2},{4,5},{5,4},{6,7},{7,6},{8,9},{9,8},{10,11... | collective-permute-start | bytes 737288 | tf_op jit(solution)/shard_map/ppermute | solution.py:269
  106.7 2.0 %collective-permute-start.12 = (bf16[960,128]{1,0:T(8,128)(2,1)}, bf16[960,128]{1,0:T(8,128)(2,1)S(1)}, u32[]{:S(2)}, u32[]{:S(2)}) collective-permute-start(bf16[960,128]{1,0:T(8,128)(2,1)} %collective-permute-done.8.refs_2_), channel_id=1, source_target_pairs={{0,1},{1,0},{2,3},{3,2},{4,5},{5,4},{6,7},{7,6},{8,9},{9,8},{10,11... | collective-permute-start | bytes 737288 | tf_op jit(solution)/shard_map/ppermute | solution.py:269
  107.1 1.9 %collective-permute-start.11 = (bf16[960,128]{1,0:T(8,128)(2,1)}, bf16[960,128]{1,0:T(8,128)(2,1)S(1)}, u32[]{:S(2)}, u32[]{:S(2)}) collective-permute-start(bf16[960,128]{1,0:T(8,128)(2,1)} %collective-permute-done.7.refs_1_), channel_id=1, source_target_pairs={{0,1},{1,0},{2,3},{3,2},{4,5},{5,4},{6,7},{7,6},{8,9},{9,8},{10,11... | collective-permute-start | bytes 737288 | tf_op jit(solution)/shard_map/ppermute | solution.py:269
  112.5 23.5 %all-to-all-start.4 = ((bf16[8,464,128]{2,1,0:T(8,128)(2,1)}), bf16[8,464,128]{2,1,0:T(8,128)(2,1)S(1)}, u32[]{:S(2)}, u32[]{:S(2)}) async-start(bf16[8,464,128]{2,1,0:T(8,128)(2,1)} %get-tuple-element.58), calls=%async_computation.4 | async-start | bytes 1900544 | tf_op jit(solution)/shard_map/all_to_all | solution.py:203
  116.4 11.2 %collective-permute-start.19 = (bf16[960,128]{1,0:T(8,128)(2,1)S(1)}, bf16[960,128]{1,0:T(8,128)(2,1)S(1)}, u32[]{:S(2)}, u32[]{:S(2)}) collective-permute-start(bf16[960,128]{1,0:T(8,128)(2,1)S(1)} %bitcast.16), channel_id=1, source_target_pairs={{0,8},{1,9},{2,10},{3,11},{4,12},{5,13},{6,14},{7,15},{8,16},{9,17... | collective-permute-start | bytes 737288 | tf_op jit(solution)/shard_map/ppermute | solution.py:273
  116.6 14.6 %collective-permute-start.18 = (bf16[960,128]{1,0:T(8,128)(2,1)S(1)}, bf16[960,128]{1,0:T(8,128)(2,1)S(1)}, u32[]{:S(2)}, u32[]{:S(2)}) collective-permute-start(bf16[960,128]{1,0:T(8,128)(2,1)S(1)} %bitcast.17), channel_id=1, source_target_pairs={{0,16},{1,17},{2,18},{3,19},{4,20},{5,21},{6,22},{7,23},{8,24},{9,... | collective-permute-start | bytes 737288 | tf_op jit(solution)/shard_map/ppermute | solution.py:273
  118.2 13.1 %collective-permute-start.17 = (bf16[960,128]{1,0:T(8,128)(2,1)S(1)}, bf16[960,128]{1,0:T(8,128)(2,1)S(1)}, u32[]{:S(2)}, u32[]{:S(2)}) collective-permute-start(bf16[960,128]{1,0:T(8,128)(2,1)S(1)} %bitcast.18), channel_id=1, source_target_pairs={{0,24},{1,25},{2,26},{3,27},{4,28},{5,29},{6,30},{7,31},{8,0},{9,1... | collective-permute-start | bytes 737288 | tf_op jit(solution)/shard_map/ppermute | solution.py:273
  119.4 1.5 copy-start.1
  120.9 12.2 %copy-start.3 = (bf16[464,928]{1,0:T(8,128)(2,1)S(1)}, bf16[464,928]{1,0:T(8,128)(2,1)}, u32[]{:S(2)}) copy-start(bf16[464,928]{1,0:T(8,128)(2,1)} %refs_8_.1) | copy-start | bytes 2583556
  123.6 8.3 %collective-permute-start.20 = (bf16[960,128]{1,0:T(8,128)(2,1)S(1)}, bf16[960,128]{1,0:T(8,128)(2,1)S(1)}, u32[]{:S(2)}, u32[]{:S(2)}) collective-permute-start(bf16[960,128]{1,0:T(8,128)(2,1)S(1)} %bitcast.19), channel_id=1, source_target_pairs={{0,1},{1,0},{2,3},{3,2},{4,5},{5,4},{6,7},{7,6},{8,9},{9,8},{10,11... | collective-permute-start | bytes 737288 | tf_op jit(solution)/shard_map/ppermute | solution.py:269
  127.6 4.8 %collective-permute-start.23 = (bf16[960,128]{1,0:T(8,128)(2,1)S(1)}, bf16[960,128]{1,0:T(8,128)(2,1)S(1)}, u32[]{:S(2)}, u32[]{:S(2)}) collective-permute-start(bf16[960,128]{1,0:T(8,128)(2,1)S(1)} %collective-permute-done.19.refs_3_), channel_id=1, source_target_pairs={{0,1},{1,0},{2,3},{3,2},{4,5},{5,4},{6,7},{7,6},{8,9},{9,8},{10,11... | collective-permute-start | bytes 737288 | tf_op jit(solution)/shard_map/ppermute | solution.py:269
  131.2 1.5 collective-permute-start.22
  131.3 1.9 %collective-permute-start.21 = (bf16[960,128]{1,0:T(8,128)(2,1)S(1)}, bf16[960,128]{1,0:T(8,128)(2,1)S(1)}, u32[]{:S(2)}, u32[]{:S(2)}) collective-permute-start(bf16[960,128]{1,0:T(8,128)(2,1)S(1)} %collective-permute-done.17.refs_1_), channel_id=1, source_target_pairs={{0,1},{1,0},{2,3},{3,2},{4,5},{5,4},{6,7},{7,6},{8,9},{9,8},{10,11... | collective-permute-start | bytes 737288 | tf_op jit(solution)/shard_map/ppermute | solution.py:269
  136.0 19.1 %all-to-all-start.7 = ((bf16[8,464,128]{2,1,0:T(8,128)(2,1)}), bf16[8,464,128]{2,1,0:T(8,128)(2,1)S(1)}, u32[]{:S(2)}, u32[]{:S(2)}) async-start(bf16[8,464,128]{2,1,0:T(8,128)(2,1)} %get-tuple-element.70), calls=%async_computation.7 | async-start | bytes 1900544 | tf_op jit(solution)/shard_map/all_to_all | solution.py:203
  141.2 1.5 copy-start.2
